TPU v7x, 256 devices: a whole 4x4x8 slice. The times are simulated.
256 devices in a mesh: pts: 32 (over x, y, core), row: 8 (over z).
Axes of the slice: x: 4, y: 4, z: 8, core: 2. Of those that a mesh axis runs over, the one named last changes fastest.
Arguments:
- g_jets: bfloat16 [96, 9, 8192], P(None, None, 'pts'), may hold values from -6 to 6
- layer_input_jets: bfloat16 [9, 128, 8192], P(None, None, 'pts'), may hold values from -5 to 5
- speed: bfloat16 [8192], P('pts'), may hold values from 0.5 to 2
- resid: bfloat16 [8192], P('pts'), may hold values from -6 to 6
- point_index: int32 [4096], P('pts'), may hold values from 0 to 255
- damping: float32 [12, 8, 128], P(None, 'row'), may hold values from 0.5 to 4
- panel: int32 [1], replicated, may hold values from 0 to 47
Outputs:
- factor: float32 [12, 8, 128, 3, 32, 128], P(None, 'row', None, None, 'pts')
- direction: float32 [12288], replicated
All inputs are finite; a program needn't handle non-finite values.
Results may differ from a plain program's by a relative error of at most 0.0036.
Values may be sent and summed in bfloat16 or wider, within the bound.
No kernel may reach another device: no remote copies, remote signals or barrier semaphores. Data moves between devices by JAX's collectives and lax.ppermute only.
A program may use at most 192 MiB of HBM per device.

v0:
```python
import jax
import jax.numpy as jnp
from jax import lax
from jax.sharding import PartitionSpec as P


def broadcast(shard, axis, root):
    mine = lax.axis_index(axis) == root
    return lax.psum(jnp.where(mine, shard, jnp.zeros_like(shard)), axis)


def weights_of(vel):
    base = jnp.array([1.0, 2.0, 1.0], jnp.float32)
    ones = jnp.ones_like(vel)
    time_part = base[:, None] * ones[None, :]
    space_part = -base[:, None] * vel[None, :]
    return jnp.concatenate([time_part, space_part, space_part], 0)


def jacobian(gpart, hidden_portion, wts):
    mixed_derivative = gpart.astype(jnp.float32) * wts[None]
    jacobian_matrix = jnp.einsum(
        "hvf,vlf->fhl",
        mixed_derivative,
        hidden_portion.astype(jnp.float32),
        precision=lax.Precision.HIGHEST,
    )
    return jacobian_matrix.reshape(jacobian_matrix.shape[0], -1).astype(jnp.bfloat16)


def interior_rows(left, right):
    return lax.dot_general(
        left, right, (((0,), (0,)), ((), ())), preferred_element_type=jnp.float32
    )


def body(g_jets, layer_input_jets, speed, resid, point_index, damping, panel):
    rows_n = lax.axis_size("row")
    cols_n = lax.axis_size("pts")
    my_row = lax.axis_index("row")
    my_col = lax.axis_index("pts")
    units, comps, pool_len = g_jets.shape
    feats = layer_input_jets.shape[1]
    count = point_index.shape[0]
    lr_n = units // rows_n
    lc_n = units // cols_n
    g_sel = jnp.take(g_jets, point_index, axis=2)
    h_sel = jnp.take(layer_input_jets, point_index, axis=2)
    extras = jnp.stack([jnp.take(speed, point_index), jnp.take(resid, point_index)])[:, None, :]
    col_jets = lax.all_to_all(
        g_sel.reshape(lc_n, cols_n, comps, count), "pts", split_axis=1, concat_axis=3, tiled=True
    )
    col_jets = col_jets.reshape(lc_n, comps, -1)
    row_jets = lax.dynamic_index_in_dim(
        g_sel.reshape(lr_n, rows_n, comps, count), my_row, 1, keepdims=False
    )
    at = panel[0]
    owner_row = at % rows_n
    owner_col = at % cols_n
    local_row = at // rows_n
    local_col = at // cols_n
    total = count * cols_n
    row_blocks = jnp.arange(lr_n) * rows_n + my_row
    col_blocks = jnp.arange(lc_n) * cols_n + my_col
    on_diag = row_blocks[:, None] == col_blocks[None, :]
    identity = jnp.eye(feats, dtype=bool)
    diag_mask = on_diag[:, None, :, None] & identity[None, :, None, :]
    later = row_blocks > at
    same = row_blocks == at
    h_piece = lax.all_gather(h_sel, "pts", axis=2, tiled=True)
    g_piece = lax.all_gather(row_jets, "pts", axis=2, tiled=True)
    e_piece = lax.all_gather(extras, "pts", axis=2, tiled=True)
    wts = weights_of(e_piece[0, 0].astype(jnp.float32))
    jac_rows = jacobian(g_piece, h_piece, wts)
    jac_cols = jacobian(col_jets, h_piece, wts)
    core_gram_running_sum = interior_rows(jac_rows, jac_cols)
    core_grad_acc = jnp.dot(e_piece[1, 0], jac_rows, preferred_element_type=jnp.float32)
    gram_running_sum, grad_acc, jac_rows, jac_cols, wts = (
        core_gram_running_sum,
        core_grad_acc,
        jac_rows,
        jac_cols,
        wts,
    )
    gram4 = (gram_running_sum / total).reshape(lr_n, feats, lc_n, feats)
    grad2 = (grad_acc / total).reshape(lr_n, feats)
    gram4 = gram4 + jnp.where(diag_mask, damping[:, 0, :][:, :, None, None], 0.0)
    column = lax.dynamic_index_in_dim(gram4, local_col, 2, keepdims=False)
    source = broadcast(column, "pts", owner_col)
    tile = lax.dynamic_index_in_dim(source, local_row, 0, keepdims=False)
    gblock = lax.dynamic_index_in_dim(grad2, local_row, 0, keepdims=True)
    packed = broadcast(jnp.concatenate([tile, gblock], 0), "row", owner_row)
    chol = jnp.linalg.cholesky(packed[:feats])
    ysol = jax.scipy.linalg.solve_triangular(chol, packed[feats], lower=True)
    panel_rows = jax.scipy.linalg.solve_triangular(
        chol, source.reshape(lr_n * feats, feats).T, lower=True
    ).T.reshape(lr_n, feats, feats)
    proj = jnp.einsum("ibc,c->ib", panel_rows, ysol, precision=lax.Precision.HIGHEST)
    dir_rows = jnp.where(
        later[:, None], grad2 - proj, jnp.where(same[:, None], ysol[None, :], grad2)
    )
    all_panel, all_dir = (
        lax.all_gather(panel_rows[:, None], "row", axis=1, tiled=True),
        lax.all_gather(dir_rows[:, None], "row", axis=1, tiled=True),
    )
    all_panel = all_panel.reshape(lc_n, cols_n, feats, feats)
    panel_cols = lax.dynamic_index_in_dim(all_panel, my_col, 1, keepdims=False)
    direction = all_dir.reshape(-1)
    update = jnp.einsum("ibc,jdc->ibjd", panel_rows, panel_cols, precision=lax.Precision.HIGHEST)
    col_later = col_blocks > at
    col_same = col_blocks == at
    trail = (later[:, None] & col_later[None, :])[:, None, :, None]
    pcol = (later[:, None] & col_same[None, :])[:, None, :, None]
    pdiag = (same[:, None] & col_same[None, :])[:, None, :, None]
    factor = jnp.where(
        trail,
        gram4 - update,
        jnp.where(pcol, panel_rows[:, :, None, :], jnp.where(pdiag, chol[None, :, None, :], gram4)),
    )
    return (factor.reshape(lr_n, 1, feats, lc_n, 1, feats), direction)


def solution(mesh):
    in_specs = (
        P(None, None, "pts"),
        P(None, None, "pts"),
        P("pts"),
        P("pts"),
        P("pts"),
        P(None, "row", None),
        P(),
    )
    out_specs = (P(None, "row", None, None, "pts", None), P())
    return jax.shard_map(body, mesh=mesh, in_specs=in_specs, out_specs=out_specs, check_vma=False)
```

profile of v0, /device:TPU:2, one launch (start us, length us, event | category | flops | bytes accessed | tf_op | source)
XLA Modules:
  0.0 537.0 jit_solution(17519262255961541510)
XLA Ops:
  8.0 1.2 gather_fusion.2
  9.9 1.8 copy.66
  12.6 1.1 copy.67
  13.7 1.0 copy.64
  16.6 7.8 %all-to-all-start = ((bf16[3,32,9,128]{3,0,2,1:T(4,128)(2,1)}), bf16[3,32,9,128]{3,0,2,1:T(4,128)(2,1)S(1)}, u32[]{:S(2)}, u32[]{:S(2)}) async-start(bf16[3,32,9,128]{3,0,2,1:T(4,128)(2,1)} %copy.72), calls=%async_computation | async-start | bytes 589824 | tf_op jit(solution)/shard_map/all_to_all | solution.py:50
  25.3 35.3 %all-gather = bf16[12,1,9,4096]{3,1,0,2:T(2,128)(2,1)S(1)} all-gather(bf16[12,1,9,128]{3,1,0,2:T(2,128)(2,1)S(1)} %broadcast_select_fusion.1), channel_id=2, replica_groups=mesh['pts'=32,'row'=8] {'pts'}, dimensions={3}, use_global_device_ids=true | all-gather | bytes 912384 | tf_op jit(solution)/shard_map/all_gather | solution.py:71
  60.6 3.0 convert_element_type.55
  63.6 1.2 gather_fusion.3
  64.9 23.3 %all-gather.1 = bf16[2,4096]{1,0:T(2,128)(2,1)S(1)} all-gather(bf16[2,128]{1,0:T(2,128)(2,1)S(1)} %pad_maximum_fusion.1), channel_id=3, replica_groups=mesh['pts'=32,'row'=8] {'pts'}, dimensions={1}, use_global_device_ids=true | all-gather | bytes 16896 | tf_op jit(solution)/shard_map/all_gather | solution.py:72
  88.4 2.9 bitcast_multiply_fusion
  91.4 17.7 %copy.68 = f32[12,9,4096]{1,0,2:T(8,128)} copy(f32[12,9,4096]{2,0,1:T(8,128)S(1)} %bitcast_multiply_fusion) | data formatting | bytes 3538944 | tf_op jit(solution)/shard_map/mul | solution.py:21
  109.7 6.0 %copy.74 = f32[3,9,4096]{1,0,2:T(4,128)} copy(f32[3,9,4096]{2,0,1:T(4,128)S(1)} %broadcast_multiply_fusion) | data formatting | bytes 884736 | tf_op jit(solution)/shard_map/mul | solution.py:21
  115.6 23.0 %copy.69 = bf16[9,128,4096]{1,0,2:T(8,128)(2,1)} copy(bf16[9,128,4096]{2,1,0:T(8,128)(2,1)} %all-gather.6.cloned.1.call-done) | data formatting | bytes 18874368 | tf_op jit(solution)/shard_map/all_gather | solution.py:70
  138.6 27.7 %convolution_convert_fusion = bf16[4096,12,128]{2,1,0:T(8,128)(2,1)} fusion(f32[12,9,4096]{1,0,2:T(8,128)} %copy.68, bf16[9,128,4096]{1,0,2:T(8,128)(2,1)} %copy.69), kind=kOutput, calls=%fused_computation.4 | convolution fusion | flops 685768704 | bytes 23789568 | tf_op jit(solution)/shard_map/hvf,vlf->fhl/dot_general | solution.py:22
  166.3 21.2 %copy.70 = bf16[4096,12,128]{0,2,1:T(8,128)(2,1)} copy(bf16[4096,12,128]{2,1,0:T(8,128)(2,1)} %convolution_convert_fusion) | data formatting | bytes 25165824 | tf_op jit(solution)/shard_map/convert_element_type | solution.py:28
  187.5 17.6 %convolution_convert_fusion.1 = bf16[4096,3,128]{2,1,0:T(4,128)(2,1)} fusion(f32[3,9,4096]{1,0,2:T(4,128)} %copy.74, bf16[9,128,4096]{1,0,2:T(8,128)(2,1)} %copy.69), kind=kOutput, calls=%fused_computation.5 | convolution fusion | flops 171442176 | bytes 13025280 | tf_op jit(solution)/shard_map/hvf,vlf->fhl/dot_general | solution.py:22
  205.1 5.5 %copy.76 = bf16[4096,3,128]{0,2,1:T(8,128)(2,1)S(1)} copy(bf16[4096,3,128]{2,1,0:T(4,128)(2,1)} %convolution_convert_fusion.1) | data formatting | bytes 6291456 | tf_op jit(solution)/shard_map/convert_element_type | solution.py:28
  210.6 10.9 %convolution_multiply_fusion = f32[1536,384]{1,0:T(8,128)} fusion(bf16[4096,1536]{0,1:T(8,128)(2,1)} %bitcast.92, bf16[4096,384]{0,1:T(8,128)(2,1)S(1)} %bitcast.98), kind=kOutput, calls=%fused_computation.6 | convolution fusion | flops 4832428032 | bytes 18087936 | tf_op jit(solution)/shard_map/dot_general | solution.py:32
  221.4 4.6 reshape.290
  226.0 2.4 copy_add_fusion
  228.4 1.0 select_bitcast_fusion.1
  229.4 7.9 %convolution_reduce_fusion = f32[1536]{0:T(1024)S(1)} fusion(bf16[4096,1536]{0,1:T(8,128)(2,1)} %bitcast.93, bf16[2,4096]{1,0:T(2,128)(2,1)S(1)} %all-gather.1), kind=kOutput, calls=%fused_computation.10 | convolution fusion | flops 12582912 | bytes 12605440 | tf_op jit(solution)/shard_map/dot_general | solution.py:77
  237.5 108.8 %all-reduce.3.cloned.1.call-done = f32[12,128,128]{2,1,0:T(8,128)} async-done(((f32[12,128,128]{2,1,0:T(8,128)}), f32[12,128,128]{2,1,0:T(8,128)}) %all-reduce.3.cloned.1.call-update) | async-done | bytes 786448 | tf_op jit(solution)/shard_map/psum | solution.py:9
  348.2 73.0 %all-reduce.5.cloned.1.call-done = f32[129,128]{0,1:T(8,128)} async-done(((f32[129,128]{0,1:T(8,128)}), f32[129,128]{0,1:T(8,128)}) %all-reduce.5.cloned.1.call-update) | async-done | bytes 66064 | tf_op jit(solution)/shard_map/psum | solution.py:9
  423.1 11.7 %cholesky.14 = f32[128,128]{1,0:T(8,128)S(1)} custom-call(f32[128,128]{1,0:T(8,128)S(1)} %fusion.6), custom_call_target="Cholesky" | custom-call | tf_op jit(solution)/shard_map/jit(cholesky)/cholesky | solution.py:93
  436.1 9.8 %custom-call.10 = f32[1,128,128]{1,2,0:T(8,128)S(1)} custom-call(f32[1,128,128]{2,1,0:T(8,128)S(1)} %get-tuple-element.13), custom_call_target="InvertDiagBlocksLowerTriangular" | custom-call | tf_op jit(solution)/shard_map/jit(_solve_triangular)/triangular_solve | solution.py:95
  445.9 2.8 fusion.4
  449.1 1.9 fusion.10
  451.1 24.8 %all-gather.2 = f32[12,1024]{1,0:T(8,128)S(1)} all-gather(f32[12,128]{1,0:T(8,128)S(1)} %fusion.7), channel_id=4, replica_groups=mesh['pts'=32,'row'=8] {'row'}, dimensions={1}, use_global_device_ids=true | all-gather | bytes 55296 | tf_op jit(solution)/shard_map/all_gather | solution.py:104
  476.6 45.6 %all-gather.8.cloned.1.call-done = f32[12,8,128,128]{3,2,1,0:T(8,128)} async-done(((f32[12,1,128,128]{3,2,1,0:T(8,128)}), f32[12,8,128,128]{3,2,1,0:T(8,128)}) %all-gather.8.cloned.1.call-update) | async-done | bytes 6291472 | tf_op jit(solution)/shard_map/all_gather | solution.py:103
  522.2 4.1 select_bitcast_fusion
  526.3 3.8 copy.83
  (70 shorter events, 11.6 us)
Async XLA Ops:
  7.2 0.8 copy-start
  7.2 6.5 %copy-start.3 = (bf16[96,9,256]{2,0,1:T(8,128)(2,1)S(1)}, bf16[96,9,256]{2,0,1:T(8,128)(2,1)}, u32[]{:S(2)}) copy-start(bf16[96,9,256]{2,0,1:T(8,128)(2,1)} %param.10) | copy-start | bytes 1327108
  7.2 108.4 %all-gather.6.cloned.1.call-start = ((), (), s32[]{:S(2)}) async-start(), calls=%async_computation.1 | async-start | bytes 9732096 | tf_op jit(solution)/shard_map/all_gather | solution.py:70
  16.6 47.0 %copy-start.2 = (bf16[256]{0:T(256)(128)(2,1)S(1)}, bf16[256]{0:T(256)(128)(2,1)}, u32[]{:S(2)}) copy-start(bf16[256]{0:T(256)(128)(2,1)} %param.13) | copy-start | bytes 1540
  16.6 92.6 %all-to-all-start = ((bf16[3,32,9,128]{3,0,2,1:T(4,128)(2,1)}), bf16[3,32,9,128]{3,0,2,1:T(4,128)(2,1)S(1)}, u32[]{:S(2)}, u32[]{:S(2)}) async-start(bf16[3,32,9,128]{3,0,2,1:T(4,128)(2,1)} %copy.72), calls=%async_computation | async-start | bytes 589824 | tf_op jit(solution)/shard_map/all_to_all | solution.py:50
  24.4 40.5 %copy-start.7 = (f32[3]{0:T(128)S(1)}, f32[3]{0:T(128)}, u32[]{:S(2)}) copy-start(f32[3]{0:T(128)} %constant.173.clone) | copy-start | bytes 40
  24.4 63.8 %copy-start.6 = (f32[3]{0:T(128)S(1)}, f32[3]{0:T(128)}, u32[]{:S(2)}) copy-start(f32[3]{0:T(128)} %constant.175) | copy-start | bytes 40
  24.4 321.9 %all-reduce.3.cloned.1.call-start = ((), (), s32[]{:S(2)}) async-start(), calls=%async_computation.2 | async-start | bytes 1572864 | tf_op jit(solution)/shard_map/psum | solution.py:9
  91.4 17.7 %copy-start.5 = (f32[12,1,128]{2,1,0:T(1,128)S(1)}, f32[12,1,128]{2,1,0:T(1,128)}, u32[]{:S(2)}) copy-start(f32[12,1,128]{2,1,0:T(1,128)} %param.15) | copy-start | bytes 18436
  229.3 191.9 %all-reduce.5.cloned.1.call-start = ((), (), s32[]{:S(2)}) async-start(), calls=%async_computation.3 | async-start | bytes 262144 | tf_op jit(solution)/shard_map/psum | solution.py:9
  347.9 174.2 %all-gather.8.cloned.1.call-start = ((), (), s32[]{:S(2)}) async-start(), calls=%async_computation.4 | async-start | bytes 7077888 | tf_op jit(solution)/shard_map/all_gather | solution.py:103
  421.2 27.7 %copy-start.4 = (f32[129,128]{0,1:T(8,128)S(1)}, f32[129,128]{0,1:T(8,128)}, u32[]{:S(2)}) copy-start(f32[129,128]{0,1:T(8,128)} %all-reduce.5.cloned.1.call-done) | copy-start | bytes 198148
  522.2 8.0 %copy-start.1 = (bf16[256]{0:T(256)(128)(2,1)S(1)}, bf16[256]{0:T(256)(128)(2,1)}, u32[]{:S(2)}) copy-start(bf16[256]{0:T(256)(128)(2,1)} %param.12) | copy-start | bytes 1540
Sparse Core Ops, SparseCore 0:
  13.8 71.5 all-gather.5
  229.5 116.7 all-reduce.2
  349.2 71.9 all-reduce.4
  448.9 73.2 all-gather.7
where the time goes:
time: 546 us; the launch traced here: 537 us
  waiting for transfers between devices  227 us (42%)
  local copies, waits for them, and re-layouts  93.7 us (17%)
  blocking collectives  83.5 us (15%)
  matrix products  73 us (13%)
  other arithmetic  36.1 us (7%)
  between operations  15.1 us (3%)
  starting transfers between devices  8.13 us (1%)
    psum x2, waiting for transfers between devices, broadcast(): return lax.psum(jnp.where(mine, shard, jnp.zeros_like(shard)), axis)  182 us
    all_gather x1, waiting for transfers between devices, body(): lax.all_gather(panel_rows[:, None], 'row', axis=1, tiled=True)  45.6 us
    dot_general x2, matrix products, jacobian(): jnp.einsum('hvf,vlf->fhl', mixed_derivative, hidden_portion.astype(jnp.fl...  45.2 us
    all_gather x1, blocking collectives, body(): g_piece = lax.all_gather(row_jets, 'pts', axis=2, tiled=True)  35.3 us
    convert_element_type x2, local copies, waits for them, and re-layouts, jacobian(): jacobian_matrix.reshape(jacobian_matrix.shape[0], -1).astype(jnp.bfloat16)  26.7 us
    all_gather x1, blocking collectives, body(): lax.all_gather(dir_rows[:, None], 'row', axis=1, tiled=True)  24.8 us
    mul x2, local copies, waits for them, and re-layouts, jacobian(): mixed_derivative = gpart.astype(jnp.float32) * wts[None]  23.6 us
    all_gather x1, blocking collectives, body(): e_piece = lax.all_gather(extras, 'pts', axis=2, tiled=True)  23.3 us
  transfers between devices with their start and end apart: 5, of which 3 were waited for; matrix products, arithmetic and copies ran while one was open for 8% of the time, Pallas kernels for 0%

commit v1 on v0

v1 whole, which is shorter than its diff:
```python
import jax
import jax.numpy as jnp
from jax import lax
from jax.experimental import pallas as pl
from jax.experimental.pallas import tpu as pltpu
from jax.sharding import Mesh, PartitionSpec as P

NX, NY, NC, NZ = 4, 4, 2, 8
A, K, C, POOL, M = 96, 128, 9, 256, 128
LR, LC = 12, 3
TOTAL = 4096
HR = C * K
BR = 1280
ROWG, KG, VR, RR = HR, HR + 108, HR + 117, HR + 118
GC = 64
RU, CU = LR * K, LC * K
JR = RU + 2 * CU + 2 * K
J_K, J_R = RU + 2 * CU, RU + 2 * CU + K
F32, BF16 = jnp.float32, jnp.bfloat16
AXES = ("x", "y", "core", "row")
HI = lax.Precision.HIGHEST
NT = (((1,), (1,)), ((), ()))
TN = (((0,), (0,)), ((), ()))
VMEM_LIMIT = 56 * 1024 * 1024
SMEM = pl.BlockSpec(memory_space=pltpu.SMEM)
VM = pl.BlockSpec(memory_space=pltpu.VMEM)


def params():
    return pltpu.CompilerParams(vmem_limit_bytes=VMEM_LIMIT)


def pack_kernel(s_ref, idx_ref, h_ref, g_ref, v_ref, r_ref, blk_ref, col_ref, gs, tail, cbuf):
    q, core, k = s_ref[0], s_ref[1], s_ref[2]
    pool = lax.broadcasted_iota(jnp.int32, (POOL, M), 0)
    sel = (pool == idx_ref[...]).astype(F32).astype(BF16)
    for c in range(C):
        blk_ref[c * K : (c + 1) * K, :] = jnp.dot(
            h_ref[c * K : (c + 1) * K, :], sel, preferred_element_type=F32
        ).astype(BF16)
    for c in range(C):
        gs[c * A : (c + 1) * A, :] = jnp.dot(
            g_ref[c * A : (c + 1) * A, :], sel, preferred_element_type=F32
        )
    tail[...] = jnp.zeros_like(tail)
    for c in range(C):
        tail[c * LR : (c + 1) * LR, :] = gs[pl.ds(c * A + q, LR, stride=NZ), :]
        tail[108 + c : 109 + c, :] = gs[pl.ds(c * A + k, 1), :]
    tail[117:118, :] = jnp.dot(v_ref[...], sel, preferred_element_type=F32)
    tail[118:119, :] = jnp.dot(r_ref[...], sel, preferred_element_type=F32)
    blk_ref[HR:BR, :] = tail[...].astype(BF16)
    cbuf[...] = jnp.zeros_like(cbuf)
    for d in range(NX * NY):
        for c in range(C):
            for o in range(2):
                cc = core if o == 0 else 1 - core
                for lc in range(LC):
                    cbuf[c * 6 + o * LC + lc : c * 6 + o * LC + lc + 1, :] = gs[
                        pl.ds(c * A + lc * 32 + 2 * d + cc, 1), :
                    ]
        col_ref[d] = cbuf[...].astype(BF16)


def pack(scal, idx, h, g, v, r):
    return pl.pallas_call(
        pack_kernel,
        out_shape=(
            jax.ShapeDtypeStruct((BR, M), BF16),
            jax.ShapeDtypeStruct((NX * NY, GC, M), BF16),
        ),
        in_specs=[SMEM, VM, VM, VM, VM, VM],
        out_specs=(VM, VM),
        scratch_shapes=[
            pltpu.VMEM((C * A, M), F32),
            pltpu.VMEM((128, M), F32),
            pltpu.VMEM((GC, M), F32),
        ],
        compiler_params=params(),
        name="pack",
    )(scal, idx, h, g, v, r)


def coefs(rows, per, v):
    row = lax.broadcasted_iota(jnp.int32, (rows, M), 0)
    c = jnp.zeros((rows, M), jnp.int32)
    for i in range(1, C):
        c = c + (row >= per * i).astype(jnp.int32)
    base = jnp.where((c == 1) | (c == 4) | (c == 7), 2.0, 1.0)
    return jnp.where(c < 3, base, -base * v)


def chunk_kernel(first, s_ref, a_ref, b_ref, gc_ref, *refs):
    if first:
        outs, (jac, wg) = refs[:5], refs[5:]
        ins = None
    else:
        ins, outs, (jac, wg) = refs[:5], refs[5:10], refs[10:]
    for blk in range(4):
        src = a_ref if blk < 2 else b_ref
        off = (blk % 2) * BR
        tail = src[off + HR : off + BR, :].astype(F32)
        v = tail[117:118, :]
        lanes = slice(blk * M, (blk + 1) * M)
        wg[blk, 0:108, :] = tail[0:108, :] * coefs(108, LR, v)
        wg[blk, 176:185, :] = tail[108:117, :] * coefs(C, 1, v)
        gc = gc_ref[s_ref[blk]].astype(F32)
        wg[blk, 112:176, :] = gc * coefs(GC, 6, v)
        jac[J_R:JR, lanes] = jnp.zeros((JR - J_R, M), BF16)
        first_row = lax.broadcasted_iota(jnp.int32, (16, M), 0) == 0
        jac[J_R : J_R + 16, lanes] = jnp.where(first_row, tail[118:119, :], 0.0).astype(BF16)

    for blk in range(4):
        src = a_ref if blk < 2 else b_ref
        off = (blk % 2) * BR
        lanes = slice(blk * M, (blk + 1) * M)

        def slab(t, carry, src=src, off=off, lanes=lanes, blk=blk):
            base = pl.multiple_of(t * 16, 16)
            h = [src[pl.ds(off + c * K + base, 16), :].astype(F32) for c in range(C)]

            def unit(rows, dst):
                acc = wg[blk, rows[0] : rows[0] + 1, :] * h[0]
                for c in range(1, C):
                    acc = acc + wg[blk, rows[c] : rows[c] + 1, :] * h[c]
                jac[pl.ds(dst + base, 16), lanes] = acc.astype(BF16)

            for u in range(LR):
                unit([c * LR + u for c in range(C)], u * K)
            for u in range(6):
                unit([112 + c * 6 + u for c in range(C)], RU + u * K)
            unit([176 + c for c in range(C)], J_K)
            return carry

        lax.fori_loop(0, K // 16, slab, 0)

    def acc(i, rows, cols, val):
        if ins is not None:
            val = val + ins[i][rows, cols]
        outs[i][rows, cols] = val

    pd = lax.dot_general(jac[RU : J_R + 16, :], jac[J_K:J_R, :], NT, preferred_element_type=F32)
    al = slice(None)
    acc(2, al, al, pd[0:CU])
    acc(3, al, al, pd[CU : 2 * CU])
    acc(4, al, al, pd[2 * CU :])
    tile = 512
    for n in range(4):
        for m in range(RU // tile):
            rows = slice(m * tile, (m + 1) * tile)
            val = lax.dot_general(
                jac[rows, :], jac[RU + n * 256 : RU + (n + 1) * 256, :], NT,
                preferred_element_type=F32,
            )
            if n == 0:
                acc(0, rows, slice(0, 256), val)
            elif n == 1:
                acc(0, rows, slice(256, 384), val[:, :128])
                acc(1, rows, slice(0, 128), val[:, 128:])
            else:
                acc(1, rows, slice(n * 256 - 384, n * 256 - 128), val)


def chunk(first, idx, a, b, gcol, accs):
    shapes = tuple(
        jax.ShapeDtypeStruct(s, F32)
        for s in ((RU, CU), (RU, CU + 2 * K), (CU, K), (CU, K), (K + 16, K))
    )
    return pl.pallas_call(
        lambda *r: chunk_kernel(first, *r),
        out_shape=shapes,
        in_specs=[SMEM, VM, VM, VM] + [VM] * len(accs),
        out_specs=(VM,) * 5,
        scratch_shapes=[pltpu.VMEM((JR, 4 * M), BF16), pltpu.VMEM((4, 192, M), F32)],
        input_output_aliases={} if first else {4 + i: i for i in range(5)},
        compiler_params=params(),
        name="chunk_first" if first else "chunk",
    )(idx, a, b, gcol, *accs)


def chol_kernel(a_ref, b_ref, d_ref, chol_ref, w_ref, yz_ref, m_ref, u_ref):
    row = lax.broadcasted_iota(jnp.int32, (K, K), 0)
    col = lax.broadcasted_iota(jnp.int32, (K, K), 1)
    eye = row == col
    gram = (a_ref[0:K, :] + b_ref[0:K, :]) * (1.0 / TOTAL)
    m_ref[:, :K] = gram + jnp.where(eye, d_ref[0:1, :], 0.0)
    m_ref[:, K:] = jnp.where(eye, 1.0, 0.0)
    sub = lax.broadcasted_iota(jnp.int32, (8, 2 * K), 0)
    for b in range(K // 8):
        p = m_ref[8 * b : 8 * b + 8, :]
        for r in range(8):
            j = 8 * b + r
            cb = p[:, j : j + 1]
            rs = lax.rsqrt(p[r : r + 1, j : j + 1])
            urow = p[r : r + 1, :] * rs
            p = jnp.where(sub > r, p - (cb * rs) * urow, jnp.where(sub == r, urow, p))
        u_ref[8 * b : 8 * b + 8, :] = p
        if b < K // 8 - 1:
            upd = lax.dot_general(p[:, :K], p, TN, precision=HI, preferred_element_type=F32)
            lo = 8 * (b + 1)
            m_ref[lo:, :] = m_ref[lo:, :] - upd[lo:, :]
    chol_ref[...] = jnp.where(col >= row, u_ref[:, :K], 0.0).T
    w = u_ref[:, K:]
    w_ref[...] = w
    g = (a_ref[K : K + 8, :] + b_ref[K : K + 8, :]) * (1.0 / TOTAL)
    y = lax.dot_general(g, w, NT, precision=HI, preferred_element_type=F32)
    z = lax.dot_general(y, w, (((1,), (0,)), ((), ())), precision=HI, preferred_element_type=F32)
    yz_ref[0:8, :] = y
    yz_ref[8:16, :] = z


def cholesky(dk, dk2, damp):
    return pl.pallas_call(
        chol_kernel,
        out_shape=(
            jax.ShapeDtypeStruct((K, K), F32),
            jax.ShapeDtypeStruct((K, K), F32),
            jax.ShapeDtypeStruct((16, K), F32),
        ),
        in_specs=[VM] * 3,
        out_specs=(VM,) * 3,
        scratch_shapes=[pltpu.VMEM((K, 2 * K), F32), pltpu.VMEM((K, 2 * K), F32)],
        compiler_params=params(),
        name="panel_factor",
    )(dk, dk2, damp)


def final_kernel(
    s_ref, g_ref, xp_ref, xr_ref, po_ref, pr_ref, chol_ref, w_ref, yz_ref, damp_ref,
    out_ref, dir_ref, lpc,
):
    q, s, k = s_ref[0], s_ref[1], s_ref[2]
    lr = pl.program_id(0)
    inv = 1.0 / TOTAL

    @pl.when(lr == 0)
    def _():
        pc = (po_ref[...] + pr_ref[...]) * inv
        lpc[...] = lax.dot_general(pc, w_ref[...], NT, precision=HI, preferred_element_type=F32)

    i = lr * NZ + q
    pe = (xp_ref[:, CU:] + xr_ref[:, CU:]) * inv
    lpan = lax.dot_general(pe[:, :K], w_ref[...], NT, precision=HI, preferred_element_type=F32)
    upd = lax.dot_general(lpan, lpc[...], NT, precision=HI, preferred_element_type=F32)
    gram = (g_ref[...] + xr_ref[:, :CU]) * inv
    row = lax.broadcasted_iota(jnp.int32, (K, K), 0)
    col = lax.broadcasted_iota(jnp.int32, (K, K), 1)
    eye = row == col
    damp = damp_ref[pl.ds(lr, 1), :]
    for lc in range(LC):
        j = lc * (NX * NY * NC) + s
        gt = gram[:, lc * K : (lc + 1) * K] + jnp.where(eye & (i == j), damp, 0.0)
        later_row = i > k
        val = jnp.where(
            later_row & (j > k),
            gt - upd[:, lc * K : (lc + 1) * K],
            jnp.where(
                later_row & (j == k),
                lpan,
                jnp.where((i == k) & (j == k), chol_ref[...], gt),
            ),
        )
        out_ref[pl.ds(lc, K, stride=LC), :] = val
    sub = lax.broadcasted_iota(jnp.int32, (8, 2 * K), 0)
    lane = lax.broadcasted_iota(jnp.int32, (8, 2 * K), 1)
    z = yz_ref[8:9, :]
    z2 = jnp.concatenate([z, jnp.zeros_like(z)], axis=1)
    lhs = jnp.where(lane == K, 1.0, jnp.where((sub == 0) & (i > k), -z2, 0.0))
    d = lax.dot_general(lhs, pe, NT, precision=HI, preferred_element_type=F32)
    dir_ref[pl.ds(lr, 1), :] = jnp.where(i == k, yz_ref[0:1, :], d[0:1, :])


def final(scal, gown, xown, xrecv, po, pr, chol, w, yz, damp):
    full = lambda shape: pl.BlockSpec(shape, lambda i: (0,) * len(shape))
    return pl.pallas_call(
        final_kernel,
        grid=(LR,),
        out_shape=(
            jax.ShapeDtypeStruct((RU * LC, K), F32),
            jax.ShapeDtypeStruct((LR, K), F32),
        ),
        in_specs=[
            SMEM,
            pl.BlockSpec((K, CU), lambda i: (i, 0)),
            pl.BlockSpec((K, CU + 2 * K), lambda i: (i, 0)),
            pl.BlockSpec((K, CU + 2 * K), lambda i: (i, 0)),
            full((CU, K)),
            full((CU, K)),
            full((K, K)),
            full((K, K)),
            full((16, K)),
            full((LR, K)),
        ],
        out_specs=(pl.BlockSpec((K * LC, K), lambda i: (i, 0)), full((LR, K))),
        scratch_shapes=[pltpu.VMEM((CU, K), F32)],
        compiler_params=params(),
        name="trailing_update",
    )(scal, gown, xown, xrecv, po, pr, chol, w, yz, damp)


def device(x, y, c, z):
    return ((x * NY + y) * NC + c) * NZ + z


def hops(along_x_core, d):
    pairs = []
    for x in range(NX):
        for y in range(NY):
            for c in range(NC):
                for z in range(NZ):
                    to = ((x + d) % NX, y) if c == along_x_core else (x, (y + d) % NY)
                    pairs.append((device(x, y, c, z), device(*to, c, z)))
    return pairs


def body(g_jets, layer_input_jets, speed, resid, point_index, damping, panel):
    x, y = lax.axis_index("x"), lax.axis_index("y")
    core, q = lax.axis_index("core"), lax.axis_index("row")
    k = panel[0]
    s = (x * NY + y) * NC + core
    one = lambda v, d: lax.ppermute(v, AXES, hops(0, d))
    two = lambda v, d: lax.ppermute(v, AXES, hops(1, d))
    swap = lambda v: lax.ppermute(v, "core", [(0, 1), (1, 0)])

    block, gcol = pack(
        jnp.stack([q, core, k]).astype(jnp.int32),
        point_index.reshape(1, M),
        layer_input_jets.reshape(HR, POOL),
        g_jets.transpose(1, 0, 2).reshape(C * A, POOL),
        speed.reshape(1, POOL),
        resid.reshape(1, POOL),
    )
    a1, a2 = one(block, 1), one(block, -1)
    gcol = lax.all_to_all(gcol, ("x", "y"), split_axis=0, concat_axis=0, tiled=True)
    half = BR // 2
    r1, r2 = one(a1[:half], 1), one(a2[half:], -1)
    ba = jnp.concatenate([block, a1])
    bb = jnp.concatenate([a2, r1, r2])
    ma, mb = two(ba, 1), two(bb, -1)
    ba, bb, ma, mb = lax.optimization_barrier((ba, bb, ma, mb))
    na, nb = two(bb, 1), two(ba, -1)
    ra, rb = two(ma, 1), two(mb, -1)

    def sources(first, second):
        out = []
        for d1, d2 in first + second:
            sx = jnp.where(core == 0, x + d1, x + d2) % NX
            sy = jnp.where(core == 0, y + d2, y + d1) % NY
            out.append(sx * NY + sy)
        return jnp.stack(out).astype(jnp.int32)

    low, high = (0, -1), (1, 2)
    pair = lambda ds, d2: [(d, d2) for d in ds]
    accs = chunk(True, sources(pair(low, 0), pair(high, 0)), ba, bb, gcol, ())
    accs = chunk(False, sources(pair(low, -1), pair(high, 1)), ma, mb, gcol, accs)
    accs = chunk(False, sources(pair(high, -1), pair(low, 1)), na, nb, gcol, accs)
    accs = chunk(False, sources(pair(low, 2), pair(high, 2)), ra, rb, gcol, accs)
    gown, xs, po, ps, dk = accs

    dsel = lax.dynamic_index_in_dim(damping[:, 0, :], k // NZ, 0, keepdims=True)
    dsel = jnp.broadcast_to(jnp.where(k % NZ == q, dsel, 0.0), (8, K))
    for bit in (1, 2, 4):
        dsel = dsel + lax.ppermute(dsel, "row", [(i, i ^ bit) for i in range(NZ)])

    dk2 = swap(dk)
    xr = swap(xs)
    pr = swap(ps)
    chol, w, yz = cholesky(dk, dk2, dsel)
    scal = jnp.stack([q, s, k]).astype(jnp.int32)
    fac, mine = final(scal, gown, xs, xr, po, pr, chol, w, yz, damping[:, 0, :])
    slot = lax.broadcasted_iota(jnp.int32, (1, NZ, 1), 1)
    full = jnp.where(slot == q, mine[:, None, :], 0.0)
    for bit in (1, 2, 4):
        full = full + lax.ppermute(full, "row", [(i, i ^ bit) for i in range(NZ)])
    return fac.reshape(LR, 1, K, LC, 1, K), full.reshape(-1)


def solution(mesh):
    grid = Mesh(mesh.devices.reshape(NX, NY, NC, NZ), AXES)
    pts = ("x", "y", "core")
    in_specs = (
        P(None, None, pts),
        P(None, None, pts),
        P(pts),
        P(pts),
        P(pts),
        P(None, "row", None),
        P(),
    )
    out_specs = (P(None, "row", None, None, pts, None), P())
    return jax.shard_map(body, mesh=grid, in_specs=in_specs, out_specs=out_specs, check_vma=False)
```

time: 546 us -> 173 us (0.32); the launches traced: 537 us -> 170 us
  waiting for transfers between devices: 227 us -> 36.2 us
  local copies, waits for them, and re-layouts: 93.7 us -> 7.07 us
  blocking collectives: 83.5 us -> 0 us
  Pallas kernels: 0 us -> 75.6 us
  matrix products: 73 us -> 0 us
  starting transfers between devices: 8.13 us -> 42.3 us
  other arithmetic: 36.1 us -> 7.17 us
  between operations: 15.1 us -> 1.47 us
    psum x2 -> x0, waiting for transfers between devices: 182 us -> none  [broadcast(): return lax.psum(jnp.where(mine, shard, jnp.zeros_like(shard)), axis)]
    all_gather x3 -> x0, blocking collectives: 83.5 us -> none  [the longest x1 35.3 us: body(): g_piece = lax.all_gather(row_jets, 'pts', axis=2, tiled=True)]
    pallas_call x0 -> x7, Pallas kernels: none -> 75.6 us  [the longest x4 40.8 us: chunk(): pl.pallas_call(lambda *r: chunk_kernel(first, *r), out_shape=shapes, in_s...]
    dot_general x6 -> x0, matrix products: 70.1 us -> none  [the longest x2 45.2 us: jacobian(): jnp.einsum('hvf,vlf->fhl', mixed_derivative, hidden_portion.astype(jnp.fl...]
    all_gather x2 -> x0, waiting for transfers between devices: 45.6 us -> none  [the longest x1 45.6 us: body(): lax.all_gather(panel_rows[:, None], 'row', axis=1, tiled=True)]
    ppermute x0 -> x19, starting transfers between devices: none -> 35.5 us  [the longest x3 12.1 us: body(): dsel = dsel + lax.ppermute(dsel, 'row', [(i, i ^ bit) for i in range(NZ)])]
    ppermute x0 -> x19, waiting for transfers between devices: none -> 29.1 us  [the longest x6 8.68 us: body(): two = lambda v, d: lax.ppermute(v, AXES, hops(1, d))]
    convert_element_type x4 -> x0, local copies, waits for them, and re-layouts: 26.9 us -> none  [the longest x2 26.7 us: jacobian(): jacobian_matrix.reshape(jacobian_matrix.shape[0], -1).astype(jnp.bfloat16)]
  transfers between devices with their start and end apart: 5 -> 20, of which waited for: 3 -> 11; matrix products, arithmetic and copies ran while one was open for 8% -> 3% of each run, Pallas kernels for 0% -> 28%
where the time goes in v1:
time: 173 us; the launch traced here: 170 us
  Pallas kernels  75.6 us (44%)
  starting transfers between devices  42.3 us (24%)
  waiting for transfers between devices  36.2 us (21%)
  other arithmetic  7.17 us (4%)
  local copies, waits for them, and re-layouts  7.07 us (4%)
    pallas_call x4, Pallas kernels, chunk(): pl.pallas_call(lambda *r: chunk_kernel(first, *r), out_shape=shapes, in_s...  40.8 us
    pallas_call x1, Pallas kernels, cholesky(): pl.pallas_call(chol_kernel, out_shape=(jax.ShapeDtypeStruct((K, K), F32),...  17.5 us
    pallas_call x1, Pallas kernels, final(): pl.pallas_call(final_kernel, grid=(LR,), out_shape=(jax.ShapeDtypeStruct(...  14.2 us
    ppermute x3, starting transfers between devices, body(): dsel = dsel + lax.ppermute(dsel, 'row', [(i, i ^ bit) for i in range(NZ)])  12.1 us
    ppermute x3, starting transfers between devices, body(): full = full + lax.ppermute(full, 'row', [(i, i ^ bit) for i in range(NZ)])  9.05 us
    ppermute x6, waiting for transfers between devices, body(): two = lambda v, d: lax.ppermute(v, AXES, hops(1, d))  8.68 us
    ppermute x6, starting transfers between devices, body(): two = lambda v, d: lax.ppermute(v, AXES, hops(1, d))  8.63 us
    ppermute x4, waiting for transfers between devices, body(): one = lambda v, d: lax.ppermute(v, AXES, hops(0, d))  8.55 us
  transfers between devices with their start and end apart: 20, of which 11 were waited for; matrix products, arithmetic and copies ran while one was open for 3% of the time, Pallas kernels for 28%

profile of v1, /device:TPU:2, one launch (start us, length us, event | category | flops | bytes accessed | tf_op | source)
XLA Modules:
  0.0 169.8 jit_solution(11059967987689330811)
XLA Ops:
  1.3 1.2 reshape.45.v_ref
  2.5 1.2 reshape.46.r_ref
  4.4 2.9 %pack.1 = (bf16[1280,128]{1,0:T(8,128)(2,1)}, bf16[16,64,128]{2,1,0:T(8,128)(2,1)}) custom-call(s32[3]{0:T(128)} %add_add_fusion.1.s_ref, s32[1,128]{1,0:T(1,128)} %bitcast.40, bf16[1152,256]{1,0:T(8,128)(2,1)} %bitcast.37, bf16[864,256]{1,0:T(8,128)(2,1)} %bitcast.38, bf16[1,256]{1,0:T(2,128)(2,1)} %reshape.45.v_ref, bf16[1,256]{1,0:T(2,128)(2,1)} %reshape.46.r_ref), custom_call_target="tpu_custom_call" | custom-call | tf_op jit(solution)/shard_map/pack/pallas_call | solution.py:65
  7.3 1.5 collective-permute-start
  9.6 1.0 constant_dynamic-update-slice_fusion.1
  10.6 4.2 %collective-permute-done = bf16[1280,128]{1,0:T(8,128)(2,1)S(1)} collective-permute-done((bf16[1280,128]{1,0:T(8,128)(2,1)}, bf16[1280,128]{1,0:T(8,128)(2,1)S(1)}, u32[]{:S(2)}, u32[]{:S(2)}) %collective-permute-start) | collective-permute-done | bytes 327712 | tf_op jit(solution)/shard_map/ppermute | solution.py:320
  14.9 1.3 collective-permute-start.2
  16.2 2.1 %collective-permute-start.3 = (bf16[640,128]{1,0:T(8,128)(2,1)S(1)}, bf16[640,128]{1,0:T(8,128)(2,1)S(1)}, u32[]{:S(2)}, u32[]{:S(2)}) collective-permute-start(bf16[640,128]{1,0:T(8,128)(2,1)S(1)} %slice.9), channel_id=1, source_target_pairs={{0,192},{1,193},{2,194},{3,195},{4,196},{5,197},{6,198},{7,199},{8... | collective-permute-start | bytes 491528 | tf_op jit(solution)/shard_map/ppermute | solution.py:320
  18.6 4.3 %collective-permute-done.2 = bf16[640,128]{1,0:T(8,128)(2,1)S(1)} collective-permute-done((bf16[640,128]{1,0:T(8,128)(2,1)S(1)}, bf16[640,128]{1,0:T(8,128)(2,1)S(1)}, u32[]{:S(2)}, u32[]{:S(2)}) %collective-permute-start.2) | collective-permute-done | bytes 163872 | tf_op jit(solution)/shard_map/ppermute | solution.py:320
  23.0 2.0 %collective-permute-start.5 = (bf16[2560,128]{1,0:T(8,128)(2,1)S(1)}, bf16[2560,128]{1,0:T(8,128)(2,1)S(1)}, u32[]{:S(2)}, u32[]{:S(2)}) collective-permute-start(bf16[2560,128]{1,0:T(8,128)(2,1)S(1)} %constant_dynamic-update-slice_fusion.2.r_2_), channel_id=1, source_target_pairs={{0,48},{1,49},{2,50},{3,51},{4,52},{5,53},{6,54},{7,55},{8,200},{9... | collective-permute-start | bytes 1966088 | tf_op jit(solution)/shard_map/ppermute | solution.py:321
  24.9 5.3 %collective-permute-done.4.r_1_ = bf16[2560,128]{1,0:T(8,128)(2,1)S(1)} collective-permute-done((bf16[2560,128]{1,0:T(8,128)(2,1)S(1)}, bf16[2560,128]{1,0:T(8,128)(2,1)S(1)}, u32[]{:S(2)}, u32[]{:S(2)}) %collective-permute-start.4) | collective-permute-done | bytes 655392 | tf_op jit(solution)/shard_map/ppermute | solution.py:321
  30.2 3.4 %collective-permute-done.5.r_2_ = bf16[2560,128]{1,0:T(8,128)(2,1)S(1)} collective-permute-done((bf16[2560,128]{1,0:T(8,128)(2,1)S(1)}, bf16[2560,128]{1,0:T(8,128)(2,1)S(1)}, u32[]{:S(2)}, u32[]{:S(2)}) %collective-permute-start.5) | collective-permute-done | bytes 655392 | tf_op jit(solution)/shard_map/ppermute | solution.py:321
  34.1 2.8 %collective-permute-start.9 = (bf16[2560,128]{1,0:T(8,128)(2,1)S(1)}, bf16[2560,128]{1,0:T(8,128)(2,1)}, u32[]{:S(2)}, u32[]{:S(2)}) collective-permute-start(bf16[2560,128]{1,0:T(8,128)(2,1)S(1)} %constant_dynamic-update-slice_fusion.r_1_), channel_id=1, source_target_pairs={{0,48},{1,49},{2,50},{3,51},{4,52},{5,53},{6,54},{7,55},{8,200},{9... | collective-permute-start | bytes 1966088 | tf_op jit(solution)/shard_map/ppermute | solution.py:321
  36.9 3.2 %collective-permute-start.7 = (bf16[2560,128]{1,0:T(8,128)(2,1)S(1)}, bf16[2560,128]{1,0:T(8,128)(2,1)}, u32[]{:S(2)}, u32[]{:S(2)}) collective-permute-start(bf16[2560,128]{1,0:T(8,128)(2,1)S(1)} %collective-permute-done.5.r_2_), channel_id=1, source_target_pairs={{0,48},{1,49},{2,50},{3,51},{4,52},{5,53},{6,54},{7,55},{8,200},{9... | collective-permute-start | bytes 1966088 | tf_op jit(solution)/shard_map/ppermute | solution.py:321
  40.1 6.9 %all-to-all-start = ((bf16[16,64,128]{2,1,0:T(8,128)(2,1)}), bf16[16,64,128]{2,1,0:T(8,128)(2,1)S(1)}, u32[]{:S(2)}, u32[]{:S(2)}) async-start(bf16[16,64,128]{2,1,0:T(8,128)(2,1)} %get-tuple-element.36), calls=%async_computation | async-start | bytes 524288 | tf_op jit(solution)/shard_map/all_to_all | solution.py:333
  49.4 7.1 %all-to-all-done.r_3_ = bf16[16,64,128]{2,1,0:T(8,128)(2,1)S(1)} async-done(((bf16[16,64,128]{2,1,0:T(8,128)(2,1)}), bf16[16,64,128]{2,1,0:T(8,128)(2,1)S(1)}, u32[]{:S(2)}, u32[]{:S(2)}) %all-to-all-start) | async-done | bytes 262176 | tf_op jit(solution)/shard_map/all_to_all | solution.py:333
  57.1 8.7 %chunk_first.1 = (f32[1536,384]{1,0:T(8,128)}, f32[1536,640]{1,0:T(8,128)}, f32[384,128]{1,0:T(8,128)}, f32[384,128]{1,0:T(8,128)}, f32[144,128]{1,0:T(8,128)}) custom-call(s32[4]{0:T(128)} %pad_add_fusion.3.r_0_, bf16[2560,128]{1,0:T(8,128)(2,1)} %copy-done.1, bf16[2560,128]{1,0:T(8,128)(2,1)} %copy-done.2, bf16[16,64,128]{2,1,0:T(8,128)(2,1)} %copy-done), custom_call_target="tpu_custom_call" | custom-call | tf_op jit(solution)/shard_map/chunk_first/pallas_call | solution.py:168
  65.8 10.7 %chunk.3 = (f32[1536,384]{1,0:T(8,128)}, f32[1536,640]{1,0:T(8,128)}, f32[384,128]{1,0:T(8,128)}, f32[384,128]{1,0:T(8,128)}, f32[144,128]{1,0:T(8,128)}) custom-call(s32[4]{0:T(128)} %pad_add_fusion.2.r_0_, bf16[2560,128]{1,0:T(8,128)(2,1)} %copy-done.3, ...), custom_call_target="tpu_custom_call", output_to_operand_aliasing={{0}: (4, {}), {1}: (5, {}), {2}: (6, {}), {3}: (7, {}), {4}... | custom-call | tf_op jit(solution)/shard_map/chunk/pallas_call | solution.py:168
  76.6 10.7 %chunk.4 = (f32[1536,384]{1,0:T(8,128)}, f32[1536,640]{1,0:T(8,128)}, f32[384,128]{1,0:T(8,128)}, f32[384,128]{1,0:T(8,128)}, f32[144,128]{1,0:T(8,128)}) custom-call(s32[4]{0:T(128)} %pad_add_fusion.1.r_0_, bf16[2560,128]{1,0:T(8,128)(2,1)} %collective-permute-done.8.r_1_, ...), custom_call_target="tpu_custom_call", output_to_operand_aliasing={{0}: (4, {}), {1}: (5, {}), {2}: (6, {}), {3}: (7, {}), {4}... | custom-call | tf_op jit(solution)/shard_map/chunk/pallas_call | solution.py:168
  88.1 10.7 %chunk.5 = (f32[1536,384]{1,0:T(8,128)}, f32[1536,640]{1,0:T(8,128)}, f32[384,128]{1,0:T(8,128)}, f32[384,128]{1,0:T(8,128)}, f32[144,128]{1,0:T(8,128)}) custom-call(s32[4]{0:T(128)} %pad_add_fusion.r_0_, bf16[2560,128]{1,0:T(8,128)(2,1)} %copy-done.5, ...), custom_call_target="tpu_custom_call", output_to_operand_aliasing={{0}: (4, {}), {1}: (5, {}), {2}: (6, {}), {3}: (7, {}), {4}... | custom-call | tf_op jit(solution)/shard_map/chunk/pallas_call | solution.py:168
  98.9 2.0 %collective-permute-start.13 = (f32[8,128]{1,0:T(8,128)S(1)}, f32[8,128]{1,0:T(8,128)S(1)}, u32[]{:S(2)}, u32[]{:S(2)}) collective-permute-start(f32[8,128]{1,0:T(8,128)S(1)} %broadcast_in_dim.31), channel_id=1, source_target_pairs={{0,1},{1,0},{2,3},{3,2},{4,5},{5,4},{6,7},{7,6},{8,9},{9,8},{10,11... | collective-permute-start | bytes 12296 | tf_op jit(solution)/shard_map/ppermute | solution.py:362
  100.9 1.7 %collective-permute-done.13 = f32[8,128]{1,0:T(8,128)S(1)} collective-permute-done((f32[8,128]{1,0:T(8,128)S(1)}, f32[8,128]{1,0:T(8,128)S(1)}, u32[]{:S(2)}, u32[]{:S(2)}) %collective-permute-start.13) | collective-permute-done | bytes 4128 | tf_op jit(solution)/shard_map/ppermute | solution.py:362
  102.6 3.3 %collective-permute-start.14 = (f32[8,128]{1,0:T(8,128)S(1)}, f32[8,128]{1,0:T(8,128)S(1)}, u32[]{:S(2)}, u32[]{:S(2)}) collective-permute-start(f32[8,128]{1,0:T(8,128)S(1)} %broadcast_add_fusion), channel_id=1, source_target_pairs={{0,2},{1,3},{2,0},{3,1},{4,6},{5,7},{6,4},{7,5},{8,10},{9,11},{10,... | collective-permute-start | bytes 12296 | tf_op jit(solution)/shard_map/ppermute | solution.py:362
  105.9 1.6 collective-permute-done.14
  107.5 6.8 %collective-permute-start.15 = (f32[8,128]{1,0:T(8,128)S(1)}, f32[8,128]{1,0:T(8,128)S(1)}, u32[]{:S(2)}, u32[]{:S(2)}) collective-permute-start(f32[8,128]{1,0:T(8,128)S(1)} %fusion.3), channel_id=1, source_target_pairs={{0,4},{1,5},{2,6},{3,7},{4,0},{5,1},{6,2},{7,3},{8,12},{9,13},{10,... | collective-permute-start | bytes 12296 | tf_op jit(solution)/shard_map/ppermute | solution.py:362
  117.1 17.5 %panel_factor.1 = (f32[128,128]{1,0:T(8,128)}, f32[128,128]{1,0:T(8,128)}, f32[16,128]{1,0:T(8,128)}) custom-call(f32[144,128]{1,0:T(8,128)} %get-tuple-element.58.a_ref, f32[144,128]{1,0:T(8,128)} %copy-done.7, f32[8,128]{1,0:T(8,128)} %add.297.d_ref), custom_call_target="tpu_custom_call" | custom-call | tf_op jit(solution)/shard_map/panel_factor/pallas_call | solution.py:212
  135.4 14.2 %trailing_update.1 = (f32[4608,128]{1,0:T(8,128)}, f32[12,128]{1,0:T(8,128)}) custom-call(s32[3]{0:T(128)} %add_add_fusion.s_ref, f32[1536,384]{1,0:T(8,128)} %get-tuple-element.54.g_ref, f32[1536,640]{1,0:T(8,128)} %get-tuple-element.55.xp_ref, f32[1536,640]{1,0:T(8,128)} %collective-permute-done.10.xr_ref, f32[384,128]{1,0:T(8,128)} %get-tuple-element.56.po_ref, ...), custom_call_target="tpu_custom_call" | custom-call | tf_op jit(solution)/shard_map/trailing_update/pallas_call | solution.py:274
  151.4 3.1 %collective-permute-done.16 = f32[12,8,128]{2,1,0:T(8,128)S(1)} collective-permute-done((f32[12,8,128]{2,1,0:T(8,128)S(1)}, f32[12,8,128]{2,1,0:T(8,128)S(1)}, u32[]{:S(2)}, u32[]{:S(2)}) %collective-permute-start.16) | collective-permute-done | bytes 49184 | tf_op jit(solution)/shard_map/ppermute | solution.py:373
  155.2 2.1 %collective-permute-start.17 = (f32[12,8,128]{2,1,0:T(8,128)S(1)}, f32[12,8,128]{2,1,0:T(8,128)S(1)}, u32[]{:S(2)}, u32[]{:S(2)}) collective-permute-start(f32[12,8,128]{2,1,0:T(8,128)S(1)} %fusion), channel_id=1, source_target_pairs={{0,2},{1,3},{2,0},{3,1},{4,6},{5,7},{6,4},{7,5},{8,10},{9,11},{10,... | collective-permute-start | bytes 147464 | tf_op jit(solution)/shard_map/ppermute | solution.py:373
  157.3 3.0 %collective-permute-done.17 = f32[12,8,128]{2,1,0:T(8,128)S(1)} collective-permute-done((f32[12,8,128]{2,1,0:T(8,128)S(1)}, f32[12,8,128]{2,1,0:T(8,128)S(1)}, u32[]{:S(2)}, u32[]{:S(2)}) %collective-permute-start.17) | collective-permute-done | bytes 49184 | tf_op jit(solution)/shard_map/ppermute | solution.py:373
  161.0 6.0 %collective-permute-start.18 = (f32[12,8,128]{2,1,0:T(8,128)S(1)}, f32[12,8,128]{2,1,0:T(8,128)S(1)}, u32[]{:S(2)}, u32[]{:S(2)}) collective-permute-start(f32[12,8,128]{2,1,0:T(8,128)S(1)} %fusion.2), channel_id=1, source_target_pairs={{0,4},{1,5},{2,6},{3,7},{4,0},{5,1},{6,2},{7,3},{8,12},{9,13},{10,... | collective-permute-start | bytes 147464 | tf_op jit(solution)/shard_map/ppermute | solution.py:373
  167.0 2.2 %collective-permute-done.18 = f32[12,8,128]{2,1,0:T(8,128)S(1)} collective-permute-done((f32[12,8,128]{2,1,0:T(8,128)S(1)}, f32[12,8,128]{2,1,0:T(8,128)S(1)}, u32[]{:S(2)}, u32[]{:S(2)}) %collective-permute-start.18) | collective-permute-done | bytes 49184 | tf_op jit(solution)/shard_map/ppermute | solution.py:373
  (59 shorter events, 13.6 us)
Async XLA Ops:
  7.3 7.5 %collective-permute-start = (bf16[1280,128]{1,0:T(8,128)(2,1)}, bf16[1280,128]{1,0:T(8,128)(2,1)S(1)}, u32[]{:S(2)}, u32[]{:S(2)}) collective-permute-start(bf16[1280,128]{1,0:T(8,128)(2,1)} %get-tuple-element.33), channel_id=1, source_target_pairs={{0,64},{1,65},{2,66},{3,67},{4,68},{5,69},{6,70},{7,71},{8,24},{9,... | collective-permute-start | bytes 983048 | tf_op jit(solution)/shard_map/ppermute | solution.py:320
  8.8 7.4 %collective-permute-start.1 = (bf16[1280,128]{1,0:T(8,128)(2,1)}, bf16[1280,128]{1,0:T(8,128)(2,1)S(1)}, u32[]{:S(2)}, u32[]{:S(2)}) collective-permute-start(bf16[1280,128]{1,0:T(8,128)(2,1)} %get-tuple-element.33), channel_id=1, source_target_pairs={{0,192},{1,193},{2,194},{3,195},{4,196},{5,197},{6,198},{7,199},{8... | collective-permute-start | bytes 983048 | tf_op jit(solution)/shard_map/ppermute | solution.py:320
  14.9 8.0 %collective-permute-start.2 = (bf16[640,128]{1,0:T(8,128)(2,1)S(1)}, bf16[640,128]{1,0:T(8,128)(2,1)S(1)}, u32[]{:S(2)}, u32[]{:S(2)}) collective-permute-start(bf16[640,128]{1,0:T(8,128)(2,1)S(1)} %slice.8), channel_id=1, source_target_pairs={{0,64},{1,65},{2,66},{3,67},{4,68},{5,69},{6,70},{7,71},{8,24},{9,... | collective-permute-start | bytes 491528 | tf_op jit(solution)/shard_map/ppermute | solution.py:320
  16.2 6.7 %collective-permute-start.3 = (bf16[640,128]{1,0:T(8,128)(2,1)S(1)}, bf16[640,128]{1,0:T(8,128)(2,1)S(1)}, u32[]{:S(2)}, u32[]{:S(2)}) collective-permute-start(bf16[640,128]{1,0:T(8,128)(2,1)S(1)} %slice.9), channel_id=1, source_target_pairs={{0,192},{1,193},{2,194},{3,195},{4,196},{5,197},{6,198},{7,199},{8... | collective-permute-start | bytes 491528 | tf_op jit(solution)/shard_map/ppermute | solution.py:320
  18.4 38.1 %copy-start.1 = (bf16[2560,128]{1,0:T(8,128)(2,1)}, bf16[2560,128]{1,0:T(8,128)(2,1)S(1)}, u32[]{:S(2)}) copy-start(bf16[2560,128]{1,0:T(8,128)(2,1)S(1)} %constant_dynamic-update-slice_fusion.r_1_) | copy-start | bytes 1966084
  18.4 11.9 %collective-permute-start.4 = (bf16[2560,128]{1,0:T(8,128)(2,1)S(1)}, bf16[2560,128]{1,0:T(8,128)(2,1)S(1)}, u32[]{:S(2)}, u32[]{:S(2)}) collective-permute-start(bf16[2560,128]{1,0:T(8,128)(2,1)S(1)} %constant_dynamic-update-slice_fusion.r_1_), channel_id=1, source_target_pairs={{0,16},{1,17},{2,18},{3,19},{4,20},{5,21},{6,22},{7,23},{8,72},{9,... | collective-permute-start | bytes 1966088 | tf_op jit(solution)/shard_map/ppermute | solution.py:321
  23.0 33.5 %copy-start.2 = (bf16[2560,128]{1,0:T(8,128)(2,1)}, bf16[2560,128]{1,0:T(8,128)(2,1)S(1)}, u32[]{:S(2)}) copy-start(bf16[2560,128]{1,0:T(8,128)(2,1)S(1)} %constant_dynamic-update-slice_fusion.2.r_2_) | copy-start | bytes 1966084
  23.0 10.7 %collective-permute-start.5 = (bf16[2560,128]{1,0:T(8,128)(2,1)S(1)}, bf16[2560,128]{1,0:T(8,128)(2,1)S(1)}, u32[]{:S(2)}, u32[]{:S(2)}) collective-permute-start(bf16[2560,128]{1,0:T(8,128)(2,1)S(1)} %constant_dynamic-update-slice_fusion.2.r_2_), channel_id=1, source_target_pairs={{0,48},{1,49},{2,50},{3,51},{4,52},{5,53},{6,54},{7,55},{8,200},{9... | collective-permute-start | bytes 1966088 | tf_op jit(solution)/shard_map/ppermute | solution.py:321
  30.2 35.6 %copy-start.3 = (bf16[2560,128]{1,0:T(8,128)(2,1)}, bf16[2560,128]{1,0:T(8,128)(2,1)S(1)}, u32[]{:S(2)}) copy-start(bf16[2560,128]{1,0:T(8,128)(2,1)S(1)} %collective-permute-done.4.r_1_) | copy-start | bytes 1966084
  33.6 32.2 %copy-start.4 = (bf16[2560,128]{1,0:T(8,128)(2,1)}, bf16[2560,128]{1,0:T(8,128)(2,1)S(1)}, u32[]{:S(2)}) copy-start(bf16[2560,128]{1,0:T(8,128)(2,1)S(1)} %collective-permute-done.5.r_2_) | copy-start | bytes 1966084
  33.6 42.9 %collective-permute-start.8 = (bf16[2560,128]{1,0:T(8,128)(2,1)S(1)}, bf16[2560,128]{1,0:T(8,128)(2,1)}, u32[]{:S(2)}, u32[]{:S(2)}) collective-permute-start(bf16[2560,128]{1,0:T(8,128)(2,1)S(1)} %constant_dynamic-update-slice_fusion.2.r_2_), channel_id=1, source_target_pairs={{0,16},{1,17},{2,18},{3,19},{4,20},{5,21},{6,22},{7,23},{8,72},{9,... | collective-permute-start | bytes 1966088 | tf_op jit(solution)/shard_map/ppermute | solution.py:321
  34.1 42.4 %collective-permute-start.9 = (bf16[2560,128]{1,0:T(8,128)(2,1)S(1)}, bf16[2560,128]{1,0:T(8,128)(2,1)}, u32[]{:S(2)}, u32[]{:S(2)}) collective-permute-start(bf16[2560,128]{1,0:T(8,128)(2,1)S(1)} %constant_dynamic-update-slice_fusion.r_1_), channel_id=1, source_target_pairs={{0,48},{1,49},{2,50},{3,51},{4,52},{5,53},{6,54},{7,55},{8,200},{9... | collective-permute-start | bytes 1966088 | tf_op jit(solution)/shard_map/ppermute | solution.py:321
  36.9 50.4 %collective-permute-start.6 = (bf16[2560,128]{1,0:T(8,128)(2,1)S(1)}, bf16[2560,128]{1,0:T(8,128)(2,1)S(1)}, u32[]{:S(2)}, u32[]{:S(2)}) collective-permute-start(bf16[2560,128]{1,0:T(8,128)(2,1)S(1)} %collective-permute-done.4.r_1_), channel_id=1, source_target_pairs={{0,16},{1,17},{2,18},{3,19},{4,20},{5,21},{6,22},{7,23},{8,72},{9,... | collective-permute-start | bytes 1966088 | tf_op jit(solution)/shard_map/ppermute | solution.py:321
  36.9 50.4 %collective-permute-start.7 = (bf16[2560,128]{1,0:T(8,128)(2,1)S(1)}, bf16[2560,128]{1,0:T(8,128)(2,1)}, u32[]{:S(2)}, u32[]{:S(2)}) collective-permute-start(bf16[2560,128]{1,0:T(8,128)(2,1)S(1)} %collective-permute-done.5.r_2_), channel_id=1, source_target_pairs={{0,48},{1,49},{2,50},{3,51},{4,52},{5,53},{6,54},{7,55},{8,200},{9... | collective-permute-start | bytes 1966088 | tf_op jit(solution)/shard_map/ppermute | solution.py:321
  40.1 16.3 %all-to-all-start = ((bf16[16,64,128]{2,1,0:T(8,128)(2,1)}), bf16[16,64,128]{2,1,0:T(8,128)(2,1)S(1)}, u32[]{:S(2)}, u32[]{:S(2)}) async-start(bf16[16,64,128]{2,1,0:T(8,128)(2,1)} %get-tuple-element.36), calls=%async_computation | async-start | bytes 524288 | tf_op jit(solution)/shard_map/all_to_all | solution.py:333
  56.4 0.7 copy-start
  87.3 0.8 copy-start.5
  88.1 10.8 %copy-start.8 = (f32[12,1,128]{2,1,0:T(1,128)S(1)}, f32[12,1,128]{2,1,0:T(1,128)}, u32[]{:S(2)}) copy-start(f32[12,1,128]{2,1,0:T(1,128)} %param.12) | copy-start | bytes 18436
  98.8 35.8 %collective-permute-start.10 = (f32[1536,640]{1,0:T(8,128)}, f32[1536,640]{1,0:T(8,128)}, u32[]{:S(2)}, u32[]{:S(2)}) collective-permute-start(f32[1536,640]{1,0:T(8,128)} %get-tuple-element.55.xp_ref), channel_id=1, source_target_pairs={{0,8},{8,0},{1,9},{9,1},{2,10},{10,2},{3,11},{11,3},{4,12},{12,4},... | collective-permute-start | bytes 11796488 | tf_op jit(solution)/shard_map/ppermute | solution.py:322
  98.9 3.7 %collective-permute-start.13 = (f32[8,128]{1,0:T(8,128)S(1)}, f32[8,128]{1,0:T(8,128)S(1)}, u32[]{:S(2)}, u32[]{:S(2)}) collective-permute-start(f32[8,128]{1,0:T(8,128)S(1)} %broadcast_in_dim.31), channel_id=1, source_target_pairs={{0,1},{1,0},{2,3},{3,2},{4,5},{5,4},{6,7},{7,6},{8,9},{9,8},{10,11... | collective-permute-start | bytes 12296 | tf_op jit(solution)/shard_map/ppermute | solution.py:362
  102.6 4.9 %collective-permute-start.14 = (f32[8,128]{1,0:T(8,128)S(1)}, f32[8,128]{1,0:T(8,128)S(1)}, u32[]{:S(2)}, u32[]{:S(2)}) collective-permute-start(f32[8,128]{1,0:T(8,128)S(1)} %broadcast_add_fusion), channel_id=1, source_target_pairs={{0,2},{1,3},{2,0},{3,1},{4,6},{5,7},{6,4},{7,5},{8,10},{9,11},{10,... | collective-permute-start | bytes 12296 | tf_op jit(solution)/shard_map/ppermute | solution.py:362
  105.9 28.8 %collective-permute-start.11 = (f32[384,128]{1,0:T(8,128)}, f32[384,128]{1,0:T(8,128)S(1)}, u32[]{:S(2)}, u32[]{:S(2)}) collective-permute-start(f32[384,128]{1,0:T(8,128)} %get-tuple-element.57), channel_id=1, source_target_pairs={{0,8},{8,0},{1,9},{9,1},{2,10},{10,2},{3,11},{11,3},{4,12},{12,4},... | collective-permute-start | bytes 589832 | tf_op jit(solution)/shard_map/ppermute | solution.py:322
  107.5 8.4 %collective-permute-start.15 = (f32[8,128]{1,0:T(8,128)S(1)}, f32[8,128]{1,0:T(8,128)S(1)}, u32[]{:S(2)}, u32[]{:S(2)}) collective-permute-start(f32[8,128]{1,0:T(8,128)S(1)} %fusion.3), channel_id=1, source_target_pairs={{0,4},{1,5},{2,6},{3,7},{4,0},{5,1},{6,2},{7,3},{8,12},{9,13},{10,... | collective-permute-start | bytes 12296 | tf_op jit(solution)/shard_map/ppermute | solution.py:362
  114.3 2.2 %collective-permute-start.12 = (f32[144,128]{1,0:T(8,128)}, f32[144,128]{1,0:T(8,128)S(1)}, u32[]{:S(2)}, u32[]{:S(2)}) collective-permute-start(f32[144,128]{1,0:T(8,128)} %get-tuple-element.58.a_ref), channel_id=1, source_target_pairs={{0,8},{8,0},{1,9},{9,1},{2,10},{10,2},{3,11},{11,3},{4,12},{12,4},... | collective-permute-start | bytes 221192 | tf_op jit(solution)/shard_map/ppermute | solution.py:322
  116.5 0.6 copy-start.7
  134.7 0.7 copy-start.6
  150.4 4.1 %collective-permute-start.16 = (f32[12,8,128]{2,1,0:T(8,128)S(1)}, f32[12,8,128]{2,1,0:T(8,128)S(1)}, u32[]{:S(2)}, u32[]{:S(2)}) collective-permute-start(f32[12,8,128]{2,1,0:T(8,128)S(1)} %broadcast_select_fusion), channel_id=1, source_target_pairs={{0,1},{1,0},{2,3},{3,2},{4,5},{5,4},{6,7},{7,6},{8,9},{9,8},{10,11... | collective-permute-start | bytes 147464 | tf_op jit(solution)/shard_map/ppermute | solution.py:373
  155.2 5.0 %collective-permute-start.17 = (f32[12,8,128]{2,1,0:T(8,128)S(1)}, f32[12,8,128]{2,1,0:T(8,128)S(1)}, u32[]{:S(2)}, u32[]{:S(2)}) collective-permute-start(f32[12,8,128]{2,1,0:T(8,128)S(1)} %fusion), channel_id=1, source_target_pairs={{0,2},{1,3},{2,0},{3,1},{4,6},{5,7},{6,4},{7,5},{8,10},{9,11},{10,... | collective-permute-start | bytes 147464 | tf_op jit(solution)/shard_map/ppermute | solution.py:373
  161.0 8.2 %collective-permute-start.18 = (f32[12,8,128]{2,1,0:T(8,128)S(1)}, f32[12,8,128]{2,1,0:T(8,128)S(1)}, u32[]{:S(2)}, u32[]{:S(2)}) collective-permute-start(f32[12,8,128]{2,1,0:T(8,128)S(1)} %fusion.2), channel_id=1, source_target_pairs={{0,4},{1,5},{2,6},{3,7},{4,0},{5,1},{6,2},{7,3},{8,12},{9,13},{10,... | collective-permute-start | bytes 147464 | tf_op jit(solution)/shard_map/ppermute | solution.py:373

commit v2 on v1

v2 whole, which is shorter than its diff:
```python
import jax
import jax.numpy as jnp
from jax import lax
from jax.experimental import pallas as pl
from jax.experimental.pallas import tpu as pltpu
from jax.sharding import Mesh, PartitionSpec as P

NX, NY, NC, NZ = 4, 4, 2, 8
A, K, C, POOL, M = 96, 128, 9, 256, 128
LR, LC = 12, 3
TOTAL = 4096
HR = C * K
BR = 1280
ROWG, KG, VR, RR = HR, HR + 108, HR + 117, HR + 118
GC = 64
HB = BR // 2
PR = BR + 6 * GC
MR = 2 * BR + 3 * GC
RU, CU = LR * K, LC * K
JR = RU + 2 * CU + 2 * K
J_K, J_R = RU + 2 * CU, RU + 2 * CU + K
F32, BF16 = jnp.float32, jnp.bfloat16
AXES = ("x", "y", "core", "row")
HI = lax.Precision.HIGHEST
NT = (((1,), (1,)), ((), ()))
TN = (((0,), (0,)), ((), ()))
VMEM_LIMIT = 20 * 1024 * 1024
SMEM = pl.BlockSpec(memory_space=pltpu.SMEM)
VM = pl.BlockSpec(memory_space=pltpu.VMEM)
ANY = pl.BlockSpec(memory_space=pl.ANY)


def params():
    return pltpu.CompilerParams(vmem_limit_bytes=VMEM_LIMIT)


def pack_kernel(k_ref, idx_ref, h_ref, g_ref, vr_ref, plus_ref, minus_ref, own_ref, gs, tail, cbuf):
    x, y = lax.axis_index("x"), lax.axis_index("y")
    core, q = lax.axis_index("core"), lax.axis_index("row")
    k = k_ref[0]
    pool = lax.broadcasted_iota(jnp.int32, (POOL, M), 0)
    sel = (pool == idx_ref[...]).astype(F32).astype(BF16)
    for c in range(C):
        val = jnp.dot(h_ref[c * K : (c + 1) * K, :], sel, preferred_element_type=F32).astype(BF16)
        lo = c * K if c < 5 else c * K + 2 * GC
        plus_ref[lo : lo + K, :] = val
        lo = c * K + HB + 2 * GC if c < 5 else c * K - HB
        minus_ref[lo : lo + K, :] = val
    for c in range(C):
        gs[c * A : (c + 1) * A, :] = jnp.dot(
            g_ref[c * A : (c + 1) * A, :], sel, preferred_element_type=F32
        )
    tail[...] = jnp.zeros_like(tail)
    for c in range(C):
        tail[c * LR : (c + 1) * LR, :] = gs[pl.ds(c * A + q, LR, stride=NZ), :]
        tail[108 + c : 109 + c, :] = gs[pl.ds(c * A + k, 1), :]
    tail[117:119, :] = jnp.dot(vr_ref[...], sel, preferred_element_type=F32)
    val = tail[...].astype(BF16)
    plus_ref[HR + 2 * GC : BR + 2 * GC, :] = val
    minus_ref[HR - HB : HB, :] = val
    cbuf[...] = jnp.zeros_like(cbuf)
    for dp in range(4):
        for dt in range(4):
            px = lax.rem(jnp.where(core == 0, x + dp, x + dt), NX)
            py = lax.rem(jnp.where(core == 0, y + dt, y + dp), NY)
            d = px * NY + py
            for c in range(C):
                for o in range(2):
                    cc = core if o == 0 else 1 - core
                    for lc in range(LC):
                        row = c * 6 + o * LC + lc
                        cbuf[row : row + 1, :] = gs[pl.ds(c * A + lc * 32 + 2 * d + cc, 1), :]
            val = cbuf[...].astype(BF16)
            if dp == 0:
                own_ref[dt * GC : (dt + 1) * GC, :] = val
            elif dp == 1:
                plus_ref[BR + (2 + dt) * GC : BR + (3 + dt) * GC, :] = val
            elif dp == 3:
                minus_ref[BR + (2 + dt) * GC : BR + (3 + dt) * GC, :] = val
            elif dt < 2:
                plus_ref[HB + dt * GC : HB + (dt + 1) * GC, :] = val
            else:
                minus_ref[HB + (dt - 2) * GC : HB + (dt - 1) * GC, :] = val


def pack(k, idx, h, g, vr):
    return pl.pallas_call(
        pack_kernel,
        out_shape=(
            jax.ShapeDtypeStruct((PR, M), BF16),
            jax.ShapeDtypeStruct((PR, M), BF16),
            jax.ShapeDtypeStruct((4 * GC, M), BF16),
        ),
        in_specs=[SMEM, VM, VM, VM, VM],
        out_specs=(VM,) * 3,
        scratch_shapes=[
            pltpu.VMEM((C * A, M), F32),
            pltpu.VMEM((128, M), F32),
            pltpu.VMEM((GC, M), F32),
        ],
        compiler_params=params(),
        name="pack",
    )(k, idx, h, g, vr)


def block_from_plus(i, cols):
    return ([(i, 0, HB), (i, HB + 2 * GC, HB)], cols)


def block_from_minus(i, cols):
    return ([(i, HB + 2 * GC, HB), (i, 0, HB)], cols)


def after(i, lo):
    return [(i, lo + e * GC) for e in range(4)]


BLOCK0 = block_from_plus(0, after(1, 0))
BLOCK1 = block_from_plus(2, after(2, BR + 2 * GC))
BLOCK2 = block_from_minus(0, after(0, BR + 2 * GC))
BLOCK3 = (
    [(1, 0, HB), (2, 0, HB)],
    [(1, HB), (1, HB + GC), (2, HB), (2, HB + GC)],
)


def message(first, second, e):
    out, at = [], 0
    for i, lo, n in first[0]:
        out.append((i, lo, n, at))
        at += n
    out.append((*first[1][2], GC, at))
    at += GC
    for i, lo, n in second[0]:
        out.append((i, lo, n, at))
        at += n
    for blk in (first, second):
        out.append((*blk[1][e], GC, at))
        at += GC
    return out


def assemble_kernel(plans, n_in, *refs):
    ins, outs, sem = refs[:n_in], refs[n_in:-1], refs[-1]
    copies, i = [], 0
    for plan, out in zip(plans, outs):
        for src, lo, n, at in plan:
            copies.append(
                pltpu.make_async_copy(ins[src].at[lo : lo + n, :], out.at[at : at + n, :], sem.at[i])
            )
            i += 1
    for cp in copies:
        cp.start()
    for cp in copies:
        cp.wait()


def assemble(first, second, *ins):
    plans = (message(first, second, 1), message(second, first, 3))
    return pl.pallas_call(
        lambda *r: assemble_kernel(plans, len(ins), *r),
        out_shape=(jax.ShapeDtypeStruct((MR, M), BF16),) * 2,
        in_specs=[ANY] * len(ins),
        out_specs=(ANY,) * 2,
        scratch_shapes=[pltpu.SemaphoreType.DMA((sum(len(p) for p in plans),))],
        name="assemble",
    )(*ins)


def coefs(rows, per, v):
    row = lax.broadcasted_iota(jnp.int32, (rows, M), 0)
    c = jnp.zeros((rows, M), jnp.int32)
    for i in range(1, C):
        c = c + (row >= per * i).astype(jnp.int32)
    base = jnp.where((c == 1) | (c == 4) | (c == 7), 2.0, 1.0)
    return jnp.where(c < 3, base, -base * v)


ACCS = ((RU, CU), (RU, CU), (RU, 2 * K), (CU, K), (CU, K), (K + 16, K))


def chunk_kernel(blocks, n_in, n_acc, *refs):
    arrs, ins = refs[:n_in], refs[n_in : n_in + n_acc]
    outs, (jac, wg) = refs[n_in + n_acc : -2], refs[-2:]
    for blk, (hs, tl, cl) in enumerate(blocks):
        tail = arrs[tl[0]][tl[1] : tl[1] + 128, :].astype(F32)
        v = tail[117:118, :]
        lanes = slice(blk * M, (blk + 1) * M)
        wg[blk, 0:108, :] = tail[0:108, :] * coefs(108, LR, v)
        wg[blk, 176:185, :] = tail[108:117, :] * coefs(C, 1, v)
        gc = arrs[cl[0]][cl[1] : cl[1] + GC, :].astype(F32)
        wg[blk, 112:176, :] = gc * coefs(GC, 6, v)
        jac[J_R:JR, lanes] = jnp.zeros((JR - J_R, M), BF16)
        first_row = lax.broadcasted_iota(jnp.int32, (16, M), 0) == 0
        jac[J_R : J_R + 16, lanes] = jnp.where(first_row, tail[118:119, :], 0.0).astype(BF16)

    for blk, (hs, tl, cl) in enumerate(blocks):
        lanes = slice(blk * M, (blk + 1) * M)

        def slab(t, carry, hs=hs, lanes=lanes, blk=blk):
            base = pl.multiple_of(t * 16, 16)
            h = [arrs[i][pl.ds(lo + base, 16), :].astype(F32) for i, lo in hs]

            def unit(rows, dst):
                acc = wg[blk, rows[0] : rows[0] + 1, :] * h[0]
                for c in range(1, C):
                    acc = acc + wg[blk, rows[c] : rows[c] + 1, :] * h[c]
                jac[pl.ds(dst + base, 16), lanes] = acc.astype(BF16)

            for u in range(LR):
                unit([c * LR + u for c in range(C)], u * K)
            for u in range(6):
                unit([112 + c * 6 + u for c in range(C)], RU + u * K)
            unit([176 + c for c in range(C)], J_K)
            return carry

        lax.fori_loop(0, K // 16, slab, 0)

    def acc(i, rows, cols, val):
        if n_acc:
            val = val + ins[i][rows, cols]
        outs[i][rows, cols] = val

    al = slice(None)
    pd = lax.dot_general(jac[RU : J_R + 16, :], jac[J_K:J_R, :], NT, preferred_element_type=F32)
    acc(3, al, al, pd[0:CU])
    acc(4, al, al, pd[CU : 2 * CU])
    acc(5, al, al, pd[2 * CU :])
    tile = 512
    for n in (3, 0, 1, 2):
        for m in range(RU // tile):
            rows = slice(m * tile, (m + 1) * tile)
            val = lax.dot_general(
                jac[rows, :], jac[RU + n * 256 : RU + (n + 1) * 256, :], NT,
                preferred_element_type=F32,
            )
            if n == 0:
                acc(0, rows, slice(0, 256), val)
            elif n == 1:
                acc(0, rows, slice(256, 384), val[:, :128])
                acc(1, rows, slice(0, 128), val[:, 128:])
            elif n == 2:
                acc(1, rows, slice(128, 384), val)
            else:
                acc(2, rows, al, val)


def chunk(blocks, arrs, accs, name):
    n = len(blocks)
    return pl.pallas_call(
        lambda *r: chunk_kernel(blocks, len(arrs), len(accs), *r),
        out_shape=tuple(jax.ShapeDtypeStruct(s, F32) for s in ACCS),
        in_specs=[VM] * (len(arrs) + len(accs)),
        out_specs=(VM,) * len(ACCS),
        scratch_shapes=[pltpu.VMEM((JR, n * M), BF16), pltpu.VMEM((n, 192, M), F32)],
        compiler_params=params(),
        name=name,
    )(*arrs, *accs)


def place(block, e, shift):
    hs, rows = [], [(i, lo + r) for i, lo, n in block[0] for r in range(0, n, K)]
    rows = [(i + shift, lo) for i, lo in rows]
    i, lo = block[1][e]
    return rows[:C], rows[C], (i + shift, lo)


def received(i, col):
    two = []
    for b in range(2):
        lo = b * (BR + GC)
        two.append(([(i, lo + c * K) for c in range(C)], (i, lo + HR), (i, col + b * GC)))
    return two


def chol_kernel(a_ref, b_ref, d_ref, chol_ref, w_ref, yz_ref, m_ref, u_ref):
    row = lax.broadcasted_iota(jnp.int32, (K, K), 0)
    col = lax.broadcasted_iota(jnp.int32, (K, K), 1)
    eye = row == col
    gram = (a_ref[0:K, :] + b_ref[0:K, :]) * (1.0 / TOTAL)
    m_ref[:, :K] = gram + jnp.where(eye, d_ref[0:1, :], 0.0)
    m_ref[:, K:] = jnp.where(eye, 1.0, 0.0)
    sub = lax.broadcasted_iota(jnp.int32, (8, 2 * K), 0)
    for b in range(K // 8):
        p = m_ref[8 * b : 8 * b + 8, :]
        for r in range(8):
            j = 8 * b + r
            cb = p[:, j : j + 1]
            rs = lax.rsqrt(p[r : r + 1, j : j + 1])
            urow = p[r : r + 1, :] * rs
            p = jnp.where(sub > r, p - (cb * rs) * urow, jnp.where(sub == r, urow, p))
        u_ref[8 * b : 8 * b + 8, :] = p
        if b < K // 8 - 1:
            upd = lax.dot_general(p[:, :K], p, TN, precision=HI, preferred_element_type=F32)
            lo = 8 * (b + 1)
            m_ref[lo:, :] = m_ref[lo:, :] - upd[lo:, :]
    chol_ref[...] = jnp.where(col >= row, u_ref[:, :K], 0.0).T
    w = u_ref[:, K:]
    w_ref[...] = w
    g = (a_ref[K : K + 8, :] + b_ref[K : K + 8, :]) * (1.0 / TOTAL)
    y = lax.dot_general(g, w, NT, precision=HI, preferred_element_type=F32)
    z = lax.dot_general(y, w, (((1,), (0,)), ((), ())), precision=HI, preferred_element_type=F32)
    yz_ref[0:8, :] = y
    yz_ref[8:16, :] = z


def cholesky(dk, dk2, damp):
    return pl.pallas_call(
        chol_kernel,
        out_shape=(
            jax.ShapeDtypeStruct((K, K), F32),
            jax.ShapeDtypeStruct((K, K), F32),
            jax.ShapeDtypeStruct((16, K), F32),
        ),
        in_specs=[VM] * 3,
        out_specs=(VM,) * 3,
        scratch_shapes=[pltpu.VMEM((K, 2 * K), F32), pltpu.VMEM((K, 2 * K), F32)],
        compiler_params=params(),
        name="panel_factor",
    )(dk, dk2, damp)


def halves(v):
    hi = v.astype(BF16)
    return hi, (v - hi.astype(F32)).astype(BF16)


def panel_kernel(k_ref, p_ref, pr_ref, po_ref, por_ref, w_ref, yz_ref, dir_ref, lpan_ref, la_ref, lb_ref):
    q, k = lax.axis_index("row"), k_ref[0]
    inv = 1.0 / TOTAL
    w_hi, w_lo = halves(w_ref[...])
    wb = jnp.concatenate([w_hi, w_lo, w_hi], axis=1)
    sub = lax.broadcasted_iota(jnp.int32, (8, 2 * K), 0)
    lane = lax.broadcasted_iota(jnp.int32, (8, 2 * K), 1)
    z = yz_ref[8:9, :]
    z2 = jnp.concatenate([z, jnp.zeros_like(z)], axis=1)
    lhs = jnp.where(lane == K, 1.0, jnp.where(sub == 0, -z2, 0.0))

    def solve(p):
        hi, lo = halves(p)
        return lax.dot_general(
            jnp.concatenate([hi, hi, lo], axis=1), wb, NT, preferred_element_type=F32
        )

    for lr in range(LR):
        rows = slice(lr * K, (lr + 1) * K)
        pe = (p_ref[rows, :] + pr_ref[rows, :]) * inv
        d = lax.dot_general(lhs, pe, NT, precision=HI, preferred_element_type=F32)
        i = lr * NZ + q
        dir_ref[lr : lr + 1, :] = jnp.where(
            i == k, yz_ref[0:1, :], jnp.where(i > k, d[0:1, :], d[1:2, :])
        )
        lpan = solve(pe[:, :K])
        lpan_ref[rows, :] = lpan
        hi, lo = halves(lpan)
        la_ref[rows, :] = jnp.concatenate([hi, hi, lo], axis=1)
    hi, lo = halves(solve((po_ref[...] + por_ref[...]) * inv))
    lb_ref[...] = jnp.concatenate([hi, lo, hi], axis=1)


def panel_solve(k, p, pr, po, por, w, yz):
    return pl.pallas_call(
        panel_kernel,
        out_shape=(
            jax.ShapeDtypeStruct((LR, K), F32),
            jax.ShapeDtypeStruct((RU, K), F32),
            jax.ShapeDtypeStruct((RU, 3 * K), BF16),
            jax.ShapeDtypeStruct((CU, 3 * K), BF16),
        ),
        in_specs=[SMEM] + [VM] * 6,
        out_specs=(VM,) * 4,
        compiler_params=params(),
        name="panel_solve",
    )(k, p, pr, po, por, w, yz)


def final_kernel(k_ref, g_ref, gr_ref, la_ref, lb_ref, lpan_ref, chol_ref, damp_ref, out_ref):
    q, k = lax.axis_index("row"), k_ref[0]
    s = (lax.axis_index("x") * NY + lax.axis_index("y")) * NC + lax.axis_index("core")
    lr = pl.program_id(0)
    i = lr * NZ + q
    upd = lax.dot_general(la_ref[...], lb_ref[...], NT, preferred_element_type=F32)
    gram = (g_ref[...] + gr_ref[...]) * (1.0 / TOTAL)
    row = lax.broadcasted_iota(jnp.int32, (K, K), 0)
    col = lax.broadcasted_iota(jnp.int32, (K, K), 1)
    damp = damp_ref[pl.ds(lr, 1), :]
    for lc in range(LC):
        j = lc * (NX * NY * NC) + s
        gt = gram[:, lc * K : (lc + 1) * K] + jnp.where((row == col) & (i == j), damp, 0.0)
        val = jnp.where(
            (i > k) & (j > k),
            gt - upd[:, lc * K : (lc + 1) * K],
            jnp.where(
                (i > k) & (j == k),
                lpan_ref[...],
                jnp.where((i == k) & (j == k), chol_ref[...], gt),
            ),
        )
        out_ref[pl.ds(lc, K, stride=LC), :] = val


def final(k, gown, grecv, la, lb, lpan, chol, damp):
    full = lambda shape: pl.BlockSpec(shape, lambda i: (0,) * len(shape))
    rows = lambda width: pl.BlockSpec((K, width), lambda i: (i, 0))
    return pl.pallas_call(
        final_kernel,
        grid=(LR,),
        out_shape=jax.ShapeDtypeStruct((RU * LC, K), F32),
        in_specs=[
            SMEM, rows(CU), rows(CU), rows(3 * K), full((CU, 3 * K)), rows(K), full((K, K)),
            full((LR, K)),
        ],
        out_specs=pl.BlockSpec((K * LC, K), lambda i: (i, 0)),
        compiler_params=params(),
        name="trailing_update",
    )(k, gown, grecv, la, lb, lpan, chol, damp)


def device(x, y, c, z):
    return ((x * NY + y) * NC + c) * NZ + z


def hops(along_x_core, d):
    pairs = []
    for x in range(NX):
        for y in range(NY):
            for c in range(NC):
                for z in range(NZ):
                    to = ((x + d) % NX, y) if c == along_x_core else (x, (y + d) % NY)
                    pairs.append((device(x, y, c, z), device(*to, c, z)))
    return pairs


def body(g_jets, layer_input_jets, speed, resid, point_index, damping, panel):
    q = lax.axis_index("row")
    k = panel[0]
    one = lambda v, d: lax.ppermute(v, AXES, hops(0, d))
    two = lambda v, d: lax.ppermute(v, AXES, hops(1, d))
    swap = lambda v: lax.ppermute(v, "core", [(0, 1), (1, 0)])
    zbit = lambda v, bit: v + lax.ppermute(v, "row", [(i, i ^ bit) for i in range(NZ)])
    bar = lax.optimization_barrier

    plus, minus, own = pack(
        panel,
        point_index.reshape(1, M),
        layer_input_jets.reshape(HR, POOL),
        g_jets.transpose(1, 0, 2).reshape(C * A, POOL),
        jnp.stack([speed, resid]),
    )
    ap, am = one(plus, 1), one(minus, -1)
    m1 = assemble(BLOCK0, BLOCK1, plus, own, ap)
    relay = HB + 2 * GC
    rp, rm = one(ap[:relay], 1), one(am[:relay], -1)
    m1p, m1m = two(m1[0], 1), two(m1[1], -1)
    m2 = assemble(BLOCK2, BLOCK3, am, rp, rm)
    dsel = lax.dynamic_index_in_dim(damping[:, 0, :], k // NZ, 0, keepdims=True)
    dsel = jnp.broadcast_to(jnp.where(k % NZ == q, dsel, 0.0), (8, K))

    line = [place(BLOCK0, 0, 0), place(BLOCK1, 0, 0), place(BLOCK2, 0, 3), place(BLOCK3, 0, 3)]
    accs = chunk(line, (plus, own, ap, am, rp, rm), (), "chunk_line")
    dsel = zbit(dsel, 1)
    m2, m1p, m1m, dsel = bar((m2, m1p, m1m, dsel))
    n1 = BR + GC
    r1p, r1m = two(m1p[:n1], 1), two(m1m[:n1], -1)
    m2p, m2m = two(m2[0], 1), two(m2[1], -1)
    near = received(0, 2 * BR + GC) + received(1, 2 * BR + GC)
    accs = chunk(near, (m1p, m1m), accs, "chunk_near1")
    dsel = zbit(dsel, 2)
    accs, dsel = bar((accs, dsel))
    far = [received(0, BR)[0], received(1, BR)[0]]
    accs = chunk(far, (r1p, r1m), accs, "chunk_far1")
    dsel = zbit(dsel, 4)
    accs, dsel = bar((accs, dsel))
    r2p, r2m = two(m2p[:n1], 1), two(m2m[:n1], -1)
    accs = chunk(near, (m2p, m2m), accs, "chunk_near2")
    accs = chunk(far, (r2p, r2m), accs, "chunk_far2")
    gown, gsib, p, po, ps, dk = accs

    dk2 = swap(dk)
    pr, por = swap(p), swap(ps)
    gr = swap(gsib)
    chol, w, yz = cholesky(dk, dk2, dsel)
    mine, lpan, la, lb = panel_solve(panel, p, pr, po, por, w, yz)
    slot = lax.broadcasted_iota(jnp.int32, (1, NZ, 1), 1)
    full = jnp.where(slot == q, mine[:, None, :], 0.0)
    for bit in (1, 2, 4):
        full = zbit(full, bit)
    fac = final(panel, gown, gr, la, lb, lpan, chol, damping[:, 0, :])
    return fac.reshape(LR, 1, K, LC, 1, K), full.reshape(-1)


def solution(mesh):
    grid = Mesh(mesh.devices.reshape(NX, NY, NC, NZ), AXES)
    pts = ("x", "y", "core")
    in_specs = (
        P(None, None, pts),
        P(None, None, pts),
        P(pts),
        P(pts),
        P(pts),
        P(None, "row", None),
        P(),
    )
    out_specs = (P(None, "row", None, None, pts, None), P())
    return jax.shard_map(body, mesh=grid, in_specs=in_specs, out_specs=out_specs, check_vma=False)
```

time: 173 us -> 226 us (1.31)
  Pallas kernels: 75.6 us -> 134 us
  starting transfers between devices: 42.3 us -> 36.2 us
  waiting for transfers between devices: 36.2 us -> 42.2 us
  other arithmetic: 7.17 us -> 1.54 us
    pallas_call x6 -> x10, Pallas kernels: 58 us -> 118 us  [the longest x2 87.8 us: assemble(): pl.pallas_call(lambda *r: assemble_kernel(plans, len(ins), *r), out_shape...]
    ppermute x4, waiting for transfers between devices: 8.55 us -> 19.2 us  [body(): one = lambda v, d: lax.ppermute(v, AXES, hops(0, d))]
    all_to_all x1 -> x0, waiting for transfers between devices: 7.07 us -> none  [body(): lax.all_to_all(gcol, ('x', 'y'), split_axis=0, concat_axis=0, tiled=True)]
    all_to_all x1 -> x0, starting transfers between devices: 6.88 us -> none  [body(): lax.all_to_all(gcol, ('x', 'y'), split_axis=0, concat_axis=0, tiled=True)]
    ppermute x3 -> x4, waiting for transfers between devices: 0.01 us -> 6.15 us  [body(): swap = lambda v: lax.ppermute(v, 'core', [(0, 1), (1, 0)])]
    ppermute x6, starting transfers between devices: 21.1 us -> 17.5 us  [body(): lax.ppermute(v, 'row', [(i, i ^ bit) for i in range(NZ)])]
    another operation x6 -> x1, other arithmetic: 3.63 us -> 0.01 us  [body(): jnp.stack([speed, resid])]
    ppermute x6 -> x8, starting transfers between devices: 8.63 us -> 11.9 us  [body(): two = lambda v, d: lax.ppermute(v, AXES, hops(1, d))]
  transfers between devices with their start and end apart: 20 -> 22, of which waited for: 11 -> 9; matrix products, arithmetic and copies ran while one was open for 3% -> 1% of each run, Pallas kernels for 28% -> 36%
where the time goes in v2:
time: 226 us; the launch traced here: 223 us
  Pallas kernels  134 us (59%)
  waiting for transfers between devices  42.2 us (19%)
  starting transfers between devices  36.2 us (16%)
  local copies, waits for them, and re-layouts  7.22 us (3%)
    pallas_call x2, Pallas kernels, assemble(): pl.pallas_call(lambda *r: assemble_kernel(plans, len(ins), *r), out_shape...  87.8 us
    pallas_call x5, Pallas kernels, chunk(): pl.pallas_call(lambda *r: chunk_kernel(blocks, len(arrs), len(accs), *r),...  21.8 us
    ppermute x4, waiting for transfers between devices, body(): one = lambda v, d: lax.ppermute(v, AXES, hops(0, d))  19.2 us
    ppermute x6, starting transfers between devices, body(): lax.ppermute(v, 'row', [(i, i ^ bit) for i in range(NZ)])  17.5 us
    pallas_call x1, Pallas kernels, cholesky(): pl.pallas_call(chol_kernel, out_shape=(jax.ShapeDtypeStruct((K, K), F32),...  16 us
    ppermute x8, starting transfers between devices, body(): two = lambda v, d: lax.ppermute(v, AXES, hops(1, d))  11.9 us
    ppermute x6, waiting for transfers between devices, body(): lax.ppermute(v, 'row', [(i, i ^ bit) for i in range(NZ)])  11 us
    ppermute x4, waiting for transfers between devices, body(): swap = lambda v: lax.ppermute(v, 'core', [(0, 1), (1, 0)])  6.15 us
  transfers between devices with their start and end apart: 22, of which 9 were waited for; matrix products, arithmetic and copies ran while one was open for 1% of the time, Pallas kernels for 36%

profile of v2, /device:TPU:2, one launch (start us, length us, event | category | flops | bytes accessed | tf_op | source)
XLA Modules:
  0.0 223.0 jit_solution(6424018946593252322)
XLA Ops:
  2.6 1.1 copy-done.10
  5.3 1.0 pack.1
  7.0 1.5 collective-permute-start.1
  8.5 6.9 %collective-permute-done.1.r_2_ = bf16[1664,128]{1,0:T(8,128)(2,1)S(1)} collective-permute-done((bf16[1664,128]{1,0:T(8,128)(2,1)S(1)}, bf16[1664,128]{1,0:T(8,128)(2,1)S(1)}, u32[]{:S(2)}, u32[]{:S(2)}) %collective-permute-start.1) | collective-permute-done | bytes 426016 | tf_op jit(solution)/shard_map/ppermute | solution.py:437
  16.2 43.9 %assemble.3 = (bf16[2752,128]{1,0:T(8,128)(2,1)}, bf16[2752,128]{1,0:T(8,128)(2,1)}) custom-call(bf16[1664,128]{1,0:T(8,128)(2,1)} %copy-done.4, bf16[256,128]{1,0:T(8,128)(2,1)} %copy-done.12, bf16[1664,128]{1,0:T(8,128)(2,1)} %copy-done), custom_call_target="tpu_custom_call" | custom-call | tf_op jit(solution)/shard_map/assemble/pallas_call | solution.py:160
  60.1 1.4 collective-permute-start.4
  61.5 1.9 collective-permute-start.5
  63.4 3.2 %collective-permute-start = (bf16[1664,128]{1,0:T(8,128)(2,1)S(1)}, bf16[1664,128]{1,0:T(8,128)(2,1)S(1)}, u32[]{:S(2)}, u32[]{:S(2)}) collective-permute-start(bf16[1664,128]{1,0:T(8,128)(2,1)S(1)} %get-tuple-element.65), channel_id=1, source_target_pairs={{0,192},{1,193},{2,194},{3,195},{4,196},{5,197},{6,198},{7,199},{8... | collective-permute-start | bytes 1277960 | tf_op jit(solution)/shard_map/ppermute | solution.py:437
  68.8 7.2 %collective-permute-done.r_0_.r_3_ = bf16[1664,128]{1,0:T(8,128)(2,1)S(1)} collective-permute-done((bf16[1664,128]{1,0:T(8,128)(2,1)S(1)}, bf16[1664,128]{1,0:T(8,128)(2,1)S(1)}, u32[]{:S(2)}, u32[]{:S(2)}) %collective-permute-start) | collective-permute-done | bytes 426016 | tf_op jit(solution)/shard_map/ppermute | solution.py:437
  76.7 5.1 %collective-permute-done.3.r_2_.r_5_ = bf16[768,128]{1,0:T(8,128)(2,1)S(1)} collective-permute-done((bf16[768,128]{1,0:T(8,128)(2,1)S(1)}, bf16[768,128]{1,0:T(8,128)(2,1)S(1)}, u32[]{:S(2)}, u32[]{:S(2)}) %collective-permute-start.3) | collective-permute-done | bytes 196640 | tf_op jit(solution)/shard_map/ppermute | solution.py:437
  82.5 43.9 %assemble.2 = (bf16[2752,128]{1,0:T(8,128)(2,1)}, bf16[2752,128]{1,0:T(8,128)(2,1)}) custom-call(bf16[1664,128]{1,0:T(8,128)(2,1)} %copy-done.2, bf16[768,128]{1,0:T(8,128)(2,1)} %copy-done.6, bf16[768,128]{1,0:T(8,128)(2,1)} %copy-done.8), custom_call_target="tpu_custom_call" | custom-call | tf_op jit(solution)/shard_map/assemble/pallas_call | solution.py:160
  126.4 1.8 collective-permute-start.9
  129.0 3.0 %collective-permute-start.12 = (bf16[1344,128]{1,0:T(8,128)(2,1)S(1)}, bf16[1344,128]{1,0:T(8,128)(2,1)S(1)}, u32[]{:S(2)}, u32[]{:S(2)}) collective-permute-start(bf16[1344,128]{1,0:T(8,128)(2,1)S(1)} %slice.23), channel_id=1, source_target_pairs={{0,48},{1,49},{2,50},{3,51},{4,52},{5,53},{6,54},{7,55},{8,200},{9... | collective-permute-start | bytes 1032200 | tf_op jit(solution)/shard_map/ppermute | solution.py:438
  132.0 5.9 %collective-permute-done.9.r_1_ = bf16[2752,128]{1,0:T(8,128)(2,1)S(1)} collective-permute-done((bf16[2752,128]{1,0:T(8,128)(2,1)}, bf16[2752,128]{1,0:T(8,128)(2,1)S(1)}, u32[]{:S(2)}, u32[]{:S(2)}) %collective-permute-start.9) | collective-permute-done | bytes 704544 | tf_op jit(solution)/shard_map/ppermute | solution.py:438
  137.9 3.0 %collective-permute-start.10 = (bf16[1344,128]{1,0:T(8,128)(2,1)S(1)}, bf16[1344,128]{1,0:T(8,128)(2,1)S(1)}, u32[]{:S(2)}, u32[]{:S(2)}) collective-permute-start(bf16[1344,128]{1,0:T(8,128)(2,1)S(1)} %slice.27), channel_id=1, source_target_pairs={{0,48},{1,49},{2,50},{3,51},{4,52},{5,53},{6,54},{7,55},{8,200},{9... | collective-permute-start | bytes 1032200 | tf_op jit(solution)/shard_map/ppermute | solution.py:438
  141.0 3.5 %collective-permute-start.13 = (f32[8,128]{1,0:T(8,128)S(1)}, f32[8,128]{1,0:T(8,128)S(1)}, u32[]{:S(2)}, u32[]{:S(2)}) collective-permute-start(f32[8,128]{1,0:T(8,128)S(1)} %broadcast_add_fusion), channel_id=1, source_target_pairs={{0,2},{1,3},{2,0},{3,1},{4,6},{5,7},{6,4},{7,5},{8,10},{9,11},{10,... | collective-permute-start | bytes 12296 | tf_op jit(solution)/shard_map/ppermute | solution.py:440
  144.6 5.4 %chunk_line.1 = (f32[1536,384]{1,0:T(8,128)S(1)}, f32[1536,384]{1,0:T(8,128)S(1)}, f32[1536,256]{1,0:T(8,128)S(1)}, f32[384,128]{1,0:T(8,128)S(1)}, f32[384,128]{1,0:T(8,128)S(1)}, /*index=5*/f32[144,128]{1,0:T(8,128)S(1)}) custom-call(bf16[1664,128]{1,0:T(8,128)(2,1)S(1)} %copy-done.5, bf16[256,128]{1,0:T(8,128)(2,1)S(1)} %copy-done.13, ...), custom_call_target="tpu_custom_call" | custom-call | tf_op jit(solution)/shard_map/chunk_line/pallas_call | solution.py:250
  150.0 5.5 %chunk_near1.1 = (f32[1536,384]{1,0:T(8,128)S(1)}, f32[1536,384]{1,0:T(8,128)S(1)}, f32[1536,256]{1,0:T(8,128)S(1)}, f32[384,128]{1,0:T(8,128)S(1)}, f32[384,128]{1,0:T(8,128)S(1)}, /*index=5*/f32[144,128]{1,0:T(8,128)S(1)}) custom-call(bf16[2752,128]{1,0:T(8,128)(2,1)S(1)} %collective-permute-done.4.r_0_, ...), custom_call_target="tpu_custom_call" | custom-call | tf_op jit(solution)/shard_map/chunk_near1/pallas_call | solution.py:250
  155.5 5.5 %collective-permute-start.14 = (f32[8,128]{1,0:T(8,128)S(1)}, f32[8,128]{1,0:T(8,128)S(1)}, u32[]{:S(2)}, u32[]{:S(2)}) collective-permute-start(f32[8,128]{1,0:T(8,128)S(1)} %add.30), channel_id=1, source_target_pairs={{0,4},{1,5},{2,6},{3,7},{4,0},{5,1},{6,2},{7,3},{8,12},{9,13},{10,... | collective-permute-start | bytes 12296 | tf_op jit(solution)/shard_map/ppermute | solution.py:440
  160.9 2.1 collective-permute-done.14
  163.1 2.8 %chunk_far1.1 = (f32[1536,384]{1,0:T(8,128)S(1)}, f32[1536,384]{1,0:T(8,128)S(1)}, f32[1536,256]{1,0:T(8,128)S(1)}, f32[384,128]{1,0:T(8,128)S(1)}, f32[384,128]{1,0:T(8,128)S(1)}, /*index=5*/f32[144,128]{1,0:T(8,128)S(1)}) custom-call(bf16[1344,128]{1,0:T(8,128)(2,1)S(1)} %collective-permute-done.11.r_0_, ...), custom_call_target="tpu_custom_call" | custom-call | tf_op jit(solution)/shard_map/chunk_far1/pallas_call | solution.py:250
  165.9 5.3 %chunk_near2.1 = (f32[1536,384]{1,0:T(8,128)S(1)}, f32[1536,384]{1,0:T(8,128)S(1)}, f32[1536,256]{1,0:T(8,128)S(1)}, f32[384,128]{1,0:T(8,128)S(1)}, f32[384,128]{1,0:T(8,128)S(1)}, /*index=5*/f32[144,128]{1,0:T(8,128)S(1)}) custom-call(bf16[2752,128]{1,0:T(8,128)(2,1)S(1)} %collective-permute-done.7.r_0_, ...), custom_call_target="tpu_custom_call" | custom-call | tf_op jit(solution)/shard_map/chunk_near2/pallas_call | solution.py:250
  171.3 2.8 %chunk_far2.1 = (f32[1536,384]{1,0:T(8,128)S(1)}, f32[1536,384]{1,0:T(8,128)S(1)}, f32[1536,256]{1,0:T(8,128)S(1)}, f32[384,128]{1,0:T(8,128)S(1)}, f32[384,128]{1,0:T(8,128)S(1)}, /*index=5*/f32[144,128]{1,0:T(8,128)S(1)}) custom-call(bf16[1344,128]{1,0:T(8,128)(2,1)S(1)} %collective-permute-done.8.r_0_, ...), custom_call_target="tpu_custom_call" | custom-call | tf_op jit(solution)/shard_map/chunk_far2/pallas_call | solution.py:250
  175.2 6.1 %collective-permute-done.18.b_ref = f32[144,128]{1,0:T(8,128)S(1)} collective-permute-done((f32[144,128]{1,0:T(8,128)S(1)}, f32[144,128]{1,0:T(8,128)S(1)}, u32[]{:S(2)}, u32[]{:S(2)}) %collective-permute-start.18) | collective-permute-done | bytes 73760 | tf_op jit(solution)/shard_map/ppermute | solution.py:439
  181.3 16.0 %panel_factor.1 = (f32[128,128]{1,0:T(8,128)S(1)}, f32[128,128]{1,0:T(8,128)S(1)}, f32[16,128]{1,0:T(8,128)S(1)}) custom-call(f32[144,128]{1,0:T(8,128)S(1)} %get-tuple-element.119.a_ref, f32[144,128]{1,0:T(8,128)S(1)} %collective-permute-done.18.b_ref, f32[8,128]{1,0:T(8,128)S(1)} %add.31.d_ref), custom_call_target="tpu_custom_call" | custom-call | tf_op jit(solution)/shard_map/panel_factor/pallas_call | solution.py:308
  197.3 1.9 panel_solve.1
  199.3 1.9 collective-permute-start.19
  201.3 2.2 collective-permute-done.19
  204.5 4.1 %collective-permute-done.20 = f32[12,8,128]{2,1,0:T(8,128)S(1)} collective-permute-done((f32[12,8,128]{2,1,0:T(8,128)S(1)}, f32[12,8,128]{2,1,0:T(8,128)S(1)}, u32[]{:S(2)}, u32[]{:S(2)}) %collective-permute-start.20) | collective-permute-done | bytes 49184 | tf_op jit(solution)/shard_map/ppermute | solution.py:440
  208.6 5.4 %collective-permute-start.21 = (f32[12,8,128]{2,1,0:T(8,128)S(1)}, f32[12,8,128]{2,1,0:T(8,128)S(1)}, u32[]{:S(2)}, u32[]{:S(2)}) collective-permute-start(f32[12,8,128]{2,1,0:T(8,128)S(1)} %fusion.2), channel_id=1, source_target_pairs={{0,4},{1,5},{2,6},{3,7},{4,0},{5,1},{6,2},{7,3},{8,12},{9,13},{10,... | collective-permute-start | bytes 147464 | tf_op jit(solution)/shard_map/ppermute | solution.py:440
  214.1 2.6 %collective-permute-done.21 = f32[12,8,128]{2,1,0:T(8,128)S(1)} collective-permute-done((f32[12,8,128]{2,1,0:T(8,128)S(1)}, f32[12,8,128]{2,1,0:T(8,128)S(1)}, u32[]{:S(2)}, u32[]{:S(2)}) %collective-permute-start.21) | collective-permute-done | bytes 49184 | tf_op jit(solution)/shard_map/ppermute | solution.py:440
  217.3 5.7 %trailing_update.1 = f32[4608,128]{1,0:T(8,128)} custom-call(s32[1]{0:T(128)} %copy.14.k_ref, f32[1536,384]{1,0:T(8,128)S(1)} %get-tuple-element.114.g_ref, f32[1536,384]{1,0:T(8,128)S(1)} %collective-permute-done.15.gr_ref, bf16[1536,384]{1,0:T(8,128)(2,1)S(1)} %get-tuple-element.123.la_ref, bf16[384,384]{1,0:T(8,128)(2,1)S(1)} %get-tuple-element.124.lb_ref, ...), custom_call_target="tpu_custom_call" | custom-call | tf_op jit(solution)/shard_map/trailing_update/pallas_call | solution.py:405
  (75 shorter events, 11.7 us)
Async XLA Ops:
  7.0 8.4 %copy-start.4 = (bf16[1664,128]{1,0:T(8,128)(2,1)}, bf16[1664,128]{1,0:T(8,128)(2,1)S(1)}, u32[]{:S(2)}) copy-start(bf16[1664,128]{1,0:T(8,128)(2,1)S(1)} %get-tuple-element.66.r_0_) | copy-start | bytes 1277956
  7.0 8.4 %collective-permute-start.1 = (bf16[1664,128]{1,0:T(8,128)(2,1)S(1)}, bf16[1664,128]{1,0:T(8,128)(2,1)S(1)}, u32[]{:S(2)}, u32[]{:S(2)}) collective-permute-start(bf16[1664,128]{1,0:T(8,128)(2,1)S(1)} %get-tuple-element.66.r_0_), channel_id=1, source_target_pairs={{0,64},{1,65},{2,66},{3,67},{4,68},{5,69},{6,70},{7,71},{8,24},{9,... | collective-permute-start | bytes 1277960 | tf_op jit(solution)/shard_map/ppermute | solution.py:437
  60.1 84.5 %copy-start.1 = (bf16[1664,128]{1,0:T(8,128)(2,1)S(1)}, bf16[1664,128]{1,0:T(8,128)(2,1)}, u32[]{:S(2)}) copy-start(bf16[1664,128]{1,0:T(8,128)(2,1)} %copy-done) | copy-start | bytes 1277956
  60.1 84.5 %copy-start.5 = (bf16[1664,128]{1,0:T(8,128)(2,1)S(1)}, bf16[1664,128]{1,0:T(8,128)(2,1)}, u32[]{:S(2)}) copy-start(bf16[1664,128]{1,0:T(8,128)(2,1)} %copy-done.4) | copy-start | bytes 1277956
  60.1 84.4 %copy-start.13 = (bf16[256,128]{1,0:T(8,128)(2,1)S(1)}, bf16[256,128]{1,0:T(8,128)(2,1)}, u32[]{:S(2)}) copy-start(bf16[256,128]{1,0:T(8,128)(2,1)} %copy-done.12) | copy-start | bytes 196612
  60.1 66.3 %collective-permute-start.4 = (bf16[2752,128]{1,0:T(8,128)(2,1)}, bf16[2752,128]{1,0:T(8,128)(2,1)S(1)}, u32[]{:S(2)}, u32[]{:S(2)}) collective-permute-start(bf16[2752,128]{1,0:T(8,128)(2,1)} %get-tuple-element.70), channel_id=1, source_target_pairs={{0,16},{1,17},{2,18},{3,19},{4,20},{5,21},{6,22},{7,23},{8,72},{9,... | collective-permute-start | bytes 2113544 | tf_op jit(solution)/shard_map/ppermute | solution.py:438
  61.5 64.9 %collective-permute-start.5 = (bf16[2752,128]{1,0:T(8,128)(2,1)}, bf16[2752,128]{1,0:T(8,128)(2,1)S(1)}, u32[]{:S(2)}, u32[]{:S(2)}) collective-permute-start(bf16[2752,128]{1,0:T(8,128)(2,1)} %get-tuple-element.71), channel_id=1, source_target_pairs={{0,48},{1,49},{2,50},{3,51},{4,52},{5,53},{6,54},{7,55},{8,200},{9... | collective-permute-start | bytes 2113544 | tf_op jit(solution)/shard_map/ppermute | solution.py:438
  63.4 12.6 %collective-permute-start = (bf16[1664,128]{1,0:T(8,128)(2,1)S(1)}, bf16[1664,128]{1,0:T(8,128)(2,1)S(1)}, u32[]{:S(2)}, u32[]{:S(2)}) collective-permute-start(bf16[1664,128]{1,0:T(8,128)(2,1)S(1)} %get-tuple-element.65), channel_id=1, source_target_pairs={{0,192},{1,193},{2,194},{3,195},{4,196},{5,197},{6,198},{7,199},{8... | collective-permute-start | bytes 1277960 | tf_op jit(solution)/shard_map/ppermute | solution.py:437
  67.3 9.3 %collective-permute-start.6 = (f32[8,128]{1,0:T(8,128)S(1)}, f32[8,128]{1,0:T(8,128)S(1)}, u32[]{:S(2)}, u32[]{:S(2)}) collective-permute-start(f32[8,128]{1,0:T(8,128)S(1)} %broadcast_in_dim.31), channel_id=1, source_target_pairs={{0,1},{1,0},{2,3},{3,2},{4,5},{5,4},{6,7},{7,6},{8,9},{9,8},{10,11... | collective-permute-start | bytes 12296 | tf_op jit(solution)/shard_map/ppermute | solution.py:440
  68.5 8.2 %collective-permute-start.2 = (bf16[768,128]{1,0:T(8,128)(2,1)S(1)}, bf16[768,128]{1,0:T(8,128)(2,1)S(1)}, u32[]{:S(2)}, u32[]{:S(2)}) collective-permute-start(bf16[768,128]{1,0:T(8,128)(2,1)S(1)} %slice.24), channel_id=1, source_target_pairs={{0,64},{1,65},{2,66},{3,67},{4,68},{5,69},{6,70},{7,71},{8,24},{9,... | collective-permute-start | bytes 589832 | tf_op jit(solution)/shard_map/ppermute | solution.py:437
  76.0 5.8 %copy-start.2 = (bf16[1664,128]{1,0:T(8,128)(2,1)}, bf16[1664,128]{1,0:T(8,128)(2,1)S(1)}, u32[]{:S(2)}) copy-start(bf16[1664,128]{1,0:T(8,128)(2,1)S(1)} %collective-permute-done.r_0_.r_3_) | copy-start | bytes 1277956
  76.1 5.7 %collective-permute-start.3 = (bf16[768,128]{1,0:T(8,128)(2,1)S(1)}, bf16[768,128]{1,0:T(8,128)(2,1)S(1)}, u32[]{:S(2)}, u32[]{:S(2)}) collective-permute-start(bf16[768,128]{1,0:T(8,128)(2,1)S(1)} %slice.25), channel_id=1, source_target_pairs={{0,192},{1,193},{2,194},{3,195},{4,196},{5,197},{6,198},{7,199},{8... | collective-permute-start | bytes 589832 | tf_op jit(solution)/shard_map/ppermute | solution.py:437
  76.7 5.1 %copy-start.6 = (bf16[768,128]{1,0:T(8,128)(2,1)}, bf16[768,128]{1,0:T(8,128)(2,1)S(1)}, u32[]{:S(2)}) copy-start(bf16[768,128]{1,0:T(8,128)(2,1)S(1)} %collective-permute-done.2.r_1_.r_4_) | copy-start | bytes 589828
  126.4 18.2 %copy-start.3 = (bf16[1664,128]{1,0:T(8,128)(2,1)S(1)}, bf16[1664,128]{1,0:T(8,128)(2,1)}, u32[]{:S(2)}) copy-start(bf16[1664,128]{1,0:T(8,128)(2,1)} %copy-done.2) | copy-start | bytes 1277956
  126.4 18.2 %copy-start.7 = (bf16[768,128]{1,0:T(8,128)(2,1)S(1)}, bf16[768,128]{1,0:T(8,128)(2,1)}, u32[]{:S(2)}) copy-start(bf16[768,128]{1,0:T(8,128)(2,1)} %copy-done.6) | copy-start | bytes 589828
  126.4 18.2 %copy-start.9 = (bf16[768,128]{1,0:T(8,128)(2,1)S(1)}, bf16[768,128]{1,0:T(8,128)(2,1)}, u32[]{:S(2)}) copy-start(bf16[768,128]{1,0:T(8,128)(2,1)} %copy-done.8) | copy-start | bytes 589828
  126.4 11.4 %collective-permute-start.9 = (bf16[2752,128]{1,0:T(8,128)(2,1)}, bf16[2752,128]{1,0:T(8,128)(2,1)S(1)}, u32[]{:S(2)}, u32[]{:S(2)}) collective-permute-start(bf16[2752,128]{1,0:T(8,128)(2,1)} %get-tuple-element.73), channel_id=1, source_target_pairs={{0,48},{1,49},{2,50},{3,51},{4,52},{5,53},{6,54},{7,55},{8,200},{9... | collective-permute-start | bytes 2113544 | tf_op jit(solution)/shard_map/ppermute | solution.py:438
  128.2 12.6 %collective-permute-start.7 = (bf16[2752,128]{1,0:T(8,128)(2,1)}, bf16[2752,128]{1,0:T(8,128)(2,1)S(1)}, u32[]{:S(2)}, u32[]{:S(2)}) collective-permute-start(bf16[2752,128]{1,0:T(8,128)(2,1)} %get-tuple-element.72), channel_id=1, source_target_pairs={{0,16},{1,17},{2,18},{3,19},{4,20},{5,21},{6,22},{7,23},{8,72},{9,... | collective-permute-start | bytes 2113544 | tf_op jit(solution)/shard_map/ppermute | solution.py:438
  128.6 34.5 %collective-permute-start.11 = (bf16[1344,128]{1,0:T(8,128)(2,1)S(1)}, bf16[1344,128]{1,0:T(8,128)(2,1)S(1)}, u32[]{:S(2)}, u32[]{:S(2)}) collective-permute-start(bf16[1344,128]{1,0:T(8,128)(2,1)S(1)} %slice.22), channel_id=1, source_target_pairs={{0,16},{1,17},{2,18},{3,19},{4,20},{5,21},{6,22},{7,23},{8,72},{9,... | collective-permute-start | bytes 1032200 | tf_op jit(solution)/shard_map/ppermute | solution.py:438
  129.0 34.1 %collective-permute-start.12 = (bf16[1344,128]{1,0:T(8,128)(2,1)S(1)}, bf16[1344,128]{1,0:T(8,128)(2,1)S(1)}, u32[]{:S(2)}, u32[]{:S(2)}) collective-permute-start(bf16[1344,128]{1,0:T(8,128)(2,1)S(1)} %slice.23), channel_id=1, source_target_pairs={{0,48},{1,49},{2,50},{3,51},{4,52},{5,53},{6,54},{7,55},{8,200},{9... | collective-permute-start | bytes 1032200 | tf_op jit(solution)/shard_map/ppermute | solution.py:438
  137.9 33.4 %collective-permute-start.10 = (bf16[1344,128]{1,0:T(8,128)(2,1)S(1)}, bf16[1344,128]{1,0:T(8,128)(2,1)S(1)}, u32[]{:S(2)}, u32[]{:S(2)}) collective-permute-start(bf16[1344,128]{1,0:T(8,128)(2,1)S(1)} %slice.27), channel_id=1, source_target_pairs={{0,48},{1,49},{2,50},{3,51},{4,52},{5,53},{6,54},{7,55},{8,200},{9... | collective-permute-start | bytes 1032200 | tf_op jit(solution)/shard_map/ppermute | solution.py:438
  140.9 30.3 %collective-permute-start.8 = (bf16[1344,128]{1,0:T(8,128)(2,1)S(1)}, bf16[1344,128]{1,0:T(8,128)(2,1)S(1)}, u32[]{:S(2)}, u32[]{:S(2)}) collective-permute-start(bf16[1344,128]{1,0:T(8,128)(2,1)S(1)} %slice.26), channel_id=1, source_target_pairs={{0,16},{1,17},{2,18},{3,19},{4,20},{5,21},{6,22},{7,23},{8,72},{9,... | collective-permute-start | bytes 1032200 | tf_op jit(solution)/shard_map/ppermute | solution.py:438
  141.0 14.5 %collective-permute-start.13 = (f32[8,128]{1,0:T(8,128)S(1)}, f32[8,128]{1,0:T(8,128)S(1)}, u32[]{:S(2)}, u32[]{:S(2)}) collective-permute-start(f32[8,128]{1,0:T(8,128)S(1)} %broadcast_add_fusion), channel_id=1, source_target_pairs={{0,2},{1,3},{2,0},{3,1},{4,6},{5,7},{6,4},{7,5},{8,10},{9,11},{10,... | collective-permute-start | bytes 12296 | tf_op jit(solution)/shard_map/ppermute | solution.py:440
  155.5 7.6 %collective-permute-start.14 = (f32[8,128]{1,0:T(8,128)S(1)}, f32[8,128]{1,0:T(8,128)S(1)}, u32[]{:S(2)}, u32[]{:S(2)}) collective-permute-start(f32[8,128]{1,0:T(8,128)S(1)} %add.30), channel_id=1, source_target_pairs={{0,4},{1,5},{2,6},{3,7},{4,0},{5,1},{6,2},{7,3},{8,12},{9,13},{10,... | collective-permute-start | bytes 12296 | tf_op jit(solution)/shard_map/ppermute | solution.py:440
  174.0 40.0 %copy-start.15 = (f32[12,1,128]{2,1,0:T(1,128)S(1)}, f32[12,1,128]{2,1,0:T(1,128)}, u32[]{:S(2)}) copy-start(f32[12,1,128]{2,1,0:T(1,128)} %param.12) | copy-start | bytes 18436
  174.0 23.3 %collective-permute-start.16 = (f32[1536,256]{1,0:T(8,128)S(1)}, f32[1536,256]{1,0:T(8,128)S(1)}, u32[]{:S(2)}, u32[]{:S(2)}) collective-permute-start(f32[1536,256]{1,0:T(8,128)S(1)} %get-tuple-element.116.p_ref), channel_id=1, source_target_pairs={{0,8},{8,0},{1,9},{9,1},{2,10},{10,2},{3,11},{11,3},{4,12},{12,4},... | collective-permute-start | bytes 4718600 | tf_op jit(solution)/shard_map/ppermute | solution.py:439
  174.2 43.1 %collective-permute-start.15 = (f32[1536,384]{1,0:T(8,128)S(1)}, f32[1536,384]{1,0:T(8,128)S(1)}, u32[]{:S(2)}, u32[]{:S(2)}) collective-permute-start(f32[1536,384]{1,0:T(8,128)S(1)} %get-tuple-element.115), channel_id=1, source_target_pairs={{0,8},{8,0},{1,9},{9,1},{2,10},{10,2},{3,11},{11,3},{4,12},{12,4},... | collective-permute-start | bytes 7077896 | tf_op jit(solution)/shard_map/ppermute | solution.py:439
  174.6 22.7 %collective-permute-start.17 = (f32[384,128]{1,0:T(8,128)S(1)}, f32[384,128]{1,0:T(8,128)S(1)}, u32[]{:S(2)}, u32[]{:S(2)}) collective-permute-start(f32[384,128]{1,0:T(8,128)S(1)} %get-tuple-element.118), channel_id=1, source_target_pairs={{0,8},{8,0},{1,9},{9,1},{2,10},{10,2},{3,11},{11,3},{4,12},{12,4},... | collective-permute-start | bytes 589832 | tf_op jit(solution)/shard_map/ppermute | solution.py:439
  174.7 6.6 %collective-permute-start.18 = (f32[144,128]{1,0:T(8,128)S(1)}, f32[144,128]{1,0:T(8,128)S(1)}, u32[]{:S(2)}, u32[]{:S(2)}) collective-permute-start(f32[144,128]{1,0:T(8,128)S(1)} %get-tuple-element.119.a_ref), channel_id=1, source_target_pairs={{0,8},{8,0},{1,9},{9,1},{2,10},{10,2},{3,11},{11,3},{4,12},{12,4},... | collective-permute-start | bytes 221192 | tf_op jit(solution)/shard_map/ppermute | solution.py:439
  199.3 4.1 %collective-permute-start.19 = (f32[12,8,128]{2,1,0:T(8,128)S(1)}, f32[12,8,128]{2,1,0:T(8,128)S(1)}, u32[]{:S(2)}, u32[]{:S(2)}) collective-permute-start(f32[12,8,128]{2,1,0:T(8,128)S(1)} %broadcast_select_fusion), channel_id=1, source_target_pairs={{0,1},{1,0},{2,3},{3,2},{4,5},{5,4},{6,7},{7,6},{8,9},{9,8},{10,11... | collective-permute-start | bytes 147464 | tf_op jit(solution)/shard_map/ppermute | solution.py:440
  203.5 5.0 %collective-permute-start.20 = (f32[12,8,128]{2,1,0:T(8,128)S(1)}, f32[12,8,128]{2,1,0:T(8,128)S(1)}, u32[]{:S(2)}, u32[]{:S(2)}) collective-permute-start(f32[12,8,128]{2,1,0:T(8,128)S(1)} %fusion), channel_id=1, source_target_pairs={{0,2},{1,3},{2,0},{3,1},{4,6},{5,7},{6,4},{7,5},{8,10},{9,11},{10,... | collective-permute-start | bytes 147464 | tf_op jit(solution)/shard_map/ppermute | solution.py:440
  208.6 8.0 %collective-permute-start.21 = (f32[12,8,128]{2,1,0:T(8,128)S(1)}, f32[12,8,128]{2,1,0:T(8,128)S(1)}, u32[]{:S(2)}, u32[]{:S(2)}) collective-permute-start(f32[12,8,128]{2,1,0:T(8,128)S(1)} %fusion.2), channel_id=1, source_target_pairs={{0,4},{1,5},{2,6},{3,7},{4,0},{5,1},{6,2},{7,3},{8,12},{9,13},{10,... | collective-permute-start | bytes 147464 | tf_op jit(solution)/shard_map/ppermute | solution.py:440
  (6 other events, 4.8 us)

commit v3 on v2

--- a/solution.py
+++ b/solution.py
@@ -27,7 +27,6 @@
 VMEM_LIMIT = 20 * 1024 * 1024
 SMEM = pl.BlockSpec(memory_space=pltpu.SMEM)
 VM = pl.BlockSpec(memory_space=pltpu.VMEM)
-ANY = pl.BlockSpec(memory_space=pl.ANY)
 
 
 def params():
@@ -141,18 +140,10 @@
 
 
 def assemble_kernel(plans, n_in, *refs):
-    ins, outs, sem = refs[:n_in], refs[n_in:-1], refs[-1]
-    copies, i = [], 0
+    ins, outs = refs[:n_in], refs[n_in:]
     for plan, out in zip(plans, outs):
         for src, lo, n, at in plan:
-            copies.append(
-                pltpu.make_async_copy(ins[src].at[lo : lo + n, :], out.at[at : at + n, :], sem.at[i])
-            )
-            i += 1
-    for cp in copies:
-        cp.start()
-    for cp in copies:
-        cp.wait()
+            out[at : at + n, :] = ins[src][lo : lo + n, :]
 
 
 def assemble(first, second, *ins):
@@ -160,9 +151,9 @@
     return pl.pallas_call(
         lambda *r: assemble_kernel(plans, len(ins), *r),
         out_shape=(jax.ShapeDtypeStruct((MR, M), BF16),) * 2,
-        in_specs=[ANY] * len(ins),
-        out_specs=(ANY,) * 2,
-        scratch_shapes=[pltpu.SemaphoreType.DMA((sum(len(p) for p in plans),))],
+        in_specs=[VM] * len(ins),
+        out_specs=(VM,) * 2,
+        compiler_params=params(),
         name="assemble",
     )(*ins)
 
@@ -447,7 +438,7 @@
         g_jets.transpose(1, 0, 2).reshape(C * A, POOL),
         jnp.stack([speed, resid]),
     )
-    ap, am = one(plus, 1), one(minus, -1)
+    ap, am = bar((one(plus, 1), one(minus, -1)))
     m1 = assemble(BLOCK0, BLOCK1, plus, own, ap)
     relay = HB + 2 * GC
     rp, rm = one(ap[:relay], 1), one(am[:relay], -1)
@@ -458,34 +449,32 @@
 
     line = [place(BLOCK0, 0, 0), place(BLOCK1, 0, 0), place(BLOCK2, 0, 3), place(BLOCK3, 0, 3)]
     accs = chunk(line, (plus, own, ap, am, rp, rm), (), "chunk_line")
-    dsel = zbit(dsel, 1)
-    m2, m1p, m1m, dsel = bar((m2, m1p, m1m, dsel))
+    m2, m1p, m1m, accs, dsel = bar((m2, m1p, m1m, accs, zbit(dsel, 1)))
     n1 = BR + GC
     r1p, r1m = two(m1p[:n1], 1), two(m1m[:n1], -1)
     m2p, m2m = two(m2[0], 1), two(m2[1], -1)
     near = received(0, 2 * BR + GC) + received(1, 2 * BR + GC)
     accs = chunk(near, (m1p, m1m), accs, "chunk_near1")
-    dsel = zbit(dsel, 2)
-    accs, dsel = bar((accs, dsel))
     far = [received(0, BR)[0], received(1, BR)[0]]
     accs = chunk(far, (r1p, r1m), accs, "chunk_far1")
-    dsel = zbit(dsel, 4)
-    accs, dsel = bar((accs, dsel))
+    m2p, m2m, accs, dsel = bar((m2p, m2m, accs, zbit(dsel, 2)))
     r2p, r2m = two(m2p[:n1], 1), two(m2m[:n1], -1)
     accs = chunk(near, (m2p, m2m), accs, "chunk_near2")
+    r2p, r2m, accs, dsel = bar((r2p, r2m, accs, zbit(dsel, 4)))
     accs = chunk(far, (r2p, r2m), accs, "chunk_far2")
     gown, gsib, p, po, ps, dk = accs
 
-    dk2 = swap(dk)
+    dk2, p, ps, gsib = bar((swap(dk), p, ps, gsib))
     pr, por = swap(p), swap(ps)
     gr = swap(gsib)
     chol, w, yz = cholesky(dk, dk2, dsel)
     mine, lpan, la, lb = panel_solve(panel, p, pr, po, por, w, yz)
     slot = lax.broadcasted_iota(jnp.int32, (1, NZ, 1), 1)
     full = jnp.where(slot == q, mine[:, None, :], 0.0)
-    for bit in (1, 2, 4):
-        full = zbit(full, bit)
+    full, la = bar((zbit(full, 1), la))
     fac = final(panel, gown, gr, la, lb, lpan, chol, damping[:, 0, :])
+    full, fac = bar((zbit(full, 2), fac))
+    full = zbit(full, 4)
     return fac.reshape(LR, 1, K, LC, 1, K), full.reshape(-1)
 
 

time: 226 us -> 117 us (0.52); the launches traced: 223 us -> 117 us
  Pallas kernels: 134 us -> 47.6 us
  waiting for transfers between devices: 42.2 us -> 27.7 us
  local copies, waits for them, and re-layouts: 7.22 us -> 4.18 us
    pallas_call x2, Pallas kernels: 87.8 us -> 1.12 us  [assemble(): pl.pallas_call(lambda *r: assemble_kernel(plans, len(ins), *r), out_shape...]
    ppermute x4, waiting for transfers between devices: 19.2 us -> 12.1 us  [body(): one = lambda v, d: lax.ppermute(v, AXES, hops(0, d))]
    ppermute x4, waiting for transfers between devices: 6.15 us -> 1.26 us  [body(): swap = lambda v: lax.ppermute(v, 'core', [(0, 1), (1, 0)])]
    ppermute x8, waiting for transfers between devices: 5.87 us -> 1.9 us  [body(): two = lambda v, d: lax.ppermute(v, AXES, hops(1, d))]
    unnamed x33 -> x9, local copies, waits for them, and re-layouts: 4.85 us -> 2.73 us
  transfers between devices with their start and end apart: 22 -> 22, of which waited for: 9 -> 10; matrix products, arithmetic and copies ran while one was open for 1% -> 1% of each run, Pallas kernels for 36% -> 32%
where the time goes in v3:
time: 117 us
  Pallas kernels  47.6 us (41%)
  starting transfers between devices  34.3 us (29%)
  waiting for transfers between devices  27.7 us (24%)
  local copies, waits for them, and re-layouts  4.18 us (4%)
  between operations  1.49 us (1%)
  other arithmetic  1.47 us (1%)
    pallas_call x5, Pallas kernels, chunk(): pl.pallas_call(lambda *r: chunk_kernel(blocks, len(arrs), len(accs), *r),...  21.7 us
    ppermute x6, starting transfers between devices, body(): lax.ppermute(v, 'row', [(i, i ^ bit) for i in range(NZ)])  16.7 us
    pallas_call x1, Pallas kernels, cholesky(): pl.pallas_call(chol_kernel, out_shape=(jax.ShapeDtypeStruct((K, K), F32),...  16 us
    ppermute x6, waiting for transfers between devices, body(): lax.ppermute(v, 'row', [(i, i ^ bit) for i in range(NZ)])  12.5 us
    ppermute x8, starting transfers between devices, body(): two = lambda v, d: lax.ppermute(v, AXES, hops(1, d))  12.1 us
    ppermute x4, waiting for transfers between devices, body(): one = lambda v, d: lax.ppermute(v, AXES, hops(0, d))  12.1 us
    pallas_call x1, Pallas kernels, final(): pl.pallas_call(final_kernel, grid=(LR,), out_shape=jax.ShapeDtypeStruct((...  5.75 us
    ppermute x4, starting transfers between devices, body(): one = lambda v, d: lax.ppermute(v, AXES, hops(0, d))  4.62 us
  transfers between devices with their start and end apart: 22, of which 10 were waited for; matrix products, arithmetic and copies ran while one was open for 1% of the time, Pallas kernels for 32%

profile of v3, /device:TPU:2, one launch (start us, length us, event | category | flops | bytes accessed | tf_op | source)
XLA Modules:
  0.0 116.7 jit_solution(14368036887583271240)
XLA Ops:
  2.6 1.1 copy-done
  6.4 1.6 %collective-permute-start = (bf16[1664,128]{1,0:T(8,128)(2,1)S(1)}, bf16[1664,128]{1,0:T(8,128)(2,1)S(1)}, u32[]{:S(2)}, u32[]{:S(2)}) collective-permute-start(bf16[1664,128]{1,0:T(8,128)(2,1)S(1)} %get-tuple-element.85.r_0_), channel_id=1, source_target_pairs={{0,64},{1,65},{2,66},{3,67},{4,68},{5,69},{6,70},{7,71},{8,24},{9,... | collective-permute-start | bytes 1277960 | tf_op jit(solution)/shard_map/ppermute | solution.py:428
  8.8 6.0 %collective-permute-done.r_2_ = bf16[1664,128]{1,0:T(8,128)(2,1)S(1)} collective-permute-done((bf16[1664,128]{1,0:T(8,128)(2,1)S(1)}, bf16[1664,128]{1,0:T(8,128)(2,1)S(1)}, u32[]{:S(2)}, u32[]{:S(2)}) %collective-permute-start) | collective-permute-done | bytes 426016 | tf_op jit(solution)/shard_map/ppermute | solution.py:428
  14.8 1.2 %collective-permute-done.1.r_0_.r_3_ = bf16[1664,128]{1,0:T(8,128)(2,1)S(1)} collective-permute-done((bf16[1664,128]{1,0:T(8,128)(2,1)S(1)}, bf16[1664,128]{1,0:T(8,128)(2,1)S(1)}, u32[]{:S(2)}, u32[]{:S(2)}) %collective-permute-start.1) | collective-permute-done | bytes 426016 | tf_op jit(solution)/shard_map/ppermute | solution.py:428
  17.1 1.6 %collective-permute-start.4 = (bf16[2752,128]{1,0:T(8,128)(2,1)}, bf16[2752,128]{1,0:T(8,128)(2,1)S(1)}, u32[]{:S(2)}, u32[]{:S(2)}) collective-permute-start(bf16[2752,128]{1,0:T(8,128)(2,1)} %get-tuple-element.92), channel_id=1, source_target_pairs={{0,16},{1,17},{2,18},{3,19},{4,20},{5,21},{6,22},{7,23},{8,72},{9,... | collective-permute-start | bytes 2113544 | tf_op jit(solution)/shard_map/ppermute | solution.py:429
  18.6 1.7 %collective-permute-start.5 = (bf16[2752,128]{1,0:T(8,128)(2,1)S(1)}, bf16[2752,128]{1,0:T(8,128)(2,1)S(1)}, u32[]{:S(2)}, u32[]{:S(2)}) collective-permute-start(bf16[2752,128]{1,0:T(8,128)(2,1)S(1)} %get-tuple-element.93), channel_id=1, source_target_pairs={{0,48},{1,49},{2,50},{3,51},{4,52},{5,53},{6,54},{7,55},{8,200},{9... | collective-permute-start | bytes 2113544 | tf_op jit(solution)/shard_map/ppermute | solution.py:429
  21.0 1.9 %collective-permute-start.6 = (f32[8,128]{1,0:T(8,128)S(1)}, f32[8,128]{1,0:T(8,128)S(1)}, u32[]{:S(2)}, u32[]{:S(2)}) collective-permute-start(f32[8,128]{1,0:T(8,128)S(1)} %broadcast_in_dim.32), channel_id=1, source_target_pairs={{0,1},{1,0},{2,3},{3,2},{4,5},{5,4},{6,7},{7,6},{8,9},{9,8},{10,11... | collective-permute-start | bytes 12296 | tf_op jit(solution)/shard_map/ppermute | solution.py:431
  22.9 1.3 %collective-permute-start.2 = (bf16[768,128]{1,0:T(8,128)(2,1)S(1)}, bf16[768,128]{1,0:T(8,128)(2,1)S(1)}, u32[]{:S(2)}, u32[]{:S(2)}) collective-permute-start(bf16[768,128]{1,0:T(8,128)(2,1)S(1)} %slice.18), channel_id=1, source_target_pairs={{0,64},{1,65},{2,66},{3,67},{4,68},{5,69},{6,70},{7,71},{8,24},{9,... | collective-permute-start | bytes 589832 | tf_op jit(solution)/shard_map/ppermute | solution.py:428
  25.1 3.5 %collective-permute-done.2.r_1_.r_4_ = bf16[768,128]{1,0:T(8,128)(2,1)S(1)} collective-permute-done((bf16[768,128]{1,0:T(8,128)(2,1)S(1)}, bf16[768,128]{1,0:T(8,128)(2,1)S(1)}, u32[]{:S(2)}, u32[]{:S(2)}) %collective-permute-start.2) | collective-permute-done | bytes 196640 | tf_op jit(solution)/shard_map/ppermute | solution.py:428
  28.6 1.3 %collective-permute-done.3.r_2_.r_5_ = bf16[768,128]{1,0:T(8,128)(2,1)S(1)} collective-permute-done((bf16[768,128]{1,0:T(8,128)(2,1)S(1)}, bf16[768,128]{1,0:T(8,128)(2,1)S(1)}, u32[]{:S(2)}, u32[]{:S(2)}) %collective-permute-start.3) | collective-permute-done | bytes 196640 | tf_op jit(solution)/shard_map/ppermute | solution.py:428
  29.9 5.4 %chunk_line.1 = (f32[1536,384]{1,0:T(8,128)S(1)}, f32[1536,384]{1,0:T(8,128)S(1)}, f32[1536,256]{1,0:T(8,128)S(1)}, f32[384,128]{1,0:T(8,128)S(1)}, f32[384,128]{1,0:T(8,128)S(1)}, /*index=5*/f32[144,128]{1,0:T(8,128)S(1)}) custom-call(bf16[1664,128]{1,0:T(8,128)(2,1)S(1)} %get-tuple-element.85.r_0_, bf16[256,128]{1,0:T(8,128)(2,1)S(1)} %get-tuple-element.91.r_1_, ...), custom_call_target="tpu_custom_call" | custom-call | tf_op jit(solution)/shard_map/chunk_line/pallas_call | solution.py:241
  36.5 2.3 %collective-permute-start.8 = (bf16[2752,128]{1,0:T(8,128)(2,1)S(1)}, bf16[2752,128]{1,0:T(8,128)(2,1)S(1)}, u32[]{:S(2)}, u32[]{:S(2)}) collective-permute-start(bf16[2752,128]{1,0:T(8,128)(2,1)S(1)} %get-tuple-element.101), channel_id=1, source_target_pairs={{0,48},{1,49},{2,50},{3,51},{4,52},{5,53},{6,54},{7,55},{8,200},{9... | collective-permute-start | bytes 2113544 | tf_op jit(solution)/shard_map/ppermute | solution.py:429
  39.8 1.2 %collective-permute-start.9 = (bf16[1344,128]{1,0:T(8,128)(2,1)S(1)}, bf16[1344,128]{1,0:T(8,128)(2,1)S(1)}, u32[]{:S(2)}, u32[]{:S(2)}) collective-permute-start(bf16[1344,128]{1,0:T(8,128)(2,1)S(1)} %slice.20), channel_id=1, source_target_pairs={{0,16},{1,17},{2,18},{3,19},{4,20},{5,21},{6,22},{7,23},{8,72},{9,... | collective-permute-start | bytes 1032200 | tf_op jit(solution)/shard_map/ppermute | solution.py:429
  41.0 3.3 %collective-permute-start.11 = (f32[8,128]{1,0:T(8,128)S(1)}, f32[8,128]{1,0:T(8,128)S(1)}, u32[]{:S(2)}, u32[]{:S(2)}) collective-permute-start(f32[8,128]{1,0:T(8,128)S(1)} %broadcast_add_fusion), channel_id=1, source_target_pairs={{0,2},{1,3},{2,0},{3,1},{4,6},{5,7},{6,4},{7,5},{8,10},{9,11},{10,... | collective-permute-start | bytes 12296 | tf_op jit(solution)/shard_map/ppermute | solution.py:431
  44.3 5.4 %chunk_near1.1 = (f32[1536,384]{1,0:T(8,128)S(1)}, f32[1536,384]{1,0:T(8,128)S(1)}, f32[1536,256]{1,0:T(8,128)S(1)}, f32[384,128]{1,0:T(8,128)S(1)}, f32[384,128]{1,0:T(8,128)S(1)}, /*index=5*/f32[144,128]{1,0:T(8,128)S(1)}) custom-call(bf16[2752,128]{1,0:T(8,128)(2,1)S(1)} %collective-permute-done.4.r_0_, ...), custom_call_target="tpu_custom_call" | custom-call | tf_op jit(solution)/shard_map/chunk_near1/pallas_call | solution.py:241
  49.7 1.6 %collective-permute-done.10.r_1_ = bf16[1344,128]{1,0:T(8,128)(2,1)S(1)} collective-permute-done((bf16[1344,128]{1,0:T(8,128)(2,1)S(1)}, bf16[1344,128]{1,0:T(8,128)(2,1)S(1)}, u32[]{:S(2)}, u32[]{:S(2)}) %collective-permute-start.10) | collective-permute-done | bytes 344096 | tf_op jit(solution)/shard_map/ppermute | solution.py:429
  51.6 2.9 %chunk_far1.1 = (f32[1536,384]{1,0:T(8,128)S(1)}, f32[1536,384]{1,0:T(8,128)S(1)}, f32[1536,256]{1,0:T(8,128)S(1)}, f32[384,128]{1,0:T(8,128)S(1)}, f32[384,128]{1,0:T(8,128)S(1)}, /*index=5*/f32[144,128]{1,0:T(8,128)S(1)}) custom-call(bf16[1344,128]{1,0:T(8,128)(2,1)S(1)} %collective-permute-done.9.r_0_, ...), custom_call_target="tpu_custom_call" | custom-call | tf_op jit(solution)/shard_map/chunk_far1/pallas_call | solution.py:241
  54.5 1.1 collective-permute-start.12
  55.6 2.3 %collective-permute-start.13 = (bf16[1344,128]{1,0:T(8,128)(2,1)S(1)}, bf16[1344,128]{1,0:T(8,128)(2,1)S(1)}, u32[]{:S(2)}, u32[]{:S(2)}) collective-permute-start(bf16[1344,128]{1,0:T(8,128)(2,1)S(1)} %slice.23), channel_id=1, source_target_pairs={{0,48},{1,49},{2,50},{3,51},{4,52},{5,53},{6,54},{7,55},{8,200},{9... | collective-permute-start | bytes 1032200 | tf_op jit(solution)/shard_map/ppermute | solution.py:429
  57.9 6.9 %collective-permute-start.14 = (f32[8,128]{1,0:T(8,128)S(1)}, f32[8,128]{1,0:T(8,128)S(1)}, u32[]{:S(2)}, u32[]{:S(2)}) collective-permute-start(f32[8,128]{1,0:T(8,128)S(1)} %add.30), channel_id=1, source_target_pairs={{0,4},{1,5},{2,6},{3,7},{4,0},{5,1},{6,2},{7,3},{8,12},{9,13},{10,... | collective-permute-start | bytes 12296 | tf_op jit(solution)/shard_map/ppermute | solution.py:431
  64.8 5.4 %chunk_near2.1 = (f32[1536,384]{1,0:T(8,128)S(1)}, f32[1536,384]{1,0:T(8,128)S(1)}, f32[1536,256]{1,0:T(8,128)S(1)}, f32[384,128]{1,0:T(8,128)S(1)}, f32[384,128]{1,0:T(8,128)S(1)}, /*index=5*/f32[144,128]{1,0:T(8,128)S(1)}) custom-call(bf16[2752,128]{1,0:T(8,128)(2,1)S(1)} %collective-permute-done.7.r_0_, ...), custom_call_target="tpu_custom_call" | custom-call | tf_op jit(solution)/shard_map/chunk_near2/pallas_call | solution.py:241
  70.3 2.8 %chunk_far2.1 = (f32[1536,384]{1,0:T(8,128)S(1)}, f32[1536,384]{1,0:T(8,128)S(1)}, f32[1536,256]{1,0:T(8,128)S(1)}, f32[384,128]{1,0:T(8,128)S(1)}, f32[384,128]{1,0:T(8,128)S(1)}, /*index=5*/f32[144,128]{1,0:T(8,128)S(1)}) custom-call(bf16[1344,128]{1,0:T(8,128)(2,1)S(1)} %collective-permute-done.12.r_0_, ...), custom_call_target="tpu_custom_call" | custom-call | tf_op jit(solution)/shard_map/chunk_far2/pallas_call | solution.py:241
  73.1 1.3 %collective-permute-done.15.b_ref = f32[144,128]{1,0:T(8,128)S(1)} collective-permute-done((f32[144,128]{1,0:T(8,128)S(1)}, f32[144,128]{1,0:T(8,128)S(1)}, u32[]{:S(2)}, u32[]{:S(2)}) %collective-permute-start.15) | collective-permute-done | bytes 73760 | tf_op jit(solution)/shard_map/ppermute | solution.py:430
  75.1 16.0 %panel_factor.1 = (f32[128,128]{1,0:T(8,128)S(1)}, f32[128,128]{1,0:T(8,128)S(1)}, f32[16,128]{1,0:T(8,128)S(1)}) custom-call(f32[144,128]{1,0:T(8,128)S(1)} %get-tuple-element.146.a_ref, f32[144,128]{1,0:T(8,128)S(1)} %collective-permute-done.15.b_ref, f32[8,128]{1,0:T(8,128)S(1)} %add.31.d_ref), custom_call_target="tpu_custom_call" | custom-call | tf_op jit(solution)/shard_map/panel_factor/pallas_call | solution.py:299
  91.1 2.0 %panel_solve.1 = (f32[12,128]{1,0:T(8,128)S(1)}, f32[1536,128]{1,0:T(8,128)S(1)}, bf16[1536,384]{1,0:T(8,128)(2,1)S(1)}, bf16[384,384]{1,0:T(8,128)(2,1)S(1)}) custom-call(s32[1]{0:T(128)} %copy.14.k_ref, f32[1536,256]{1,0:T(8,128)S(1)} %get-tuple-element.150.p_ref, f32[1536,256]{1,0:T(8,128)S(1)} %collective-permute-done.16.pr_ref, ...), custom_call_target="tpu_custom_call" | custom-call | tf_op jit(solution)/shard_map/panel_solve/pallas_call | solution.py:353
  93.1 1.0 collective-permute-start.18
  94.2 3.1 %collective-permute-done.18 = f32[12,8,128]{2,1,0:T(8,128)S(1)} collective-permute-done((f32[12,8,128]{2,1,0:T(8,128)S(1)}, f32[12,8,128]{2,1,0:T(8,128)S(1)}, u32[]{:S(2)}, u32[]{:S(2)}) %collective-permute-start.18) | collective-permute-done | bytes 49184 | tf_op jit(solution)/shard_map/ppermute | solution.py:431
  97.3 1.5 %collective-permute-start.19 = (f32[12,8,128]{2,1,0:T(8,128)S(1)}, f32[12,8,128]{2,1,0:T(8,128)S(1)}, u32[]{:S(2)}, u32[]{:S(2)}) collective-permute-start(f32[12,8,128]{2,1,0:T(8,128)S(1)} %fusion), channel_id=1, source_target_pairs={{0,2},{1,3},{2,0},{3,1},{4,6},{5,7},{6,4},{7,5},{8,10},{9,11},{10,... | collective-permute-start | bytes 147464 | tf_op jit(solution)/shard_map/ppermute | solution.py:431
  98.8 3.5 %collective-permute-done.19 = f32[12,8,128]{2,1,0:T(8,128)S(1)} collective-permute-done((f32[12,8,128]{2,1,0:T(8,128)S(1)}, f32[12,8,128]{2,1,0:T(8,128)S(1)}, u32[]{:S(2)}, u32[]{:S(2)}) %collective-permute-start.19) | collective-permute-done | bytes 49184 | tf_op jit(solution)/shard_map/ppermute | solution.py:431
  102.4 5.7 %trailing_update.1 = f32[4608,128]{1,0:T(8,128)} custom-call(s32[1]{0:T(128)} %copy.14.k_ref, f32[1536,384]{1,0:T(8,128)S(1)} %get-tuple-element.160.g_ref, f32[1536,384]{1,0:T(8,128)S(1)} %collective-permute-done.20.gr_ref, bf16[1536,384]{1,0:T(8,128)(2,1)S(1)} %get-tuple-element.162.la_ref, bf16[384,384]{1,0:T(8,128)(2,1)S(1)} %get-tuple-element.163.lb_ref, ...), custom_call_target="tpu_custom_call" | custom-call | tf_op jit(solution)/shard_map/trailing_update/pallas_call | solution.py:396
  108.1 2.1 %collective-permute-start.21 = (f32[12,8,128]{2,1,0:T(8,128)S(1)}, f32[12,8,128]{2,1,0:T(8,128)S(1)}, u32[]{:S(2)}, u32[]{:S(2)}) collective-permute-start(f32[12,8,128]{2,1,0:T(8,128)S(1)} %add.33), channel_id=1, source_target_pairs={{0,4},{1,5},{2,6},{3,7},{4,0},{5,1},{6,2},{7,3},{8,12},{9,13},{10,... | collective-permute-start | bytes 147464 | tf_op jit(solution)/shard_map/ppermute | solution.py:431
  110.2 5.9 %collective-permute-done.21 = f32[12,8,128]{2,1,0:T(8,128)S(1)} collective-permute-done((f32[12,8,128]{2,1,0:T(8,128)S(1)}, f32[12,8,128]{2,1,0:T(8,128)S(1)}, u32[]{:S(2)}, u32[]{:S(2)}) %collective-permute-start.21) | collective-permute-done | bytes 49184 | tf_op jit(solution)/shard_map/ppermute | solution.py:431
  (51 shorter events, 11.6 us)
Async XLA Ops:
  2.6 1.1 copy-start
  3.7 1.0 copy-start.1
  4.7 0.7 copy-start.2
  6.4 8.5 %collective-permute-start = (bf16[1664,128]{1,0:T(8,128)(2,1)S(1)}, bf16[1664,128]{1,0:T(8,128)(2,1)S(1)}, u32[]{:S(2)}, u32[]{:S(2)}) collective-permute-start(bf16[1664,128]{1,0:T(8,128)(2,1)S(1)} %get-tuple-element.85.r_0_), channel_id=1, source_target_pairs={{0,64},{1,65},{2,66},{3,67},{4,68},{5,69},{6,70},{7,71},{8,24},{9,... | collective-permute-start | bytes 1277960 | tf_op jit(solution)/shard_map/ppermute | solution.py:428
  8.0 8.1 %collective-permute-start.1 = (bf16[1664,128]{1,0:T(8,128)(2,1)S(1)}, bf16[1664,128]{1,0:T(8,128)(2,1)S(1)}, u32[]{:S(2)}, u32[]{:S(2)}) collective-permute-start(bf16[1664,128]{1,0:T(8,128)(2,1)S(1)} %get-tuple-element.86), channel_id=1, source_target_pairs={{0,192},{1,193},{2,194},{3,195},{4,196},{5,197},{6,198},{7,199},{8... | collective-permute-start | bytes 1277960 | tf_op jit(solution)/shard_map/ppermute | solution.py:428
  17.1 18.4 %collective-permute-start.4 = (bf16[2752,128]{1,0:T(8,128)(2,1)}, bf16[2752,128]{1,0:T(8,128)(2,1)S(1)}, u32[]{:S(2)}, u32[]{:S(2)}) collective-permute-start(bf16[2752,128]{1,0:T(8,128)(2,1)} %get-tuple-element.92), channel_id=1, source_target_pairs={{0,16},{1,17},{2,18},{3,19},{4,20},{5,21},{6,22},{7,23},{8,72},{9,... | collective-permute-start | bytes 2113544 | tf_op jit(solution)/shard_map/ppermute | solution.py:429
  18.6 16.8 %collective-permute-start.5 = (bf16[2752,128]{1,0:T(8,128)(2,1)S(1)}, bf16[2752,128]{1,0:T(8,128)(2,1)S(1)}, u32[]{:S(2)}, u32[]{:S(2)}) collective-permute-start(bf16[2752,128]{1,0:T(8,128)(2,1)S(1)} %get-tuple-element.93), channel_id=1, source_target_pairs={{0,48},{1,49},{2,50},{3,51},{4,52},{5,53},{6,54},{7,55},{8,200},{9... | collective-permute-start | bytes 2113544 | tf_op jit(solution)/shard_map/ppermute | solution.py:429
  21.0 4.1 %collective-permute-start.6 = (f32[8,128]{1,0:T(8,128)S(1)}, f32[8,128]{1,0:T(8,128)S(1)}, u32[]{:S(2)}, u32[]{:S(2)}) collective-permute-start(f32[8,128]{1,0:T(8,128)S(1)} %broadcast_in_dim.32), channel_id=1, source_target_pairs={{0,1},{1,0},{2,3},{3,2},{4,5},{5,4},{6,7},{7,6},{8,9},{9,8},{10,11... | collective-permute-start | bytes 12296 | tf_op jit(solution)/shard_map/ppermute | solution.py:431
  22.9 5.7 %collective-permute-start.2 = (bf16[768,128]{1,0:T(8,128)(2,1)S(1)}, bf16[768,128]{1,0:T(8,128)(2,1)S(1)}, u32[]{:S(2)}, u32[]{:S(2)}) collective-permute-start(bf16[768,128]{1,0:T(8,128)(2,1)S(1)} %slice.18), channel_id=1, source_target_pairs={{0,64},{1,65},{2,66},{3,67},{4,68},{5,69},{6,70},{7,71},{8,24},{9,... | collective-permute-start | bytes 589832 | tf_op jit(solution)/shard_map/ppermute | solution.py:428
  24.2 5.7 %collective-permute-start.3 = (bf16[768,128]{1,0:T(8,128)(2,1)S(1)}, bf16[768,128]{1,0:T(8,128)(2,1)S(1)}, u32[]{:S(2)}, u32[]{:S(2)}) collective-permute-start(bf16[768,128]{1,0:T(8,128)(2,1)S(1)} %slice.19), channel_id=1, source_target_pairs={{0,192},{1,193},{2,194},{3,195},{4,196},{5,197},{6,198},{7,199},{8... | collective-permute-start | bytes 589832 | tf_op jit(solution)/shard_map/ppermute | solution.py:428
  35.5 19.0 %collective-permute-start.7 = (bf16[2752,128]{1,0:T(8,128)(2,1)S(1)}, bf16[2752,128]{1,0:T(8,128)(2,1)S(1)}, u32[]{:S(2)}, u32[]{:S(2)}) collective-permute-start(bf16[2752,128]{1,0:T(8,128)(2,1)S(1)} %get-tuple-element.100), channel_id=1, source_target_pairs={{0,16},{1,17},{2,18},{3,19},{4,20},{5,21},{6,22},{7,23},{8,72},{9,... | collective-permute-start | bytes 2113544 | tf_op jit(solution)/shard_map/ppermute | solution.py:429
  36.5 17.9 %collective-permute-start.8 = (bf16[2752,128]{1,0:T(8,128)(2,1)S(1)}, bf16[2752,128]{1,0:T(8,128)(2,1)S(1)}, u32[]{:S(2)}, u32[]{:S(2)}) collective-permute-start(bf16[2752,128]{1,0:T(8,128)(2,1)S(1)} %get-tuple-element.101), channel_id=1, source_target_pairs={{0,48},{1,49},{2,50},{3,51},{4,52},{5,53},{6,54},{7,55},{8,200},{9... | collective-permute-start | bytes 2113544 | tf_op jit(solution)/shard_map/ppermute | solution.py:429
  38.8 12.5 %collective-permute-start.10 = (bf16[1344,128]{1,0:T(8,128)(2,1)S(1)}, bf16[1344,128]{1,0:T(8,128)(2,1)S(1)}, u32[]{:S(2)}, u32[]{:S(2)}) collective-permute-start(bf16[1344,128]{1,0:T(8,128)(2,1)S(1)} %slice.21), channel_id=1, source_target_pairs={{0,48},{1,49},{2,50},{3,51},{4,52},{5,53},{6,54},{7,55},{8,200},{9... | collective-permute-start | bytes 1032200 | tf_op jit(solution)/shard_map/ppermute | solution.py:429
  39.8 11.8 %collective-permute-start.9 = (bf16[1344,128]{1,0:T(8,128)(2,1)S(1)}, bf16[1344,128]{1,0:T(8,128)(2,1)S(1)}, u32[]{:S(2)}, u32[]{:S(2)}) collective-permute-start(bf16[1344,128]{1,0:T(8,128)(2,1)S(1)} %slice.20), channel_id=1, source_target_pairs={{0,16},{1,17},{2,18},{3,19},{4,20},{5,21},{6,22},{7,23},{8,72},{9,... | collective-permute-start | bytes 1032200 | tf_op jit(solution)/shard_map/ppermute | solution.py:429
  41.0 8.6 %collective-permute-start.11 = (f32[8,128]{1,0:T(8,128)S(1)}, f32[8,128]{1,0:T(8,128)S(1)}, u32[]{:S(2)}, u32[]{:S(2)}) collective-permute-start(f32[8,128]{1,0:T(8,128)S(1)} %broadcast_add_fusion), channel_id=1, source_target_pairs={{0,2},{1,3},{2,0},{3,1},{4,6},{5,7},{6,4},{7,5},{8,10},{9,11},{10,... | collective-permute-start | bytes 12296 | tf_op jit(solution)/shard_map/ppermute | solution.py:431
  54.5 15.7 %collective-permute-start.12 = (bf16[1344,128]{1,0:T(8,128)(2,1)S(1)}, bf16[1344,128]{1,0:T(8,128)(2,1)S(1)}, u32[]{:S(2)}, u32[]{:S(2)}) collective-permute-start(bf16[1344,128]{1,0:T(8,128)(2,1)S(1)} %slice.22), channel_id=1, source_target_pairs={{0,16},{1,17},{2,18},{3,19},{4,20},{5,21},{6,22},{7,23},{8,72},{9,... | collective-permute-start | bytes 1032200 | tf_op jit(solution)/shard_map/ppermute | solution.py:429
  55.6 14.6 %collective-permute-start.13 = (bf16[1344,128]{1,0:T(8,128)(2,1)S(1)}, bf16[1344,128]{1,0:T(8,128)(2,1)S(1)}, u32[]{:S(2)}, u32[]{:S(2)}) collective-permute-start(bf16[1344,128]{1,0:T(8,128)(2,1)S(1)} %slice.23), channel_id=1, source_target_pairs={{0,48},{1,49},{2,50},{3,51},{4,52},{5,53},{6,54},{7,55},{8,200},{9... | collective-permute-start | bytes 1032200 | tf_op jit(solution)/shard_map/ppermute | solution.py:429
  57.9 12.3 %collective-permute-start.14 = (f32[8,128]{1,0:T(8,128)S(1)}, f32[8,128]{1,0:T(8,128)S(1)}, u32[]{:S(2)}, u32[]{:S(2)}) collective-permute-start(f32[8,128]{1,0:T(8,128)S(1)} %add.30), channel_id=1, source_target_pairs={{0,4},{1,5},{2,6},{3,7},{4,0},{5,1},{6,2},{7,3},{8,12},{9,13},{10,... | collective-permute-start | bytes 12296 | tf_op jit(solution)/shard_map/ppermute | solution.py:431
  73.0 25.8 %copy-start.3 = (f32[12,1,128]{2,1,0:T(1,128)S(1)}, f32[12,1,128]{2,1,0:T(1,128)}, u32[]{:S(2)}) copy-start(f32[12,1,128]{2,1,0:T(1,128)} %param.12) | copy-start | bytes 18436
  73.0 1.4 %collective-permute-start.15 = (f32[144,128]{1,0:T(8,128)S(1)}, f32[144,128]{1,0:T(8,128)S(1)}, u32[]{:S(2)}, u32[]{:S(2)}) collective-permute-start(f32[144,128]{1,0:T(8,128)S(1)} %get-tuple-element.146.a_ref), channel_id=1, source_target_pairs={{0,8},{8,0},{1,9},{9,1},{2,10},{10,2},{3,11},{11,3},{4,12},{12,4},... | collective-permute-start | bytes 221192 | tf_op jit(solution)/shard_map/ppermute | solution.py:430
  74.4 28.0 %collective-permute-start.20 = (f32[1536,384]{1,0:T(8,128)S(1)}, f32[1536,384]{1,0:T(8,128)S(1)}, u32[]{:S(2)}, u32[]{:S(2)}) collective-permute-start(f32[1536,384]{1,0:T(8,128)S(1)} %get-tuple-element.161), channel_id=1, source_target_pairs={{0,8},{8,0},{1,9},{9,1},{2,10},{10,2},{3,11},{11,3},{4,12},{12,4},... | collective-permute-start | bytes 7077896 | tf_op jit(solution)/shard_map/ppermute | solution.py:430
  74.6 16.5 %collective-permute-start.16 = (f32[1536,256]{1,0:T(8,128)S(1)}, f32[1536,256]{1,0:T(8,128)S(1)}, u32[]{:S(2)}, u32[]{:S(2)}) collective-permute-start(f32[1536,256]{1,0:T(8,128)S(1)} %get-tuple-element.150.p_ref), channel_id=1, source_target_pairs={{0,8},{8,0},{1,9},{9,1},{2,10},{10,2},{3,11},{11,3},{4,12},{12,4},... | collective-permute-start | bytes 4718600 | tf_op jit(solution)/shard_map/ppermute | solution.py:430
  74.9 16.2 %collective-permute-start.17 = (f32[384,128]{1,0:T(8,128)S(1)}, f32[384,128]{1,0:T(8,128)S(1)}, u32[]{:S(2)}, u32[]{:S(2)}) collective-permute-start(f32[384,128]{1,0:T(8,128)S(1)} %get-tuple-element.152), channel_id=1, source_target_pairs={{0,8},{8,0},{1,9},{9,1},{2,10},{10,2},{3,11},{11,3},{4,12},{12,4},... | collective-permute-start | bytes 589832 | tf_op jit(solution)/shard_map/ppermute | solution.py:430
  93.1 4.1 %collective-permute-start.18 = (f32[12,8,128]{2,1,0:T(8,128)S(1)}, f32[12,8,128]{2,1,0:T(8,128)S(1)}, u32[]{:S(2)}, u32[]{:S(2)}) collective-permute-start(f32[12,8,128]{2,1,0:T(8,128)S(1)} %broadcast_select_fusion), channel_id=1, source_target_pairs={{0,1},{1,0},{2,3},{3,2},{4,5},{5,4},{6,7},{7,6},{8,9},{9,8},{10,11... | collective-permute-start | bytes 147464 | tf_op jit(solution)/shard_map/ppermute | solution.py:431
  97.3 5.0 %collective-permute-start.19 = (f32[12,8,128]{2,1,0:T(8,128)S(1)}, f32[12,8,128]{2,1,0:T(8,128)S(1)}, u32[]{:S(2)}, u32[]{:S(2)}) collective-permute-start(f32[12,8,128]{2,1,0:T(8,128)S(1)} %fusion), channel_id=1, source_target_pairs={{0,2},{1,3},{2,0},{3,1},{4,6},{5,7},{6,4},{7,5},{8,10},{9,11},{10,... | collective-permute-start | bytes 147464 | tf_op jit(solution)/shard_map/ppermute | solution.py:431
  108.1 8.0 %collective-permute-start.21 = (f32[12,8,128]{2,1,0:T(8,128)S(1)}, f32[12,8,128]{2,1,0:T(8,128)S(1)}, u32[]{:S(2)}, u32[]{:S(2)}) collective-permute-start(f32[12,8,128]{2,1,0:T(8,128)S(1)} %add.33), channel_id=1, source_target_pairs={{0,4},{1,5},{2,6},{3,7},{4,0},{5,1},{6,2},{7,3},{8,12},{9,13},{10,... | collective-permute-start | bytes 147464 | tf_op jit(solution)/shard_map/ppermute | solution.py:431

commit v4 on v3

--- a/solution.py
+++ b/solution.py
@@ -245,6 +245,9 @@
         out_specs=(VM,) * len(ACCS),
         scratch_shapes=[pltpu.VMEM((JR, n * M), BF16), pltpu.VMEM((n, 192, M), F32)],
         compiler_params=params(),
+        cost_estimate=pl.CostEstimate(
+            flops=n * 2 * JR * K * (RU + C), bytes_accessed=n * 4_000_000, transcendentals=0
+        ),
         name=name,
     )(*arrs, *accs)
 
@@ -271,20 +274,33 @@
     gram = (a_ref[0:K, :] + b_ref[0:K, :]) * (1.0 / TOTAL)
     m_ref[:, :K] = gram + jnp.where(eye, d_ref[0:1, :], 0.0)
     m_ref[:, K:] = jnp.where(eye, 1.0, 0.0)
-    sub = lax.broadcasted_iota(jnp.int32, (8, 2 * K), 0)
+    sub = lax.broadcasted_iota(jnp.int32, (8, K), 0)
+    pick = lambda v, r: jnp.broadcast_to(v[r : r + 1, :], (8, v.shape[1]))
     for b in range(K // 8):
-        p = m_ref[8 * b : 8 * b + 8, :]
+        lo = 8 * b
+        p = m_ref[lo : lo + 8, :]
+        left, right = p[:, :K], p[:, K:]
+        cols = [jnp.broadcast_to(p[:, lo + c : lo + c + 1], (8, K)) for c in range(8)]
+        scale = jnp.ones((8, K), F32)
         for r in range(8):
-            j = 8 * b + r
-            cb = p[:, j : j + 1]
-            rs = lax.rsqrt(p[r : r + 1, j : j + 1])
-            urow = p[r : r + 1, :] * rs
-            p = jnp.where(sub > r, p - (cb * rs) * urow, jnp.where(sub == r, urow, p))
-        u_ref[8 * b : 8 * b + 8, :] = p
+            rs = lax.rsqrt(pick(cols[r], r))
+            mult = jnp.where(sub > r, cols[r] * (rs * rs), 0.0)
+            for c in range(r + 1, 8):
+                cols[c] = cols[c] - mult * pick(cols[c], r)
+            scale = jnp.where(sub == r, rs, scale)
+            left = left - mult * pick(left, r)
+            right = right - mult * pick(right, r)
+        p = jnp.concatenate([left * scale, right * scale], axis=1)
+        u_ref[lo : lo + 8, :] = p
         if b < K // 8 - 1:
-            upd = lax.dot_general(p[:, :K], p, TN, precision=HI, preferred_element_type=F32)
-            lo = 8 * (b + 1)
-            m_ref[lo:, :] = m_ref[lo:, :] - upd[lo:, :]
+            ut = p[:, :K].T
+            rows = [pick(p, r) for r in range(8)]
+            for t in range(b + 1, K // 8):
+                at = slice(8 * t, 8 * t + 8)
+                acc = m_ref[at, :]
+                for r in range(8):
+                    acc = acc - jnp.broadcast_to(ut[at, r : r + 1], (8, 2 * K)) * rows[r]
+                m_ref[at, :] = acc
     chol_ref[...] = jnp.where(col >= row, u_ref[:, :K], 0.0).T
     w = u_ref[:, K:]
     w_ref[...] = w
@@ -365,10 +381,11 @@
     )(k, p, pr, po, por, w, yz)
 
 
-def final_kernel(k_ref, g_ref, gr_ref, la_ref, lb_ref, lpan_ref, chol_ref, damp_ref, out_ref):
+def final_kernel(start, k_ref, g_ref, gr_ref, la_ref, lb_ref, lpan_ref, chol_ref, damp_ref, *refs):
+    out_ref = refs[-1]
     q, k = lax.axis_index("row"), k_ref[0]
     s = (lax.axis_index("x") * NY + lax.axis_index("y")) * NC + lax.axis_index("core")
-    lr = pl.program_id(0)
+    lr = start + pl.program_id(0)
     i = lr * NZ + q
     upd = lax.dot_general(la_ref[...], lb_ref[...], NT, preferred_element_type=F32)
     gram = (g_ref[...] + gr_ref[...]) * (1.0 / TOTAL)
@@ -390,21 +407,25 @@
         out_ref[pl.ds(lc, K, stride=LC), :] = val
 
 
-def final(k, gown, grecv, la, lb, lpan, chol, damp):
+def final(start, count, k, gown, grecv, la, lb, lpan, chol, damp, *prev):
     full = lambda shape: pl.BlockSpec(shape, lambda i: (0,) * len(shape))
-    rows = lambda width: pl.BlockSpec((K, width), lambda i: (i, 0))
+    rows = lambda width: pl.BlockSpec((K, width), lambda i: (i + start, 0))
     return pl.pallas_call(
-        final_kernel,
-        grid=(LR,),
+        lambda *r: final_kernel(start, *r),
+        grid=(count,),
         out_shape=jax.ShapeDtypeStruct((RU * LC, K), F32),
         in_specs=[
             SMEM, rows(CU), rows(CU), rows(3 * K), full((CU, 3 * K)), rows(K), full((K, K)),
             full((LR, K)),
-        ],
-        out_specs=pl.BlockSpec((K * LC, K), lambda i: (i, 0)),
+        ] + [pl.BlockSpec(memory_space=pl.ANY)] * len(prev),
+        out_specs=pl.BlockSpec((K * LC, K), lambda i: (i + start, 0)),
+        input_output_aliases={8: 0} if prev else {},
         compiler_params=params(),
+        cost_estimate=pl.CostEstimate(
+            flops=count * 6 * K * CU * K, bytes_accessed=count * 1_500_000, transcendentals=0
+        ),
         name="trailing_update",
-    )(k, gown, grecv, la, lb, lpan, chol, damp)
+    )(k, gown, grecv, la, lb, lpan, chol, damp, *prev)
 
 
 def device(x, y, c, z):
@@ -438,29 +459,27 @@
         g_jets.transpose(1, 0, 2).reshape(C * A, POOL),
         jnp.stack([speed, resid]),
     )
-    ap, am = bar((one(plus, 1), one(minus, -1)))
+    dsel = lax.dynamic_index_in_dim(damping[:, 0, :], k // NZ, 0, keepdims=True)
+    dsel = jnp.broadcast_to(jnp.where(k % NZ == q, dsel, 0.0), (8, K))
+    ap, am, dsel = bar((one(plus, 1), one(minus, -1), zbit(dsel, 1)))
     m1 = assemble(BLOCK0, BLOCK1, plus, own, ap)
     relay = HB + 2 * GC
     rp, rm = one(ap[:relay], 1), one(am[:relay], -1)
     m1p, m1m = two(m1[0], 1), two(m1[1], -1)
+    accs = chunk([place(BLOCK0, 0, 0), place(BLOCK1, 0, 0)], (plus, own, ap), (), "chunk_line1")
+    rp, rm, accs, dsel = bar((rp, rm, accs, zbit(dsel, 2)))
     m2 = assemble(BLOCK2, BLOCK3, am, rp, rm)
-    dsel = lax.dynamic_index_in_dim(damping[:, 0, :], k // NZ, 0, keepdims=True)
-    dsel = jnp.broadcast_to(jnp.where(k % NZ == q, dsel, 0.0), (8, K))
-
-    line = [place(BLOCK0, 0, 0), place(BLOCK1, 0, 0), place(BLOCK2, 0, 3), place(BLOCK3, 0, 3)]
-    accs = chunk(line, (plus, own, ap, am, rp, rm), (), "chunk_line")
-    m2, m1p, m1m, accs, dsel = bar((m2, m1p, m1m, accs, zbit(dsel, 1)))
+    m2p, m2m = two(m2[0], 1), two(m2[1], -1)
     n1 = BR + GC
     r1p, r1m = two(m1p[:n1], 1), two(m1m[:n1], -1)
-    m2p, m2m = two(m2[0], 1), two(m2[1], -1)
-    near = received(0, 2 * BR + GC) + received(1, 2 * BR + GC)
-    accs = chunk(near, (m1p, m1m), accs, "chunk_near1")
+    e1 = 2 * BR + GC
+    blocks = received(0, e1) + received(1, e1) + [place(BLOCK2, 0, 2), place(BLOCK3, 0, 2)]
+    accs = chunk(blocks, (m1p, m1m, am, rp, rm), accs, "chunk_line2")
+    r1p, r1m, m2p, m2m, accs, dsel = bar((r1p, r1m, m2p, m2m, accs, zbit(dsel, 4)))
+    r2p, r2m = two(m2p[:n1], 1), two(m2m[:n1], -1)
+    blocks = [received(0, BR)[0], received(1, BR)[0]] + received(2, e1) + received(3, e1)
+    accs = chunk(blocks, (r1p, r1m, m2p, m2m), accs, "chunk_far1")
     far = [received(0, BR)[0], received(1, BR)[0]]
-    accs = chunk(far, (r1p, r1m), accs, "chunk_far1")
-    m2p, m2m, accs, dsel = bar((m2p, m2m, accs, zbit(dsel, 2)))
-    r2p, r2m = two(m2p[:n1], 1), two(m2m[:n1], -1)
-    accs = chunk(near, (m2p, m2m), accs, "chunk_near2")
-    r2p, r2m, accs, dsel = bar((r2p, r2m, accs, zbit(dsel, 4)))
     accs = chunk(far, (r2p, r2m), accs, "chunk_far2")
     gown, gsib, p, po, ps, dk = accs
 
@@ -472,7 +491,9 @@
     slot = lax.broadcasted_iota(jnp.int32, (1, NZ, 1), 1)
     full = jnp.where(slot == q, mine[:, None, :], 0.0)
     full, la = bar((zbit(full, 1), la))
-    fac = final(panel, gown, gr, la, lb, lpan, chol, damping[:, 0, :])
+    rest = (panel, gown, gr, la, lb, lpan, chol, damping[:, 0, :])
+    fac = final(0, 9, *rest)
+    fac = final(9, 3, *rest, fac)
     full, fac = bar((zbit(full, 2), fac))
     full = zbit(full, 4)
     return fac.reshape(LR, 1, K, LC, 1, K), full.reshape(-1)

time: 117 us -> 102 us (0.87)
  waiting for transfers between devices: 27.7 us -> 17 us
  Pallas kernels: 47.6 us -> 37.3 us
  starting transfers between devices: 34.3 us -> 40 us
    pallas_call x1, Pallas kernels: 16 us -> 6.21 us  [cholesky(): pl.pallas_call(chol_kernel, out_shape=(jax.ShapeDtypeStruct((K, K), F32),...]
    ppermute x4, waiting for transfers between devices: 12.1 us -> 3.7 us  [body(): one = lambda v, d: lax.ppermute(v, AXES, hops(0, d))]
    ppermute x6, starting transfers between devices: 16.7 us -> 21.1 us  [body(): lax.ppermute(v, 'row', [(i, i ^ bit) for i in range(NZ)])]
    ppermute x8, waiting for transfers between devices: 1.9 us -> 0.02 us  [body(): two = lambda v, d: lax.ppermute(v, AXES, hops(1, d))]
    ppermute x8, starting transfers between devices: 12.1 us -> 13.6 us  [body(): two = lambda v, d: lax.ppermute(v, AXES, hops(1, d))]
    pallas_call x1 -> x2, Pallas kernels: 5.75 us -> 6.41 us  [final(): pl.pallas_call(lambda *r: final_kernel(start, *r), grid=(count,), out_sha...]
    pallas_call x5 -> x4, Pallas kernels: 21.7 us -> 21.5 us  [chunk(): pl.pallas_call(lambda *r: chunk_kernel(blocks, len(arrs), len(accs), *r),...]
  transfers between devices with their start and end apart: 22 -> 22, of which waited for: 10 -> 10; matrix products, arithmetic and copies ran while one was open for 1% -> 1% of each run, Pallas kernels for 32% -> 27%
where the time goes in v4:
time: 102 us
  starting transfers between devices  40 us (39%)
  Pallas kernels  37.3 us (37%)
  waiting for transfers between devices  17 us (17%)
  local copies, waits for them, and re-layouts  4.18 us (4%)
  between operations  1.5 us (1%)
  other arithmetic  1.47 us (1%)
    pallas_call x4, Pallas kernels, chunk(): pl.pallas_call(lambda *r: chunk_kernel(blocks, len(arrs), len(accs), *r),...  21.5 us
    ppermute x6, starting transfers between devices, body(): lax.ppermute(v, 'row', [(i, i ^ bit) for i in range(NZ)])  21.1 us
    ppermute x8, starting transfers between devices, body(): two = lambda v, d: lax.ppermute(v, AXES, hops(1, d))  13.6 us
    ppermute x6, waiting for transfers between devices, body(): lax.ppermute(v, 'row', [(i, i ^ bit) for i in range(NZ)])  11.8 us
    pallas_call x2, Pallas kernels, final(): pl.pallas_call(lambda *r: final_kernel(start, *r), grid=(count,), out_sha...  6.41 us
    pallas_call x1, Pallas kernels, cholesky(): pl.pallas_call(chol_kernel, out_shape=(jax.ShapeDtypeStruct((K, K), F32),...  6.21 us
    ppermute x4, starting transfers between devices, body(): one = lambda v, d: lax.ppermute(v, AXES, hops(0, d))  4.62 us
    ppermute x4, waiting for transfers between devices, body(): one = lambda v, d: lax.ppermute(v, AXES, hops(0, d))  3.7 us
  transfers between devices with their start and end apart: 22, of which 10 were waited for; matrix products, arithmetic and copies ran while one was open for 1% of the time, Pallas kernels for 27%

profile of v4, /device:TPU:2, one launch (start us, length us, event | category | flops | bytes accessed | tf_op | source)
XLA Modules:
  0.0 101.5 jit_solution(9659913685617224234)
XLA Ops:
  2.6 1.1 %copy-done = bf16[9,128,256]{2,1,0:T(8,128)(2,1)S(1)} copy-done((bf16[9,128,256]{2,1,0:T(8,128)(2,1)S(1)}, bf16[9,128,256]{2,1,0:T(8,128)(2,1)}, u32[]{:S(2)}) %copy-start) | copy-done | bytes 589848
  3.7 1.0 copy-done.1
  5.3 1.0 %pack.1 = (bf16[1664,128]{1,0:T(8,128)(2,1)S(1)}, bf16[1664,128]{1,0:T(8,128)(2,1)S(1)}, bf16[256,128]{1,0:T(8,128)(2,1)S(1)}) custom-call(s32[1]{0:T(128)} %copy.16.k_ref.r_0_, s32[1,128]{1,0:T(1,128)S(1)} %bitcast.22, bf16[1152,256]{1,0:T(8,128)(2,1)S(1)} %bitcast.18, bf16[864,256]{1,0:T(8,128)(2,1)S(1)} %bitcast.19, bf16[2,256]{1,0:T(2,128)(2,1)S(1)} %pad_maximum_fusion.vr_ref), custom_call_target="tpu_custom_call" | custom-call | tf_op jit(solution)/shard_map/pack/pallas_call | solution.py:86
  6.4 1.6 %collective-permute-start = (bf16[1664,128]{1,0:T(8,128)(2,1)S(1)}, bf16[1664,128]{1,0:T(8,128)(2,1)S(1)}, u32[]{:S(2)}, u32[]{:S(2)}) collective-permute-start(bf16[1664,128]{1,0:T(8,128)(2,1)S(1)} %get-tuple-element.71.r_0_), channel_id=1, source_target_pairs={{0,64},{1,65},{2,66},{3,67},{4,68},{5,69},{6,70},{7,71},{8,24},{9,... | collective-permute-start | bytes 1277960 | tf_op jit(solution)/shard_map/ppermute | solution.py:449
  9.5 1.6 %collective-permute-start.2 = (f32[8,128]{1,0:T(8,128)S(1)}, f32[8,128]{1,0:T(8,128)S(1)}, u32[]{:S(2)}, u32[]{:S(2)}) collective-permute-start(f32[8,128]{1,0:T(8,128)S(1)} %broadcast_in_dim.32), channel_id=1, source_target_pairs={{0,1},{1,0},{2,3},{3,2},{4,5},{5,4},{6,7},{7,6},{8,9},{9,8},{10,11... | collective-permute-start | bytes 12296 | tf_op jit(solution)/shard_map/ppermute | solution.py:452
  11.1 2.0 %collective-permute-done.2 = f32[8,128]{1,0:T(8,128)S(1)} collective-permute-done((f32[8,128]{1,0:T(8,128)S(1)}, f32[8,128]{1,0:T(8,128)S(1)}, u32[]{:S(2)}, u32[]{:S(2)}) %collective-permute-start.2) | collective-permute-done | bytes 4128 | tf_op jit(solution)/shard_map/ppermute | solution.py:452
  13.1 1.7 %collective-permute-done.r_2_ = bf16[1664,128]{1,0:T(8,128)(2,1)S(1)} collective-permute-done((bf16[1664,128]{1,0:T(8,128)(2,1)S(1)}, bf16[1664,128]{1,0:T(8,128)(2,1)S(1)}, u32[]{:S(2)}, u32[]{:S(2)}) %collective-permute-start) | collective-permute-done | bytes 426016 | tf_op jit(solution)/shard_map/ppermute | solution.py:449
  14.8 1.2 %collective-permute-done.1.r_0_.r_2_ = bf16[1664,128]{1,0:T(8,128)(2,1)S(1)} collective-permute-done((bf16[1664,128]{1,0:T(8,128)(2,1)S(1)}, bf16[1664,128]{1,0:T(8,128)(2,1)S(1)}, u32[]{:S(2)}, u32[]{:S(2)}) %collective-permute-start.1) | collective-permute-done | bytes 426016 | tf_op jit(solution)/shard_map/ppermute | solution.py:449
  16.2 1.7 %collective-permute-start.3 = (bf16[2752,128]{1,0:T(8,128)(2,1)S(1)}, bf16[2752,128]{1,0:T(8,128)(2,1)S(1)}, u32[]{:S(2)}, u32[]{:S(2)}) collective-permute-start(bf16[2752,128]{1,0:T(8,128)(2,1)S(1)} %get-tuple-element.75), channel_id=1, source_target_pairs={{0,16},{1,17},{2,18},{3,19},{4,20},{5,21},{6,22},{7,23},{8,72},{9,... | collective-permute-start | bytes 2113544 | tf_op jit(solution)/shard_map/ppermute | solution.py:450
  17.9 1.7 %collective-permute-start.5 = (bf16[2752,128]{1,0:T(8,128)(2,1)S(1)}, bf16[2752,128]{1,0:T(8,128)(2,1)S(1)}, u32[]{:S(2)}, u32[]{:S(2)}) collective-permute-start(bf16[2752,128]{1,0:T(8,128)(2,1)S(1)} %get-tuple-element.76), channel_id=1, source_target_pairs={{0,48},{1,49},{2,50},{3,51},{4,52},{5,53},{6,54},{7,55},{8,200},{9... | collective-permute-start | bytes 2113544 | tf_op jit(solution)/shard_map/ppermute | solution.py:450
  19.5 1.5 %collective-permute-start.7 = (bf16[768,128]{1,0:T(8,128)(2,1)S(1)}, bf16[768,128]{1,0:T(8,128)(2,1)S(1)}, u32[]{:S(2)}, u32[]{:S(2)}) collective-permute-start(bf16[768,128]{1,0:T(8,128)(2,1)S(1)} %slice.20), channel_id=1, source_target_pairs={{0,64},{1,65},{2,66},{3,67},{4,68},{5,69},{6,70},{7,71},{8,24},{9,... | collective-permute-start | bytes 589832 | tf_op jit(solution)/shard_map/ppermute | solution.py:449
  21.7 3.3 %collective-permute-start.9 = (f32[8,128]{1,0:T(8,128)S(1)}, f32[8,128]{1,0:T(8,128)S(1)}, u32[]{:S(2)}, u32[]{:S(2)}) collective-permute-start(f32[8,128]{1,0:T(8,128)S(1)} %broadcast_add_fusion), channel_id=1, source_target_pairs={{0,2},{1,3},{2,0},{3,1},{4,6},{5,7},{6,4},{7,5},{8,10},{9,11},{10,... | collective-permute-start | bytes 12296 | tf_op jit(solution)/shard_map/ppermute | solution.py:452
  25.0 2.8 %chunk_line1.1 = (f32[1536,384]{1,0:T(8,128)S(1)}, f32[1536,384]{1,0:T(8,128)S(1)}, f32[1536,256]{1,0:T(8,128)S(1)}, f32[384,128]{1,0:T(8,128)S(1)}, f32[384,128]{1,0:T(8,128)S(1)}, /*index=5*/f32[144,128]{1,0:T(8,128)S(1)}) custom-call(bf16[1664,128]{1,0:T(8,128)(2,1)S(1)} %get-tuple-element.71.r_0_, bf16[256,128]{1,0:T(8,128)(2,1)S(1)} %get-tuple-element.72.r_1_, ...), custom_call_target="tpu_custom_call" | custom-call | flops 2025062400 | bytes 8000000 | tf_op jit(solution)/shard_map/chunk_line1/pallas_call | solution.py:241
  29.3 2.6 %collective-permute-start.11 = (bf16[2752,128]{1,0:T(8,128)(2,1)S(1)}, bf16[2752,128]{1,0:T(8,128)(2,1)S(1)}, u32[]{:S(2)}, u32[]{:S(2)}) collective-permute-start(bf16[2752,128]{1,0:T(8,128)(2,1)S(1)} %get-tuple-element.88), channel_id=1, source_target_pairs={{0,48},{1,49},{2,50},{3,51},{4,52},{5,53},{6,54},{7,55},{8,200},{9... | collective-permute-start | bytes 2113544 | tf_op jit(solution)/shard_map/ppermute | solution.py:450
  32.0 7.2 %collective-permute-start.12 = (f32[8,128]{1,0:T(8,128)S(1)}, f32[8,128]{1,0:T(8,128)S(1)}, u32[]{:S(2)}, u32[]{:S(2)}) collective-permute-start(f32[8,128]{1,0:T(8,128)S(1)} %add.30), channel_id=1, source_target_pairs={{0,4},{1,5},{2,6},{3,7},{4,0},{5,1},{6,2},{7,3},{8,12},{9,13},{10,... | collective-permute-start | bytes 12296 | tf_op jit(solution)/shard_map/ppermute | solution.py:452
  39.2 1.6 %collective-permute-done.12 = f32[8,128]{1,0:T(8,128)S(1)} collective-permute-done((f32[8,128]{1,0:T(8,128)S(1)}, f32[8,128]{1,0:T(8,128)S(1)}, u32[]{:S(2)}, u32[]{:S(2)}) %collective-permute-start.12) | collective-permute-done | bytes 4128 | tf_op jit(solution)/shard_map/ppermute | solution.py:452
  40.9 3.5 %collective-permute-start.6 = (bf16[1344,128]{1,0:T(8,128)(2,1)S(1)}, bf16[1344,128]{1,0:T(8,128)(2,1)S(1)}, u32[]{:S(2)}, u32[]{:S(2)}) collective-permute-start(bf16[1344,128]{1,0:T(8,128)(2,1)S(1)} %slice.25), channel_id=1, source_target_pairs={{0,48},{1,49},{2,50},{3,51},{4,52},{5,53},{6,54},{7,55},{8,200},{9... | collective-permute-start | bytes 1032200 | tf_op jit(solution)/shard_map/ppermute | solution.py:450
  44.4 7.9 %chunk_line2.1 = (f32[1536,384]{1,0:T(8,128)S(1)}, f32[1536,384]{1,0:T(8,128)S(1)}, f32[1536,256]{1,0:T(8,128)S(1)}, f32[384,128]{1,0:T(8,128)S(1)}, f32[384,128]{1,0:T(8,128)S(1)}, /*index=5*/f32[144,128]{1,0:T(8,128)S(1)}) custom-call(bf16[2752,128]{1,0:T(8,128)(2,1)S(1)} %collective-permute-done.3.r_0_, ...), custom_call_target="tpu_custom_call" | custom-call | flops 6075187200 | bytes 24000000 | tf_op jit(solution)/shard_map/chunk_line2/pallas_call | solution.py:241
  52.6 3.3 %collective-permute-start.14 = (bf16[1344,128]{1,0:T(8,128)(2,1)S(1)}, bf16[1344,128]{1,0:T(8,128)(2,1)S(1)}, u32[]{:S(2)}, u32[]{:S(2)}) collective-permute-start(bf16[1344,128]{1,0:T(8,128)(2,1)S(1)} %slice.23), channel_id=1, source_target_pairs={{0,48},{1,49},{2,50},{3,51},{4,52},{5,53},{6,54},{7,55},{8,200},{9... | collective-permute-start | bytes 1032200 | tf_op jit(solution)/shard_map/ppermute | solution.py:450
  55.9 7.9 %chunk_far1.1 = (f32[1536,384]{1,0:T(8,128)S(1)}, f32[1536,384]{1,0:T(8,128)S(1)}, f32[1536,256]{1,0:T(8,128)S(1)}, f32[384,128]{1,0:T(8,128)S(1)}, f32[384,128]{1,0:T(8,128)S(1)}, /*index=5*/f32[144,128]{1,0:T(8,128)S(1)}) custom-call(bf16[1344,128]{1,0:T(8,128)(2,1)S(1)} %collective-permute-done.4.r_0_, bf16[1344,128]{1,0:T(8,128)(2,1)S(1)} %collective-permute-done.6.r_1_, ...), custom_call_target="tpu_custom_call" | custom-call | flops 6075187200 | bytes 24000000 | tf_op jit(solution)/shard_map/chunk_far1/pallas_call | solution.py:241
  63.8 2.9 %chunk_far2.1 = (f32[1536,384]{1,0:T(8,128)S(1)}, f32[1536,384]{1,0:T(8,128)S(1)}, f32[1536,256]{1,0:T(8,128)S(1)}, f32[384,128]{1,0:T(8,128)S(1)}, f32[384,128]{1,0:T(8,128)S(1)}, /*index=5*/f32[144,128]{1,0:T(8,128)S(1)}) custom-call(bf16[1344,128]{1,0:T(8,128)(2,1)S(1)} %collective-permute-done.13.r_0_, ...), custom_call_target="tpu_custom_call" | custom-call | flops 2025062400 | bytes 8000000 | tf_op jit(solution)/shard_map/chunk_far2/pallas_call | solution.py:241
  66.8 1.3 %collective-permute-done.15.b_ref = f32[144,128]{1,0:T(8,128)S(1)} collective-permute-done((f32[144,128]{1,0:T(8,128)S(1)}, f32[144,128]{1,0:T(8,128)S(1)}, u32[]{:S(2)}, u32[]{:S(2)}) %collective-permute-start.15) | collective-permute-done | bytes 73760 | tf_op jit(solution)/shard_map/ppermute | solution.py:451
  68.7 6.2 %panel_factor.1 = (f32[128,128]{1,0:T(8,128)S(1)}, f32[128,128]{1,0:T(8,128)S(1)}, f32[16,128]{1,0:T(8,128)S(1)}) custom-call(f32[144,128]{1,0:T(8,128)S(1)} %get-tuple-element.118.a_ref, f32[144,128]{1,0:T(8,128)S(1)} %collective-permute-done.15.b_ref, f32[8,128]{1,0:T(8,128)S(1)} %add.31.d_ref), custom_call_target="tpu_custom_call" | custom-call | tf_op jit(solution)/shard_map/panel_factor/pallas_call | solution.py:315
  75.1 1.9 %panel_solve.1 = (f32[12,128]{1,0:T(8,128)S(1)}, f32[1536,128]{1,0:T(8,128)S(1)}, bf16[1536,384]{1,0:T(8,128)(2,1)S(1)}, bf16[384,384]{1,0:T(8,128)(2,1)S(1)}) custom-call(s32[1]{0:T(128)} %copy.16.k_ref.r_0_, f32[1536,256]{1,0:T(8,128)S(1)} %get-tuple-element.122.p_ref, f32[1536,256]{1,0:T(8,128)S(1)} %collective-permute-done.16.pr_ref, ...), custom_call_target="tpu_custom_call" | custom-call | tf_op jit(solution)/shard_map/panel_solve/pallas_call | solution.py:369
  77.1 1.0 %collective-permute-start.18 = (f32[12,8,128]{2,1,0:T(8,128)S(1)}, f32[12,8,128]{2,1,0:T(8,128)S(1)}, u32[]{:S(2)}, u32[]{:S(2)}) collective-permute-start(f32[12,8,128]{2,1,0:T(8,128)S(1)} %broadcast_select_fusion), channel_id=1, source_target_pairs={{0,1},{1,0},{2,3},{3,2},{4,5},{5,4},{6,7},{7,6},{8,9},{9,8},{10,11... | collective-permute-start | bytes 147464 | tf_op jit(solution)/shard_map/ppermute | solution.py:452
  78.2 3.1 %collective-permute-done.18 = f32[12,8,128]{2,1,0:T(8,128)S(1)} collective-permute-done((f32[12,8,128]{2,1,0:T(8,128)S(1)}, f32[12,8,128]{2,1,0:T(8,128)S(1)}, u32[]{:S(2)}, u32[]{:S(2)}) %collective-permute-start.18) | collective-permute-done | bytes 49184 | tf_op jit(solution)/shard_map/ppermute | solution.py:452
  81.3 2.0 %collective-permute-start.19 = (f32[12,8,128]{2,1,0:T(8,128)S(1)}, f32[12,8,128]{2,1,0:T(8,128)S(1)}, u32[]{:S(2)}, u32[]{:S(2)}) collective-permute-start(f32[12,8,128]{2,1,0:T(8,128)S(1)} %fusion), channel_id=1, source_target_pairs={{0,2},{1,3},{2,0},{3,1},{4,6},{5,7},{6,4},{7,5},{8,10},{9,11},{10,... | collective-permute-start | bytes 147464 | tf_op jit(solution)/shard_map/ppermute | solution.py:452
  83.3 3.0 %collective-permute-done.19 = f32[12,8,128]{2,1,0:T(8,128)S(1)} collective-permute-done((f32[12,8,128]{2,1,0:T(8,128)S(1)}, f32[12,8,128]{2,1,0:T(8,128)S(1)}, u32[]{:S(2)}, u32[]{:S(2)}) %collective-permute-start.19) | collective-permute-done | bytes 49184 | tf_op jit(solution)/shard_map/ppermute | solution.py:452
  86.4 4.6 %trailing_update.2.r_8_ = f32[4608,128]{1,0:T(8,128)} custom-call(s32[1]{0:T(128)} %copy.16.k_ref.r_0_, f32[1536,384]{1,0:T(8,128)S(1)} %get-tuple-element.132.r_1_, f32[1536,384]{1,0:T(8,128)S(1)} %collective-permute-done.20.r_2_, bf16[1536,384]{1,0:T(8,128)(2,1)S(1)} %get-tuple-element.134.r_3_, bf16[384,384]{1,0:T(8,128)(2,1)S(1)} %get-tuple-element.135.r_4_, ...), custom_call_target="tpu_custom_call" | custom-call | flops 339738624 | bytes 13500000 | tf_op jit(solution)/shard_map/trailing_update/pallas_call | solution.py:413
  90.9 1.8 %trailing_update.3 = f32[4608,128]{1,0:T(8,128)} custom-call(s32[1]{0:T(128)} %copy.16.k_ref.r_0_, f32[1536,384]{1,0:T(8,128)S(1)} %get-tuple-element.132.r_1_, f32[1536,384]{1,0:T(8,128)S(1)} %collective-permute-done.20.r_2_, bf16[1536,384]{1,0:T(8,128)(2,1)S(1)} %get-tuple-element.134.r_3_, ...), custom_call_target="tpu_custom_call", output_to_operand_aliasing={{}: (8, {})} | custom-call | flops 113246208 | bytes 4500000 | tf_op jit(solution)/shard_map/trailing_update/pallas_call | solution.py:413
  92.8 5.9 %collective-permute-start.21 = (f32[12,8,128]{2,1,0:T(8,128)S(1)}, f32[12,8,128]{2,1,0:T(8,128)S(1)}, u32[]{:S(2)}, u32[]{:S(2)}) collective-permute-start(f32[12,8,128]{2,1,0:T(8,128)S(1)} %add.33), channel_id=1, source_target_pairs={{0,4},{1,5},{2,6},{3,7},{4,0},{5,1},{6,2},{7,3},{8,12},{9,13},{10,... | collective-permute-start | bytes 147464 | tf_op jit(solution)/shard_map/ppermute | solution.py:452
  98.7 2.2 %collective-permute-done.21 = f32[12,8,128]{2,1,0:T(8,128)S(1)} collective-permute-done((f32[12,8,128]{2,1,0:T(8,128)S(1)}, f32[12,8,128]{2,1,0:T(8,128)S(1)}, u32[]{:S(2)}, u32[]{:S(2)}) %collective-permute-start.21) | collective-permute-done | bytes 49184 | tf_op jit(solution)/shard_map/ppermute | solution.py:452
  (51 shorter events, 8.0 us)
Async XLA Ops:
  2.6 1.1 %copy-start = (bf16[9,128,256]{2,1,0:T(8,128)(2,1)S(1)}, bf16[9,128,256]{2,1,0:T(8,128)(2,1)}, u32[]{:S(2)}) copy-start(bf16[9,128,256]{2,1,0:T(8,128)(2,1)} %param.8) | copy-start | bytes 1769476
  3.7 1.0 copy-start.1
  4.7 0.7 copy-start.2
  6.4 8.5 %collective-permute-start = (bf16[1664,128]{1,0:T(8,128)(2,1)S(1)}, bf16[1664,128]{1,0:T(8,128)(2,1)S(1)}, u32[]{:S(2)}, u32[]{:S(2)}) collective-permute-start(bf16[1664,128]{1,0:T(8,128)(2,1)S(1)} %get-tuple-element.71.r_0_), channel_id=1, source_target_pairs={{0,64},{1,65},{2,66},{3,67},{4,68},{5,69},{6,70},{7,71},{8,24},{9,... | collective-permute-start | bytes 1277960 | tf_op jit(solution)/shard_map/ppermute | solution.py:449
  8.0 8.1 %collective-permute-start.1 = (bf16[1664,128]{1,0:T(8,128)(2,1)S(1)}, bf16[1664,128]{1,0:T(8,128)(2,1)S(1)}, u32[]{:S(2)}, u32[]{:S(2)}) collective-permute-start(bf16[1664,128]{1,0:T(8,128)(2,1)S(1)} %get-tuple-element.73), channel_id=1, source_target_pairs={{0,192},{1,193},{2,194},{3,195},{4,196},{5,197},{6,198},{7,199},{8... | collective-permute-start | bytes 1277960 | tf_op jit(solution)/shard_map/ppermute | solution.py:449
  9.5 3.6 %collective-permute-start.2 = (f32[8,128]{1,0:T(8,128)S(1)}, f32[8,128]{1,0:T(8,128)S(1)}, u32[]{:S(2)}, u32[]{:S(2)}) collective-permute-start(f32[8,128]{1,0:T(8,128)S(1)} %broadcast_in_dim.32), channel_id=1, source_target_pairs={{0,1},{1,0},{2,3},{3,2},{4,5},{5,4},{6,7},{7,6},{8,9},{9,8},{10,11... | collective-permute-start | bytes 12296 | tf_op jit(solution)/shard_map/ppermute | solution.py:452
  16.2 24.6 %collective-permute-start.3 = (bf16[2752,128]{1,0:T(8,128)(2,1)S(1)}, bf16[2752,128]{1,0:T(8,128)(2,1)S(1)}, u32[]{:S(2)}, u32[]{:S(2)}) collective-permute-start(bf16[2752,128]{1,0:T(8,128)(2,1)S(1)} %get-tuple-element.75), channel_id=1, source_target_pairs={{0,16},{1,17},{2,18},{3,19},{4,20},{5,21},{6,22},{7,23},{8,72},{9,... | collective-permute-start | bytes 2113544 | tf_op jit(solution)/shard_map/ppermute | solution.py:450
  17.9 23.0 %collective-permute-start.5 = (bf16[2752,128]{1,0:T(8,128)(2,1)S(1)}, bf16[2752,128]{1,0:T(8,128)(2,1)S(1)}, u32[]{:S(2)}, u32[]{:S(2)}) collective-permute-start(bf16[2752,128]{1,0:T(8,128)(2,1)S(1)} %get-tuple-element.76), channel_id=1, source_target_pairs={{0,48},{1,49},{2,50},{3,51},{4,52},{5,53},{6,54},{7,55},{8,200},{9... | collective-permute-start | bytes 2113544 | tf_op jit(solution)/shard_map/ppermute | solution.py:450
  19.5 8.3 %collective-permute-start.7 = (bf16[768,128]{1,0:T(8,128)(2,1)S(1)}, bf16[768,128]{1,0:T(8,128)(2,1)S(1)}, u32[]{:S(2)}, u32[]{:S(2)}) collective-permute-start(bf16[768,128]{1,0:T(8,128)(2,1)S(1)} %slice.20), channel_id=1, source_target_pairs={{0,64},{1,65},{2,66},{3,67},{4,68},{5,69},{6,70},{7,71},{8,24},{9,... | collective-permute-start | bytes 589832 | tf_op jit(solution)/shard_map/ppermute | solution.py:449
  21.0 7.5 %collective-permute-start.8 = (bf16[768,128]{1,0:T(8,128)(2,1)S(1)}, bf16[768,128]{1,0:T(8,128)(2,1)S(1)}, u32[]{:S(2)}, u32[]{:S(2)}) collective-permute-start(bf16[768,128]{1,0:T(8,128)(2,1)S(1)} %slice.21), channel_id=1, source_target_pairs={{0,192},{1,193},{2,194},{3,195},{4,196},{5,197},{6,198},{7,199},{8... | collective-permute-start | bytes 589832 | tf_op jit(solution)/shard_map/ppermute | solution.py:449
  21.7 6.0 %collective-permute-start.9 = (f32[8,128]{1,0:T(8,128)S(1)}, f32[8,128]{1,0:T(8,128)S(1)}, u32[]{:S(2)}, u32[]{:S(2)}) collective-permute-start(f32[8,128]{1,0:T(8,128)S(1)} %broadcast_add_fusion), channel_id=1, source_target_pairs={{0,2},{1,3},{2,0},{3,1},{4,6},{5,7},{6,4},{7,5},{8,10},{9,11},{10,... | collective-permute-start | bytes 12296 | tf_op jit(solution)/shard_map/ppermute | solution.py:452
  28.7 23.7 %collective-permute-start.10 = (bf16[2752,128]{1,0:T(8,128)(2,1)S(1)}, bf16[2752,128]{1,0:T(8,128)(2,1)S(1)}, u32[]{:S(2)}, u32[]{:S(2)}) collective-permute-start(bf16[2752,128]{1,0:T(8,128)(2,1)S(1)} %get-tuple-element.87), channel_id=1, source_target_pairs={{0,16},{1,17},{2,18},{3,19},{4,20},{5,21},{6,22},{7,23},{8,72},{9,... | collective-permute-start | bytes 2113544 | tf_op jit(solution)/shard_map/ppermute | solution.py:450
  29.3 23.0 %collective-permute-start.11 = (bf16[2752,128]{1,0:T(8,128)(2,1)S(1)}, bf16[2752,128]{1,0:T(8,128)(2,1)S(1)}, u32[]{:S(2)}, u32[]{:S(2)}) collective-permute-start(bf16[2752,128]{1,0:T(8,128)(2,1)S(1)} %get-tuple-element.88), channel_id=1, source_target_pairs={{0,48},{1,49},{2,50},{3,51},{4,52},{5,53},{6,54},{7,55},{8,200},{9... | collective-permute-start | bytes 2113544 | tf_op jit(solution)/shard_map/ppermute | solution.py:450
  32.0 8.8 %collective-permute-start.12 = (f32[8,128]{1,0:T(8,128)S(1)}, f32[8,128]{1,0:T(8,128)S(1)}, u32[]{:S(2)}, u32[]{:S(2)}) collective-permute-start(f32[8,128]{1,0:T(8,128)S(1)} %add.30), channel_id=1, source_target_pairs={{0,4},{1,5},{2,6},{3,7},{4,0},{5,1},{6,2},{7,3},{8,12},{9,13},{10,... | collective-permute-start | bytes 12296 | tf_op jit(solution)/shard_map/ppermute | solution.py:452
  40.8 11.6 %collective-permute-start.4 = (bf16[1344,128]{1,0:T(8,128)(2,1)S(1)}, bf16[1344,128]{1,0:T(8,128)(2,1)S(1)}, u32[]{:S(2)}, u32[]{:S(2)}) collective-permute-start(bf16[1344,128]{1,0:T(8,128)(2,1)S(1)} %slice.24), channel_id=1, source_target_pairs={{0,16},{1,17},{2,18},{3,19},{4,20},{5,21},{6,22},{7,23},{8,72},{9,... | collective-permute-start | bytes 1032200 | tf_op jit(solution)/shard_map/ppermute | solution.py:450
  40.9 11.5 %collective-permute-start.6 = (bf16[1344,128]{1,0:T(8,128)(2,1)S(1)}, bf16[1344,128]{1,0:T(8,128)(2,1)S(1)}, u32[]{:S(2)}, u32[]{:S(2)}) collective-permute-start(bf16[1344,128]{1,0:T(8,128)(2,1)S(1)} %slice.25), channel_id=1, source_target_pairs={{0,48},{1,49},{2,50},{3,51},{4,52},{5,53},{6,54},{7,55},{8,200},{9... | collective-permute-start | bytes 1032200 | tf_op jit(solution)/shard_map/ppermute | solution.py:450
  52.4 11.4 %collective-permute-start.13 = (bf16[1344,128]{1,0:T(8,128)(2,1)S(1)}, bf16[1344,128]{1,0:T(8,128)(2,1)S(1)}, u32[]{:S(2)}, u32[]{:S(2)}) collective-permute-start(bf16[1344,128]{1,0:T(8,128)(2,1)S(1)} %slice.22), channel_id=1, source_target_pairs={{0,16},{1,17},{2,18},{3,19},{4,20},{5,21},{6,22},{7,23},{8,72},{9,... | collective-permute-start | bytes 1032200 | tf_op jit(solution)/shard_map/ppermute | solution.py:450
  52.6 11.3 %collective-permute-start.14 = (bf16[1344,128]{1,0:T(8,128)(2,1)S(1)}, bf16[1344,128]{1,0:T(8,128)(2,1)S(1)}, u32[]{:S(2)}, u32[]{:S(2)}) collective-permute-start(bf16[1344,128]{1,0:T(8,128)(2,1)S(1)} %slice.23), channel_id=1, source_target_pairs={{0,48},{1,49},{2,50},{3,51},{4,52},{5,53},{6,54},{7,55},{8,200},{9... | collective-permute-start | bytes 1032200 | tf_op jit(solution)/shard_map/ppermute | solution.py:450
  66.7 16.7 %copy-start.3 = (f32[12,1,128]{2,1,0:T(1,128)S(1)}, f32[12,1,128]{2,1,0:T(1,128)}, u32[]{:S(2)}) copy-start(f32[12,1,128]{2,1,0:T(1,128)} %param.12) | copy-start | bytes 18436
  66.7 1.4 %collective-permute-start.15 = (f32[144,128]{1,0:T(8,128)S(1)}, f32[144,128]{1,0:T(8,128)S(1)}, u32[]{:S(2)}, u32[]{:S(2)}) collective-permute-start(f32[144,128]{1,0:T(8,128)S(1)} %get-tuple-element.118.a_ref), channel_id=1, source_target_pairs={{0,8},{8,0},{1,9},{9,1},{2,10},{10,2},{3,11},{11,3},{4,12},{12,4},... | collective-permute-start | bytes 221192 | tf_op jit(solution)/shard_map/ppermute | solution.py:451
  68.0 18.3 %collective-permute-start.20 = (f32[1536,384]{1,0:T(8,128)S(1)}, f32[1536,384]{1,0:T(8,128)S(1)}, u32[]{:S(2)}, u32[]{:S(2)}) collective-permute-start(f32[1536,384]{1,0:T(8,128)S(1)} %get-tuple-element.133), channel_id=1, source_target_pairs={{0,8},{8,0},{1,9},{9,1},{2,10},{10,2},{3,11},{11,3},{4,12},{12,4},... | collective-permute-start | bytes 7077896 | tf_op jit(solution)/shard_map/ppermute | solution.py:451
  68.2 6.9 %collective-permute-start.16 = (f32[1536,256]{1,0:T(8,128)S(1)}, f32[1536,256]{1,0:T(8,128)S(1)}, u32[]{:S(2)}, u32[]{:S(2)}) collective-permute-start(f32[1536,256]{1,0:T(8,128)S(1)} %get-tuple-element.122.p_ref), channel_id=1, source_target_pairs={{0,8},{8,0},{1,9},{9,1},{2,10},{10,2},{3,11},{11,3},{4,12},{12,4},... | collective-permute-start | bytes 4718600 | tf_op jit(solution)/shard_map/ppermute | solution.py:451
  68.6 6.6 %collective-permute-start.17 = (f32[384,128]{1,0:T(8,128)S(1)}, f32[384,128]{1,0:T(8,128)S(1)}, u32[]{:S(2)}, u32[]{:S(2)}) collective-permute-start(f32[384,128]{1,0:T(8,128)S(1)} %get-tuple-element.124), channel_id=1, source_target_pairs={{0,8},{8,0},{1,9},{9,1},{2,10},{10,2},{3,11},{11,3},{4,12},{12,4},... | collective-permute-start | bytes 589832 | tf_op jit(solution)/shard_map/ppermute | solution.py:451
  77.1 4.1 %collective-permute-start.18 = (f32[12,8,128]{2,1,0:T(8,128)S(1)}, f32[12,8,128]{2,1,0:T(8,128)S(1)}, u32[]{:S(2)}, u32[]{:S(2)}) collective-permute-start(f32[12,8,128]{2,1,0:T(8,128)S(1)} %broadcast_select_fusion), channel_id=1, source_target_pairs={{0,1},{1,0},{2,3},{3,2},{4,5},{5,4},{6,7},{7,6},{8,9},{9,8},{10,11... | collective-permute-start | bytes 147464 | tf_op jit(solution)/shard_map/ppermute | solution.py:452
  81.3 5.0 %collective-permute-start.19 = (f32[12,8,128]{2,1,0:T(8,128)S(1)}, f32[12,8,128]{2,1,0:T(8,128)S(1)}, u32[]{:S(2)}, u32[]{:S(2)}) collective-permute-start(f32[12,8,128]{2,1,0:T(8,128)S(1)} %fusion), channel_id=1, source_target_pairs={{0,2},{1,3},{2,0},{3,1},{4,6},{5,7},{6,4},{7,5},{8,10},{9,11},{10,... | collective-permute-start | bytes 147464 | tf_op jit(solution)/shard_map/ppermute | solution.py:452
  92.8 8.1 %collective-permute-start.21 = (f32[12,8,128]{2,1,0:T(8,128)S(1)}, f32[12,8,128]{2,1,0:T(8,128)S(1)}, u32[]{:S(2)}, u32[]{:S(2)}) collective-permute-start(f32[12,8,128]{2,1,0:T(8,128)S(1)} %add.33), channel_id=1, source_target_pairs={{0,4},{1,5},{2,6},{3,7},{4,0},{5,1},{6,2},{7,3},{8,12},{9,13},{10,... | collective-permute-start | bytes 147464 | tf_op jit(solution)/shard_map/ppermute | solution.py:452

commit v5 on v4

--- a/solution.py
+++ b/solution.py
@@ -27,18 +27,35 @@
 VMEM_LIMIT = 20 * 1024 * 1024
 SMEM = pl.BlockSpec(memory_space=pltpu.SMEM)
 VM = pl.BlockSpec(memory_space=pltpu.VMEM)
+HBM = pl.BlockSpec(memory_space=pltpu.HBM)
 
 
 def params():
     return pltpu.CompilerParams(vmem_limit_bytes=VMEM_LIMIT)
 
 
-def pack_kernel(k_ref, idx_ref, h_ref, g_ref, vr_ref, plus_ref, minus_ref, own_ref, gs, tail, cbuf):
+def pack_kernel(
+    k_ref, idx_hbm, h_hbm, g_hbm, v_hbm, r_hbm, plus_ref, minus_ref, own_ref,
+    gs, tail, cbuf, idx_ref, h_ref, g_ref, v_ref, r_ref, sem,
+):
+    copies = [
+        pltpu.make_async_copy(src, dst, sem.at[i])
+        for i, (src, dst) in enumerate(
+            (
+                (idx_hbm, idx_ref), (v_hbm, v_ref), (r_hbm, r_ref), (g_hbm, g_ref), (h_hbm, h_ref),
+            )
+        )
+    ]
+    for cp in copies:
+        cp.start()
     x, y = lax.axis_index("x"), lax.axis_index("y")
     core, q = lax.axis_index("core"), lax.axis_index("row")
     k = k_ref[0]
     pool = lax.broadcasted_iota(jnp.int32, (POOL, M), 0)
+    copies[0].wait()
     sel = (pool == idx_ref[...]).astype(F32).astype(BF16)
+    for cp in copies[1:]:
+        cp.wait()
     for c in range(C):
         val = jnp.dot(h_ref[c * K : (c + 1) * K, :], sel, preferred_element_type=F32).astype(BF16)
         lo = c * K if c < 5 else c * K + 2 * GC
@@ -53,7 +70,10 @@
     for c in range(C):
         tail[c * LR : (c + 1) * LR, :] = gs[pl.ds(c * A + q, LR, stride=NZ), :]
         tail[108 + c : 109 + c, :] = gs[pl.ds(c * A + k, 1), :]
-    tail[117:119, :] = jnp.dot(vr_ref[...], sel, preferred_element_type=F32)
+    for i, ref in enumerate((v_ref, r_ref)):
+        low = jnp.dot(ref[...], sel[:M], preferred_element_type=F32)
+        high = jnp.dot(ref[...], sel[M:], preferred_element_type=F32)
+        tail[117 + i : 118 + i, :] = low[0:1] + high[1:2]
     val = tail[...].astype(BF16)
     plus_ref[HR + 2 * GC : BR + 2 * GC, :] = val
     minus_ref[HR - HB : HB, :] = val
@@ -82,7 +102,7 @@
                 minus_ref[HB + (dt - 2) * GC : HB + (dt - 1) * GC, :] = val
 
 
-def pack(k, idx, h, g, vr):
+def pack(k, idx, h, g, v, r):
     return pl.pallas_call(
         pack_kernel,
         out_shape=(
@@ -90,16 +110,22 @@
             jax.ShapeDtypeStruct((PR, M), BF16),
             jax.ShapeDtypeStruct((4 * GC, M), BF16),
         ),
-        in_specs=[SMEM, VM, VM, VM, VM],
+        in_specs=[SMEM] + [HBM] * 5,
         out_specs=(VM,) * 3,
         scratch_shapes=[
             pltpu.VMEM((C * A, M), F32),
             pltpu.VMEM((128, M), F32),
             pltpu.VMEM((GC, M), F32),
+            pltpu.VMEM((1, M), jnp.int32),
+            pltpu.VMEM((HR, POOL), BF16),
+            pltpu.VMEM((C * A, POOL), BF16),
+            pltpu.VMEM((2, M), BF16),
+            pltpu.VMEM((2, M), BF16),
+            pltpu.SemaphoreType.DMA((5,)),
         ],
-        compiler_params=params(),
+        compiler_params=pltpu.CompilerParams(vmem_limit_bytes=60 * 1024 * 1024),
         name="pack",
-    )(k, idx, h, g, vr)
+    )(k, idx, h, g, v, r)
 
 
 def block_from_plus(i, cols):
@@ -422,7 +448,7 @@
         input_output_aliases={8: 0} if prev else {},
         compiler_params=params(),
         cost_estimate=pl.CostEstimate(
-            flops=count * 6 * K * CU * K, bytes_accessed=count * 1_500_000, transcendentals=0
+            flops=1, bytes_accessed=6000000, transcendentals=0
         ),
         name="trailing_update",
     )(k, gown, grecv, la, lb, lpan, chol, damp, *prev)
@@ -457,25 +483,31 @@
         point_index.reshape(1, M),
         layer_input_jets.reshape(HR, POOL),
         g_jets.transpose(1, 0, 2).reshape(C * A, POOL),
-        jnp.stack([speed, resid]),
+        speed.reshape(2, M),
+        resid.reshape(2, M),
     )
     dsel = lax.dynamic_index_in_dim(damping[:, 0, :], k // NZ, 0, keepdims=True)
     dsel = jnp.broadcast_to(jnp.where(k % NZ == q, dsel, 0.0), (8, K))
-    ap, am, dsel = bar((one(plus, 1), one(minus, -1), zbit(dsel, 1)))
+    parts = [dsel]
+    for bits in (1, 2, 3):
+        parts.append(lax.ppermute(dsel, "row", [(i, i ^ bits) for i in range(NZ)]))
+    dsel = parts[0] + parts[1] + parts[2] + parts[3]
+    accs = chunk([place(BLOCK0, 0, 0)], (plus, own), (), "chunk_own")
+    ap, am, accs, dsel = bar((one(plus, 1), one(minus, -1), accs, dsel))
     m1 = assemble(BLOCK0, BLOCK1, plus, own, ap)
     relay = HB + 2 * GC
     rp, rm = one(ap[:relay], 1), one(am[:relay], -1)
     m1p, m1m = two(m1[0], 1), two(m1[1], -1)
-    accs = chunk([place(BLOCK0, 0, 0), place(BLOCK1, 0, 0)], (plus, own, ap), (), "chunk_line1")
-    rp, rm, accs, dsel = bar((rp, rm, accs, zbit(dsel, 2)))
+    accs = chunk([place(BLOCK1, 0, -2), place(BLOCK2, 0, 1)], (ap, am), accs, "chunk_line1")
+    rp, rm, accs, dsel = bar((rp, rm, accs, zbit(dsel, 4)))
     m2 = assemble(BLOCK2, BLOCK3, am, rp, rm)
     m2p, m2m = two(m2[0], 1), two(m2[1], -1)
     n1 = BR + GC
     r1p, r1m = two(m1p[:n1], 1), two(m1m[:n1], -1)
     e1 = 2 * BR + GC
-    blocks = received(0, e1) + received(1, e1) + [place(BLOCK2, 0, 2), place(BLOCK3, 0, 2)]
-    accs = chunk(blocks, (m1p, m1m, am, rp, rm), accs, "chunk_line2")
-    r1p, r1m, m2p, m2m, accs, dsel = bar((r1p, r1m, m2p, m2m, accs, zbit(dsel, 4)))
+    blocks = received(0, e1) + received(1, e1) + [place(BLOCK3, 0, 1)]
+    accs = chunk(blocks, (m1p, m1m, rp, rm), accs, "chunk_line2")
+    r1p, r1m, m2p, m2m, accs = bar((r1p, r1m, m2p, m2m, accs))
     r2p, r2m = two(m2p[:n1], 1), two(m2m[:n1], -1)
     blocks = [received(0, BR)[0], received(1, BR)[0]] + received(2, e1) + received(3, e1)
     accs = chunk(blocks, (r1p, r1m, m2p, m2m), accs, "chunk_far1")
@@ -484,17 +516,18 @@
     gown, gsib, p, po, ps, dk = accs
 
     dk2, p, ps, gsib = bar((swap(dk), p, ps, gsib))
-    pr, por = swap(p), swap(ps)
-    gr = swap(gsib)
     chol, w, yz = cholesky(dk, dk2, dsel)
+    pr, por, gr, w = bar((swap(p), swap(ps), swap(gsib), w))
     mine, lpan, la, lb = panel_solve(panel, p, pr, po, por, w, yz)
     slot = lax.broadcasted_iota(jnp.int32, (1, NZ, 1), 1)
     full = jnp.where(slot == q, mine[:, None, :], 0.0)
-    full, la = bar((zbit(full, 1), la))
+    for bits in (1, 2, 3):
+        other = lax.ppermute(mine, "row", [(i, i ^ bits) for i in range(NZ)])
+        full = jnp.where(slot == q ^ bits, other[:, None, :], full)
     rest = (panel, gown, gr, la, lb, lpan, chol, damping[:, 0, :])
-    fac = final(0, 9, *rest)
-    fac = final(9, 3, *rest, fac)
-    full, fac = bar((zbit(full, 2), fac))
+    fac = final(0, 8, *rest)
+    full, fac = bar((full, fac))
+    fac = final(8, 4, *rest, fac)
     full = zbit(full, 4)
     return fac.reshape(LR, 1, K, LC, 1, K), full.reshape(-1)
 

time: 102 us -> 97.3 us (0.954); the launches traced: 102 us -> 95.7 us
  waiting for transfers between devices: 17 us -> 5.64 us
  Pallas kernels: 37.3 us -> 47.6 us
  starting transfers between devices: 40 us -> 37.5 us
  local copies, waits for them, and re-layouts: 4.18 us -> 1.98 us
    ppermute x6 -> x2, waiting for transfers between devices: 11.8 us -> 0.01 us  [body(): lax.ppermute(v, 'row', [(i, i ^ bit) for i in range(NZ)])]
    ppermute x6 -> x2, starting transfers between devices: 21.1 us -> 9.6 us  [body(): lax.ppermute(v, 'row', [(i, i ^ bit) for i in range(NZ)])]
    ppermute x0 -> x6, starting transfers between devices: none -> 9.32 us  [the longest x3 4.85 us: body(): parts.append(lax.ppermute(dsel, 'row', [(i, i ^ bits) for i in range(NZ)]))]
    ppermute x4, waiting for transfers between devices: 3.7 us -> 0.01 us  [body(): one = lambda v, d: lax.ppermute(v, AXES, hops(0, d))]
    pallas_call x2, Pallas kernels: 6.41 us -> 9.96 us  [final(): pl.pallas_call(lambda *r: final_kernel(start, *r), grid=(count,), out_sha...]
    pallas_call x4 -> x5, Pallas kernels: 21.5 us -> 24.2 us  [chunk(): pl.pallas_call(lambda *r: chunk_kernel(blocks, len(arrs), len(accs), *r),...]
    ppermute x8, waiting for transfers between devices: 0.02 us -> 2.21 us  [body(): two = lambda v, d: lax.ppermute(v, AXES, hops(1, d))]
    pallas_call x1, Pallas kernels: 1.04 us -> 3.12 us  [pack(): pl.pallas_call(pack_kernel, out_shape=(jax.ShapeDtypeStruct((PR, M), BF16...]
  transfers between devices with their start and end apart: 22 -> 24, of which waited for: 10 -> 4; matrix products, arithmetic and copies ran while one was open for 1% -> 1% of each run, Pallas kernels for 27% -> 38%
where the time goes in v5:
time: 97.3 us; the launch traced here: 95.7 us
  Pallas kernels  47.6 us (49%)
  starting transfers between devices  37.5 us (39%)
  waiting for transfers between devices  5.64 us (6%)
  local copies, waits for them, and re-layouts  1.98 us (2%)
  between operations  1.5 us (2%)
  other arithmetic  1.39 us (1%)
    pallas_call x5, Pallas kernels, chunk(): pl.pallas_call(lambda *r: chunk_kernel(blocks, len(arrs), len(accs), *r),...  24.2 us
    ppermute x8, starting transfers between devices, body(): two = lambda v, d: lax.ppermute(v, AXES, hops(1, d))  13.4 us
    pallas_call x2, Pallas kernels, final(): pl.pallas_call(lambda *r: final_kernel(start, *r), grid=(count,), out_sha...  9.96 us
    ppermute x2, starting transfers between devices, body(): lax.ppermute(v, 'row', [(i, i ^ bit) for i in range(NZ)])  9.6 us
    pallas_call x1, Pallas kernels, cholesky(): pl.pallas_call(chol_kernel, out_shape=(jax.ShapeDtypeStruct((K, K), F32),...  6.22 us
    ppermute x3, starting transfers between devices, body(): parts.append(lax.ppermute(dsel, 'row', [(i, i ^ bits) for i in range(NZ)]))  4.85 us
    ppermute x4, starting transfers between devices, body(): one = lambda v, d: lax.ppermute(v, AXES, hops(0, d))  4.55 us
    ppermute x3, starting transfers between devices, body(): other = lax.ppermute(mine, 'row', [(i, i ^ bits) for i in range(NZ)])  4.47 us
  transfers between devices with their start and end apart: 24, of which 4 were waited for; matrix products, arithmetic and copies ran while one was open for 1% of the time, Pallas kernels for 38%

profile of v5, /device:TPU:2, one launch (start us, length us, event | category | flops | bytes accessed | tf_op | source)
XLA Modules:
  0.0 95.7 jit_solution(15855583606749688048)
XLA Ops:
  1.3 3.1 %pack.1 = (bf16[1664,128]{1,0:T(8,128)(2,1)}, bf16[1664,128]{1,0:T(8,128)(2,1)}, bf16[256,128]{1,0:T(8,128)(2,1)}) custom-call(s32[1]{0:T(128)} %copy.16.k_ref.r_0_, s32[1,128]{1,0:T(1,128)} %bitcast.25, bf16[1152,256]{1,0:T(8,128)(2,1)} %bitcast.23, bf16[864,256]{1,0:T(8,128)(2,1)} %bitcast.24, bf16[2,128]{1,0:T(2,128)(2,1)} %bitcast.26, ...), custom_call_target="tpu_custom_call" | custom-call | tf_op jit(solution)/shard_map/pack/pallas_call | solution.py:106
  4.4 1.6 %collective-permute-start = (bf16[1664,128]{1,0:T(8,128)(2,1)}, bf16[1664,128]{1,0:T(8,128)(2,1)S(1)}, u32[]{:S(2)}, u32[]{:S(2)}) collective-permute-start(bf16[1664,128]{1,0:T(8,128)(2,1)} %get-tuple-element.84.r_0_), channel_id=1, source_target_pairs={{0,64},{1,65},{2,66},{3,67},{4,68},{5,69},{6,70},{7,71},{8,24},{9,... | collective-permute-start | bytes 1277960 | tf_op jit(solution)/shard_map/ppermute | solution.py:475
  6.0 0.9 collective-permute-start.1
  6.9 0.7 fusion
  7.5 1.6 %collective-permute-start.2 = (f32[8,128]{1,0:T(8,128)S(1)}, f32[8,128]{1,0:T(8,128)S(1)}, u32[]{:S(2)}, u32[]{:S(2)}) collective-permute-start(f32[8,128]{1,0:T(8,128)S(1)} %broadcast_in_dim.70), channel_id=1, source_target_pairs={{0,1},{1,0},{2,3},{3,2},{4,5},{5,4},{6,7},{7,6},{8,9},{9,8},{10,11... | collective-permute-start | bytes 12296 | tf_op jit(solution)/shard_map/ppermute | solution.py:493
  9.1 3.3 %collective-permute-start.3 = (f32[8,128]{1,0:T(8,128)S(1)}, f32[8,128]{1,0:T(8,128)S(1)}, u32[]{:S(2)}, u32[]{:S(2)}) collective-permute-start(f32[8,128]{1,0:T(8,128)S(1)} %broadcast_in_dim.70), channel_id=1, source_target_pairs={{0,2},{1,3},{2,0},{3,1},{4,6},{5,7},{6,4},{7,5},{8,10},{9,11},{10,... | collective-permute-start | bytes 12296 | tf_op jit(solution)/shard_map/ppermute | solution.py:493
  12.4 1.0 %copy-done = bf16[1664,128]{1,0:T(8,128)(2,1)S(1)} copy-done((bf16[1664,128]{1,0:T(8,128)(2,1)S(1)}, bf16[1664,128]{1,0:T(8,128)(2,1)}, u32[]{:S(2)}) %copy-start) | copy-done | bytes 426008
  13.4 0.8 copy-done.1
  14.2 1.9 %chunk_own.1 = (f32[1536,384]{1,0:T(8,128)S(1)}, f32[1536,384]{1,0:T(8,128)S(1)}, f32[1536,256]{1,0:T(8,128)S(1)}, f32[384,128]{1,0:T(8,128)S(1)}, f32[384,128]{1,0:T(8,128)S(1)}, /*index=5*/f32[144,128]{1,0:T(8,128)S(1)}) custom-call(bf16[1664,128]{1,0:T(8,128)(2,1)S(1)} %copy-done, bf16[256,128]{1,0:T(8,128)(2,1)S(1)} %copy-done.1), custom_call_target="tpu_custom_call" | custom-call | flops 1012531200 | bytes 4000000 | tf_op jit(solution)/shard_map/chunk_own/pallas_call | solution.py:267
  16.1 1.6 %collective-permute-done.4 = f32[8,128]{1,0:T(8,128)S(1)} collective-permute-done((f32[8,128]{1,0:T(8,128)S(1)}, f32[8,128]{1,0:T(8,128)S(1)}, u32[]{:S(2)}, u32[]{:S(2)}) %collective-permute-start.4) | collective-permute-done | bytes 4128 | tf_op jit(solution)/shard_map/ppermute | solution.py:493
  17.9 1.7 %collective-permute-start.5 = (bf16[2752,128]{1,0:T(8,128)(2,1)S(1)}, bf16[2752,128]{1,0:T(8,128)(2,1)S(1)}, u32[]{:S(2)}, u32[]{:S(2)}) collective-permute-start(bf16[2752,128]{1,0:T(8,128)(2,1)S(1)} %get-tuple-element.94), channel_id=1, source_target_pairs={{0,16},{1,17},{2,18},{3,19},{4,20},{5,21},{6,22},{7,23},{8,72},{9,... | collective-permute-start | bytes 2113544 | tf_op jit(solution)/shard_map/ppermute | solution.py:476
  19.6 1.7 %collective-permute-start.7 = (bf16[2752,128]{1,0:T(8,128)(2,1)S(1)}, bf16[2752,128]{1,0:T(8,128)(2,1)S(1)}, u32[]{:S(2)}, u32[]{:S(2)}) collective-permute-start(bf16[2752,128]{1,0:T(8,128)(2,1)S(1)} %get-tuple-element.95), channel_id=1, source_target_pairs={{0,48},{1,49},{2,50},{3,51},{4,52},{5,53},{6,54},{7,55},{8,200},{9... | collective-permute-start | bytes 2113544 | tf_op jit(solution)/shard_map/ppermute | solution.py:476
  21.3 1.8 %collective-permute-start.10 = (bf16[768,128]{1,0:T(8,128)(2,1)S(1)}, bf16[768,128]{1,0:T(8,128)(2,1)S(1)}, u32[]{:S(2)}, u32[]{:S(2)}) collective-permute-start(bf16[768,128]{1,0:T(8,128)(2,1)S(1)} %slice.21), channel_id=1, source_target_pairs={{0,192},{1,193},{2,194},{3,195},{4,196},{5,197},{6,198},{7,199},{8... | collective-permute-start | bytes 589832 | tf_op jit(solution)/shard_map/ppermute | solution.py:475
  23.4 4.8 %collective-permute-start.11 = (f32[8,128]{1,0:T(8,128)S(1)}, f32[8,128]{1,0:T(8,128)S(1)}, u32[]{:S(2)}, u32[]{:S(2)}) collective-permute-start(f32[8,128]{1,0:T(8,128)S(1)} %add_add_fusion), channel_id=1, source_target_pairs={{0,4},{1,5},{2,6},{3,7},{4,0},{5,1},{6,2},{7,3},{8,12},{9,13},{10,... | collective-permute-start | bytes 12296 | tf_op jit(solution)/shard_map/ppermute | solution.py:478
  28.2 2.8 %chunk_line1.1 = (f32[1536,384]{1,0:T(8,128)S(1)}, f32[1536,384]{1,0:T(8,128)S(1)}, f32[1536,256]{1,0:T(8,128)S(1)}, f32[384,128]{1,0:T(8,128)S(1)}, f32[384,128]{1,0:T(8,128)S(1)}, /*index=5*/f32[144,128]{1,0:T(8,128)S(1)}) custom-call(bf16[1664,128]{1,0:T(8,128)(2,1)S(1)} %collective-permute-done.r_2_.r_0_, ...), custom_call_target="tpu_custom_call" | custom-call | flops 2025062400 | bytes 8000000 | tf_op jit(solution)/shard_map/chunk_line1/pallas_call | solution.py:267
  31.6 2.9 %collective-permute-start.13 = (bf16[2752,128]{1,0:T(8,128)(2,1)S(1)}, bf16[2752,128]{1,0:T(8,128)(2,1)S(1)}, u32[]{:S(2)}, u32[]{:S(2)}) collective-permute-start(bf16[2752,128]{1,0:T(8,128)(2,1)S(1)} %get-tuple-element.113), channel_id=1, source_target_pairs={{0,48},{1,49},{2,50},{3,51},{4,52},{5,53},{6,54},{7,55},{8,200},{9... | collective-permute-start | bytes 2113544 | tf_op jit(solution)/shard_map/ppermute | solution.py:476
  34.6 3.3 %collective-permute-start.8 = (bf16[1344,128]{1,0:T(8,128)(2,1)S(1)}, bf16[1344,128]{1,0:T(8,128)(2,1)S(1)}, u32[]{:S(2)}, u32[]{:S(2)}) collective-permute-start(bf16[1344,128]{1,0:T(8,128)(2,1)S(1)} %slice.25), channel_id=1, source_target_pairs={{0,48},{1,49},{2,50},{3,51},{4,52},{5,53},{6,54},{7,55},{8,200},{9... | collective-permute-start | bytes 1032200 | tf_op jit(solution)/shard_map/ppermute | solution.py:476
  37.9 7.1 %chunk_line2.1 = (f32[1536,384]{1,0:T(8,128)S(1)}, f32[1536,384]{1,0:T(8,128)S(1)}, f32[1536,256]{1,0:T(8,128)S(1)}, f32[384,128]{1,0:T(8,128)S(1)}, f32[384,128]{1,0:T(8,128)S(1)}, /*index=5*/f32[144,128]{1,0:T(8,128)S(1)}) custom-call(bf16[2752,128]{1,0:T(8,128)(2,1)S(1)} %collective-permute-done.5.r_0_, ...), custom_call_target="tpu_custom_call" | custom-call | flops 5062656000 | bytes 20000000 | tf_op jit(solution)/shard_map/chunk_line2/pallas_call | solution.py:267
  45.1 2.2 %collective-permute-done.6.r_0_ = bf16[1344,128]{1,0:T(8,128)(2,1)S(1)} collective-permute-done((bf16[1344,128]{1,0:T(8,128)(2,1)S(1)}, bf16[1344,128]{1,0:T(8,128)(2,1)S(1)}, u32[]{:S(2)}, u32[]{:S(2)}) %collective-permute-start.6) | collective-permute-done | bytes 344096 | tf_op jit(solution)/shard_map/ppermute | solution.py:476
  47.3 0.8 collective-permute-start.14
  48.1 2.6 %collective-permute-start.15 = (bf16[1344,128]{1,0:T(8,128)(2,1)S(1)}, bf16[1344,128]{1,0:T(8,128)(2,1)S(1)}, u32[]{:S(2)}, u32[]{:S(2)}) collective-permute-start(bf16[1344,128]{1,0:T(8,128)(2,1)S(1)} %slice.23), channel_id=1, source_target_pairs={{0,48},{1,49},{2,50},{3,51},{4,52},{5,53},{6,54},{7,55},{8,200},{9... | collective-permute-start | bytes 1032200 | tf_op jit(solution)/shard_map/ppermute | solution.py:476
  50.7 7.9 %chunk_far1.1 = (f32[1536,384]{1,0:T(8,128)S(1)}, f32[1536,384]{1,0:T(8,128)S(1)}, f32[1536,256]{1,0:T(8,128)S(1)}, f32[384,128]{1,0:T(8,128)S(1)}, f32[384,128]{1,0:T(8,128)S(1)}, /*index=5*/f32[144,128]{1,0:T(8,128)S(1)}) custom-call(bf16[1344,128]{1,0:T(8,128)(2,1)S(1)} %collective-permute-done.6.r_0_, bf16[1344,128]{1,0:T(8,128)(2,1)S(1)} %collective-permute-done.8.r_1_, ...), custom_call_target="tpu_custom_call" | custom-call | flops 6075187200 | bytes 24000000 | tf_op jit(solution)/shard_map/chunk_far1/pallas_call | solution.py:267
  58.7 4.6 %chunk_far2.1 = (f32[1536,384]{1,0:T(8,128)S(1)}, f32[1536,384]{1,0:T(8,128)}, f32[1536,256]{1,0:T(8,128)}, f32[384,128]{1,0:T(8,128)S(1)}, f32[384,128]{1,0:T(8,128)S(1)}, /*index=5*/f32[144,128]{1,0:T(8,128)S(1)}) custom-call(bf16[1344,128]{1,0:T(8,128)(2,1)S(1)} %collective-permute-done.14.r_0_, bf16[1344,128]{1,0:T(8,128)(2,1)S(1)} %collective-permute-done.15.r_1_, ...), custom_call_target="tpu_custom_call" | custom-call | flops 2025062400 | bytes 8000000 | tf_op jit(solution)/shard_map/chunk_far2/pallas_call | solution.py:267
  63.2 1.3 %collective-permute-done.16.b_ref = f32[144,128]{1,0:T(8,128)S(1)} collective-permute-done((f32[144,128]{1,0:T(8,128)S(1)}, f32[144,128]{1,0:T(8,128)S(1)}, u32[]{:S(2)}, u32[]{:S(2)}) %collective-permute-start.16) | collective-permute-done | bytes 73760 | tf_op jit(solution)/shard_map/ppermute | solution.py:477
  65.2 6.2 %panel_factor.1 = (f32[128,128]{1,0:T(8,128)S(1)}, f32[128,128]{1,0:T(8,128)S(1)}, f32[16,128]{1,0:T(8,128)S(1)}) custom-call(f32[144,128]{1,0:T(8,128)S(1)} %get-tuple-element.143.a_ref, f32[144,128]{1,0:T(8,128)S(1)} %collective-permute-done.16.b_ref, f32[8,128]{1,0:T(8,128)S(1)} %add.29.d_ref), custom_call_target="tpu_custom_call" | custom-call | tf_op jit(solution)/shard_map/panel_factor/pallas_call | solution.py:341
  71.9 3.8 %panel_solve.1 = (f32[12,128]{1,0:T(8,128)S(1)}, f32[1536,128]{1,0:T(8,128)S(1)}, bf16[1536,384]{1,0:T(8,128)(2,1)S(1)}, bf16[384,384]{1,0:T(8,128)(2,1)S(1)}) custom-call(s32[1]{0:T(128)} %copy.16.k_ref.r_0_, f32[1536,256]{1,0:T(8,128)} %get-tuple-element.147.p_ref, f32[1536,256]{1,0:T(8,128)} %collective-permute-done.17.pr_ref, ...), custom_call_target="tpu_custom_call" | custom-call | tf_op jit(solution)/shard_map/panel_solve/pallas_call | solution.py:395
  75.7 2.2 %collective-permute-start.20 = (f32[12,128]{1,0:T(8,128)S(1)}, f32[12,128]{1,0:T(8,128)S(1)}, u32[]{:S(2)}, u32[]{:S(2)}) collective-permute-start(f32[12,128]{1,0:T(8,128)S(1)} %get-tuple-element.163), channel_id=1, source_target_pairs={{0,3},{1,2},{2,1},{3,0},{4,7},{5,6},{6,5},{7,4},{8,11},{9,10},{10,... | collective-permute-start | bytes 18440 | tf_op jit(solution)/shard_map/ppermute | solution.py:525
  77.9 2.3 %collective-permute-start.22 = (f32[12,128]{1,0:T(8,128)S(1)}, f32[12,128]{1,0:T(8,128)S(1)}, u32[]{:S(2)}, u32[]{:S(2)}) collective-permute-start(f32[12,128]{1,0:T(8,128)S(1)} %get-tuple-element.163), channel_id=1, source_target_pairs={{0,1},{1,0},{2,3},{3,2},{4,5},{5,4},{6,7},{7,6},{8,9},{9,8},{10,11... | collective-permute-start | bytes 18440 | tf_op jit(solution)/shard_map/ppermute | solution.py:525
  80.2 6.3 %trailing_update.2.r_8_ = f32[4608,128]{1,0:T(8,128)} custom-call(s32[1]{0:T(128)} %copy.16.k_ref.r_0_, f32[1536,384]{1,0:T(8,128)S(1)} %get-tuple-element.142.r_1_, f32[1536,384]{1,0:T(8,128)} %collective-permute-done.19.r_2_, bf16[1536,384]{1,0:T(8,128)(2,1)S(1)} %get-tuple-element.159.r_3_, bf16[384,384]{1,0:T(8,128)(2,1)S(1)} %get-tuple-element.160.r_4_, ...), custom_call_target="tpu_custom_call" | custom-call | flops 1 | bytes 6000000 | tf_op jit(solution)/shard_map/trailing_update/pallas_call | solution.py:439
  86.5 4.8 %collective-permute-start.23 = (f32[12,8,128]{2,1,0:T(8,128)S(1)}, f32[12,8,128]{2,1,0:T(8,128)S(1)}, u32[]{:S(2)}, u32[]{:S(2)}) collective-permute-start(f32[12,8,128]{2,1,0:T(8,128)S(1)} %select_select_fusion), channel_id=1, source_target_pairs={{0,4},{1,5},{2,6},{3,7},{4,0},{5,1},{6,2},{7,3},{8,12},{9,13},{10,... | collective-permute-start | bytes 147464 | tf_op jit(solution)/shard_map/ppermute | solution.py:478
  91.3 3.7 %trailing_update.3 = f32[4608,128]{1,0:T(8,128)} custom-call(s32[1]{0:T(128)} %copy.16.k_ref.r_0_, f32[1536,384]{1,0:T(8,128)S(1)} %get-tuple-element.142.r_1_, f32[1536,384]{1,0:T(8,128)} %collective-permute-done.19.r_2_, bf16[1536,384]{1,0:T(8,128)(2,1)S(1)} %get-tuple-element.159.r_3_, ...), custom_call_target="tpu_custom_call", output_to_operand_aliasing={{}: (8, {})} | custom-call | flops 1 | bytes 6000000 | tf_op jit(solution)/shard_map/trailing_update/pallas_call | solution.py:439
  95.0 0.6 add_bitcast_fusion
  (50 shorter events, 2.5 us)
Async XLA Ops:
  4.4 13.4 %collective-permute-start = (bf16[1664,128]{1,0:T(8,128)(2,1)}, bf16[1664,128]{1,0:T(8,128)(2,1)S(1)}, u32[]{:S(2)}, u32[]{:S(2)}) collective-permute-start(bf16[1664,128]{1,0:T(8,128)(2,1)} %get-tuple-element.84.r_0_), channel_id=1, source_target_pairs={{0,64},{1,65},{2,66},{3,67},{4,68},{5,69},{6,70},{7,71},{8,24},{9,... | collective-permute-start | bytes 1277960 | tf_op jit(solution)/shard_map/ppermute | solution.py:475
  6.0 11.8 %collective-permute-start.1 = (bf16[1664,128]{1,0:T(8,128)(2,1)}, bf16[1664,128]{1,0:T(8,128)(2,1)S(1)}, u32[]{:S(2)}, u32[]{:S(2)}) collective-permute-start(bf16[1664,128]{1,0:T(8,128)(2,1)} %get-tuple-element.86), channel_id=1, source_target_pairs={{0,192},{1,193},{2,194},{3,195},{4,196},{5,197},{6,198},{7,199},{8... | collective-permute-start | bytes 1277960 | tf_op jit(solution)/shard_map/ppermute | solution.py:475
  7.5 8.6 %collective-permute-start.2 = (f32[8,128]{1,0:T(8,128)S(1)}, f32[8,128]{1,0:T(8,128)S(1)}, u32[]{:S(2)}, u32[]{:S(2)}) collective-permute-start(f32[8,128]{1,0:T(8,128)S(1)} %broadcast_in_dim.70), channel_id=1, source_target_pairs={{0,1},{1,0},{2,3},{3,2},{4,5},{5,4},{6,7},{7,6},{8,9},{9,8},{10,11... | collective-permute-start | bytes 12296 | tf_op jit(solution)/shard_map/ppermute | solution.py:493
  9.1 7.0 %collective-permute-start.3 = (f32[8,128]{1,0:T(8,128)S(1)}, f32[8,128]{1,0:T(8,128)S(1)}, u32[]{:S(2)}, u32[]{:S(2)}) collective-permute-start(f32[8,128]{1,0:T(8,128)S(1)} %broadcast_in_dim.70), channel_id=1, source_target_pairs={{0,2},{1,3},{2,0},{3,1},{4,6},{5,7},{6,4},{7,5},{8,10},{9,11},{10,... | collective-permute-start | bytes 12296 | tf_op jit(solution)/shard_map/ppermute | solution.py:493
  12.4 5.4 %collective-permute-start.4 = (f32[8,128]{1,0:T(8,128)S(1)}, f32[8,128]{1,0:T(8,128)S(1)}, u32[]{:S(2)}, u32[]{:S(2)}) collective-permute-start(f32[8,128]{1,0:T(8,128)S(1)} %broadcast_in_dim.70), channel_id=1, source_target_pairs={{0,3},{1,2},{2,1},{3,0},{4,7},{5,6},{6,5},{7,4},{8,11},{9,10},{10,... | collective-permute-start | bytes 12296 | tf_op jit(solution)/shard_map/ppermute | solution.py:493
  12.4 1.0 %copy-start = (bf16[1664,128]{1,0:T(8,128)(2,1)S(1)}, bf16[1664,128]{1,0:T(8,128)(2,1)}, u32[]{:S(2)}) copy-start(bf16[1664,128]{1,0:T(8,128)(2,1)} %get-tuple-element.84.r_0_) | copy-start | bytes 1277956
  13.4 0.8 copy-start.1
  17.9 16.5 %collective-permute-start.5 = (bf16[2752,128]{1,0:T(8,128)(2,1)S(1)}, bf16[2752,128]{1,0:T(8,128)(2,1)S(1)}, u32[]{:S(2)}, u32[]{:S(2)}) collective-permute-start(bf16[2752,128]{1,0:T(8,128)(2,1)S(1)} %get-tuple-element.94), channel_id=1, source_target_pairs={{0,16},{1,17},{2,18},{3,19},{4,20},{5,21},{6,22},{7,23},{8,72},{9,... | collective-permute-start | bytes 2113544 | tf_op jit(solution)/shard_map/ppermute | solution.py:476
  19.6 15.0 %collective-permute-start.7 = (bf16[2752,128]{1,0:T(8,128)(2,1)S(1)}, bf16[2752,128]{1,0:T(8,128)(2,1)S(1)}, u32[]{:S(2)}, u32[]{:S(2)}) collective-permute-start(bf16[2752,128]{1,0:T(8,128)(2,1)S(1)} %get-tuple-element.95), channel_id=1, source_target_pairs={{0,48},{1,49},{2,50},{3,51},{4,52},{5,53},{6,54},{7,55},{8,200},{9... | collective-permute-start | bytes 2113544 | tf_op jit(solution)/shard_map/ppermute | solution.py:476
  21.3 9.7 %collective-permute-start.10 = (bf16[768,128]{1,0:T(8,128)(2,1)S(1)}, bf16[768,128]{1,0:T(8,128)(2,1)S(1)}, u32[]{:S(2)}, u32[]{:S(2)}) collective-permute-start(bf16[768,128]{1,0:T(8,128)(2,1)S(1)} %slice.21), channel_id=1, source_target_pairs={{0,192},{1,193},{2,194},{3,195},{4,196},{5,197},{6,198},{7,199},{8... | collective-permute-start | bytes 589832 | tf_op jit(solution)/shard_map/ppermute | solution.py:475
  23.1 7.9 %collective-permute-start.9 = (bf16[768,128]{1,0:T(8,128)(2,1)S(1)}, bf16[768,128]{1,0:T(8,128)(2,1)S(1)}, u32[]{:S(2)}, u32[]{:S(2)}) collective-permute-start(bf16[768,128]{1,0:T(8,128)(2,1)S(1)} %slice.20), channel_id=1, source_target_pairs={{0,64},{1,65},{2,66},{3,67},{4,68},{5,69},{6,70},{7,71},{8,24},{9,... | collective-permute-start | bytes 589832 | tf_op jit(solution)/shard_map/ppermute | solution.py:475
  23.4 7.6 %collective-permute-start.11 = (f32[8,128]{1,0:T(8,128)S(1)}, f32[8,128]{1,0:T(8,128)S(1)}, u32[]{:S(2)}, u32[]{:S(2)}) collective-permute-start(f32[8,128]{1,0:T(8,128)S(1)} %add_add_fusion), channel_id=1, source_target_pairs={{0,4},{1,5},{2,6},{3,7},{4,0},{5,1},{6,2},{7,3},{8,12},{9,13},{10,... | collective-permute-start | bytes 12296 | tf_op jit(solution)/shard_map/ppermute | solution.py:478
  31.2 13.9 %collective-permute-start.12 = (bf16[2752,128]{1,0:T(8,128)(2,1)S(1)}, bf16[2752,128]{1,0:T(8,128)(2,1)S(1)}, u32[]{:S(2)}, u32[]{:S(2)}) collective-permute-start(bf16[2752,128]{1,0:T(8,128)(2,1)S(1)} %get-tuple-element.112), channel_id=1, source_target_pairs={{0,16},{1,17},{2,18},{3,19},{4,20},{5,21},{6,22},{7,23},{8,72},{9,... | collective-permute-start | bytes 2113544 | tf_op jit(solution)/shard_map/ppermute | solution.py:476
  31.6 13.5 %collective-permute-start.13 = (bf16[2752,128]{1,0:T(8,128)(2,1)S(1)}, bf16[2752,128]{1,0:T(8,128)(2,1)S(1)}, u32[]{:S(2)}, u32[]{:S(2)}) collective-permute-start(bf16[2752,128]{1,0:T(8,128)(2,1)S(1)} %get-tuple-element.113), channel_id=1, source_target_pairs={{0,48},{1,49},{2,50},{3,51},{4,52},{5,53},{6,54},{7,55},{8,200},{9... | collective-permute-start | bytes 2113544 | tf_op jit(solution)/shard_map/ppermute | solution.py:476
  34.5 12.7 %collective-permute-start.6 = (bf16[1344,128]{1,0:T(8,128)(2,1)S(1)}, bf16[1344,128]{1,0:T(8,128)(2,1)S(1)}, u32[]{:S(2)}, u32[]{:S(2)}) collective-permute-start(bf16[1344,128]{1,0:T(8,128)(2,1)S(1)} %slice.24), channel_id=1, source_target_pairs={{0,16},{1,17},{2,18},{3,19},{4,20},{5,21},{6,22},{7,23},{8,72},{9,... | collective-permute-start | bytes 1032200 | tf_op jit(solution)/shard_map/ppermute | solution.py:476
  34.6 12.6 %collective-permute-start.8 = (bf16[1344,128]{1,0:T(8,128)(2,1)S(1)}, bf16[1344,128]{1,0:T(8,128)(2,1)S(1)}, u32[]{:S(2)}, u32[]{:S(2)}) collective-permute-start(bf16[1344,128]{1,0:T(8,128)(2,1)S(1)} %slice.25), channel_id=1, source_target_pairs={{0,48},{1,49},{2,50},{3,51},{4,52},{5,53},{6,54},{7,55},{8,200},{9... | collective-permute-start | bytes 1032200 | tf_op jit(solution)/shard_map/ppermute | solution.py:476
  47.3 11.4 %collective-permute-start.14 = (bf16[1344,128]{1,0:T(8,128)(2,1)S(1)}, bf16[1344,128]{1,0:T(8,128)(2,1)S(1)}, u32[]{:S(2)}, u32[]{:S(2)}) collective-permute-start(bf16[1344,128]{1,0:T(8,128)(2,1)S(1)} %slice.22), channel_id=1, source_target_pairs={{0,16},{1,17},{2,18},{3,19},{4,20},{5,21},{6,22},{7,23},{8,72},{9,... | collective-permute-start | bytes 1032200 | tf_op jit(solution)/shard_map/ppermute | solution.py:476
  48.1 10.6 %collective-permute-start.15 = (bf16[1344,128]{1,0:T(8,128)(2,1)S(1)}, bf16[1344,128]{1,0:T(8,128)(2,1)S(1)}, u32[]{:S(2)}, u32[]{:S(2)}) collective-permute-start(bf16[1344,128]{1,0:T(8,128)(2,1)S(1)} %slice.23), channel_id=1, source_target_pairs={{0,48},{1,49},{2,50},{3,51},{4,52},{5,53},{6,54},{7,55},{8,200},{9... | collective-permute-start | bytes 1032200 | tf_op jit(solution)/shard_map/ppermute | solution.py:476
  63.2 17.0 %copy-start.2 = (f32[12,1,128]{2,1,0:T(1,128)S(1)}, f32[12,1,128]{2,1,0:T(1,128)}, u32[]{:S(2)}) copy-start(f32[12,1,128]{2,1,0:T(1,128)} %param.12) | copy-start | bytes 18436
  63.2 1.3 %collective-permute-start.16 = (f32[144,128]{1,0:T(8,128)S(1)}, f32[144,128]{1,0:T(8,128)S(1)}, u32[]{:S(2)}, u32[]{:S(2)}) collective-permute-start(f32[144,128]{1,0:T(8,128)S(1)} %get-tuple-element.143.a_ref), channel_id=1, source_target_pairs={{0,8},{8,0},{1,9},{9,1},{2,10},{10,2},{3,11},{11,3},{4,12},{12,4},... | collective-permute-start | bytes 221192 | tf_op jit(solution)/shard_map/ppermute | solution.py:477
  64.5 7.4 %collective-permute-start.19 = (f32[1536,384]{1,0:T(8,128)}, f32[1536,384]{1,0:T(8,128)}, u32[]{:S(2)}, u32[]{:S(2)}) collective-permute-start(f32[1536,384]{1,0:T(8,128)} %get-tuple-element.149), channel_id=1, source_target_pairs={{0,8},{8,0},{1,9},{9,1},{2,10},{10,2},{3,11},{11,3},{4,12},{12,4},... | collective-permute-start | bytes 7077896 | tf_op jit(solution)/shard_map/ppermute | solution.py:477
  64.6 7.3 %collective-permute-start.17 = (f32[1536,256]{1,0:T(8,128)}, f32[1536,256]{1,0:T(8,128)}, u32[]{:S(2)}, u32[]{:S(2)}) collective-permute-start(f32[1536,256]{1,0:T(8,128)} %get-tuple-element.147.p_ref), channel_id=1, source_target_pairs={{0,8},{8,0},{1,9},{9,1},{2,10},{10,2},{3,11},{11,3},{4,12},{12,4},... | collective-permute-start | bytes 4718600 | tf_op jit(solution)/shard_map/ppermute | solution.py:477
  65.0 6.4 %collective-permute-start.18 = (f32[384,128]{1,0:T(8,128)S(1)}, f32[384,128]{1,0:T(8,128)S(1)}, u32[]{:S(2)}, u32[]{:S(2)}) collective-permute-start(f32[384,128]{1,0:T(8,128)S(1)} %get-tuple-element.148), channel_id=1, source_target_pairs={{0,8},{8,0},{1,9},{9,1},{2,10},{10,2},{3,11},{11,3},{4,12},{12,4},... | collective-permute-start | bytes 589832 | tf_op jit(solution)/shard_map/ppermute | solution.py:477
  75.7 10.8 %collective-permute-start.20 = (f32[12,128]{1,0:T(8,128)S(1)}, f32[12,128]{1,0:T(8,128)S(1)}, u32[]{:S(2)}, u32[]{:S(2)}) collective-permute-start(f32[12,128]{1,0:T(8,128)S(1)} %get-tuple-element.163), channel_id=1, source_target_pairs={{0,3},{1,2},{2,1},{3,0},{4,7},{5,6},{6,5},{7,4},{8,11},{9,10},{10,... | collective-permute-start | bytes 18440 | tf_op jit(solution)/shard_map/ppermute | solution.py:525
  77.9 8.5 %collective-permute-start.21 = (f32[12,128]{1,0:T(8,128)S(1)}, f32[12,128]{1,0:T(8,128)S(1)}, u32[]{:S(2)}, u32[]{:S(2)}) collective-permute-start(f32[12,128]{1,0:T(8,128)S(1)} %get-tuple-element.163), channel_id=1, source_target_pairs={{0,2},{1,3},{2,0},{3,1},{4,6},{5,7},{6,4},{7,5},{8,10},{9,11},{10,... | collective-permute-start | bytes 18440 | tf_op jit(solution)/shard_map/ppermute | solution.py:525
  77.9 8.5 %collective-permute-start.22 = (f32[12,128]{1,0:T(8,128)S(1)}, f32[12,128]{1,0:T(8,128)S(1)}, u32[]{:S(2)}, u32[]{:S(2)}) collective-permute-start(f32[12,128]{1,0:T(8,128)S(1)} %get-tuple-element.163), channel_id=1, source_target_pairs={{0,1},{1,0},{2,3},{3,2},{4,5},{5,4},{6,7},{7,6},{8,9},{9,8},{10,11... | collective-permute-start | bytes 18440 | tf_op jit(solution)/shard_map/ppermute | solution.py:525
  86.5 8.5 %collective-permute-start.23 = (f32[12,8,128]{2,1,0:T(8,128)S(1)}, f32[12,8,128]{2,1,0:T(8,128)S(1)}, u32[]{:S(2)}, u32[]{:S(2)}) collective-permute-start(f32[12,8,128]{2,1,0:T(8,128)S(1)} %select_select_fusion), channel_id=1, source_target_pairs={{0,4},{1,5},{2,6},{3,7},{4,0},{5,1},{6,2},{7,3},{8,12},{9,13},{10,... | collective-permute-start | bytes 147464 | tf_op jit(solution)/shard_map/ppermute | solution.py:478

commit v6 on v5

--- a/solution.py
+++ b/solution.py
@@ -521,9 +521,10 @@
     mine, lpan, la, lb = panel_solve(panel, p, pr, po, por, w, yz)
     slot = lax.broadcasted_iota(jnp.int32, (1, NZ, 1), 1)
     full = jnp.where(slot == q, mine[:, None, :], 0.0)
+    parts = [full]
     for bits in (1, 2, 3):
-        other = lax.ppermute(mine, "row", [(i, i ^ bits) for i in range(NZ)])
-        full = jnp.where(slot == q ^ bits, other[:, None, :], full)
+        parts.append(lax.ppermute(parts[0], "row", [(i, i ^ bits) for i in range(NZ)]))
+    full = parts[0] + parts[1] + parts[2] + parts[3]
     rest = (panel, gown, gr, la, lb, lpan, chol, damping[:, 0, :])
     fac = final(0, 8, *rest)
     full, fac = bar((full, fac))

time: 97.3 us -> 91.4 us (0.939)
  Pallas kernels: 47.6 us -> 40.2 us
  waiting for transfers between devices: 5.64 us -> 7.48 us
    pallas_call x2, Pallas kernels: 9.96 us -> 5.96 us  [final(): pl.pallas_call(lambda *r: final_kernel(start, *r), grid=(count,), out_sha...]
    ppermute x2, waiting for transfers between devices: 0.01 us -> 1.97 us  [body(): lax.ppermute(v, 'row', [(i, i ^ bit) for i in range(NZ)])]
    pallas_call x1, Pallas kernels: 3.79 us -> 1.92 us  [panel_solve(): pl.pallas_call(panel_kernel, out_shape=(jax.ShapeDtypeStruct((LR, K), F32...]
    pallas_call x5, Pallas kernels: 24.2 us -> 22.7 us  [chunk(): pl.pallas_call(lambda *r: chunk_kernel(blocks, len(arrs), len(accs), *r),...]
  transfers between devices with their start and end apart: 24 -> 24, of which waited for: 4 -> 6; matrix products, arithmetic and copies ran while one was open for 1% -> 1% of each run, Pallas kernels for 38% -> 36%
where the time goes in v6:
time: 91.4 us; the launch traced here: 90 us
  Pallas kernels  40.2 us (44%)
  starting transfers between devices  37.4 us (41%)
  waiting for transfers between devices  7.48 us (8%)
  local copies, waits for them, and re-layouts  1.98 us (2%)
  between operations  1.52 us (2%)
  other arithmetic  1.45 us (2%)
    pallas_call x5, Pallas kernels, chunk(): pl.pallas_call(lambda *r: chunk_kernel(blocks, len(arrs), len(accs), *r),...  22.7 us
    ppermute x8, starting transfers between devices, body(): two = lambda v, d: lax.ppermute(v, AXES, hops(1, d))  13.4 us
    ppermute x2, starting transfers between devices, body(): lax.ppermute(v, 'row', [(i, i ^ bit) for i in range(NZ)])  9.39 us
    pallas_call x1, Pallas kernels, cholesky(): pl.pallas_call(chol_kernel, out_shape=(jax.ShapeDtypeStruct((K, K), F32),...  6.21 us
    pallas_call x2, Pallas kernels, final(): pl.pallas_call(lambda *r: final_kernel(start, *r), grid=(count,), out_sha...  5.96 us
    ppermute x3, starting transfers between devices, body(): parts.append(lax.ppermute(dsel, 'row', [(i, i ^ bits) for i in range(NZ)]))  4.85 us
    ppermute x4, starting transfers between devices, body(): one = lambda v, d: lax.ppermute(v, AXES, hops(0, d))  4.55 us
    ppermute x3, starting transfers between devices, body(): lax.ppermute(parts[0], 'row', [(i, i ^ bits) for i in range(NZ)])  4.42 us
  transfers between devices with their start and end apart: 24, of which 6 were waited for; matrix products, arithmetic and copies ran while one was open for 1% of the time, Pallas kernels for 36%

profile of v6, /device:TPU:2, one launch (start us, length us, event | category | flops | bytes accessed | tf_op | source)
XLA Modules:
  0.0 90.0 jit_solution(4296416698346473333)
XLA Ops:
  1.3 3.1 %pack.1 = (bf16[1664,128]{1,0:T(8,128)(2,1)}, bf16[1664,128]{1,0:T(8,128)(2,1)}, bf16[256,128]{1,0:T(8,128)(2,1)}) custom-call(s32[1]{0:T(128)} %copy.16.k_ref.r_0_, s32[1,128]{1,0:T(1,128)} %bitcast.25, bf16[1152,256]{1,0:T(8,128)(2,1)} %bitcast.23, bf16[864,256]{1,0:T(8,128)(2,1)} %bitcast.24, bf16[2,128]{1,0:T(2,128)(2,1)} %bitcast.26, ...), custom_call_target="tpu_custom_call" | custom-call | tf_op jit(solution)/shard_map/pack/pallas_call | solution.py:106
  4.4 1.6 %collective-permute-start = (bf16[1664,128]{1,0:T(8,128)(2,1)}, bf16[1664,128]{1,0:T(8,128)(2,1)S(1)}, u32[]{:S(2)}, u32[]{:S(2)}) collective-permute-start(bf16[1664,128]{1,0:T(8,128)(2,1)} %get-tuple-element.84.r_0_), channel_id=1, source_target_pairs={{0,64},{1,65},{2,66},{3,67},{4,68},{5,69},{6,70},{7,71},{8,24},{9,... | collective-permute-start | bytes 1277960 | tf_op jit(solution)/shard_map/ppermute | solution.py:475
  6.0 0.9 collective-permute-start.1
  6.9 0.7 fusion
  7.5 1.6 %collective-permute-start.2 = (f32[8,128]{1,0:T(8,128)S(1)}, f32[8,128]{1,0:T(8,128)S(1)}, u32[]{:S(2)}, u32[]{:S(2)}) collective-permute-start(f32[8,128]{1,0:T(8,128)S(1)} %broadcast_in_dim.31), channel_id=1, source_target_pairs={{0,1},{1,0},{2,3},{3,2},{4,5},{5,4},{6,7},{7,6},{8,9},{9,8},{10,11... | collective-permute-start | bytes 12296 | tf_op jit(solution)/shard_map/ppermute | solution.py:493
  9.1 3.3 %collective-permute-start.3 = (f32[8,128]{1,0:T(8,128)S(1)}, f32[8,128]{1,0:T(8,128)S(1)}, u32[]{:S(2)}, u32[]{:S(2)}) collective-permute-start(f32[8,128]{1,0:T(8,128)S(1)} %broadcast_in_dim.31), channel_id=1, source_target_pairs={{0,2},{1,3},{2,0},{3,1},{4,6},{5,7},{6,4},{7,5},{8,10},{9,11},{10,... | collective-permute-start | bytes 12296 | tf_op jit(solution)/shard_map/ppermute | solution.py:493
  12.4 1.0 %copy-done = bf16[1664,128]{1,0:T(8,128)(2,1)S(1)} copy-done((bf16[1664,128]{1,0:T(8,128)(2,1)S(1)}, bf16[1664,128]{1,0:T(8,128)(2,1)}, u32[]{:S(2)}) %copy-start) | copy-done | bytes 426008
  13.4 0.8 copy-done.1
  14.2 1.9 %chunk_own.1 = (f32[1536,384]{1,0:T(8,128)S(1)}, f32[1536,384]{1,0:T(8,128)S(1)}, f32[1536,256]{1,0:T(8,128)S(1)}, f32[384,128]{1,0:T(8,128)S(1)}, f32[384,128]{1,0:T(8,128)S(1)}, /*index=5*/f32[144,128]{1,0:T(8,128)S(1)}) custom-call(bf16[1664,128]{1,0:T(8,128)(2,1)S(1)} %copy-done, bf16[256,128]{1,0:T(8,128)(2,1)S(1)} %copy-done.1), custom_call_target="tpu_custom_call" | custom-call | flops 1012531200 | bytes 4000000 | tf_op jit(solution)/shard_map/chunk_own/pallas_call | solution.py:267
  16.2 1.6 %collective-permute-done.4 = f32[8,128]{1,0:T(8,128)S(1)} collective-permute-done((f32[8,128]{1,0:T(8,128)S(1)}, f32[8,128]{1,0:T(8,128)S(1)}, u32[]{:S(2)}, u32[]{:S(2)}) %collective-permute-start.4) | collective-permute-done | bytes 4128 | tf_op jit(solution)/shard_map/ppermute | solution.py:493
  17.9 1.7 %collective-permute-start.5 = (bf16[2752,128]{1,0:T(8,128)(2,1)S(1)}, bf16[2752,128]{1,0:T(8,128)(2,1)S(1)}, u32[]{:S(2)}, u32[]{:S(2)}) collective-permute-start(bf16[2752,128]{1,0:T(8,128)(2,1)S(1)} %get-tuple-element.94), channel_id=1, source_target_pairs={{0,16},{1,17},{2,18},{3,19},{4,20},{5,21},{6,22},{7,23},{8,72},{9,... | collective-permute-start | bytes 2113544 | tf_op jit(solution)/shard_map/ppermute | solution.py:476
  19.6 1.7 %collective-permute-start.7 = (bf16[2752,128]{1,0:T(8,128)(2,1)S(1)}, bf16[2752,128]{1,0:T(8,128)(2,1)S(1)}, u32[]{:S(2)}, u32[]{:S(2)}) collective-permute-start(bf16[2752,128]{1,0:T(8,128)(2,1)S(1)} %get-tuple-element.95), channel_id=1, source_target_pairs={{0,48},{1,49},{2,50},{3,51},{4,52},{5,53},{6,54},{7,55},{8,200},{9... | collective-permute-start | bytes 2113544 | tf_op jit(solution)/shard_map/ppermute | solution.py:476
  21.3 1.8 %collective-permute-start.10 = (bf16[768,128]{1,0:T(8,128)(2,1)S(1)}, bf16[768,128]{1,0:T(8,128)(2,1)S(1)}, u32[]{:S(2)}, u32[]{:S(2)}) collective-permute-start(bf16[768,128]{1,0:T(8,128)(2,1)S(1)} %slice.21), channel_id=1, source_target_pairs={{0,192},{1,193},{2,194},{3,195},{4,196},{5,197},{6,198},{7,199},{8... | collective-permute-start | bytes 589832 | tf_op jit(solution)/shard_map/ppermute | solution.py:475
  23.4 4.8 %collective-permute-start.11 = (f32[8,128]{1,0:T(8,128)S(1)}, f32[8,128]{1,0:T(8,128)S(1)}, u32[]{:S(2)}, u32[]{:S(2)}) collective-permute-start(f32[8,128]{1,0:T(8,128)S(1)} %add_add_fusion.1), channel_id=1, source_target_pairs={{0,4},{1,5},{2,6},{3,7},{4,0},{5,1},{6,2},{7,3},{8,12},{9,13},{10,... | collective-permute-start | bytes 12296 | tf_op jit(solution)/shard_map/ppermute | solution.py:478
  28.2 2.8 %chunk_line1.1 = (f32[1536,384]{1,0:T(8,128)S(1)}, f32[1536,384]{1,0:T(8,128)S(1)}, f32[1536,256]{1,0:T(8,128)S(1)}, f32[384,128]{1,0:T(8,128)S(1)}, f32[384,128]{1,0:T(8,128)S(1)}, /*index=5*/f32[144,128]{1,0:T(8,128)S(1)}) custom-call(bf16[1664,128]{1,0:T(8,128)(2,1)S(1)} %collective-permute-done.r_2_.r_0_, ...), custom_call_target="tpu_custom_call" | custom-call | flops 2025062400 | bytes 8000000 | tf_op jit(solution)/shard_map/chunk_line1/pallas_call | solution.py:267
  31.6 2.9 %collective-permute-start.13 = (bf16[2752,128]{1,0:T(8,128)(2,1)S(1)}, bf16[2752,128]{1,0:T(8,128)(2,1)S(1)}, u32[]{:S(2)}, u32[]{:S(2)}) collective-permute-start(bf16[2752,128]{1,0:T(8,128)(2,1)S(1)} %get-tuple-element.113), channel_id=1, source_target_pairs={{0,48},{1,49},{2,50},{3,51},{4,52},{5,53},{6,54},{7,55},{8,200},{9... | collective-permute-start | bytes 2113544 | tf_op jit(solution)/shard_map/ppermute | solution.py:476
  34.6 3.3 %collective-permute-start.8 = (bf16[1344,128]{1,0:T(8,128)(2,1)S(1)}, bf16[1344,128]{1,0:T(8,128)(2,1)S(1)}, u32[]{:S(2)}, u32[]{:S(2)}) collective-permute-start(bf16[1344,128]{1,0:T(8,128)(2,1)S(1)} %slice.25), channel_id=1, source_target_pairs={{0,48},{1,49},{2,50},{3,51},{4,52},{5,53},{6,54},{7,55},{8,200},{9... | collective-permute-start | bytes 1032200 | tf_op jit(solution)/shard_map/ppermute | solution.py:476
  37.9 7.2 %chunk_line2.1 = (f32[1536,384]{1,0:T(8,128)S(1)}, f32[1536,384]{1,0:T(8,128)S(1)}, f32[1536,256]{1,0:T(8,128)S(1)}, f32[384,128]{1,0:T(8,128)S(1)}, f32[384,128]{1,0:T(8,128)S(1)}, /*index=5*/f32[144,128]{1,0:T(8,128)S(1)}) custom-call(bf16[2752,128]{1,0:T(8,128)(2,1)S(1)} %collective-permute-done.5.r_0_, ...), custom_call_target="tpu_custom_call" | custom-call | flops 5062656000 | bytes 20000000 | tf_op jit(solution)/shard_map/chunk_line2/pallas_call | solution.py:267
  45.1 2.1 %collective-permute-done.6.r_0_ = bf16[1344,128]{1,0:T(8,128)(2,1)S(1)} collective-permute-done((bf16[1344,128]{1,0:T(8,128)(2,1)S(1)}, bf16[1344,128]{1,0:T(8,128)(2,1)S(1)}, u32[]{:S(2)}, u32[]{:S(2)}) %collective-permute-start.6) | collective-permute-done | bytes 344096 | tf_op jit(solution)/shard_map/ppermute | solution.py:476
  47.3 0.8 collective-permute-start.14
  48.1 2.6 %collective-permute-start.15 = (bf16[1344,128]{1,0:T(8,128)(2,1)S(1)}, bf16[1344,128]{1,0:T(8,128)(2,1)S(1)}, u32[]{:S(2)}, u32[]{:S(2)}) collective-permute-start(bf16[1344,128]{1,0:T(8,128)(2,1)S(1)} %slice.23), channel_id=1, source_target_pairs={{0,48},{1,49},{2,50},{3,51},{4,52},{5,53},{6,54},{7,55},{8,200},{9... | collective-permute-start | bytes 1032200 | tf_op jit(solution)/shard_map/ppermute | solution.py:476
  50.7 8.0 %chunk_far1.1 = (f32[1536,384]{1,0:T(8,128)S(1)}, f32[1536,384]{1,0:T(8,128)S(1)}, f32[1536,256]{1,0:T(8,128)S(1)}, f32[384,128]{1,0:T(8,128)S(1)}, f32[384,128]{1,0:T(8,128)S(1)}, /*index=5*/f32[144,128]{1,0:T(8,128)S(1)}) custom-call(bf16[1344,128]{1,0:T(8,128)(2,1)S(1)} %collective-permute-done.6.r_0_, bf16[1344,128]{1,0:T(8,128)(2,1)S(1)} %collective-permute-done.8.r_1_, ...), custom_call_target="tpu_custom_call" | custom-call | flops 6075187200 | bytes 24000000 | tf_op jit(solution)/shard_map/chunk_far1/pallas_call | solution.py:267
  58.8 2.9 %chunk_far2.1 = (f32[1536,384]{1,0:T(8,128)S(1)}, f32[1536,384]{1,0:T(8,128)S(1)}, f32[1536,256]{1,0:T(8,128)S(1)}, f32[384,128]{1,0:T(8,128)S(1)}, f32[384,128]{1,0:T(8,128)S(1)}, /*index=5*/f32[144,128]{1,0:T(8,128)S(1)}) custom-call(bf16[1344,128]{1,0:T(8,128)(2,1)S(1)} %collective-permute-done.14.r_0_, ...), custom_call_target="tpu_custom_call" | custom-call | flops 2025062400 | bytes 8000000 | tf_op jit(solution)/shard_map/chunk_far2/pallas_call | solution.py:267
  61.8 1.3 %collective-permute-done.16.b_ref = f32[144,128]{1,0:T(8,128)S(1)} collective-permute-done((f32[144,128]{1,0:T(8,128)S(1)}, f32[144,128]{1,0:T(8,128)S(1)}, u32[]{:S(2)}, u32[]{:S(2)}) %collective-permute-start.16) | collective-permute-done | bytes 73760 | tf_op jit(solution)/shard_map/ppermute | solution.py:477
  63.7 6.2 %panel_factor.1 = (f32[128,128]{1,0:T(8,128)S(1)}, f32[128,128]{1,0:T(8,128)S(1)}, f32[16,128]{1,0:T(8,128)S(1)}) custom-call(f32[144,128]{1,0:T(8,128)S(1)} %get-tuple-element.143.a_ref, f32[144,128]{1,0:T(8,128)S(1)} %collective-permute-done.16.b_ref, f32[8,128]{1,0:T(8,128)S(1)} %add.38.d_ref), custom_call_target="tpu_custom_call" | custom-call | tf_op jit(solution)/shard_map/panel_factor/pallas_call | solution.py:341
  70.1 1.9 %panel_solve.1 = (f32[12,128]{1,0:T(8,128)S(1)}, f32[1536,128]{1,0:T(8,128)S(1)}, bf16[1536,384]{1,0:T(8,128)(2,1)S(1)}, bf16[384,384]{1,0:T(8,128)(2,1)S(1)}) custom-call(s32[1]{0:T(128)} %copy.16.k_ref.r_0_, f32[1536,256]{1,0:T(8,128)S(1)} %get-tuple-element.147.p_ref, f32[1536,256]{1,0:T(8,128)S(1)} %collective-permute-done.17.pr_ref, ...), custom_call_target="tpu_custom_call" | custom-call | tf_op jit(solution)/shard_map/panel_solve/pallas_call | solution.py:395
  72.2 2.6 %collective-permute-start.21 = (f32[12,8,128]{2,1,0:T(8,128)S(1)}, f32[12,8,128]{2,1,0:T(8,128)S(1)}, u32[]{:S(2)}, u32[]{:S(2)}) collective-permute-start(f32[12,8,128]{2,1,0:T(8,128)S(1)} %broadcast_select_fusion), channel_id=1, source_target_pairs={{0,2},{1,3},{2,0},{3,1},{4,6},{5,7},{6,4},{7,5},{8,10},{9,11},{10,... | collective-permute-start | bytes 147464 | tf_op jit(solution)/shard_map/ppermute | solution.py:526
  74.8 1.7 %collective-permute-start.22 = (f32[12,8,128]{2,1,0:T(8,128)S(1)}, f32[12,8,128]{2,1,0:T(8,128)S(1)}, u32[]{:S(2)}, u32[]{:S(2)}) collective-permute-start(f32[12,8,128]{2,1,0:T(8,128)S(1)} %broadcast_select_fusion), channel_id=1, source_target_pairs={{0,3},{1,2},{2,1},{3,0},{4,7},{5,6},{6,5},{7,4},{8,11},{9,10},{10,... | collective-permute-start | bytes 147464 | tf_op jit(solution)/shard_map/ppermute | solution.py:526
  76.5 3.9 %trailing_update.2.r_8_ = f32[4608,128]{1,0:T(8,128)} custom-call(s32[1]{0:T(128)} %copy.16.k_ref.r_0_, f32[1536,384]{1,0:T(8,128)S(1)} %get-tuple-element.142.r_1_, f32[1536,384]{1,0:T(8,128)S(1)} %collective-permute-done.19.r_2_, bf16[1536,384]{1,0:T(8,128)(2,1)S(1)} %get-tuple-element.159.r_3_, bf16[384,384]{1,0:T(8,128)(2,1)S(1)} %get-tuple-element.160.r_4_, ...), custom_call_target="tpu_custom_call" | custom-call | flops 1 | bytes 6000000 | tf_op jit(solution)/shard_map/trailing_update/pallas_call | solution.py:439
  80.8 4.6 %collective-permute-start.23 = (f32[12,8,128]{2,1,0:T(8,128)S(1)}, f32[12,8,128]{2,1,0:T(8,128)S(1)}, u32[]{:S(2)}, u32[]{:S(2)}) collective-permute-start(f32[12,8,128]{2,1,0:T(8,128)S(1)} %add_add_fusion), channel_id=1, source_target_pairs={{0,4},{1,5},{2,6},{3,7},{4,0},{5,1},{6,2},{7,3},{8,12},{9,13},{10,... | collective-permute-start | bytes 147464 | tf_op jit(solution)/shard_map/ppermute | solution.py:478
  85.4 2.1 %trailing_update.3 = f32[4608,128]{1,0:T(8,128)} custom-call(s32[1]{0:T(128)} %copy.16.k_ref.r_0_, f32[1536,384]{1,0:T(8,128)S(1)} %get-tuple-element.142.r_1_, f32[1536,384]{1,0:T(8,128)S(1)} %collective-permute-done.19.r_2_, bf16[1536,384]{1,0:T(8,128)(2,1)S(1)} %get-tuple-element.159.r_3_, ...), custom_call_target="tpu_custom_call", output_to_operand_aliasing={{}: (8, {})} | custom-call | flops 1 | bytes 6000000 | tf_op jit(solution)/shard_map/trailing_update/pallas_call | solution.py:439
  87.4 2.0 %collective-permute-done.23 = f32[12,8,128]{2,1,0:T(8,128)S(1)} collective-permute-done((f32[12,8,128]{2,1,0:T(8,128)S(1)}, f32[12,8,128]{2,1,0:T(8,128)S(1)}, u32[]{:S(2)}, u32[]{:S(2)}) %collective-permute-start.23) | collective-permute-done | bytes 49184 | tf_op jit(solution)/shard_map/ppermute | solution.py:478
  (49 shorter events, 3.4 us)
Async XLA Ops:
  4.4 13.4 %collective-permute-start = (bf16[1664,128]{1,0:T(8,128)(2,1)}, bf16[1664,128]{1,0:T(8,128)(2,1)S(1)}, u32[]{:S(2)}, u32[]{:S(2)}) collective-permute-start(bf16[1664,128]{1,0:T(8,128)(2,1)} %get-tuple-element.84.r_0_), channel_id=1, source_target_pairs={{0,64},{1,65},{2,66},{3,67},{4,68},{5,69},{6,70},{7,71},{8,24},{9,... | collective-permute-start | bytes 1277960 | tf_op jit(solution)/shard_map/ppermute | solution.py:475
  6.0 11.8 %collective-permute-start.1 = (bf16[1664,128]{1,0:T(8,128)(2,1)}, bf16[1664,128]{1,0:T(8,128)(2,1)S(1)}, u32[]{:S(2)}, u32[]{:S(2)}) collective-permute-start(bf16[1664,128]{1,0:T(8,128)(2,1)} %get-tuple-element.86), channel_id=1, source_target_pairs={{0,192},{1,193},{2,194},{3,195},{4,196},{5,197},{6,198},{7,199},{8... | collective-permute-start | bytes 1277960 | tf_op jit(solution)/shard_map/ppermute | solution.py:475
  7.5 8.6 %collective-permute-start.2 = (f32[8,128]{1,0:T(8,128)S(1)}, f32[8,128]{1,0:T(8,128)S(1)}, u32[]{:S(2)}, u32[]{:S(2)}) collective-permute-start(f32[8,128]{1,0:T(8,128)S(1)} %broadcast_in_dim.31), channel_id=1, source_target_pairs={{0,1},{1,0},{2,3},{3,2},{4,5},{5,4},{6,7},{7,6},{8,9},{9,8},{10,11... | collective-permute-start | bytes 12296 | tf_op jit(solution)/shard_map/ppermute | solution.py:493
  9.1 7.0 %collective-permute-start.3 = (f32[8,128]{1,0:T(8,128)S(1)}, f32[8,128]{1,0:T(8,128)S(1)}, u32[]{:S(2)}, u32[]{:S(2)}) collective-permute-start(f32[8,128]{1,0:T(8,128)S(1)} %broadcast_in_dim.31), channel_id=1, source_target_pairs={{0,2},{1,3},{2,0},{3,1},{4,6},{5,7},{6,4},{7,5},{8,10},{9,11},{10,... | collective-permute-start | bytes 12296 | tf_op jit(solution)/shard_map/ppermute | solution.py:493
  12.4 5.4 %collective-permute-start.4 = (f32[8,128]{1,0:T(8,128)S(1)}, f32[8,128]{1,0:T(8,128)S(1)}, u32[]{:S(2)}, u32[]{:S(2)}) collective-permute-start(f32[8,128]{1,0:T(8,128)S(1)} %broadcast_in_dim.31), channel_id=1, source_target_pairs={{0,3},{1,2},{2,1},{3,0},{4,7},{5,6},{6,5},{7,4},{8,11},{9,10},{10,... | collective-permute-start | bytes 12296 | tf_op jit(solution)/shard_map/ppermute | solution.py:493
  12.4 1.0 %copy-start = (bf16[1664,128]{1,0:T(8,128)(2,1)S(1)}, bf16[1664,128]{1,0:T(8,128)(2,1)}, u32[]{:S(2)}) copy-start(bf16[1664,128]{1,0:T(8,128)(2,1)} %get-tuple-element.84.r_0_) | copy-start | bytes 1277956
  13.4 0.8 copy-start.1
  17.9 16.5 %collective-permute-start.5 = (bf16[2752,128]{1,0:T(8,128)(2,1)S(1)}, bf16[2752,128]{1,0:T(8,128)(2,1)S(1)}, u32[]{:S(2)}, u32[]{:S(2)}) collective-permute-start(bf16[2752,128]{1,0:T(8,128)(2,1)S(1)} %get-tuple-element.94), channel_id=1, source_target_pairs={{0,16},{1,17},{2,18},{3,19},{4,20},{5,21},{6,22},{7,23},{8,72},{9,... | collective-permute-start | bytes 2113544 | tf_op jit(solution)/shard_map/ppermute | solution.py:476
  19.6 15.0 %collective-permute-start.7 = (bf16[2752,128]{1,0:T(8,128)(2,1)S(1)}, bf16[2752,128]{1,0:T(8,128)(2,1)S(1)}, u32[]{:S(2)}, u32[]{:S(2)}) collective-permute-start(bf16[2752,128]{1,0:T(8,128)(2,1)S(1)} %get-tuple-element.95), channel_id=1, source_target_pairs={{0,48},{1,49},{2,50},{3,51},{4,52},{5,53},{6,54},{7,55},{8,200},{9... | collective-permute-start | bytes 2113544 | tf_op jit(solution)/shard_map/ppermute | solution.py:476
  21.3 9.7 %collective-permute-start.10 = (bf16[768,128]{1,0:T(8,128)(2,1)S(1)}, bf16[768,128]{1,0:T(8,128)(2,1)S(1)}, u32[]{:S(2)}, u32[]{:S(2)}) collective-permute-start(bf16[768,128]{1,0:T(8,128)(2,1)S(1)} %slice.21), channel_id=1, source_target_pairs={{0,192},{1,193},{2,194},{3,195},{4,196},{5,197},{6,198},{7,199},{8... | collective-permute-start | bytes 589832 | tf_op jit(solution)/shard_map/ppermute | solution.py:475
  23.1 7.9 %collective-permute-start.9 = (bf16[768,128]{1,0:T(8,128)(2,1)S(1)}, bf16[768,128]{1,0:T(8,128)(2,1)S(1)}, u32[]{:S(2)}, u32[]{:S(2)}) collective-permute-start(bf16[768,128]{1,0:T(8,128)(2,1)S(1)} %slice.20), channel_id=1, source_target_pairs={{0,64},{1,65},{2,66},{3,67},{4,68},{5,69},{6,70},{7,71},{8,24},{9,... | collective-permute-start | bytes 589832 | tf_op jit(solution)/shard_map/ppermute | solution.py:475
  23.4 7.6 %collective-permute-start.11 = (f32[8,128]{1,0:T(8,128)S(1)}, f32[8,128]{1,0:T(8,128)S(1)}, u32[]{:S(2)}, u32[]{:S(2)}) collective-permute-start(f32[8,128]{1,0:T(8,128)S(1)} %add_add_fusion.1), channel_id=1, source_target_pairs={{0,4},{1,5},{2,6},{3,7},{4,0},{5,1},{6,2},{7,3},{8,12},{9,13},{10,... | collective-permute-start | bytes 12296 | tf_op jit(solution)/shard_map/ppermute | solution.py:478
  31.2 13.9 %collective-permute-start.12 = (bf16[2752,128]{1,0:T(8,128)(2,1)S(1)}, bf16[2752,128]{1,0:T(8,128)(2,1)S(1)}, u32[]{:S(2)}, u32[]{:S(2)}) collective-permute-start(bf16[2752,128]{1,0:T(8,128)(2,1)S(1)} %get-tuple-element.112), channel_id=1, source_target_pairs={{0,16},{1,17},{2,18},{3,19},{4,20},{5,21},{6,22},{7,23},{8,72},{9,... | collective-permute-start | bytes 2113544 | tf_op jit(solution)/shard_map/ppermute | solution.py:476
  31.6 13.5 %collective-permute-start.13 = (bf16[2752,128]{1,0:T(8,128)(2,1)S(1)}, bf16[2752,128]{1,0:T(8,128)(2,1)S(1)}, u32[]{:S(2)}, u32[]{:S(2)}) collective-permute-start(bf16[2752,128]{1,0:T(8,128)(2,1)S(1)} %get-tuple-element.113), channel_id=1, source_target_pairs={{0,48},{1,49},{2,50},{3,51},{4,52},{5,53},{6,54},{7,55},{8,200},{9... | collective-permute-start | bytes 2113544 | tf_op jit(solution)/shard_map/ppermute | solution.py:476
  34.5 12.7 %collective-permute-start.6 = (bf16[1344,128]{1,0:T(8,128)(2,1)S(1)}, bf16[1344,128]{1,0:T(8,128)(2,1)S(1)}, u32[]{:S(2)}, u32[]{:S(2)}) collective-permute-start(bf16[1344,128]{1,0:T(8,128)(2,1)S(1)} %slice.24), channel_id=1, source_target_pairs={{0,16},{1,17},{2,18},{3,19},{4,20},{5,21},{6,22},{7,23},{8,72},{9,... | collective-permute-start | bytes 1032200 | tf_op jit(solution)/shard_map/ppermute | solution.py:476
  34.6 12.6 %collective-permute-start.8 = (bf16[1344,128]{1,0:T(8,128)(2,1)S(1)}, bf16[1344,128]{1,0:T(8,128)(2,1)S(1)}, u32[]{:S(2)}, u32[]{:S(2)}) collective-permute-start(bf16[1344,128]{1,0:T(8,128)(2,1)S(1)} %slice.25), channel_id=1, source_target_pairs={{0,48},{1,49},{2,50},{3,51},{4,52},{5,53},{6,54},{7,55},{8,200},{9... | collective-permute-start | bytes 1032200 | tf_op jit(solution)/shard_map/ppermute | solution.py:476
  47.3 11.5 %collective-permute-start.14 = (bf16[1344,128]{1,0:T(8,128)(2,1)S(1)}, bf16[1344,128]{1,0:T(8,128)(2,1)S(1)}, u32[]{:S(2)}, u32[]{:S(2)}) collective-permute-start(bf16[1344,128]{1,0:T(8,128)(2,1)S(1)} %slice.22), channel_id=1, source_target_pairs={{0,16},{1,17},{2,18},{3,19},{4,20},{5,21},{6,22},{7,23},{8,72},{9,... | collective-permute-start | bytes 1032200 | tf_op jit(solution)/shard_map/ppermute | solution.py:476
  48.1 10.7 %collective-permute-start.15 = (bf16[1344,128]{1,0:T(8,128)(2,1)S(1)}, bf16[1344,128]{1,0:T(8,128)(2,1)S(1)}, u32[]{:S(2)}, u32[]{:S(2)}) collective-permute-start(bf16[1344,128]{1,0:T(8,128)(2,1)S(1)} %slice.23), channel_id=1, source_target_pairs={{0,48},{1,49},{2,50},{3,51},{4,52},{5,53},{6,54},{7,55},{8,200},{9... | collective-permute-start | bytes 1032200 | tf_op jit(solution)/shard_map/ppermute | solution.py:476
  61.7 14.9 %copy-start.2 = (f32[12,1,128]{2,1,0:T(1,128)S(1)}, f32[12,1,128]{2,1,0:T(1,128)}, u32[]{:S(2)}) copy-start(f32[12,1,128]{2,1,0:T(1,128)} %param.12) | copy-start | bytes 18436
  61.7 1.4 %collective-permute-start.16 = (f32[144,128]{1,0:T(8,128)S(1)}, f32[144,128]{1,0:T(8,128)S(1)}, u32[]{:S(2)}, u32[]{:S(2)}) collective-permute-start(f32[144,128]{1,0:T(8,128)S(1)} %get-tuple-element.143.a_ref), channel_id=1, source_target_pairs={{0,8},{8,0},{1,9},{9,1},{2,10},{10,2},{3,11},{11,3},{4,12},{12,4},... | collective-permute-start | bytes 221192 | tf_op jit(solution)/shard_map/ppermute | solution.py:477
  63.0 7.1 %collective-permute-start.19 = (f32[1536,384]{1,0:T(8,128)S(1)}, f32[1536,384]{1,0:T(8,128)S(1)}, u32[]{:S(2)}, u32[]{:S(2)}) collective-permute-start(f32[1536,384]{1,0:T(8,128)S(1)} %get-tuple-element.149), channel_id=1, source_target_pairs={{0,8},{8,0},{1,9},{9,1},{2,10},{10,2},{3,11},{11,3},{4,12},{12,4},... | collective-permute-start | bytes 7077896 | tf_op jit(solution)/shard_map/ppermute | solution.py:477
  63.2 6.9 %collective-permute-start.17 = (f32[1536,256]{1,0:T(8,128)S(1)}, f32[1536,256]{1,0:T(8,128)S(1)}, u32[]{:S(2)}, u32[]{:S(2)}) collective-permute-start(f32[1536,256]{1,0:T(8,128)S(1)} %get-tuple-element.147.p_ref), channel_id=1, source_target_pairs={{0,8},{8,0},{1,9},{9,1},{2,10},{10,2},{3,11},{11,3},{4,12},{12,4},... | collective-permute-start | bytes 4718600 | tf_op jit(solution)/shard_map/ppermute | solution.py:477
  63.5 6.6 %collective-permute-start.18 = (f32[384,128]{1,0:T(8,128)S(1)}, f32[384,128]{1,0:T(8,128)S(1)}, u32[]{:S(2)}, u32[]{:S(2)}) collective-permute-start(f32[384,128]{1,0:T(8,128)S(1)} %get-tuple-element.148), channel_id=1, source_target_pairs={{0,8},{8,0},{1,9},{9,1},{2,10},{10,2},{3,11},{11,3},{4,12},{12,4},... | collective-permute-start | bytes 589832 | tf_op jit(solution)/shard_map/ppermute | solution.py:477
  72.1 8.3 %collective-permute-start.20 = (f32[12,8,128]{2,1,0:T(8,128)S(1)}, f32[12,8,128]{2,1,0:T(8,128)S(1)}, u32[]{:S(2)}, u32[]{:S(2)}) collective-permute-start(f32[12,8,128]{2,1,0:T(8,128)S(1)} %broadcast_select_fusion), channel_id=1, source_target_pairs={{0,1},{1,0},{2,3},{3,2},{4,5},{5,4},{6,7},{7,6},{8,9},{9,8},{10,11... | collective-permute-start | bytes 147464 | tf_op jit(solution)/shard_map/ppermute | solution.py:526
  72.2 8.2 %collective-permute-start.21 = (f32[12,8,128]{2,1,0:T(8,128)S(1)}, f32[12,8,128]{2,1,0:T(8,128)S(1)}, u32[]{:S(2)}, u32[]{:S(2)}) collective-permute-start(f32[12,8,128]{2,1,0:T(8,128)S(1)} %broadcast_select_fusion), channel_id=1, source_target_pairs={{0,2},{1,3},{2,0},{3,1},{4,6},{5,7},{6,4},{7,5},{8,10},{9,11},{10,... | collective-permute-start | bytes 147464 | tf_op jit(solution)/shard_map/ppermute | solution.py:526
  74.8 5.9 %collective-permute-start.22 = (f32[12,8,128]{2,1,0:T(8,128)S(1)}, f32[12,8,128]{2,1,0:T(8,128)S(1)}, u32[]{:S(2)}, u32[]{:S(2)}) collective-permute-start(f32[12,8,128]{2,1,0:T(8,128)S(1)} %broadcast_select_fusion), channel_id=1, source_target_pairs={{0,3},{1,2},{2,1},{3,0},{4,7},{5,6},{6,5},{7,4},{8,11},{9,10},{10,... | collective-permute-start | bytes 147464 | tf_op jit(solution)/shard_map/ppermute | solution.py:526
  80.8 8.6 %collective-permute-start.23 = (f32[12,8,128]{2,1,0:T(8,128)S(1)}, f32[12,8,128]{2,1,0:T(8,128)S(1)}, u32[]{:S(2)}, u32[]{:S(2)}) collective-permute-start(f32[12,8,128]{2,1,0:T(8,128)S(1)} %add_add_fusion), channel_id=1, source_target_pairs={{0,4},{1,5},{2,6},{3,7},{4,0},{5,1},{6,2},{7,3},{8,12},{9,13},{10,... | collective-permute-start | bytes 147464 | tf_op jit(solution)/shard_map/ppermute | solution.py:478

commit v7 on v6

--- a/solution.py
+++ b/solution.py
@@ -14,7 +14,8 @@
 ROWG, KG, VR, RR = HR, HR + 108, HR + 117, HR + 118
 GC = 64
 HB = BR // 2
-PR = BR + 6 * GC
+PR = BR + 4 * GC
+FR = HB + 2 * GC
 MR = 2 * BR + 3 * GC
 RU, CU = LR * K, LC * K
 JR = RU + 2 * CU + 2 * K
@@ -35,7 +36,7 @@
 
 
 def pack_kernel(
-    k_ref, idx_hbm, h_hbm, g_hbm, v_hbm, r_hbm, plus_ref, minus_ref, own_ref,
+    k_ref, idx_hbm, h_hbm, g_hbm, v_hbm, r_hbm, plus_ref, minus_ref, low_ref, high_ref, own_ref,
     gs, tail, cbuf, idx_ref, h_ref, g_ref, v_ref, r_ref, sem,
 ):
     copies = [
@@ -58,10 +59,12 @@
         cp.wait()
     for c in range(C):
         val = jnp.dot(h_ref[c * K : (c + 1) * K, :], sel, preferred_element_type=F32).astype(BF16)
-        lo = c * K if c < 5 else c * K + 2 * GC
-        plus_ref[lo : lo + K, :] = val
-        lo = c * K + HB + 2 * GC if c < 5 else c * K - HB
-        minus_ref[lo : lo + K, :] = val
+        plus_ref[c * K : (c + 1) * K, :] = val
+        minus_ref[c * K : (c + 1) * K, :] = val
+        if c < 5:
+            low_ref[c * K : (c + 1) * K, :] = val
+        else:
+            high_ref[c * K - HB : (c + 1) * K - HB, :] = val
     for c in range(C):
         gs[c * A : (c + 1) * A, :] = jnp.dot(
             g_ref[c * A : (c + 1) * A, :], sel, preferred_element_type=F32
@@ -75,8 +78,9 @@
         high = jnp.dot(ref[...], sel[M:], preferred_element_type=F32)
         tail[117 + i : 118 + i, :] = low[0:1] + high[1:2]
     val = tail[...].astype(BF16)
-    plus_ref[HR + 2 * GC : BR + 2 * GC, :] = val
-    minus_ref[HR - HB : HB, :] = val
+    plus_ref[HR:BR, :] = val
+    minus_ref[HR:BR, :] = val
+    high_ref[HR - HB : HB, :] = val
     cbuf[...] = jnp.zeros_like(cbuf)
     for dp in range(4):
         for dt in range(4):
@@ -93,13 +97,13 @@
             if dp == 0:
                 own_ref[dt * GC : (dt + 1) * GC, :] = val
             elif dp == 1:
-                plus_ref[BR + (2 + dt) * GC : BR + (3 + dt) * GC, :] = val
+                plus_ref[BR + dt * GC : BR + (1 + dt) * GC, :] = val
             elif dp == 3:
-                minus_ref[BR + (2 + dt) * GC : BR + (3 + dt) * GC, :] = val
+                minus_ref[BR + dt * GC : BR + (1 + dt) * GC, :] = val
             elif dt < 2:
-                plus_ref[HB + dt * GC : HB + (dt + 1) * GC, :] = val
+                low_ref[HB + dt * GC : HB + (dt + 1) * GC, :] = val
             else:
-                minus_ref[HB + (dt - 2) * GC : HB + (dt - 1) * GC, :] = val
+                high_ref[HB + (dt - 2) * GC : HB + (dt - 1) * GC, :] = val
 
 
 def pack(k, idx, h, g, v, r):
@@ -108,10 +112,12 @@
         out_shape=(
             jax.ShapeDtypeStruct((PR, M), BF16),
             jax.ShapeDtypeStruct((PR, M), BF16),
+            jax.ShapeDtypeStruct((FR, M), BF16),
+            jax.ShapeDtypeStruct((FR, M), BF16),
             jax.ShapeDtypeStruct((4 * GC, M), BF16),
         ),
         in_specs=[SMEM] + [HBM] * 5,
-        out_specs=(VM,) * 3,
+        out_specs=(VM,) * 5,
         scratch_shapes=[
             pltpu.VMEM((C * A, M), F32),
             pltpu.VMEM((128, M), F32),
@@ -128,21 +134,17 @@
     )(k, idx, h, g, v, r)
 
 
-def block_from_plus(i, cols):
-    return ([(i, 0, HB), (i, HB + 2 * GC, HB)], cols)
-
-
-def block_from_minus(i, cols):
-    return ([(i, HB + 2 * GC, HB), (i, 0, HB)], cols)
+def block(i, cols):
+    return ([(i, 0, HB), (i, HB, HB)], cols)
 
 
 def after(i, lo):
     return [(i, lo + e * GC) for e in range(4)]
 
 
-BLOCK0 = block_from_plus(0, after(1, 0))
-BLOCK1 = block_from_plus(2, after(2, BR + 2 * GC))
-BLOCK2 = block_from_minus(0, after(0, BR + 2 * GC))
+BLOCK0 = block(0, after(1, 0))
+BLOCK1 = block(2, after(2, BR))
+BLOCK2 = block(0, after(0, BR))
 BLOCK3 = (
     [(1, 0, HB), (2, 0, HB)],
     [(1, HB), (1, HB + GC), (2, HB), (2, HB + GC)],
@@ -278,10 +280,10 @@
     )(*arrs, *accs)
 
 
-def place(block, e, shift):
-    hs, rows = [], [(i, lo + r) for i, lo, n in block[0] for r in range(0, n, K)]
+def place(blk, e, shift):
+    hs, rows = [], [(i, lo + r) for i, lo, n in blk[0] for r in range(0, n, K)]
     rows = [(i + shift, lo) for i, lo in rows]
-    i, lo = block[1][e]
+    i, lo = blk[1][e]
     return rows[:C], rows[C], (i + shift, lo)
 
 
@@ -478,7 +480,7 @@
     zbit = lambda v, bit: v + lax.ppermute(v, "row", [(i, i ^ bit) for i in range(NZ)])
     bar = lax.optimization_barrier
 
-    plus, minus, own = pack(
+    plus, minus, low, high, own = pack(
         panel,
         point_index.reshape(1, M),
         layer_input_jets.reshape(HR, POOL),
@@ -488,30 +490,24 @@
     )
     dsel = lax.dynamic_index_in_dim(damping[:, 0, :], k // NZ, 0, keepdims=True)
     dsel = jnp.broadcast_to(jnp.where(k % NZ == q, dsel, 0.0), (8, K))
-    parts = [dsel]
-    for bits in (1, 2, 3):
-        parts.append(lax.ppermute(dsel, "row", [(i, i ^ bits) for i in range(NZ)]))
-    dsel = parts[0] + parts[1] + parts[2] + parts[3]
     accs = chunk([place(BLOCK0, 0, 0)], (plus, own), (), "chunk_own")
-    ap, am, accs, dsel = bar((one(plus, 1), one(minus, -1), accs, dsel))
+    ap, am, rp, rm = one(plus, 1), one(minus, -1), one(low, 2), one(high, 2)
+    ap, am, rp, rm, accs, dsel = bar((ap, am, rp, rm, accs, zbit(zbit(dsel, 1), 2)))
     m1 = assemble(BLOCK0, BLOCK1, plus, own, ap)
-    relay = HB + 2 * GC
-    rp, rm = one(ap[:relay], 1), one(am[:relay], -1)
-    m1p, m1m = two(m1[0], 1), two(m1[1], -1)
-    accs = chunk([place(BLOCK1, 0, -2), place(BLOCK2, 0, 1)], (ap, am), accs, "chunk_line1")
-    rp, rm, accs, dsel = bar((rp, rm, accs, zbit(dsel, 4)))
     m2 = assemble(BLOCK2, BLOCK3, am, rp, rm)
-    m2p, m2m = two(m2[0], 1), two(m2[1], -1)
+    m1p, m1m, m2p, m2m = two(m1[0], 1), two(m1[1], -1), two(m2[0], 1), two(m2[1], -1)
+    line = [place(BLOCK1, 0, -2), place(BLOCK2, 0, 1), place(BLOCK3, 0, 1)]
+    accs = chunk(line, (ap, am, rp, rm), accs, "chunk_line")
+    m1p, m1m, accs, dsel = bar((m1p, m1m, accs, zbit(dsel, 4)))
     n1 = BR + GC
     r1p, r1m = two(m1p[:n1], 1), two(m1m[:n1], -1)
     e1 = 2 * BR + GC
-    blocks = received(0, e1) + received(1, e1) + [place(BLOCK3, 0, 1)]
-    accs = chunk(blocks, (m1p, m1m, rp, rm), accs, "chunk_line2")
-    r1p, r1m, m2p, m2m, accs = bar((r1p, r1m, m2p, m2m, accs))
+    near = received(0, e1) + received(1, e1)
+    accs = chunk(near, (m1p, m1m), accs, "chunk_near1")
+    m2p, m2m, accs = bar((m2p, m2m, accs))
     r2p, r2m = two(m2p[:n1], 1), two(m2m[:n1], -1)
-    blocks = [received(0, BR)[0], received(1, BR)[0]] + received(2, e1) + received(3, e1)
-    accs = chunk(blocks, (r1p, r1m, m2p, m2m), accs, "chunk_far1")
     far = [received(0, BR)[0], received(1, BR)[0]]
+    accs = chunk(far + received(2, e1) + received(3, e1), (r1p, r1m, m2p, m2m), accs, "chunk_far1")
     accs = chunk(far, (r2p, r2m), accs, "chunk_far2")
     gown, gsib, p, po, ps, dk = accs
 

time: 91.4 us -> 90.7 us (level); the launches traced: 90 us -> 90.5 us
  starting transfers between devices: 37.4 us -> 38.8 us
  waiting for transfers between devices: 7.48 us -> 6.38 us
    ppermute x2 -> x4, starting transfers between devices: 9.39 us -> 14.5 us  [body(): lax.ppermute(v, 'row', [(i, i ^ bit) for i in range(NZ)])]
    ppermute x3 -> x0, starting transfers between devices: 4.85 us -> none  [body(): parts.append(lax.ppermute(dsel, 'row', [(i, i ^ bits) for i in range(NZ)]))]
    ppermute x8, waiting for transfers between devices: 2.14 us -> 0.02 us  [body(): two = lambda v, d: lax.ppermute(v, AXES, hops(1, d))]
    ppermute x4, waiting for transfers between devices: 0.01 us -> 1.7 us  [body(): one = lambda v, d: lax.ppermute(v, AXES, hops(0, d))]
    ppermute x3 -> x0, waiting for transfers between devices: 1.62 us -> none  [body(): parts.append(lax.ppermute(dsel, 'row', [(i, i ^ bits) for i in range(NZ)]))]
    ppermute x4, starting transfers between devices: 4.55 us -> 5.63 us  [body(): one = lambda v, d: lax.ppermute(v, AXES, hops(0, d))]
    ppermute x2 -> x4, waiting for transfers between devices: 1.97 us -> 3.04 us  [body(): lax.ppermute(v, 'row', [(i, i ^ bit) for i in range(NZ)])]
  transfers between devices with their start and end apart: 24 -> 23, of which waited for: 6 -> 5; matrix products, arithmetic and copies ran while one was open for 1% -> 0% of each run, Pallas kernels for 36% -> 39%
where the time goes in v7:
time: 90.7 us; the launch traced here: 90.5 us
  Pallas kernels  40.3 us (44%)
  starting transfers between devices  38.8 us (43%)
  waiting for transfers between devices  6.38 us (7%)
  local copies, waits for them, and re-layouts  1.94 us (2%)
  between operations  1.54 us (2%)
  other arithmetic  1.46 us (2%)
    pallas_call x5, Pallas kernels, chunk(): pl.pallas_call(lambda *r: chunk_kernel(blocks, len(arrs), len(accs), *r),...  22.7 us
    ppermute x4, starting transfers between devices, body(): lax.ppermute(v, 'row', [(i, i ^ bit) for i in range(NZ)])  14.5 us
    ppermute x8, starting transfers between devices, body(): two = lambda v, d: lax.ppermute(v, AXES, hops(1, d))  13.6 us
    pallas_call x1, Pallas kernels, cholesky(): pl.pallas_call(chol_kernel, out_shape=(jax.ShapeDtypeStruct((K, K), F32),...  6.21 us
    pallas_call x2, Pallas kernels, final(): pl.pallas_call(lambda *r: final_kernel(start, *r), grid=(count,), out_sha...  5.97 us
    ppermute x4, starting transfers between devices, body(): one = lambda v, d: lax.ppermute(v, AXES, hops(0, d))  5.63 us
    ppermute x3, starting transfers between devices, body(): lax.ppermute(parts[0], 'row', [(i, i ^ bits) for i in range(NZ)])  4.42 us
    pallas_call x1, Pallas kernels, pack(): pl.pallas_call(pack_kernel, out_shape=(jax.ShapeDtypeStruct((PR, M), BF16...  3.23 us
  transfers between devices with their start and end apart: 23, of which 5 were waited for; matrix products, arithmetic and copies ran while one was open for 0% of the time, Pallas kernels for 39%

profile of v7, /device:TPU:2, one launch (start us, length us, event | category | flops | bytes accessed | tf_op | source)
XLA Modules:
  0.0 90.5 jit_solution(12799281627354427050)
XLA Ops:
  1.3 0.7 fusion
  2.0 1.9 %collective-permute-start.4 = (f32[8,128]{1,0:T(8,128)S(1)}, f32[8,128]{1,0:T(8,128)S(1)}, u32[]{:S(2)}, u32[]{:S(2)}) collective-permute-start(f32[8,128]{1,0:T(8,128)S(1)} %broadcast_in_dim.31), channel_id=1, source_target_pairs={{0,1},{1,0},{2,3},{3,2},{4,5},{5,4},{6,7},{7,6},{8,9},{9,8},{10,11... | collective-permute-start | bytes 12296 | tf_op jit(solution)/shard_map/ppermute | solution.py:480
  3.9 3.2 %pack.1 = (bf16[1536,128]{1,0:T(8,128)(2,1)}, bf16[1536,128]{1,0:T(8,128)(2,1)}, bf16[768,128]{1,0:T(8,128)(2,1)}, bf16[768,128]{1,0:T(8,128)(2,1)}, bf16[256,128]{1,0:T(8,128)(2,1)}) custom-call(s32[1]{0:T(128)} %copy.16.k_ref.r_0_, s32[1,128]{1,0:T(1,128)} %bitcast.25, bf16[1152,256]{1,0:T(8,128)(2,1)} %bitcast.23, bf16[864,256]{1,0:T(8,128)(2,1)} %bitcast.24, ...), custom_call_target="tpu_custom_call" | custom-call | tf_op jit(solution)/shard_map/pack/pallas_call | solution.py:110
  7.1 1.6 %collective-permute-start = (bf16[1536,128]{1,0:T(8,128)(2,1)}, bf16[1536,128]{1,0:T(8,128)(2,1)S(1)}, u32[]{:S(2)}, u32[]{:S(2)}) collective-permute-start(bf16[1536,128]{1,0:T(8,128)(2,1)} %get-tuple-element.86.r_0_), channel_id=1, source_target_pairs={{0,64},{1,65},{2,66},{3,67},{4,68},{5,69},{6,70},{7,71},{8,24},{9,... | collective-permute-start | bytes 1179656 | tf_op jit(solution)/shard_map/ppermute | solution.py:477
  9.2 2.1 %collective-permute-start.2 = (bf16[768,128]{1,0:T(8,128)(2,1)}, bf16[768,128]{1,0:T(8,128)(2,1)S(1)}, u32[]{:S(2)}, u32[]{:S(2)}) collective-permute-start(bf16[768,128]{1,0:T(8,128)(2,1)} %get-tuple-element.88), channel_id=1, source_target_pairs={{0,128},{1,129},{2,130},{3,131},{4,132},{5,133},{6,134},{7,135},{8... | collective-permute-start | bytes 589832 | tf_op jit(solution)/shard_map/ppermute | solution.py:477
  11.4 1.4 %collective-permute-start.3 = (bf16[768,128]{1,0:T(8,128)(2,1)}, bf16[768,128]{1,0:T(8,128)(2,1)S(1)}, u32[]{:S(2)}, u32[]{:S(2)}) collective-permute-start(bf16[768,128]{1,0:T(8,128)(2,1)} %get-tuple-element.89), channel_id=1, source_target_pairs={{0,128},{1,129},{2,130},{3,131},{4,132},{5,133},{6,134},{7,135},{8... | collective-permute-start | bytes 589832 | tf_op jit(solution)/shard_map/ppermute | solution.py:477
  12.8 3.3 %collective-permute-start.5 = (f32[8,128]{1,0:T(8,128)S(1)}, f32[8,128]{1,0:T(8,128)S(1)}, u32[]{:S(2)}, u32[]{:S(2)}) collective-permute-start(f32[8,128]{1,0:T(8,128)S(1)} %broadcast_add_fusion), channel_id=1, source_target_pairs={{0,2},{1,3},{2,0},{3,1},{4,6},{5,7},{6,4},{7,5},{8,10},{9,11},{10,... | collective-permute-start | bytes 12296 | tf_op jit(solution)/shard_map/ppermute | solution.py:480
  16.1 1.0 %copy-done = bf16[1536,128]{1,0:T(8,128)(2,1)S(1)} copy-done((bf16[1536,128]{1,0:T(8,128)(2,1)S(1)}, bf16[1536,128]{1,0:T(8,128)(2,1)}, u32[]{:S(2)}) %copy-start) | copy-done | bytes 393240
  17.1 0.8 copy-done.1
  17.9 1.9 %chunk_own.1 = (f32[1536,384]{1,0:T(8,128)S(1)}, f32[1536,384]{1,0:T(8,128)S(1)}, f32[1536,256]{1,0:T(8,128)S(1)}, f32[384,128]{1,0:T(8,128)S(1)}, f32[384,128]{1,0:T(8,128)S(1)}, /*index=5*/f32[144,128]{1,0:T(8,128)S(1)}) custom-call(bf16[1536,128]{1,0:T(8,128)(2,1)S(1)} %copy-done, bf16[256,128]{1,0:T(8,128)(2,1)S(1)} %copy-done.1), custom_call_target="tpu_custom_call" | custom-call | flops 1012531200 | bytes 4000000 | tf_op jit(solution)/shard_map/chunk_own/pallas_call | solution.py:269
  19.8 1.7 %collective-permute-done.3.r_2_.r_3_ = bf16[768,128]{1,0:T(8,128)(2,1)S(1)} collective-permute-done((bf16[768,128]{1,0:T(8,128)(2,1)}, bf16[768,128]{1,0:T(8,128)(2,1)S(1)}, u32[]{:S(2)}, u32[]{:S(2)}) %collective-permute-start.3) | collective-permute-done | bytes 196640 | tf_op jit(solution)/shard_map/ppermute | solution.py:477
  21.7 1.7 %collective-permute-start.8 = (bf16[2752,128]{1,0:T(8,128)(2,1)S(1)}, bf16[2752,128]{1,0:T(8,128)(2,1)S(1)}, u32[]{:S(2)}, u32[]{:S(2)}) collective-permute-start(bf16[2752,128]{1,0:T(8,128)(2,1)S(1)} %get-tuple-element.103), channel_id=1, source_target_pairs={{0,16},{1,17},{2,18},{3,19},{4,20},{5,21},{6,22},{7,23},{8,72},{9,... | collective-permute-start | bytes 2113544 | tf_op jit(solution)/shard_map/ppermute | solution.py:478
  23.3 1.7 %collective-permute-start.9 = (bf16[2752,128]{1,0:T(8,128)(2,1)S(1)}, bf16[2752,128]{1,0:T(8,128)(2,1)S(1)}, u32[]{:S(2)}, u32[]{:S(2)}) collective-permute-start(bf16[2752,128]{1,0:T(8,128)(2,1)S(1)} %get-tuple-element.104), channel_id=1, source_target_pairs={{0,48},{1,49},{2,50},{3,51},{4,52},{5,53},{6,54},{7,55},{8,200},{9... | collective-permute-start | bytes 2113544 | tf_op jit(solution)/shard_map/ppermute | solution.py:478
  25.6 2.9 %collective-permute-start.7 = (bf16[2752,128]{1,0:T(8,128)(2,1)S(1)}, bf16[2752,128]{1,0:T(8,128)(2,1)S(1)}, u32[]{:S(2)}, u32[]{:S(2)}) collective-permute-start(bf16[2752,128]{1,0:T(8,128)(2,1)S(1)} %get-tuple-element.101), channel_id=1, source_target_pairs={{0,48},{1,49},{2,50},{3,51},{4,52},{5,53},{6,54},{7,55},{8,200},{9... | collective-permute-start | bytes 2113544 | tf_op jit(solution)/shard_map/ppermute | solution.py:478
  28.5 6.3 %collective-permute-start.10 = (f32[8,128]{1,0:T(8,128)S(1)}, f32[8,128]{1,0:T(8,128)S(1)}, u32[]{:S(2)}, u32[]{:S(2)}) collective-permute-start(f32[8,128]{1,0:T(8,128)S(1)} %fusion.1), channel_id=1, source_target_pairs={{0,4},{1,5},{2,6},{3,7},{4,0},{5,1},{6,2},{7,3},{8,12},{9,13},{10,... | collective-permute-start | bytes 12296 | tf_op jit(solution)/shard_map/ppermute | solution.py:480
  34.7 4.6 %chunk_line.1 = (f32[1536,384]{1,0:T(8,128)S(1)}, f32[1536,384]{1,0:T(8,128)S(1)}, f32[1536,256]{1,0:T(8,128)S(1)}, f32[384,128]{1,0:T(8,128)S(1)}, f32[384,128]{1,0:T(8,128)S(1)}, /*index=5*/f32[144,128]{1,0:T(8,128)S(1)}) custom-call(bf16[1536,128]{1,0:T(8,128)(2,1)S(1)} %collective-permute-done.r_2_.r_0_, ...), custom_call_target="tpu_custom_call" | custom-call | flops 3037593600 | bytes 12000000 | tf_op jit(solution)/shard_map/chunk_line/pallas_call | solution.py:269
  39.7 3.3 %collective-permute-start.14 = (bf16[1344,128]{1,0:T(8,128)(2,1)S(1)}, bf16[1344,128]{1,0:T(8,128)(2,1)S(1)}, u32[]{:S(2)}, u32[]{:S(2)}) collective-permute-start(bf16[1344,128]{1,0:T(8,128)(2,1)S(1)} %slice.15), channel_id=1, source_target_pairs={{0,48},{1,49},{2,50},{3,51},{4,52},{5,53},{6,54},{7,55},{8,200},{9... | collective-permute-start | bytes 1032200 | tf_op jit(solution)/shard_map/ppermute | solution.py:478
  43.0 5.5 %chunk_near1.1 = (f32[1536,384]{1,0:T(8,128)S(1)}, f32[1536,384]{1,0:T(8,128)S(1)}, f32[1536,256]{1,0:T(8,128)S(1)}, f32[384,128]{1,0:T(8,128)S(1)}, f32[384,128]{1,0:T(8,128)S(1)}, /*index=5*/f32[144,128]{1,0:T(8,128)S(1)}) custom-call(bf16[2752,128]{1,0:T(8,128)(2,1)S(1)} %collective-permute-done.8.r_0_, ...), custom_call_target="tpu_custom_call" | custom-call | flops 4050124800 | bytes 16000000 | tf_op jit(solution)/shard_map/chunk_near1/pallas_call | solution.py:269
  48.7 3.3 %collective-permute-start.12 = (bf16[1344,128]{1,0:T(8,128)(2,1)S(1)}, bf16[1344,128]{1,0:T(8,128)(2,1)S(1)}, u32[]{:S(2)}, u32[]{:S(2)}) collective-permute-start(bf16[1344,128]{1,0:T(8,128)(2,1)S(1)} %slice.13), channel_id=1, source_target_pairs={{0,48},{1,49},{2,50},{3,51},{4,52},{5,53},{6,54},{7,55},{8,200},{9... | collective-permute-start | bytes 1032200 | tf_op jit(solution)/shard_map/ppermute | solution.py:478
  52.0 7.9 %chunk_far1.1 = (f32[1536,384]{1,0:T(8,128)S(1)}, f32[1536,384]{1,0:T(8,128)S(1)}, f32[1536,256]{1,0:T(8,128)S(1)}, f32[384,128]{1,0:T(8,128)S(1)}, f32[384,128]{1,0:T(8,128)S(1)}, /*index=5*/f32[144,128]{1,0:T(8,128)S(1)}) custom-call(bf16[1344,128]{1,0:T(8,128)(2,1)S(1)} %collective-permute-done.13.r_0_, ...), custom_call_target="tpu_custom_call" | custom-call | flops 6075187200 | bytes 24000000 | tf_op jit(solution)/shard_map/chunk_far1/pallas_call | solution.py:269
  59.9 2.8 %chunk_far2.1 = (f32[1536,384]{1,0:T(8,128)S(1)}, f32[1536,384]{1,0:T(8,128)S(1)}, f32[1536,256]{1,0:T(8,128)S(1)}, f32[384,128]{1,0:T(8,128)S(1)}, f32[384,128]{1,0:T(8,128)S(1)}, /*index=5*/f32[144,128]{1,0:T(8,128)S(1)}) custom-call(bf16[1344,128]{1,0:T(8,128)(2,1)S(1)} %collective-permute-done.11.r_0_, ...), custom_call_target="tpu_custom_call" | custom-call | flops 2025062400 | bytes 8000000 | tf_op jit(solution)/shard_map/chunk_far2/pallas_call | solution.py:269
  62.9 1.3 %collective-permute-done.15.b_ref = f32[144,128]{1,0:T(8,128)S(1)} collective-permute-done((f32[144,128]{1,0:T(8,128)S(1)}, f32[144,128]{1,0:T(8,128)S(1)}, u32[]{:S(2)}, u32[]{:S(2)}) %collective-permute-start.15) | collective-permute-done | bytes 73760 | tf_op jit(solution)/shard_map/ppermute | solution.py:479
  64.8 6.2 %panel_factor.1 = (f32[128,128]{1,0:T(8,128)S(1)}, f32[128,128]{1,0:T(8,128)S(1)}, f32[16,128]{1,0:T(8,128)S(1)}) custom-call(f32[144,128]{1,0:T(8,128)S(1)} %get-tuple-element.147.a_ref, f32[144,128]{1,0:T(8,128)S(1)} %collective-permute-done.15.b_ref, f32[8,128]{1,0:T(8,128)S(1)} %add.34.d_ref), custom_call_target="tpu_custom_call" | custom-call | tf_op jit(solution)/shard_map/panel_factor/pallas_call | solution.py:343
  71.2 1.9 %panel_solve.1 = (f32[12,128]{1,0:T(8,128)S(1)}, f32[1536,128]{1,0:T(8,128)S(1)}, bf16[1536,384]{1,0:T(8,128)(2,1)S(1)}, bf16[384,384]{1,0:T(8,128)(2,1)S(1)}) custom-call(s32[1]{0:T(128)} %copy.16.k_ref.r_0_, f32[1536,256]{1,0:T(8,128)S(1)} %get-tuple-element.151.p_ref, f32[1536,256]{1,0:T(8,128)S(1)} %collective-permute-done.16.pr_ref, ...), custom_call_target="tpu_custom_call" | custom-call | tf_op jit(solution)/shard_map/panel_solve/pallas_call | solution.py:397
  73.2 1.0 %collective-permute-start.19 = (f32[12,8,128]{2,1,0:T(8,128)S(1)}, f32[12,8,128]{2,1,0:T(8,128)S(1)}, u32[]{:S(2)}, u32[]{:S(2)}) collective-permute-start(f32[12,8,128]{2,1,0:T(8,128)S(1)} %broadcast_select_fusion), channel_id=1, source_target_pairs={{0,1},{1,0},{2,3},{3,2},{4,5},{5,4},{6,7},{7,6},{8,9},{9,8},{10,11... | collective-permute-start | bytes 147464 | tf_op jit(solution)/shard_map/ppermute | solution.py:522
  74.2 1.5 %collective-permute-start.20 = (f32[12,8,128]{2,1,0:T(8,128)S(1)}, f32[12,8,128]{2,1,0:T(8,128)S(1)}, u32[]{:S(2)}, u32[]{:S(2)}) collective-permute-start(f32[12,8,128]{2,1,0:T(8,128)S(1)} %broadcast_select_fusion), channel_id=1, source_target_pairs={{0,2},{1,3},{2,0},{3,1},{4,6},{5,7},{6,4},{7,5},{8,10},{9,11},{10,... | collective-permute-start | bytes 147464 | tf_op jit(solution)/shard_map/ppermute | solution.py:522
  75.7 1.9 %collective-permute-start.21 = (f32[12,8,128]{2,1,0:T(8,128)S(1)}, f32[12,8,128]{2,1,0:T(8,128)S(1)}, u32[]{:S(2)}, u32[]{:S(2)}) collective-permute-start(f32[12,8,128]{2,1,0:T(8,128)S(1)} %broadcast_select_fusion), channel_id=1, source_target_pairs={{0,3},{1,2},{2,1},{3,0},{4,7},{5,6},{6,5},{7,4},{8,11},{9,10},{10,... | collective-permute-start | bytes 147464 | tf_op jit(solution)/shard_map/ppermute | solution.py:522
  77.6 3.9 %trailing_update.2.r_8_ = f32[4608,128]{1,0:T(8,128)} custom-call(s32[1]{0:T(128)} %copy.16.k_ref.r_0_, f32[1536,384]{1,0:T(8,128)S(1)} %get-tuple-element.146.r_1_, f32[1536,384]{1,0:T(8,128)S(1)} %collective-permute-done.18.r_2_, bf16[1536,384]{1,0:T(8,128)(2,1)S(1)} %get-tuple-element.163.r_3_, bf16[384,384]{1,0:T(8,128)(2,1)S(1)} %get-tuple-element.164.r_4_, ...), custom_call_target="tpu_custom_call" | custom-call | flops 1 | bytes 6000000 | tf_op jit(solution)/shard_map/trailing_update/pallas_call | solution.py:441
  81.8 3.0 %collective-permute-start.22 = (f32[12,8,128]{2,1,0:T(8,128)S(1)}, f32[12,8,128]{2,1,0:T(8,128)S(1)}, u32[]{:S(2)}, u32[]{:S(2)}) collective-permute-start(f32[12,8,128]{2,1,0:T(8,128)S(1)} %add_add_fusion), channel_id=1, source_target_pairs={{0,4},{1,5},{2,6},{3,7},{4,0},{5,1},{6,2},{7,3},{8,12},{9,13},{10,... | collective-permute-start | bytes 147464 | tf_op jit(solution)/shard_map/ppermute | solution.py:480
  84.8 2.1 %trailing_update.3 = f32[4608,128]{1,0:T(8,128)} custom-call(s32[1]{0:T(128)} %copy.16.k_ref.r_0_, f32[1536,384]{1,0:T(8,128)S(1)} %get-tuple-element.146.r_1_, f32[1536,384]{1,0:T(8,128)S(1)} %collective-permute-done.18.r_2_, bf16[1536,384]{1,0:T(8,128)(2,1)S(1)} %get-tuple-element.163.r_3_, ...), custom_call_target="tpu_custom_call", output_to_operand_aliasing={{}: (8, {})} | custom-call | flops 1 | bytes 6000000 | tf_op jit(solution)/shard_map/trailing_update/pallas_call | solution.py:441
  86.8 3.0 %collective-permute-done.22 = f32[12,8,128]{2,1,0:T(8,128)S(1)} collective-permute-done((f32[12,8,128]{2,1,0:T(8,128)S(1)}, f32[12,8,128]{2,1,0:T(8,128)S(1)}, u32[]{:S(2)}, u32[]{:S(2)}) %collective-permute-start.22) | collective-permute-done | bytes 49184 | tf_op jit(solution)/shard_map/ppermute | solution.py:480
  89.9 0.6 add_bitcast_fusion
  (46 shorter events, 3.0 us)
Async XLA Ops:
  2.0 10.8 %collective-permute-start.4 = (f32[8,128]{1,0:T(8,128)S(1)}, f32[8,128]{1,0:T(8,128)S(1)}, u32[]{:S(2)}, u32[]{:S(2)}) collective-permute-start(f32[8,128]{1,0:T(8,128)S(1)} %broadcast_in_dim.31), channel_id=1, source_target_pairs={{0,1},{1,0},{2,3},{3,2},{4,5},{5,4},{6,7},{7,6},{8,9},{9,8},{10,11... | collective-permute-start | bytes 12296 | tf_op jit(solution)/shard_map/ppermute | solution.py:480
  7.1 14.4 %collective-permute-start = (bf16[1536,128]{1,0:T(8,128)(2,1)}, bf16[1536,128]{1,0:T(8,128)(2,1)S(1)}, u32[]{:S(2)}, u32[]{:S(2)}) collective-permute-start(bf16[1536,128]{1,0:T(8,128)(2,1)} %get-tuple-element.86.r_0_), channel_id=1, source_target_pairs={{0,64},{1,65},{2,66},{3,67},{4,68},{5,69},{6,70},{7,71},{8,24},{9,... | collective-permute-start | bytes 1179656 | tf_op jit(solution)/shard_map/ppermute | solution.py:477
  8.7 12.8 %collective-permute-start.1 = (bf16[1536,128]{1,0:T(8,128)(2,1)}, bf16[1536,128]{1,0:T(8,128)(2,1)S(1)}, u32[]{:S(2)}, u32[]{:S(2)}) collective-permute-start(bf16[1536,128]{1,0:T(8,128)(2,1)} %get-tuple-element.87), channel_id=1, source_target_pairs={{0,192},{1,193},{2,194},{3,195},{4,196},{5,197},{6,198},{7,199},{8... | collective-permute-start | bytes 1179656 | tf_op jit(solution)/shard_map/ppermute | solution.py:477
  9.2 10.6 %collective-permute-start.2 = (bf16[768,128]{1,0:T(8,128)(2,1)}, bf16[768,128]{1,0:T(8,128)(2,1)S(1)}, u32[]{:S(2)}, u32[]{:S(2)}) collective-permute-start(bf16[768,128]{1,0:T(8,128)(2,1)} %get-tuple-element.88), channel_id=1, source_target_pairs={{0,128},{1,129},{2,130},{3,131},{4,132},{5,133},{6,134},{7,135},{8... | collective-permute-start | bytes 589832 | tf_op jit(solution)/shard_map/ppermute | solution.py:477
  11.4 10.2 %collective-permute-start.3 = (bf16[768,128]{1,0:T(8,128)(2,1)}, bf16[768,128]{1,0:T(8,128)(2,1)S(1)}, u32[]{:S(2)}, u32[]{:S(2)}) collective-permute-start(bf16[768,128]{1,0:T(8,128)(2,1)} %get-tuple-element.89), channel_id=1, source_target_pairs={{0,128},{1,129},{2,130},{3,131},{4,132},{5,133},{6,134},{7,135},{8... | collective-permute-start | bytes 589832 | tf_op jit(solution)/shard_map/ppermute | solution.py:477
  12.8 7.0 %collective-permute-start.5 = (f32[8,128]{1,0:T(8,128)S(1)}, f32[8,128]{1,0:T(8,128)S(1)}, u32[]{:S(2)}, u32[]{:S(2)}) collective-permute-start(f32[8,128]{1,0:T(8,128)S(1)} %broadcast_add_fusion), channel_id=1, source_target_pairs={{0,2},{1,3},{2,0},{3,1},{4,6},{5,7},{6,4},{7,5},{8,10},{9,11},{10,... | collective-permute-start | bytes 12296 | tf_op jit(solution)/shard_map/ppermute | solution.py:480
  16.1 1.0 %copy-start = (bf16[1536,128]{1,0:T(8,128)(2,1)S(1)}, bf16[1536,128]{1,0:T(8,128)(2,1)}, u32[]{:S(2)}) copy-start(bf16[1536,128]{1,0:T(8,128)(2,1)} %get-tuple-element.86.r_0_) | copy-start | bytes 1179652
  17.1 0.8 copy-start.1
  21.7 17.7 %collective-permute-start.8 = (bf16[2752,128]{1,0:T(8,128)(2,1)S(1)}, bf16[2752,128]{1,0:T(8,128)(2,1)S(1)}, u32[]{:S(2)}, u32[]{:S(2)}) collective-permute-start(bf16[2752,128]{1,0:T(8,128)(2,1)S(1)} %get-tuple-element.103), channel_id=1, source_target_pairs={{0,16},{1,17},{2,18},{3,19},{4,20},{5,21},{6,22},{7,23},{8,72},{9,... | collective-permute-start | bytes 2113544 | tf_op jit(solution)/shard_map/ppermute | solution.py:478
  23.3 16.0 %collective-permute-start.9 = (bf16[2752,128]{1,0:T(8,128)(2,1)S(1)}, bf16[2752,128]{1,0:T(8,128)(2,1)S(1)}, u32[]{:S(2)}, u32[]{:S(2)}) collective-permute-start(bf16[2752,128]{1,0:T(8,128)(2,1)S(1)} %get-tuple-element.104), channel_id=1, source_target_pairs={{0,48},{1,49},{2,50},{3,51},{4,52},{5,53},{6,54},{7,55},{8,200},{9... | collective-permute-start | bytes 2113544 | tf_op jit(solution)/shard_map/ppermute | solution.py:478
  25.1 23.3 %collective-permute-start.6 = (bf16[2752,128]{1,0:T(8,128)(2,1)S(1)}, bf16[2752,128]{1,0:T(8,128)(2,1)S(1)}, u32[]{:S(2)}, u32[]{:S(2)}) collective-permute-start(bf16[2752,128]{1,0:T(8,128)(2,1)S(1)} %get-tuple-element.100), channel_id=1, source_target_pairs={{0,16},{1,17},{2,18},{3,19},{4,20},{5,21},{6,22},{7,23},{8,72},{9,... | collective-permute-start | bytes 2113544 | tf_op jit(solution)/shard_map/ppermute | solution.py:478
  25.6 22.9 %collective-permute-start.7 = (bf16[2752,128]{1,0:T(8,128)(2,1)S(1)}, bf16[2752,128]{1,0:T(8,128)(2,1)S(1)}, u32[]{:S(2)}, u32[]{:S(2)}) collective-permute-start(bf16[2752,128]{1,0:T(8,128)(2,1)S(1)} %get-tuple-element.101), channel_id=1, source_target_pairs={{0,48},{1,49},{2,50},{3,51},{4,52},{5,53},{6,54},{7,55},{8,200},{9... | collective-permute-start | bytes 2113544 | tf_op jit(solution)/shard_map/ppermute | solution.py:478
  28.5 10.9 %collective-permute-start.10 = (f32[8,128]{1,0:T(8,128)S(1)}, f32[8,128]{1,0:T(8,128)S(1)}, u32[]{:S(2)}, u32[]{:S(2)}) collective-permute-start(f32[8,128]{1,0:T(8,128)S(1)} %fusion.1), channel_id=1, source_target_pairs={{0,4},{1,5},{2,6},{3,7},{4,0},{5,1},{6,2},{7,3},{8,12},{9,13},{10,... | collective-permute-start | bytes 12296 | tf_op jit(solution)/shard_map/ppermute | solution.py:480
  39.4 12.5 %collective-permute-start.13 = (bf16[1344,128]{1,0:T(8,128)(2,1)S(1)}, bf16[1344,128]{1,0:T(8,128)(2,1)S(1)}, u32[]{:S(2)}, u32[]{:S(2)}) collective-permute-start(bf16[1344,128]{1,0:T(8,128)(2,1)S(1)} %slice.14), channel_id=1, source_target_pairs={{0,16},{1,17},{2,18},{3,19},{4,20},{5,21},{6,22},{7,23},{8,72},{9,... | collective-permute-start | bytes 1032200 | tf_op jit(solution)/shard_map/ppermute | solution.py:478
  39.7 12.2 %collective-permute-start.14 = (bf16[1344,128]{1,0:T(8,128)(2,1)S(1)}, bf16[1344,128]{1,0:T(8,128)(2,1)S(1)}, u32[]{:S(2)}, u32[]{:S(2)}) collective-permute-start(bf16[1344,128]{1,0:T(8,128)(2,1)S(1)} %slice.15), channel_id=1, source_target_pairs={{0,48},{1,49},{2,50},{3,51},{4,52},{5,53},{6,54},{7,55},{8,200},{9... | collective-permute-start | bytes 1032200 | tf_op jit(solution)/shard_map/ppermute | solution.py:478
  48.5 11.4 %collective-permute-start.11 = (bf16[1344,128]{1,0:T(8,128)(2,1)S(1)}, bf16[1344,128]{1,0:T(8,128)(2,1)S(1)}, u32[]{:S(2)}, u32[]{:S(2)}) collective-permute-start(bf16[1344,128]{1,0:T(8,128)(2,1)S(1)} %slice.12), channel_id=1, source_target_pairs={{0,16},{1,17},{2,18},{3,19},{4,20},{5,21},{6,22},{7,23},{8,72},{9,... | collective-permute-start | bytes 1032200 | tf_op jit(solution)/shard_map/ppermute | solution.py:478
  48.7 11.2 %collective-permute-start.12 = (bf16[1344,128]{1,0:T(8,128)(2,1)S(1)}, bf16[1344,128]{1,0:T(8,128)(2,1)S(1)}, u32[]{:S(2)}, u32[]{:S(2)}) collective-permute-start(bf16[1344,128]{1,0:T(8,128)(2,1)S(1)} %slice.13), channel_id=1, source_target_pairs={{0,48},{1,49},{2,50},{3,51},{4,52},{5,53},{6,54},{7,55},{8,200},{9... | collective-permute-start | bytes 1032200 | tf_op jit(solution)/shard_map/ppermute | solution.py:478
  62.8 14.9 %copy-start.2 = (f32[12,1,128]{2,1,0:T(1,128)S(1)}, f32[12,1,128]{2,1,0:T(1,128)}, u32[]{:S(2)}) copy-start(f32[12,1,128]{2,1,0:T(1,128)} %param.12) | copy-start | bytes 18436
  62.8 1.4 %collective-permute-start.15 = (f32[144,128]{1,0:T(8,128)S(1)}, f32[144,128]{1,0:T(8,128)S(1)}, u32[]{:S(2)}, u32[]{:S(2)}) collective-permute-start(f32[144,128]{1,0:T(8,128)S(1)} %get-tuple-element.147.a_ref), channel_id=1, source_target_pairs={{0,8},{8,0},{1,9},{9,1},{2,10},{10,2},{3,11},{11,3},{4,12},{12,4},... | collective-permute-start | bytes 221192 | tf_op jit(solution)/shard_map/ppermute | solution.py:479
  64.1 7.1 %collective-permute-start.18 = (f32[1536,384]{1,0:T(8,128)S(1)}, f32[1536,384]{1,0:T(8,128)S(1)}, u32[]{:S(2)}, u32[]{:S(2)}) collective-permute-start(f32[1536,384]{1,0:T(8,128)S(1)} %get-tuple-element.153), channel_id=1, source_target_pairs={{0,8},{8,0},{1,9},{9,1},{2,10},{10,2},{3,11},{11,3},{4,12},{12,4},... | collective-permute-start | bytes 7077896 | tf_op jit(solution)/shard_map/ppermute | solution.py:479
  64.3 6.9 %collective-permute-start.16 = (f32[1536,256]{1,0:T(8,128)S(1)}, f32[1536,256]{1,0:T(8,128)S(1)}, u32[]{:S(2)}, u32[]{:S(2)}) collective-permute-start(f32[1536,256]{1,0:T(8,128)S(1)} %get-tuple-element.151.p_ref), channel_id=1, source_target_pairs={{0,8},{8,0},{1,9},{9,1},{2,10},{10,2},{3,11},{11,3},{4,12},{12,4},... | collective-permute-start | bytes 4718600 | tf_op jit(solution)/shard_map/ppermute | solution.py:479
  64.6 6.6 %collective-permute-start.17 = (f32[384,128]{1,0:T(8,128)S(1)}, f32[384,128]{1,0:T(8,128)S(1)}, u32[]{:S(2)}, u32[]{:S(2)}) collective-permute-start(f32[384,128]{1,0:T(8,128)S(1)} %get-tuple-element.152), channel_id=1, source_target_pairs={{0,8},{8,0},{1,9},{9,1},{2,10},{10,2},{3,11},{11,3},{4,12},{12,4},... | collective-permute-start | bytes 589832 | tf_op jit(solution)/shard_map/ppermute | solution.py:479
  73.2 8.3 %collective-permute-start.19 = (f32[12,8,128]{2,1,0:T(8,128)S(1)}, f32[12,8,128]{2,1,0:T(8,128)S(1)}, u32[]{:S(2)}, u32[]{:S(2)}) collective-permute-start(f32[12,8,128]{2,1,0:T(8,128)S(1)} %broadcast_select_fusion), channel_id=1, source_target_pairs={{0,1},{1,0},{2,3},{3,2},{4,5},{5,4},{6,7},{7,6},{8,9},{9,8},{10,11... | collective-permute-start | bytes 147464 | tf_op jit(solution)/shard_map/ppermute | solution.py:522
  74.2 7.3 %collective-permute-start.20 = (f32[12,8,128]{2,1,0:T(8,128)S(1)}, f32[12,8,128]{2,1,0:T(8,128)S(1)}, u32[]{:S(2)}, u32[]{:S(2)}) collective-permute-start(f32[12,8,128]{2,1,0:T(8,128)S(1)} %broadcast_select_fusion), channel_id=1, source_target_pairs={{0,2},{1,3},{2,0},{3,1},{4,6},{5,7},{6,4},{7,5},{8,10},{9,11},{10,... | collective-permute-start | bytes 147464 | tf_op jit(solution)/shard_map/ppermute | solution.py:522
  75.7 6.0 %collective-permute-start.21 = (f32[12,8,128]{2,1,0:T(8,128)S(1)}, f32[12,8,128]{2,1,0:T(8,128)S(1)}, u32[]{:S(2)}, u32[]{:S(2)}) collective-permute-start(f32[12,8,128]{2,1,0:T(8,128)S(1)} %broadcast_select_fusion), channel_id=1, source_target_pairs={{0,3},{1,2},{2,1},{3,0},{4,7},{5,6},{6,5},{7,4},{8,11},{9,10},{10,... | collective-permute-start | bytes 147464 | tf_op jit(solution)/shard_map/ppermute | solution.py:522
  81.8 8.1 %collective-permute-start.22 = (f32[12,8,128]{2,1,0:T(8,128)S(1)}, f32[12,8,128]{2,1,0:T(8,128)S(1)}, u32[]{:S(2)}, u32[]{:S(2)}) collective-permute-start(f32[12,8,128]{2,1,0:T(8,128)S(1)} %add_add_fusion), channel_id=1, source_target_pairs={{0,4},{1,5},{2,6},{3,7},{4,0},{5,1},{6,2},{7,3},{8,12},{9,13},{10,... | collective-permute-start | bytes 147464 | tf_op jit(solution)/shard_map/ppermute | solution.py:480

commit v8 on v7

--- a/solution.py
+++ b/solution.py
@@ -491,14 +491,15 @@
     dsel = lax.dynamic_index_in_dim(damping[:, 0, :], k // NZ, 0, keepdims=True)
     dsel = jnp.broadcast_to(jnp.where(k % NZ == q, dsel, 0.0), (8, K))
     accs = chunk([place(BLOCK0, 0, 0)], (plus, own), (), "chunk_own")
+    dsel = zbit(zbit(zbit(dsel, 1), 2), 4)
     ap, am, rp, rm = one(plus, 1), one(minus, -1), one(low, 2), one(high, 2)
-    ap, am, rp, rm, accs, dsel = bar((ap, am, rp, rm, accs, zbit(zbit(dsel, 1), 2)))
+    ap, am, rp, rm, accs, dsel = bar((ap, am, rp, rm, accs, dsel))
     m1 = assemble(BLOCK0, BLOCK1, plus, own, ap)
     m2 = assemble(BLOCK2, BLOCK3, am, rp, rm)
     m1p, m1m, m2p, m2m = two(m1[0], 1), two(m1[1], -1), two(m2[0], 1), two(m2[1], -1)
     line = [place(BLOCK1, 0, -2), place(BLOCK2, 0, 1), place(BLOCK3, 0, 1)]
     accs = chunk(line, (ap, am, rp, rm), accs, "chunk_line")
-    m1p, m1m, accs, dsel = bar((m1p, m1m, accs, zbit(dsel, 4)))
+    m1p, m1m, accs = bar((m1p, m1m, accs))
     n1 = BR + GC
     r1p, r1m = two(m1p[:n1], 1), two(m1m[:n1], -1)
     e1 = 2 * BR + GC
@@ -522,9 +523,9 @@
         parts.append(lax.ppermute(parts[0], "row", [(i, i ^ bits) for i in range(NZ)]))
     full = parts[0] + parts[1] + parts[2] + parts[3]
     rest = (panel, gown, gr, la, lb, lpan, chol, damping[:, 0, :])
-    fac = final(0, 8, *rest)
+    fac = final(0, 6, *rest)
     full, fac = bar((full, fac))
-    fac = final(8, 4, *rest, fac)
+    fac = final(6, 6, *rest, fac)
     full = zbit(full, 4)
     return fac.reshape(LR, 1, K, LC, 1, K), full.reshape(-1)
 

time: 90.7 us -> 91.5 us (level)
  waiting for transfers between devices: 6.38 us -> 8.3 us
  starting transfers between devices: 38.8 us -> 37.8 us
    ppermute x8, waiting for transfers between devices: 0.02 us -> 4.2 us  [body(): two = lambda v, d: lax.ppermute(v, AXES, hops(1, d))]
    ppermute x4, waiting for transfers between devices: 1.7 us -> 0.01 us  [body(): one = lambda v, d: lax.ppermute(v, AXES, hops(0, d))]
    ppermute x4, waiting for transfers between devices: 3.04 us -> 1.58 us  [body(): lax.ppermute(v, 'row', [(i, i ^ bit) for i in range(NZ)])]
    ppermute x4, starting transfers between devices: 14.5 us -> 13.5 us  [body(): lax.ppermute(v, 'row', [(i, i ^ bit) for i in range(NZ)])]
  transfers between devices with their start and end apart: 23 -> 23, of which waited for: 5 -> 7; matrix products, arithmetic and copies ran while one was open for 0% -> 0% of each run, Pallas kernels for 39% -> 39%
where the time goes in v8:
time: 91.5 us; the launch traced here: 91.3 us
  Pallas kernels  40.3 us (44%)
  starting transfers between devices  37.8 us (41%)
  waiting for transfers between devices  8.3 us (9%)
  local copies, waits for them, and re-layouts  1.94 us (2%)
  between operations  1.53 us (2%)
  other arithmetic  1.46 us (2%)
    pallas_call x5, Pallas kernels, chunk(): pl.pallas_call(lambda *r: chunk_kernel(blocks, len(arrs), len(accs), *r),...  22.7 us
    ppermute x4, starting transfers between devices, body(): lax.ppermute(v, 'row', [(i, i ^ bit) for i in range(NZ)])  13.5 us
    ppermute x8, starting transfers between devices, body(): two = lambda v, d: lax.ppermute(v, AXES, hops(1, d))  13.4 us
    pallas_call x1, Pallas kernels, cholesky(): pl.pallas_call(chol_kernel, out_shape=(jax.ShapeDtypeStruct((K, K), F32),...  6.21 us
    pallas_call x2, Pallas kernels, final(): pl.pallas_call(lambda *r: final_kernel(start, *r), grid=(count,), out_sha...  5.96 us
    ppermute x4, starting transfers between devices, body(): one = lambda v, d: lax.ppermute(v, AXES, hops(0, d))  5.63 us
    ppermute x3, starting transfers between devices, body(): lax.ppermute(parts[0], 'row', [(i, i ^ bits) for i in range(NZ)])  4.42 us
    ppermute x8, waiting for transfers between devices, body(): two = lambda v, d: lax.ppermute(v, AXES, hops(1, d))  4.2 us
  transfers between devices with their start and end apart: 23, of which 7 were waited for; matrix products, arithmetic and copies ran while one was open for 0% of the time, Pallas kernels for 39%

profile of v8, /device:TPU:2, one launch (start us, length us, event | category | flops | bytes accessed | tf_op | source)
XLA Modules:
  0.0 91.3 jit_solution(4563573667498219594)
XLA Ops:
  1.3 0.7 fusion
  2.0 1.9 %collective-permute-start.4 = (f32[8,128]{1,0:T(8,128)S(1)}, f32[8,128]{1,0:T(8,128)S(1)}, u32[]{:S(2)}, u32[]{:S(2)}) collective-permute-start(f32[8,128]{1,0:T(8,128)S(1)} %broadcast_in_dim.31), channel_id=1, source_target_pairs={{0,1},{1,0},{2,3},{3,2},{4,5},{5,4},{6,7},{7,6},{8,9},{9,8},{10,11... | collective-permute-start | bytes 12296 | tf_op jit(solution)/shard_map/ppermute | solution.py:480
  3.9 3.2 %pack.1 = (bf16[1536,128]{1,0:T(8,128)(2,1)}, bf16[1536,128]{1,0:T(8,128)(2,1)}, bf16[768,128]{1,0:T(8,128)(2,1)}, bf16[768,128]{1,0:T(8,128)(2,1)}, bf16[256,128]{1,0:T(8,128)(2,1)}) custom-call(s32[1]{0:T(128)} %copy.16.k_ref.r_0_, s32[1,128]{1,0:T(1,128)} %bitcast.25, bf16[1152,256]{1,0:T(8,128)(2,1)} %bitcast.23, bf16[864,256]{1,0:T(8,128)(2,1)} %bitcast.24, ...), custom_call_target="tpu_custom_call" | custom-call | tf_op jit(solution)/shard_map/pack/pallas_call | solution.py:110
  7.1 1.6 %collective-permute-start = (bf16[1536,128]{1,0:T(8,128)(2,1)}, bf16[1536,128]{1,0:T(8,128)(2,1)S(1)}, u32[]{:S(2)}, u32[]{:S(2)}) collective-permute-start(bf16[1536,128]{1,0:T(8,128)(2,1)} %get-tuple-element.85.r_0_), channel_id=1, source_target_pairs={{0,64},{1,65},{2,66},{3,67},{4,68},{5,69},{6,70},{7,71},{8,24},{9,... | collective-permute-start | bytes 1179656 | tf_op jit(solution)/shard_map/ppermute | solution.py:477
  9.2 3.3 %collective-permute-start.5 = (f32[8,128]{1,0:T(8,128)S(1)}, f32[8,128]{1,0:T(8,128)S(1)}, u32[]{:S(2)}, u32[]{:S(2)}) collective-permute-start(f32[8,128]{1,0:T(8,128)S(1)} %broadcast_add_fusion), channel_id=1, source_target_pairs={{0,2},{1,3},{2,0},{3,1},{4,6},{5,7},{6,4},{7,5},{8,10},{9,11},{10,... | collective-permute-start | bytes 12296 | tf_op jit(solution)/shard_map/ppermute | solution.py:480
  12.5 2.1 %collective-permute-start.2 = (bf16[768,128]{1,0:T(8,128)(2,1)}, bf16[768,128]{1,0:T(8,128)(2,1)S(1)}, u32[]{:S(2)}, u32[]{:S(2)}) collective-permute-start(bf16[768,128]{1,0:T(8,128)(2,1)} %get-tuple-element.87), channel_id=1, source_target_pairs={{0,128},{1,129},{2,130},{3,131},{4,132},{5,133},{6,134},{7,135},{8... | collective-permute-start | bytes 589832 | tf_op jit(solution)/shard_map/ppermute | solution.py:477
  14.7 1.4 %collective-permute-start.3 = (bf16[768,128]{1,0:T(8,128)(2,1)}, bf16[768,128]{1,0:T(8,128)(2,1)S(1)}, u32[]{:S(2)}, u32[]{:S(2)}) collective-permute-start(bf16[768,128]{1,0:T(8,128)(2,1)} %get-tuple-element.88), channel_id=1, source_target_pairs={{0,128},{1,129},{2,130},{3,131},{4,132},{5,133},{6,134},{7,135},{8... | collective-permute-start | bytes 589832 | tf_op jit(solution)/shard_map/ppermute | solution.py:477
  16.1 4.5 %collective-permute-start.6 = (f32[8,128]{1,0:T(8,128)S(1)}, f32[8,128]{1,0:T(8,128)S(1)}, u32[]{:S(2)}, u32[]{:S(2)}) collective-permute-start(f32[8,128]{1,0:T(8,128)S(1)} %fusion.1), channel_id=1, source_target_pairs={{0,4},{1,5},{2,6},{3,7},{4,0},{5,1},{6,2},{7,3},{8,12},{9,13},{10,... | collective-permute-start | bytes 12296 | tf_op jit(solution)/shard_map/ppermute | solution.py:480
  20.6 1.0 %copy-done = bf16[1536,128]{1,0:T(8,128)(2,1)S(1)} copy-done((bf16[1536,128]{1,0:T(8,128)(2,1)S(1)}, bf16[1536,128]{1,0:T(8,128)(2,1)}, u32[]{:S(2)}) %copy-start) | copy-done | bytes 393240
  21.5 0.8 copy-done.1
  22.4 1.9 %chunk_own.1 = (f32[1536,384]{1,0:T(8,128)S(1)}, f32[1536,384]{1,0:T(8,128)S(1)}, f32[1536,256]{1,0:T(8,128)S(1)}, f32[384,128]{1,0:T(8,128)S(1)}, f32[384,128]{1,0:T(8,128)S(1)}, /*index=5*/f32[144,128]{1,0:T(8,128)S(1)}) custom-call(bf16[1536,128]{1,0:T(8,128)(2,1)S(1)} %copy-done, bf16[256,128]{1,0:T(8,128)(2,1)S(1)} %copy-done.1), custom_call_target="tpu_custom_call" | custom-call | flops 1012531200 | bytes 4000000 | tf_op jit(solution)/shard_map/chunk_own/pallas_call | solution.py:269
  24.5 3.1 %collective-permute-start.10 = (bf16[2752,128]{1,0:T(8,128)(2,1)S(1)}, bf16[2752,128]{1,0:T(8,128)(2,1)S(1)}, u32[]{:S(2)}, u32[]{:S(2)}) collective-permute-start(bf16[2752,128]{1,0:T(8,128)(2,1)S(1)} %get-tuple-element.103), channel_id=1, source_target_pairs={{0,48},{1,49},{2,50},{3,51},{4,52},{5,53},{6,54},{7,55},{8,200},{9... | collective-permute-start | bytes 2113544 | tf_op jit(solution)/shard_map/ppermute | solution.py:478
  27.7 0.7 collective-permute-start.7
  28.4 2.7 %collective-permute-start.8 = (bf16[2752,128]{1,0:T(8,128)(2,1)S(1)}, bf16[2752,128]{1,0:T(8,128)(2,1)S(1)}, u32[]{:S(2)}, u32[]{:S(2)}) collective-permute-start(bf16[2752,128]{1,0:T(8,128)(2,1)S(1)} %get-tuple-element.100), channel_id=1, source_target_pairs={{0,48},{1,49},{2,50},{3,51},{4,52},{5,53},{6,54},{7,55},{8,200},{9... | collective-permute-start | bytes 2113544 | tf_op jit(solution)/shard_map/ppermute | solution.py:478
  31.1 4.6 %chunk_line.1 = (f32[1536,384]{1,0:T(8,128)S(1)}, f32[1536,384]{1,0:T(8,128)S(1)}, f32[1536,256]{1,0:T(8,128)S(1)}, f32[384,128]{1,0:T(8,128)S(1)}, f32[384,128]{1,0:T(8,128)S(1)}, /*index=5*/f32[144,128]{1,0:T(8,128)S(1)}) custom-call(bf16[1536,128]{1,0:T(8,128)(2,1)S(1)} %collective-permute-done.r_2_.r_0_, ...), custom_call_target="tpu_custom_call" | custom-call | flops 3037593600 | bytes 12000000 | tf_op jit(solution)/shard_map/chunk_line/pallas_call | solution.py:269
  36.2 3.7 %collective-permute-done.9.r_0_ = bf16[2752,128]{1,0:T(8,128)(2,1)S(1)} collective-permute-done((bf16[2752,128]{1,0:T(8,128)(2,1)S(1)}, bf16[2752,128]{1,0:T(8,128)(2,1)S(1)}, u32[]{:S(2)}, u32[]{:S(2)}) %collective-permute-start.9) | collective-permute-done | bytes 704544 | tf_op jit(solution)/shard_map/ppermute | solution.py:478
  40.3 3.3 %collective-permute-start.14 = (bf16[1344,128]{1,0:T(8,128)(2,1)S(1)}, bf16[1344,128]{1,0:T(8,128)(2,1)S(1)}, u32[]{:S(2)}, u32[]{:S(2)}) collective-permute-start(bf16[1344,128]{1,0:T(8,128)(2,1)S(1)} %slice.15), channel_id=1, source_target_pairs={{0,48},{1,49},{2,50},{3,51},{4,52},{5,53},{6,54},{7,55},{8,200},{9... | collective-permute-start | bytes 1032200 | tf_op jit(solution)/shard_map/ppermute | solution.py:478
  43.5 5.5 %chunk_near1.1 = (f32[1536,384]{1,0:T(8,128)S(1)}, f32[1536,384]{1,0:T(8,128)S(1)}, f32[1536,256]{1,0:T(8,128)S(1)}, f32[384,128]{1,0:T(8,128)S(1)}, f32[384,128]{1,0:T(8,128)S(1)}, /*index=5*/f32[144,128]{1,0:T(8,128)S(1)}) custom-call(bf16[2752,128]{1,0:T(8,128)(2,1)S(1)} %collective-permute-done.9.r_0_, ...), custom_call_target="tpu_custom_call" | custom-call | flops 4050124800 | bytes 16000000 | tf_op jit(solution)/shard_map/chunk_near1/pallas_call | solution.py:269
  49.2 3.3 %collective-permute-start.12 = (bf16[1344,128]{1,0:T(8,128)(2,1)S(1)}, bf16[1344,128]{1,0:T(8,128)(2,1)S(1)}, u32[]{:S(2)}, u32[]{:S(2)}) collective-permute-start(bf16[1344,128]{1,0:T(8,128)(2,1)S(1)} %slice.13), channel_id=1, source_target_pairs={{0,48},{1,49},{2,50},{3,51},{4,52},{5,53},{6,54},{7,55},{8,200},{9... | collective-permute-start | bytes 1032200 | tf_op jit(solution)/shard_map/ppermute | solution.py:478
  52.5 7.9 %chunk_far1.1 = (f32[1536,384]{1,0:T(8,128)S(1)}, f32[1536,384]{1,0:T(8,128)S(1)}, f32[1536,256]{1,0:T(8,128)S(1)}, f32[384,128]{1,0:T(8,128)S(1)}, f32[384,128]{1,0:T(8,128)S(1)}, /*index=5*/f32[144,128]{1,0:T(8,128)S(1)}) custom-call(bf16[1344,128]{1,0:T(8,128)(2,1)S(1)} %collective-permute-done.13.r_0_, ...), custom_call_target="tpu_custom_call" | custom-call | flops 6075187200 | bytes 24000000 | tf_op jit(solution)/shard_map/chunk_far1/pallas_call | solution.py:269
  60.4 2.9 %chunk_far2.1 = (f32[1536,384]{1,0:T(8,128)S(1)}, f32[1536,384]{1,0:T(8,128)S(1)}, f32[1536,256]{1,0:T(8,128)S(1)}, f32[384,128]{1,0:T(8,128)S(1)}, f32[384,128]{1,0:T(8,128)S(1)}, /*index=5*/f32[144,128]{1,0:T(8,128)S(1)}) custom-call(bf16[1344,128]{1,0:T(8,128)(2,1)S(1)} %collective-permute-done.11.r_0_, ...), custom_call_target="tpu_custom_call" | custom-call | flops 2025062400 | bytes 8000000 | tf_op jit(solution)/shard_map/chunk_far2/pallas_call | solution.py:269
  63.4 1.3 %collective-permute-done.15.b_ref = f32[144,128]{1,0:T(8,128)S(1)} collective-permute-done((f32[144,128]{1,0:T(8,128)S(1)}, f32[144,128]{1,0:T(8,128)S(1)}, u32[]{:S(2)}, u32[]{:S(2)}) %collective-permute-start.15) | collective-permute-done | bytes 73760 | tf_op jit(solution)/shard_map/ppermute | solution.py:479
  65.4 6.2 %panel_factor.1 = (f32[128,128]{1,0:T(8,128)S(1)}, f32[128,128]{1,0:T(8,128)S(1)}, f32[16,128]{1,0:T(8,128)S(1)}) custom-call(f32[144,128]{1,0:T(8,128)S(1)} %get-tuple-element.145.a_ref, f32[144,128]{1,0:T(8,128)S(1)} %collective-permute-done.15.b_ref, f32[8,128]{1,0:T(8,128)S(1)} %add.34.d_ref), custom_call_target="tpu_custom_call" | custom-call | tf_op jit(solution)/shard_map/panel_factor/pallas_call | solution.py:343
  71.7 1.9 %panel_solve.1 = (f32[12,128]{1,0:T(8,128)S(1)}, f32[1536,128]{1,0:T(8,128)S(1)}, bf16[1536,384]{1,0:T(8,128)(2,1)S(1)}, bf16[384,384]{1,0:T(8,128)(2,1)S(1)}) custom-call(s32[1]{0:T(128)} %copy.16.k_ref.r_0_, f32[1536,256]{1,0:T(8,128)S(1)} %get-tuple-element.149.p_ref, f32[1536,256]{1,0:T(8,128)S(1)} %collective-permute-done.16.pr_ref, ...), custom_call_target="tpu_custom_call" | custom-call | tf_op jit(solution)/shard_map/panel_solve/pallas_call | solution.py:397
  73.8 1.0 %collective-permute-start.19 = (f32[12,8,128]{2,1,0:T(8,128)S(1)}, f32[12,8,128]{2,1,0:T(8,128)S(1)}, u32[]{:S(2)}, u32[]{:S(2)}) collective-permute-start(f32[12,8,128]{2,1,0:T(8,128)S(1)} %broadcast_select_fusion), channel_id=1, source_target_pairs={{0,1},{1,0},{2,3},{3,2},{4,5},{5,4},{6,7},{7,6},{8,9},{9,8},{10,11... | collective-permute-start | bytes 147464 | tf_op jit(solution)/shard_map/ppermute | solution.py:523
  74.8 1.4 %collective-permute-start.20 = (f32[12,8,128]{2,1,0:T(8,128)S(1)}, f32[12,8,128]{2,1,0:T(8,128)S(1)}, u32[]{:S(2)}, u32[]{:S(2)}) collective-permute-start(f32[12,8,128]{2,1,0:T(8,128)S(1)} %broadcast_select_fusion), channel_id=1, source_target_pairs={{0,2},{1,3},{2,0},{3,1},{4,6},{5,7},{6,4},{7,5},{8,10},{9,11},{10,... | collective-permute-start | bytes 147464 | tf_op jit(solution)/shard_map/ppermute | solution.py:523
  76.2 1.9 %collective-permute-start.21 = (f32[12,8,128]{2,1,0:T(8,128)S(1)}, f32[12,8,128]{2,1,0:T(8,128)S(1)}, u32[]{:S(2)}, u32[]{:S(2)}) collective-permute-start(f32[12,8,128]{2,1,0:T(8,128)S(1)} %broadcast_select_fusion), channel_id=1, source_target_pairs={{0,3},{1,2},{2,1},{3,0},{4,7},{5,6},{6,5},{7,4},{8,11},{9,10},{10,... | collective-permute-start | bytes 147464 | tf_op jit(solution)/shard_map/ppermute | solution.py:523
  78.2 3.0 %trailing_update.2.r_8_ = f32[4608,128]{1,0:T(8,128)} custom-call(s32[1]{0:T(128)} %copy.16.k_ref.r_0_, f32[1536,384]{1,0:T(8,128)S(1)} %get-tuple-element.144.r_1_, f32[1536,384]{1,0:T(8,128)S(1)} %collective-permute-done.18.r_2_, bf16[1536,384]{1,0:T(8,128)(2,1)S(1)} %get-tuple-element.161.r_3_, bf16[384,384]{1,0:T(8,128)(2,1)S(1)} %get-tuple-element.162.r_4_, ...), custom_call_target="tpu_custom_call" | custom-call | flops 1 | bytes 6000000 | tf_op jit(solution)/shard_map/trailing_update/pallas_call | solution.py:441
  81.4 0.8 collective-permute-done.21
  82.3 3.8 %collective-permute-start.22 = (f32[12,8,128]{2,1,0:T(8,128)S(1)}, f32[12,8,128]{2,1,0:T(8,128)S(1)}, u32[]{:S(2)}, u32[]{:S(2)}) collective-permute-start(f32[12,8,128]{2,1,0:T(8,128)S(1)} %add_add_fusion), channel_id=1, source_target_pairs={{0,4},{1,5},{2,6},{3,7},{4,0},{5,1},{6,2},{7,3},{8,12},{9,13},{10,... | collective-permute-start | bytes 147464 | tf_op jit(solution)/shard_map/ppermute | solution.py:480
  86.1 3.0 %trailing_update.3 = f32[4608,128]{1,0:T(8,128)} custom-call(s32[1]{0:T(128)} %copy.16.k_ref.r_0_, f32[1536,384]{1,0:T(8,128)S(1)} %get-tuple-element.144.r_1_, f32[1536,384]{1,0:T(8,128)S(1)} %collective-permute-done.18.r_2_, bf16[1536,384]{1,0:T(8,128)(2,1)S(1)} %get-tuple-element.161.r_3_, ...), custom_call_target="tpu_custom_call", output_to_operand_aliasing={{}: (8, {})} | custom-call | flops 1 | bytes 6000000 | tf_op jit(solution)/shard_map/trailing_update/pallas_call | solution.py:441
  89.1 1.6 %collective-permute-done.22 = f32[12,8,128]{2,1,0:T(8,128)S(1)} collective-permute-done((f32[12,8,128]{2,1,0:T(8,128)S(1)}, f32[12,8,128]{2,1,0:T(8,128)S(1)}, u32[]{:S(2)}, u32[]{:S(2)}) %collective-permute-start.22) | collective-permute-done | bytes 49184 | tf_op jit(solution)/shard_map/ppermute | solution.py:480
  (46 shorter events, 3.8 us)
Async XLA Ops:
  2.0 7.3 %collective-permute-start.4 = (f32[8,128]{1,0:T(8,128)S(1)}, f32[8,128]{1,0:T(8,128)S(1)}, u32[]{:S(2)}, u32[]{:S(2)}) collective-permute-start(f32[8,128]{1,0:T(8,128)S(1)} %broadcast_in_dim.31), channel_id=1, source_target_pairs={{0,1},{1,0},{2,3},{3,2},{4,5},{5,4},{6,7},{7,6},{8,9},{9,8},{10,11... | collective-permute-start | bytes 12296 | tf_op jit(solution)/shard_map/ppermute | solution.py:480
  7.1 17.2 %collective-permute-start = (bf16[1536,128]{1,0:T(8,128)(2,1)}, bf16[1536,128]{1,0:T(8,128)(2,1)S(1)}, u32[]{:S(2)}, u32[]{:S(2)}) collective-permute-start(bf16[1536,128]{1,0:T(8,128)(2,1)} %get-tuple-element.85.r_0_), channel_id=1, source_target_pairs={{0,64},{1,65},{2,66},{3,67},{4,68},{5,69},{6,70},{7,71},{8,24},{9,... | collective-permute-start | bytes 1179656 | tf_op jit(solution)/shard_map/ppermute | solution.py:477
  8.7 15.7 %collective-permute-start.1 = (bf16[1536,128]{1,0:T(8,128)(2,1)}, bf16[1536,128]{1,0:T(8,128)(2,1)S(1)}, u32[]{:S(2)}, u32[]{:S(2)}) collective-permute-start(bf16[1536,128]{1,0:T(8,128)(2,1)} %get-tuple-element.86), channel_id=1, source_target_pairs={{0,192},{1,193},{2,194},{3,195},{4,196},{5,197},{6,198},{7,199},{8... | collective-permute-start | bytes 1179656 | tf_op jit(solution)/shard_map/ppermute | solution.py:477
  9.2 6.8 %collective-permute-start.5 = (f32[8,128]{1,0:T(8,128)S(1)}, f32[8,128]{1,0:T(8,128)S(1)}, u32[]{:S(2)}, u32[]{:S(2)}) collective-permute-start(f32[8,128]{1,0:T(8,128)S(1)} %broadcast_add_fusion), channel_id=1, source_target_pairs={{0,2},{1,3},{2,0},{3,1},{4,6},{5,7},{6,4},{7,5},{8,10},{9,11},{10,... | collective-permute-start | bytes 12296 | tf_op jit(solution)/shard_map/ppermute | solution.py:480
  12.5 11.8 %collective-permute-start.2 = (bf16[768,128]{1,0:T(8,128)(2,1)}, bf16[768,128]{1,0:T(8,128)(2,1)S(1)}, u32[]{:S(2)}, u32[]{:S(2)}) collective-permute-start(bf16[768,128]{1,0:T(8,128)(2,1)} %get-tuple-element.87), channel_id=1, source_target_pairs={{0,128},{1,129},{2,130},{3,131},{4,132},{5,133},{6,134},{7,135},{8... | collective-permute-start | bytes 589832 | tf_op jit(solution)/shard_map/ppermute | solution.py:477
  14.7 9.7 %collective-permute-start.3 = (bf16[768,128]{1,0:T(8,128)(2,1)}, bf16[768,128]{1,0:T(8,128)(2,1)S(1)}, u32[]{:S(2)}, u32[]{:S(2)}) collective-permute-start(bf16[768,128]{1,0:T(8,128)(2,1)} %get-tuple-element.88), channel_id=1, source_target_pairs={{0,128},{1,129},{2,130},{3,131},{4,132},{5,133},{6,134},{7,135},{8... | collective-permute-start | bytes 589832 | tf_op jit(solution)/shard_map/ppermute | solution.py:477
  16.1 8.2 %collective-permute-start.6 = (f32[8,128]{1,0:T(8,128)S(1)}, f32[8,128]{1,0:T(8,128)S(1)}, u32[]{:S(2)}, u32[]{:S(2)}) collective-permute-start(f32[8,128]{1,0:T(8,128)S(1)} %fusion.1), channel_id=1, source_target_pairs={{0,4},{1,5},{2,6},{3,7},{4,0},{5,1},{6,2},{7,3},{8,12},{9,13},{10,... | collective-permute-start | bytes 12296 | tf_op jit(solution)/shard_map/ppermute | solution.py:480
  20.5 1.0 %copy-start = (bf16[1536,128]{1,0:T(8,128)(2,1)S(1)}, bf16[1536,128]{1,0:T(8,128)(2,1)}, u32[]{:S(2)}) copy-start(bf16[1536,128]{1,0:T(8,128)(2,1)} %get-tuple-element.85.r_0_) | copy-start | bytes 1179652
  21.5 0.8 copy-start.1
  24.5 11.7 %collective-permute-start.10 = (bf16[2752,128]{1,0:T(8,128)(2,1)S(1)}, bf16[2752,128]{1,0:T(8,128)(2,1)S(1)}, u32[]{:S(2)}, u32[]{:S(2)}) collective-permute-start(bf16[2752,128]{1,0:T(8,128)(2,1)S(1)} %get-tuple-element.103), channel_id=1, source_target_pairs={{0,48},{1,49},{2,50},{3,51},{4,52},{5,53},{6,54},{7,55},{8,200},{9... | collective-permute-start | bytes 2113544 | tf_op jit(solution)/shard_map/ppermute | solution.py:478
  27.6 12.3 %collective-permute-start.9 = (bf16[2752,128]{1,0:T(8,128)(2,1)S(1)}, bf16[2752,128]{1,0:T(8,128)(2,1)S(1)}, u32[]{:S(2)}, u32[]{:S(2)}) collective-permute-start(bf16[2752,128]{1,0:T(8,128)(2,1)S(1)} %get-tuple-element.102), channel_id=1, source_target_pairs={{0,16},{1,17},{2,18},{3,19},{4,20},{5,21},{6,22},{7,23},{8,72},{9,... | collective-permute-start | bytes 2113544 | tf_op jit(solution)/shard_map/ppermute | solution.py:478
  27.7 21.3 %collective-permute-start.7 = (bf16[2752,128]{1,0:T(8,128)(2,1)S(1)}, bf16[2752,128]{1,0:T(8,128)(2,1)S(1)}, u32[]{:S(2)}, u32[]{:S(2)}) collective-permute-start(bf16[2752,128]{1,0:T(8,128)(2,1)S(1)} %get-tuple-element.99), channel_id=1, source_target_pairs={{0,16},{1,17},{2,18},{3,19},{4,20},{5,21},{6,22},{7,23},{8,72},{9,... | collective-permute-start | bytes 2113544 | tf_op jit(solution)/shard_map/ppermute | solution.py:478
  28.4 20.6 %collective-permute-start.8 = (bf16[2752,128]{1,0:T(8,128)(2,1)S(1)}, bf16[2752,128]{1,0:T(8,128)(2,1)S(1)}, u32[]{:S(2)}, u32[]{:S(2)}) collective-permute-start(bf16[2752,128]{1,0:T(8,128)(2,1)S(1)} %get-tuple-element.100), channel_id=1, source_target_pairs={{0,48},{1,49},{2,50},{3,51},{4,52},{5,53},{6,54},{7,55},{8,200},{9... | collective-permute-start | bytes 2113544 | tf_op jit(solution)/shard_map/ppermute | solution.py:478
  39.9 12.5 %collective-permute-start.13 = (bf16[1344,128]{1,0:T(8,128)(2,1)S(1)}, bf16[1344,128]{1,0:T(8,128)(2,1)S(1)}, u32[]{:S(2)}, u32[]{:S(2)}) collective-permute-start(bf16[1344,128]{1,0:T(8,128)(2,1)S(1)} %slice.14), channel_id=1, source_target_pairs={{0,16},{1,17},{2,18},{3,19},{4,20},{5,21},{6,22},{7,23},{8,72},{9,... | collective-permute-start | bytes 1032200 | tf_op jit(solution)/shard_map/ppermute | solution.py:478
  40.3 12.2 %collective-permute-start.14 = (bf16[1344,128]{1,0:T(8,128)(2,1)S(1)}, bf16[1344,128]{1,0:T(8,128)(2,1)S(1)}, u32[]{:S(2)}, u32[]{:S(2)}) collective-permute-start(bf16[1344,128]{1,0:T(8,128)(2,1)S(1)} %slice.15), channel_id=1, source_target_pairs={{0,48},{1,49},{2,50},{3,51},{4,52},{5,53},{6,54},{7,55},{8,200},{9... | collective-permute-start | bytes 1032200 | tf_op jit(solution)/shard_map/ppermute | solution.py:478
  49.1 11.4 %collective-permute-start.11 = (bf16[1344,128]{1,0:T(8,128)(2,1)S(1)}, bf16[1344,128]{1,0:T(8,128)(2,1)S(1)}, u32[]{:S(2)}, u32[]{:S(2)}) collective-permute-start(bf16[1344,128]{1,0:T(8,128)(2,1)S(1)} %slice.12), channel_id=1, source_target_pairs={{0,16},{1,17},{2,18},{3,19},{4,20},{5,21},{6,22},{7,23},{8,72},{9,... | collective-permute-start | bytes 1032200 | tf_op jit(solution)/shard_map/ppermute | solution.py:478
  49.2 11.2 %collective-permute-start.12 = (bf16[1344,128]{1,0:T(8,128)(2,1)S(1)}, bf16[1344,128]{1,0:T(8,128)(2,1)S(1)}, u32[]{:S(2)}, u32[]{:S(2)}) collective-permute-start(bf16[1344,128]{1,0:T(8,128)(2,1)S(1)} %slice.13), channel_id=1, source_target_pairs={{0,48},{1,49},{2,50},{3,51},{4,52},{5,53},{6,54},{7,55},{8,200},{9... | collective-permute-start | bytes 1032200 | tf_op jit(solution)/shard_map/ppermute | solution.py:478
  63.3 14.9 %copy-start.2 = (f32[12,1,128]{2,1,0:T(1,128)S(1)}, f32[12,1,128]{2,1,0:T(1,128)}, u32[]{:S(2)}) copy-start(f32[12,1,128]{2,1,0:T(1,128)} %param.12) | copy-start | bytes 18436
  63.3 1.4 %collective-permute-start.15 = (f32[144,128]{1,0:T(8,128)S(1)}, f32[144,128]{1,0:T(8,128)S(1)}, u32[]{:S(2)}, u32[]{:S(2)}) collective-permute-start(f32[144,128]{1,0:T(8,128)S(1)} %get-tuple-element.145.a_ref), channel_id=1, source_target_pairs={{0,8},{8,0},{1,9},{9,1},{2,10},{10,2},{3,11},{11,3},{4,12},{12,4},... | collective-permute-start | bytes 221192 | tf_op jit(solution)/shard_map/ppermute | solution.py:479
  64.7 7.1 %collective-permute-start.18 = (f32[1536,384]{1,0:T(8,128)S(1)}, f32[1536,384]{1,0:T(8,128)S(1)}, u32[]{:S(2)}, u32[]{:S(2)}) collective-permute-start(f32[1536,384]{1,0:T(8,128)S(1)} %get-tuple-element.151), channel_id=1, source_target_pairs={{0,8},{8,0},{1,9},{9,1},{2,10},{10,2},{3,11},{11,3},{4,12},{12,4},... | collective-permute-start | bytes 7077896 | tf_op jit(solution)/shard_map/ppermute | solution.py:479
  64.8 6.9 %collective-permute-start.16 = (f32[1536,256]{1,0:T(8,128)S(1)}, f32[1536,256]{1,0:T(8,128)S(1)}, u32[]{:S(2)}, u32[]{:S(2)}) collective-permute-start(f32[1536,256]{1,0:T(8,128)S(1)} %get-tuple-element.149.p_ref), channel_id=1, source_target_pairs={{0,8},{8,0},{1,9},{9,1},{2,10},{10,2},{3,11},{11,3},{4,12},{12,4},... | collective-permute-start | bytes 4718600 | tf_op jit(solution)/shard_map/ppermute | solution.py:479
  65.2 6.6 %collective-permute-start.17 = (f32[384,128]{1,0:T(8,128)S(1)}, f32[384,128]{1,0:T(8,128)S(1)}, u32[]{:S(2)}, u32[]{:S(2)}) collective-permute-start(f32[384,128]{1,0:T(8,128)S(1)} %get-tuple-element.150), channel_id=1, source_target_pairs={{0,8},{8,0},{1,9},{9,1},{2,10},{10,2},{3,11},{11,3},{4,12},{12,4},... | collective-permute-start | bytes 589832 | tf_op jit(solution)/shard_map/ppermute | solution.py:479
  73.8 7.4 %collective-permute-start.19 = (f32[12,8,128]{2,1,0:T(8,128)S(1)}, f32[12,8,128]{2,1,0:T(8,128)S(1)}, u32[]{:S(2)}, u32[]{:S(2)}) collective-permute-start(f32[12,8,128]{2,1,0:T(8,128)S(1)} %broadcast_select_fusion), channel_id=1, source_target_pairs={{0,1},{1,0},{2,3},{3,2},{4,5},{5,4},{6,7},{7,6},{8,9},{9,8},{10,11... | collective-permute-start | bytes 147464 | tf_op jit(solution)/shard_map/ppermute | solution.py:523
  74.8 6.6 %collective-permute-start.20 = (f32[12,8,128]{2,1,0:T(8,128)S(1)}, f32[12,8,128]{2,1,0:T(8,128)S(1)}, u32[]{:S(2)}, u32[]{:S(2)}) collective-permute-start(f32[12,8,128]{2,1,0:T(8,128)S(1)} %broadcast_select_fusion), channel_id=1, source_target_pairs={{0,2},{1,3},{2,0},{3,1},{4,6},{5,7},{6,4},{7,5},{8,10},{9,11},{10,... | collective-permute-start | bytes 147464 | tf_op jit(solution)/shard_map/ppermute | solution.py:523
  76.2 6.0 %collective-permute-start.21 = (f32[12,8,128]{2,1,0:T(8,128)S(1)}, f32[12,8,128]{2,1,0:T(8,128)S(1)}, u32[]{:S(2)}, u32[]{:S(2)}) collective-permute-start(f32[12,8,128]{2,1,0:T(8,128)S(1)} %broadcast_select_fusion), channel_id=1, source_target_pairs={{0,3},{1,2},{2,1},{3,0},{4,7},{5,6},{6,5},{7,4},{8,11},{9,10},{10,... | collective-permute-start | bytes 147464 | tf_op jit(solution)/shard_map/ppermute | solution.py:523
  82.3 8.4 %collective-permute-start.22 = (f32[12,8,128]{2,1,0:T(8,128)S(1)}, f32[12,8,128]{2,1,0:T(8,128)S(1)}, u32[]{:S(2)}, u32[]{:S(2)}) collective-permute-start(f32[12,8,128]{2,1,0:T(8,128)S(1)} %add_add_fusion), channel_id=1, source_target_pairs={{0,4},{1,5},{2,6},{3,7},{4,0},{5,1},{6,2},{7,3},{8,12},{9,13},{10,... | collective-permute-start | bytes 147464 | tf_op jit(solution)/shard_map/ppermute | solution.py:480

commit v9 on v7

--- a/solution.py
+++ b/solution.py
@@ -55,16 +55,8 @@
     pool = lax.broadcasted_iota(jnp.int32, (POOL, M), 0)
     copies[0].wait()
     sel = (pool == idx_ref[...]).astype(F32).astype(BF16)
-    for cp in copies[1:]:
+    for cp in copies[1:4]:
         cp.wait()
-    for c in range(C):
-        val = jnp.dot(h_ref[c * K : (c + 1) * K, :], sel, preferred_element_type=F32).astype(BF16)
-        plus_ref[c * K : (c + 1) * K, :] = val
-        minus_ref[c * K : (c + 1) * K, :] = val
-        if c < 5:
-            low_ref[c * K : (c + 1) * K, :] = val
-        else:
-            high_ref[c * K - HB : (c + 1) * K - HB, :] = val
     for c in range(C):
         gs[c * A : (c + 1) * A, :] = jnp.dot(
             g_ref[c * A : (c + 1) * A, :], sel, preferred_element_type=F32
@@ -104,6 +96,15 @@
                 low_ref[HB + dt * GC : HB + (dt + 1) * GC, :] = val
             else:
                 high_ref[HB + (dt - 2) * GC : HB + (dt - 1) * GC, :] = val
+    copies[4].wait()
+    for c in range(C):
+        val = jnp.dot(h_ref[c * K : (c + 1) * K, :], sel, preferred_element_type=F32).astype(BF16)
+        plus_ref[c * K : (c + 1) * K, :] = val
+        minus_ref[c * K : (c + 1) * K, :] = val
+        if c < 5:
+            low_ref[c * K : (c + 1) * K, :] = val
+        else:
+            high_ref[c * K - HB : (c + 1) * K - HB, :] = val
 
 
 def pack(k, idx, h, g, v, r):
@@ -498,7 +499,7 @@
     m1p, m1m, m2p, m2m = two(m1[0], 1), two(m1[1], -1), two(m2[0], 1), two(m2[1], -1)
     line = [place(BLOCK1, 0, -2), place(BLOCK2, 0, 1), place(BLOCK3, 0, 1)]
     accs = chunk(line, (ap, am, rp, rm), accs, "chunk_line")
-    m1p, m1m, accs, dsel = bar((m1p, m1m, accs, zbit(dsel, 4)))
+    m1p, m1m, accs, dsel = bar((m1p, m1m, accs, zbit(dsel, 6)))
     n1 = BR + GC
     r1p, r1m = two(m1p[:n1], 1), two(m1m[:n1], -1)
     e1 = 2 * BR + GC
@@ -522,10 +523,10 @@
         parts.append(lax.ppermute(parts[0], "row", [(i, i ^ bits) for i in range(NZ)]))
     full = parts[0] + parts[1] + parts[2] + parts[3]
     rest = (panel, gown, gr, la, lb, lpan, chol, damping[:, 0, :])
-    fac = final(0, 8, *rest)
+    fac = final(0, 7, *rest)
     full, fac = bar((full, fac))
-    fac = final(8, 4, *rest, fac)
-    full = zbit(full, 4)
+    fac = final(7, 5, *rest, fac)
+    full = zbit(full, 6)
     return fac.reshape(LR, 1, K, LC, 1, K), full.reshape(-1)
 
 

time: 90.7 us -> 88.1 us (0.971)
  starting transfers between devices: 38.8 us -> 36.1 us
    ppermute x4, starting transfers between devices: 14.5 us -> 11.8 us  [body(): lax.ppermute(v, 'row', [(i, i ^ bit) for i in range(NZ)])]
  transfers between devices with their start and end apart: 23 -> 23, of which waited for: 5 -> 5; matrix products, arithmetic and copies ran while one was open for 0% -> 0% of each run, Pallas kernels for 39% -> 41%
where the time goes in v9:
time: 88.1 us; the launch traced here: 87.9 us
  Pallas kernels  40.8 us (46%)
  starting transfers between devices  36.1 us (41%)
  waiting for transfers between devices  5.98 us (7%)
  local copies, waits for them, and re-layouts  1.94 us (2%)
  between operations  1.54 us (2%)
  other arithmetic  1.46 us (2%)
    pallas_call x5, Pallas kernels, chunk(): pl.pallas_call(lambda *r: chunk_kernel(blocks, len(arrs), len(accs), *r),...  22.7 us
    ppermute x8, starting transfers between devices, body(): two = lambda v, d: lax.ppermute(v, AXES, hops(1, d))  13.6 us
    ppermute x4, starting transfers between devices, body(): lax.ppermute(v, 'row', [(i, i ^ bit) for i in range(NZ)])  11.8 us
    pallas_call x2, Pallas kernels, final(): pl.pallas_call(lambda *r: final_kernel(start, *r), grid=(count,), out_sha...  6.37 us
    pallas_call x1, Pallas kernels, cholesky(): pl.pallas_call(chol_kernel, out_shape=(jax.ShapeDtypeStruct((K, K), F32),...  6.21 us
    ppermute x4, starting transfers between devices, body(): one = lambda v, d: lax.ppermute(v, AXES, hops(0, d))  5.63 us
    ppermute x3, starting transfers between devices, body(): lax.ppermute(parts[0], 'row', [(i, i ^ bits) for i in range(NZ)])  4.42 us
    pallas_call x1, Pallas kernels, pack(): pl.pallas_call(pack_kernel, out_shape=(jax.ShapeDtypeStruct((PR, M), BF16...  3.31 us
  transfers between devices with their start and end apart: 23, of which 5 were waited for; matrix products, arithmetic and copies ran while one was open for 0% of the time, Pallas kernels for 41%

profile of v9, /device:TPU:2, one launch (start us, length us, event | category | flops | bytes accessed | tf_op | source)
XLA Modules:
  0.0 87.9 jit_solution(13825208200046537172)
XLA Ops:
  1.3 0.7 fusion
  2.0 1.9 %collective-permute-start.4 = (f32[8,128]{1,0:T(8,128)S(1)}, f32[8,128]{1,0:T(8,128)S(1)}, u32[]{:S(2)}, u32[]{:S(2)}) collective-permute-start(f32[8,128]{1,0:T(8,128)S(1)} %broadcast_in_dim.31), channel_id=1, source_target_pairs={{0,1},{1,0},{2,3},{3,2},{4,5},{5,4},{6,7},{7,6},{8,9},{9,8},{10,11... | collective-permute-start | bytes 12296 | tf_op jit(solution)/shard_map/ppermute | solution.py:481
  3.9 3.3 %pack.1 = (bf16[1536,128]{1,0:T(8,128)(2,1)}, bf16[1536,128]{1,0:T(8,128)(2,1)}, bf16[768,128]{1,0:T(8,128)(2,1)}, bf16[768,128]{1,0:T(8,128)(2,1)}, bf16[256,128]{1,0:T(8,128)(2,1)}) custom-call(s32[1]{0:T(128)} %copy.16.k_ref.r_0_, s32[1,128]{1,0:T(1,128)} %bitcast.25, bf16[1152,256]{1,0:T(8,128)(2,1)} %bitcast.23, bf16[864,256]{1,0:T(8,128)(2,1)} %bitcast.24, ...), custom_call_target="tpu_custom_call" | custom-call | tf_op jit(solution)/shard_map/pack/pallas_call | solution.py:111
  7.2 1.6 %collective-permute-start = (bf16[1536,128]{1,0:T(8,128)(2,1)}, bf16[1536,128]{1,0:T(8,128)(2,1)S(1)}, u32[]{:S(2)}, u32[]{:S(2)}) collective-permute-start(bf16[1536,128]{1,0:T(8,128)(2,1)} %get-tuple-element.86.r_0_), channel_id=1, source_target_pairs={{0,64},{1,65},{2,66},{3,67},{4,68},{5,69},{6,70},{7,71},{8,24},{9,... | collective-permute-start | bytes 1179656 | tf_op jit(solution)/shard_map/ppermute | solution.py:478
  9.3 2.1 %collective-permute-start.2 = (bf16[768,128]{1,0:T(8,128)(2,1)}, bf16[768,128]{1,0:T(8,128)(2,1)S(1)}, u32[]{:S(2)}, u32[]{:S(2)}) collective-permute-start(bf16[768,128]{1,0:T(8,128)(2,1)} %get-tuple-element.88), channel_id=1, source_target_pairs={{0,128},{1,129},{2,130},{3,131},{4,132},{5,133},{6,134},{7,135},{8... | collective-permute-start | bytes 589832 | tf_op jit(solution)/shard_map/ppermute | solution.py:478
  11.4 1.4 %collective-permute-start.3 = (bf16[768,128]{1,0:T(8,128)(2,1)}, bf16[768,128]{1,0:T(8,128)(2,1)S(1)}, u32[]{:S(2)}, u32[]{:S(2)}) collective-permute-start(bf16[768,128]{1,0:T(8,128)(2,1)} %get-tuple-element.89), channel_id=1, source_target_pairs={{0,128},{1,129},{2,130},{3,131},{4,132},{5,133},{6,134},{7,135},{8... | collective-permute-start | bytes 589832 | tf_op jit(solution)/shard_map/ppermute | solution.py:478
  12.9 3.3 %collective-permute-start.5 = (f32[8,128]{1,0:T(8,128)S(1)}, f32[8,128]{1,0:T(8,128)S(1)}, u32[]{:S(2)}, u32[]{:S(2)}) collective-permute-start(f32[8,128]{1,0:T(8,128)S(1)} %broadcast_add_fusion), channel_id=1, source_target_pairs={{0,2},{1,3},{2,0},{3,1},{4,6},{5,7},{6,4},{7,5},{8,10},{9,11},{10,... | collective-permute-start | bytes 12296 | tf_op jit(solution)/shard_map/ppermute | solution.py:481
  16.1 1.0 %copy-done = bf16[1536,128]{1,0:T(8,128)(2,1)S(1)} copy-done((bf16[1536,128]{1,0:T(8,128)(2,1)S(1)}, bf16[1536,128]{1,0:T(8,128)(2,1)}, u32[]{:S(2)}) %copy-start) | copy-done | bytes 393240
  17.1 0.8 copy-done.1
  18.0 1.9 %chunk_own.1 = (f32[1536,384]{1,0:T(8,128)S(1)}, f32[1536,384]{1,0:T(8,128)S(1)}, f32[1536,256]{1,0:T(8,128)S(1)}, f32[384,128]{1,0:T(8,128)S(1)}, f32[384,128]{1,0:T(8,128)S(1)}, /*index=5*/f32[144,128]{1,0:T(8,128)S(1)}) custom-call(bf16[1536,128]{1,0:T(8,128)(2,1)S(1)} %copy-done, bf16[256,128]{1,0:T(8,128)(2,1)S(1)} %copy-done.1), custom_call_target="tpu_custom_call" | custom-call | flops 1012531200 | bytes 4000000 | tf_op jit(solution)/shard_map/chunk_own/pallas_call | solution.py:270
  19.9 1.7 %collective-permute-done.3.r_2_.r_3_ = bf16[768,128]{1,0:T(8,128)(2,1)S(1)} collective-permute-done((bf16[768,128]{1,0:T(8,128)(2,1)}, bf16[768,128]{1,0:T(8,128)(2,1)S(1)}, u32[]{:S(2)}, u32[]{:S(2)}) %collective-permute-start.3) | collective-permute-done | bytes 196640 | tf_op jit(solution)/shard_map/ppermute | solution.py:478
  21.8 1.7 %collective-permute-start.8 = (bf16[2752,128]{1,0:T(8,128)(2,1)S(1)}, bf16[2752,128]{1,0:T(8,128)(2,1)S(1)}, u32[]{:S(2)}, u32[]{:S(2)}) collective-permute-start(bf16[2752,128]{1,0:T(8,128)(2,1)S(1)} %get-tuple-element.103), channel_id=1, source_target_pairs={{0,16},{1,17},{2,18},{3,19},{4,20},{5,21},{6,22},{7,23},{8,72},{9,... | collective-permute-start | bytes 2113544 | tf_op jit(solution)/shard_map/ppermute | solution.py:479
  23.4 1.7 %collective-permute-start.9 = (bf16[2752,128]{1,0:T(8,128)(2,1)S(1)}, bf16[2752,128]{1,0:T(8,128)(2,1)S(1)}, u32[]{:S(2)}, u32[]{:S(2)}) collective-permute-start(bf16[2752,128]{1,0:T(8,128)(2,1)S(1)} %get-tuple-element.104), channel_id=1, source_target_pairs={{0,48},{1,49},{2,50},{3,51},{4,52},{5,53},{6,54},{7,55},{8,200},{9... | collective-permute-start | bytes 2113544 | tf_op jit(solution)/shard_map/ppermute | solution.py:479
  25.7 2.9 %collective-permute-start.7 = (bf16[2752,128]{1,0:T(8,128)(2,1)S(1)}, bf16[2752,128]{1,0:T(8,128)(2,1)S(1)}, u32[]{:S(2)}, u32[]{:S(2)}) collective-permute-start(bf16[2752,128]{1,0:T(8,128)(2,1)S(1)} %get-tuple-element.101), channel_id=1, source_target_pairs={{0,48},{1,49},{2,50},{3,51},{4,52},{5,53},{6,54},{7,55},{8,200},{9... | collective-permute-start | bytes 2113544 | tf_op jit(solution)/shard_map/ppermute | solution.py:479
  28.5 5.4 %collective-permute-start.10 = (f32[8,128]{1,0:T(8,128)S(1)}, f32[8,128]{1,0:T(8,128)S(1)}, u32[]{:S(2)}, u32[]{:S(2)}) collective-permute-start(f32[8,128]{1,0:T(8,128)S(1)} %fusion.1), channel_id=1, source_target_pairs={{0,6},{1,7},{2,4},{3,5},{4,2},{5,3},{6,0},{7,1},{8,14},{9,15},{10,... | collective-permute-start | bytes 12296 | tf_op jit(solution)/shard_map/ppermute | solution.py:481
  33.9 4.6 %chunk_line.1 = (f32[1536,384]{1,0:T(8,128)S(1)}, f32[1536,384]{1,0:T(8,128)S(1)}, f32[1536,256]{1,0:T(8,128)S(1)}, f32[384,128]{1,0:T(8,128)S(1)}, f32[384,128]{1,0:T(8,128)S(1)}, /*index=5*/f32[144,128]{1,0:T(8,128)S(1)}) custom-call(bf16[1536,128]{1,0:T(8,128)(2,1)S(1)} %collective-permute-done.r_2_.r_0_, ...), custom_call_target="tpu_custom_call" | custom-call | flops 3037593600 | bytes 12000000 | tf_op jit(solution)/shard_map/chunk_line/pallas_call | solution.py:270
  38.9 3.3 %collective-permute-start.14 = (bf16[1344,128]{1,0:T(8,128)(2,1)S(1)}, bf16[1344,128]{1,0:T(8,128)(2,1)S(1)}, u32[]{:S(2)}, u32[]{:S(2)}) collective-permute-start(bf16[1344,128]{1,0:T(8,128)(2,1)S(1)} %slice.15), channel_id=1, source_target_pairs={{0,48},{1,49},{2,50},{3,51},{4,52},{5,53},{6,54},{7,55},{8,200},{9... | collective-permute-start | bytes 1032200 | tf_op jit(solution)/shard_map/ppermute | solution.py:479
  42.2 5.5 %chunk_near1.1 = (f32[1536,384]{1,0:T(8,128)S(1)}, f32[1536,384]{1,0:T(8,128)S(1)}, f32[1536,256]{1,0:T(8,128)S(1)}, f32[384,128]{1,0:T(8,128)S(1)}, f32[384,128]{1,0:T(8,128)S(1)}, /*index=5*/f32[144,128]{1,0:T(8,128)S(1)}) custom-call(bf16[2752,128]{1,0:T(8,128)(2,1)S(1)} %collective-permute-done.8.r_0_, ...), custom_call_target="tpu_custom_call" | custom-call | flops 4050124800 | bytes 16000000 | tf_op jit(solution)/shard_map/chunk_near1/pallas_call | solution.py:270
  47.8 3.3 %collective-permute-start.12 = (bf16[1344,128]{1,0:T(8,128)(2,1)S(1)}, bf16[1344,128]{1,0:T(8,128)(2,1)S(1)}, u32[]{:S(2)}, u32[]{:S(2)}) collective-permute-start(bf16[1344,128]{1,0:T(8,128)(2,1)S(1)} %slice.13), channel_id=1, source_target_pairs={{0,48},{1,49},{2,50},{3,51},{4,52},{5,53},{6,54},{7,55},{8,200},{9... | collective-permute-start | bytes 1032200 | tf_op jit(solution)/shard_map/ppermute | solution.py:479
  51.1 7.9 %chunk_far1.1 = (f32[1536,384]{1,0:T(8,128)S(1)}, f32[1536,384]{1,0:T(8,128)S(1)}, f32[1536,256]{1,0:T(8,128)S(1)}, f32[384,128]{1,0:T(8,128)S(1)}, f32[384,128]{1,0:T(8,128)S(1)}, /*index=5*/f32[144,128]{1,0:T(8,128)S(1)}) custom-call(bf16[1344,128]{1,0:T(8,128)(2,1)S(1)} %collective-permute-done.13.r_0_, ...), custom_call_target="tpu_custom_call" | custom-call | flops 6075187200 | bytes 24000000 | tf_op jit(solution)/shard_map/chunk_far1/pallas_call | solution.py:270
  59.1 2.9 %chunk_far2.1 = (f32[1536,384]{1,0:T(8,128)S(1)}, f32[1536,384]{1,0:T(8,128)S(1)}, f32[1536,256]{1,0:T(8,128)S(1)}, f32[384,128]{1,0:T(8,128)S(1)}, f32[384,128]{1,0:T(8,128)S(1)}, /*index=5*/f32[144,128]{1,0:T(8,128)S(1)}) custom-call(bf16[1344,128]{1,0:T(8,128)(2,1)S(1)} %collective-permute-done.11.r_0_, ...), custom_call_target="tpu_custom_call" | custom-call | flops 2025062400 | bytes 8000000 | tf_op jit(solution)/shard_map/chunk_far2/pallas_call | solution.py:270
  62.1 1.3 %collective-permute-done.15.b_ref = f32[144,128]{1,0:T(8,128)S(1)} collective-permute-done((f32[144,128]{1,0:T(8,128)S(1)}, f32[144,128]{1,0:T(8,128)S(1)}, u32[]{:S(2)}, u32[]{:S(2)}) %collective-permute-start.15) | collective-permute-done | bytes 73760 | tf_op jit(solution)/shard_map/ppermute | solution.py:480
  64.0 6.2 %panel_factor.1 = (f32[128,128]{1,0:T(8,128)S(1)}, f32[128,128]{1,0:T(8,128)S(1)}, f32[16,128]{1,0:T(8,128)S(1)}) custom-call(f32[144,128]{1,0:T(8,128)S(1)} %get-tuple-element.147.a_ref, f32[144,128]{1,0:T(8,128)S(1)} %collective-permute-done.15.b_ref, f32[8,128]{1,0:T(8,128)S(1)} %add.34.d_ref), custom_call_target="tpu_custom_call" | custom-call | tf_op jit(solution)/shard_map/panel_factor/pallas_call | solution.py:344
  70.4 1.9 %panel_solve.1 = (f32[12,128]{1,0:T(8,128)S(1)}, f32[1536,128]{1,0:T(8,128)S(1)}, bf16[1536,384]{1,0:T(8,128)(2,1)S(1)}, bf16[384,384]{1,0:T(8,128)(2,1)S(1)}) custom-call(s32[1]{0:T(128)} %copy.16.k_ref.r_0_, f32[1536,256]{1,0:T(8,128)S(1)} %get-tuple-element.151.p_ref, f32[1536,256]{1,0:T(8,128)S(1)} %collective-permute-done.16.pr_ref, ...), custom_call_target="tpu_custom_call" | custom-call | tf_op jit(solution)/shard_map/panel_solve/pallas_call | solution.py:398
  72.4 1.0 %collective-permute-start.19 = (f32[12,8,128]{2,1,0:T(8,128)S(1)}, f32[12,8,128]{2,1,0:T(8,128)S(1)}, u32[]{:S(2)}, u32[]{:S(2)}) collective-permute-start(f32[12,8,128]{2,1,0:T(8,128)S(1)} %broadcast_select_fusion), channel_id=1, source_target_pairs={{0,1},{1,0},{2,3},{3,2},{4,5},{5,4},{6,7},{7,6},{8,9},{9,8},{10,11... | collective-permute-start | bytes 147464 | tf_op jit(solution)/shard_map/ppermute | solution.py:523
  73.4 1.5 %collective-permute-start.20 = (f32[12,8,128]{2,1,0:T(8,128)S(1)}, f32[12,8,128]{2,1,0:T(8,128)S(1)}, u32[]{:S(2)}, u32[]{:S(2)}) collective-permute-start(f32[12,8,128]{2,1,0:T(8,128)S(1)} %broadcast_select_fusion), channel_id=1, source_target_pairs={{0,2},{1,3},{2,0},{3,1},{4,6},{5,7},{6,4},{7,5},{8,10},{9,11},{10,... | collective-permute-start | bytes 147464 | tf_op jit(solution)/shard_map/ppermute | solution.py:523
  74.9 1.9 %collective-permute-start.21 = (f32[12,8,128]{2,1,0:T(8,128)S(1)}, f32[12,8,128]{2,1,0:T(8,128)S(1)}, u32[]{:S(2)}, u32[]{:S(2)}) collective-permute-start(f32[12,8,128]{2,1,0:T(8,128)S(1)} %broadcast_select_fusion), channel_id=1, source_target_pairs={{0,3},{1,2},{2,1},{3,0},{4,7},{5,6},{6,5},{7,4},{8,11},{9,10},{10,... | collective-permute-start | bytes 147464 | tf_op jit(solution)/shard_map/ppermute | solution.py:523
  76.8 3.6 %trailing_update.2.r_8_ = f32[4608,128]{1,0:T(8,128)} custom-call(s32[1]{0:T(128)} %copy.16.k_ref.r_0_, f32[1536,384]{1,0:T(8,128)S(1)} %get-tuple-element.146.r_1_, f32[1536,384]{1,0:T(8,128)S(1)} %collective-permute-done.18.r_2_, bf16[1536,384]{1,0:T(8,128)(2,1)S(1)} %get-tuple-element.163.r_3_, bf16[384,384]{1,0:T(8,128)(2,1)S(1)} %get-tuple-element.164.r_4_, ...), custom_call_target="tpu_custom_call" | custom-call | flops 1 | bytes 6000000 | tf_op jit(solution)/shard_map/trailing_update/pallas_call | solution.py:442
  81.0 1.2 %collective-permute-start.22 = (f32[12,8,128]{2,1,0:T(8,128)S(1)}, f32[12,8,128]{2,1,0:T(8,128)S(1)}, u32[]{:S(2)}, u32[]{:S(2)}) collective-permute-start(f32[12,8,128]{2,1,0:T(8,128)S(1)} %add_add_fusion), channel_id=1, source_target_pairs={{0,6},{1,7},{2,4},{3,5},{4,2},{5,3},{6,0},{7,1},{8,14},{9,15},{10,... | collective-permute-start | bytes 147464 | tf_op jit(solution)/shard_map/ppermute | solution.py:481
  82.1 2.7 %trailing_update.3 = f32[4608,128]{1,0:T(8,128)} custom-call(s32[1]{0:T(128)} %copy.16.k_ref.r_0_, f32[1536,384]{1,0:T(8,128)S(1)} %get-tuple-element.146.r_1_, f32[1536,384]{1,0:T(8,128)S(1)} %collective-permute-done.18.r_2_, bf16[1536,384]{1,0:T(8,128)(2,1)S(1)} %get-tuple-element.163.r_3_, ...), custom_call_target="tpu_custom_call", output_to_operand_aliasing={{}: (8, {})} | custom-call | flops 1 | bytes 6000000 | tf_op jit(solution)/shard_map/trailing_update/pallas_call | solution.py:442
  84.9 2.4 %collective-permute-done.22 = f32[12,8,128]{2,1,0:T(8,128)S(1)} collective-permute-done((f32[12,8,128]{2,1,0:T(8,128)S(1)}, f32[12,8,128]{2,1,0:T(8,128)S(1)}, u32[]{:S(2)}, u32[]{:S(2)}) %collective-permute-start.22) | collective-permute-done | bytes 49184 | tf_op jit(solution)/shard_map/ppermute | solution.py:481
  87.2 0.6 add_bitcast_fusion
  (46 shorter events, 3.3 us)
Async XLA Ops:
  2.0 10.9 %collective-permute-start.4 = (f32[8,128]{1,0:T(8,128)S(1)}, f32[8,128]{1,0:T(8,128)S(1)}, u32[]{:S(2)}, u32[]{:S(2)}) collective-permute-start(f32[8,128]{1,0:T(8,128)S(1)} %broadcast_in_dim.31), channel_id=1, source_target_pairs={{0,1},{1,0},{2,3},{3,2},{4,5},{5,4},{6,7},{7,6},{8,9},{9,8},{10,11... | collective-permute-start | bytes 12296 | tf_op jit(solution)/shard_map/ppermute | solution.py:481
  7.2 14.4 %collective-permute-start = (bf16[1536,128]{1,0:T(8,128)(2,1)}, bf16[1536,128]{1,0:T(8,128)(2,1)S(1)}, u32[]{:S(2)}, u32[]{:S(2)}) collective-permute-start(bf16[1536,128]{1,0:T(8,128)(2,1)} %get-tuple-element.86.r_0_), channel_id=1, source_target_pairs={{0,64},{1,65},{2,66},{3,67},{4,68},{5,69},{6,70},{7,71},{8,24},{9,... | collective-permute-start | bytes 1179656 | tf_op jit(solution)/shard_map/ppermute | solution.py:478
  8.8 12.8 %collective-permute-start.1 = (bf16[1536,128]{1,0:T(8,128)(2,1)}, bf16[1536,128]{1,0:T(8,128)(2,1)S(1)}, u32[]{:S(2)}, u32[]{:S(2)}) collective-permute-start(bf16[1536,128]{1,0:T(8,128)(2,1)} %get-tuple-element.87), channel_id=1, source_target_pairs={{0,192},{1,193},{2,194},{3,195},{4,196},{5,197},{6,198},{7,199},{8... | collective-permute-start | bytes 1179656 | tf_op jit(solution)/shard_map/ppermute | solution.py:478
  9.3 10.6 %collective-permute-start.2 = (bf16[768,128]{1,0:T(8,128)(2,1)}, bf16[768,128]{1,0:T(8,128)(2,1)S(1)}, u32[]{:S(2)}, u32[]{:S(2)}) collective-permute-start(bf16[768,128]{1,0:T(8,128)(2,1)} %get-tuple-element.88), channel_id=1, source_target_pairs={{0,128},{1,129},{2,130},{3,131},{4,132},{5,133},{6,134},{7,135},{8... | collective-permute-start | bytes 589832 | tf_op jit(solution)/shard_map/ppermute | solution.py:478
  11.4 10.2 %collective-permute-start.3 = (bf16[768,128]{1,0:T(8,128)(2,1)}, bf16[768,128]{1,0:T(8,128)(2,1)S(1)}, u32[]{:S(2)}, u32[]{:S(2)}) collective-permute-start(bf16[768,128]{1,0:T(8,128)(2,1)} %get-tuple-element.89), channel_id=1, source_target_pairs={{0,128},{1,129},{2,130},{3,131},{4,132},{5,133},{6,134},{7,135},{8... | collective-permute-start | bytes 589832 | tf_op jit(solution)/shard_map/ppermute | solution.py:478
  12.9 7.0 %collective-permute-start.5 = (f32[8,128]{1,0:T(8,128)S(1)}, f32[8,128]{1,0:T(8,128)S(1)}, u32[]{:S(2)}, u32[]{:S(2)}) collective-permute-start(f32[8,128]{1,0:T(8,128)S(1)} %broadcast_add_fusion), channel_id=1, source_target_pairs={{0,2},{1,3},{2,0},{3,1},{4,6},{5,7},{6,4},{7,5},{8,10},{9,11},{10,... | collective-permute-start | bytes 12296 | tf_op jit(solution)/shard_map/ppermute | solution.py:481
  16.1 1.0 %copy-start = (bf16[1536,128]{1,0:T(8,128)(2,1)S(1)}, bf16[1536,128]{1,0:T(8,128)(2,1)}, u32[]{:S(2)}) copy-start(bf16[1536,128]{1,0:T(8,128)(2,1)} %get-tuple-element.86.r_0_) | copy-start | bytes 1179652
  17.1 0.8 copy-start.1
  21.8 16.8 %collective-permute-start.8 = (bf16[2752,128]{1,0:T(8,128)(2,1)S(1)}, bf16[2752,128]{1,0:T(8,128)(2,1)S(1)}, u32[]{:S(2)}, u32[]{:S(2)}) collective-permute-start(bf16[2752,128]{1,0:T(8,128)(2,1)S(1)} %get-tuple-element.103), channel_id=1, source_target_pairs={{0,16},{1,17},{2,18},{3,19},{4,20},{5,21},{6,22},{7,23},{8,72},{9,... | collective-permute-start | bytes 2113544 | tf_op jit(solution)/shard_map/ppermute | solution.py:479
  23.4 15.1 %collective-permute-start.9 = (bf16[2752,128]{1,0:T(8,128)(2,1)S(1)}, bf16[2752,128]{1,0:T(8,128)(2,1)S(1)}, u32[]{:S(2)}, u32[]{:S(2)}) collective-permute-start(bf16[2752,128]{1,0:T(8,128)(2,1)S(1)} %get-tuple-element.104), channel_id=1, source_target_pairs={{0,48},{1,49},{2,50},{3,51},{4,52},{5,53},{6,54},{7,55},{8,200},{9... | collective-permute-start | bytes 2113544 | tf_op jit(solution)/shard_map/ppermute | solution.py:479
  25.2 22.4 %collective-permute-start.6 = (bf16[2752,128]{1,0:T(8,128)(2,1)S(1)}, bf16[2752,128]{1,0:T(8,128)(2,1)S(1)}, u32[]{:S(2)}, u32[]{:S(2)}) collective-permute-start(bf16[2752,128]{1,0:T(8,128)(2,1)S(1)} %get-tuple-element.100), channel_id=1, source_target_pairs={{0,16},{1,17},{2,18},{3,19},{4,20},{5,21},{6,22},{7,23},{8,72},{9,... | collective-permute-start | bytes 2113544 | tf_op jit(solution)/shard_map/ppermute | solution.py:479
  25.7 22.0 %collective-permute-start.7 = (bf16[2752,128]{1,0:T(8,128)(2,1)S(1)}, bf16[2752,128]{1,0:T(8,128)(2,1)S(1)}, u32[]{:S(2)}, u32[]{:S(2)}) collective-permute-start(bf16[2752,128]{1,0:T(8,128)(2,1)S(1)} %get-tuple-element.101), channel_id=1, source_target_pairs={{0,48},{1,49},{2,50},{3,51},{4,52},{5,53},{6,54},{7,55},{8,200},{9... | collective-permute-start | bytes 2113544 | tf_op jit(solution)/shard_map/ppermute | solution.py:479
  28.5 10.0 %collective-permute-start.10 = (f32[8,128]{1,0:T(8,128)S(1)}, f32[8,128]{1,0:T(8,128)S(1)}, u32[]{:S(2)}, u32[]{:S(2)}) collective-permute-start(f32[8,128]{1,0:T(8,128)S(1)} %fusion.1), channel_id=1, source_target_pairs={{0,6},{1,7},{2,4},{3,5},{4,2},{5,3},{6,0},{7,1},{8,14},{9,15},{10,... | collective-permute-start | bytes 12296 | tf_op jit(solution)/shard_map/ppermute | solution.py:481
  38.6 12.5 %collective-permute-start.13 = (bf16[1344,128]{1,0:T(8,128)(2,1)S(1)}, bf16[1344,128]{1,0:T(8,128)(2,1)S(1)}, u32[]{:S(2)}, u32[]{:S(2)}) collective-permute-start(bf16[1344,128]{1,0:T(8,128)(2,1)S(1)} %slice.14), channel_id=1, source_target_pairs={{0,16},{1,17},{2,18},{3,19},{4,20},{5,21},{6,22},{7,23},{8,72},{9,... | collective-permute-start | bytes 1032200 | tf_op jit(solution)/shard_map/ppermute | solution.py:479
  38.9 12.2 %collective-permute-start.14 = (bf16[1344,128]{1,0:T(8,128)(2,1)S(1)}, bf16[1344,128]{1,0:T(8,128)(2,1)S(1)}, u32[]{:S(2)}, u32[]{:S(2)}) collective-permute-start(bf16[1344,128]{1,0:T(8,128)(2,1)S(1)} %slice.15), channel_id=1, source_target_pairs={{0,48},{1,49},{2,50},{3,51},{4,52},{5,53},{6,54},{7,55},{8,200},{9... | collective-permute-start | bytes 1032200 | tf_op jit(solution)/shard_map/ppermute | solution.py:479
  47.7 11.4 %collective-permute-start.11 = (bf16[1344,128]{1,0:T(8,128)(2,1)S(1)}, bf16[1344,128]{1,0:T(8,128)(2,1)S(1)}, u32[]{:S(2)}, u32[]{:S(2)}) collective-permute-start(bf16[1344,128]{1,0:T(8,128)(2,1)S(1)} %slice.12), channel_id=1, source_target_pairs={{0,16},{1,17},{2,18},{3,19},{4,20},{5,21},{6,22},{7,23},{8,72},{9,... | collective-permute-start | bytes 1032200 | tf_op jit(solution)/shard_map/ppermute | solution.py:479
  47.8 11.2 %collective-permute-start.12 = (bf16[1344,128]{1,0:T(8,128)(2,1)S(1)}, bf16[1344,128]{1,0:T(8,128)(2,1)S(1)}, u32[]{:S(2)}, u32[]{:S(2)}) collective-permute-start(bf16[1344,128]{1,0:T(8,128)(2,1)S(1)} %slice.13), channel_id=1, source_target_pairs={{0,48},{1,49},{2,50},{3,51},{4,52},{5,53},{6,54},{7,55},{8,200},{9... | collective-permute-start | bytes 1032200 | tf_op jit(solution)/shard_map/ppermute | solution.py:479
  61.9 14.9 %copy-start.2 = (f32[12,1,128]{2,1,0:T(1,128)S(1)}, f32[12,1,128]{2,1,0:T(1,128)}, u32[]{:S(2)}) copy-start(f32[12,1,128]{2,1,0:T(1,128)} %param.12) | copy-start | bytes 18436
  62.0 1.4 %collective-permute-start.15 = (f32[144,128]{1,0:T(8,128)S(1)}, f32[144,128]{1,0:T(8,128)S(1)}, u32[]{:S(2)}, u32[]{:S(2)}) collective-permute-start(f32[144,128]{1,0:T(8,128)S(1)} %get-tuple-element.147.a_ref), channel_id=1, source_target_pairs={{0,8},{8,0},{1,9},{9,1},{2,10},{10,2},{3,11},{11,3},{4,12},{12,4},... | collective-permute-start | bytes 221192 | tf_op jit(solution)/shard_map/ppermute | solution.py:480
  63.3 7.1 %collective-permute-start.18 = (f32[1536,384]{1,0:T(8,128)S(1)}, f32[1536,384]{1,0:T(8,128)S(1)}, u32[]{:S(2)}, u32[]{:S(2)}) collective-permute-start(f32[1536,384]{1,0:T(8,128)S(1)} %get-tuple-element.153), channel_id=1, source_target_pairs={{0,8},{8,0},{1,9},{9,1},{2,10},{10,2},{3,11},{11,3},{4,12},{12,4},... | collective-permute-start | bytes 7077896 | tf_op jit(solution)/shard_map/ppermute | solution.py:480
  63.5 6.9 %collective-permute-start.16 = (f32[1536,256]{1,0:T(8,128)S(1)}, f32[1536,256]{1,0:T(8,128)S(1)}, u32[]{:S(2)}, u32[]{:S(2)}) collective-permute-start(f32[1536,256]{1,0:T(8,128)S(1)} %get-tuple-element.151.p_ref), channel_id=1, source_target_pairs={{0,8},{8,0},{1,9},{9,1},{2,10},{10,2},{3,11},{11,3},{4,12},{12,4},... | collective-permute-start | bytes 4718600 | tf_op jit(solution)/shard_map/ppermute | solution.py:480
  63.8 6.6 %collective-permute-start.17 = (f32[384,128]{1,0:T(8,128)S(1)}, f32[384,128]{1,0:T(8,128)S(1)}, u32[]{:S(2)}, u32[]{:S(2)}) collective-permute-start(f32[384,128]{1,0:T(8,128)S(1)} %get-tuple-element.152), channel_id=1, source_target_pairs={{0,8},{8,0},{1,9},{9,1},{2,10},{10,2},{3,11},{11,3},{4,12},{12,4},... | collective-permute-start | bytes 589832 | tf_op jit(solution)/shard_map/ppermute | solution.py:480
  72.4 8.1 %collective-permute-start.19 = (f32[12,8,128]{2,1,0:T(8,128)S(1)}, f32[12,8,128]{2,1,0:T(8,128)S(1)}, u32[]{:S(2)}, u32[]{:S(2)}) collective-permute-start(f32[12,8,128]{2,1,0:T(8,128)S(1)} %broadcast_select_fusion), channel_id=1, source_target_pairs={{0,1},{1,0},{2,3},{3,2},{4,5},{5,4},{6,7},{7,6},{8,9},{9,8},{10,11... | collective-permute-start | bytes 147464 | tf_op jit(solution)/shard_map/ppermute | solution.py:523
  73.4 7.0 %collective-permute-start.20 = (f32[12,8,128]{2,1,0:T(8,128)S(1)}, f32[12,8,128]{2,1,0:T(8,128)S(1)}, u32[]{:S(2)}, u32[]{:S(2)}) collective-permute-start(f32[12,8,128]{2,1,0:T(8,128)S(1)} %broadcast_select_fusion), channel_id=1, source_target_pairs={{0,2},{1,3},{2,0},{3,1},{4,6},{5,7},{6,4},{7,5},{8,10},{9,11},{10,... | collective-permute-start | bytes 147464 | tf_op jit(solution)/shard_map/ppermute | solution.py:523
  74.9 6.0 %collective-permute-start.21 = (f32[12,8,128]{2,1,0:T(8,128)S(1)}, f32[12,8,128]{2,1,0:T(8,128)S(1)}, u32[]{:S(2)}, u32[]{:S(2)}) collective-permute-start(f32[12,8,128]{2,1,0:T(8,128)S(1)} %broadcast_select_fusion), channel_id=1, source_target_pairs={{0,3},{1,2},{2,1},{3,0},{4,7},{5,6},{6,5},{7,4},{8,11},{9,10},{10,... | collective-permute-start | bytes 147464 | tf_op jit(solution)/shard_map/ppermute | solution.py:523
  81.0 6.3 %collective-permute-start.22 = (f32[12,8,128]{2,1,0:T(8,128)S(1)}, f32[12,8,128]{2,1,0:T(8,128)S(1)}, u32[]{:S(2)}, u32[]{:S(2)}) collective-permute-start(f32[12,8,128]{2,1,0:T(8,128)S(1)} %add_add_fusion), channel_id=1, source_target_pairs={{0,6},{1,7},{2,4},{3,5},{4,2},{5,3},{6,0},{7,1},{8,14},{9,15},{10,... | collective-permute-start | bytes 147464 | tf_op jit(solution)/shard_map/ppermute | solution.py:481

commit v10 on v9

--- a/solution.py
+++ b/solution.py
@@ -499,13 +499,13 @@
     m1p, m1m, m2p, m2m = two(m1[0], 1), two(m1[1], -1), two(m2[0], 1), two(m2[1], -1)
     line = [place(BLOCK1, 0, -2), place(BLOCK2, 0, 1), place(BLOCK3, 0, 1)]
     accs = chunk(line, (ap, am, rp, rm), accs, "chunk_line")
-    m1p, m1m, accs, dsel = bar((m1p, m1m, accs, zbit(dsel, 6)))
+    m1p, m1m, accs, dsel = bar((m1p, m1m, accs, dsel))
     n1 = BR + GC
     r1p, r1m = two(m1p[:n1], 1), two(m1m[:n1], -1)
     e1 = 2 * BR + GC
     near = received(0, e1) + received(1, e1)
     accs = chunk(near, (m1p, m1m), accs, "chunk_near1")
-    m2p, m2m, accs = bar((m2p, m2m, accs))
+    m2p, m2m, accs, dsel = bar((m2p, m2m, accs, zbit(dsel, 6)))
     r2p, r2m = two(m2p[:n1], 1), two(m2m[:n1], -1)
     far = [received(0, BR)[0], received(1, BR)[0]]
     accs = chunk(far + received(2, e1) + received(3, e1), (r1p, r1m, m2p, m2m), accs, "chunk_far1")

time: 88.1 us -> 89.4 us (1.015)
  waiting for transfers between devices: 5.98 us -> 8.47 us
  starting transfers between devices: 36.1 us -> 35.1 us
    ppermute x8, waiting for transfers between devices: 0.02 us -> 1.48 us  [body(): two = lambda v, d: lax.ppermute(v, AXES, hops(1, d))]
    ppermute x4, starting transfers between devices: 11.8 us -> 10.7 us  [body(): lax.ppermute(v, 'row', [(i, i ^ bit) for i in range(NZ)])]
    ppermute x4, waiting for transfers between devices: 2.38 us -> 3.42 us  [body(): lax.ppermute(v, 'row', [(i, i ^ bit) for i in range(NZ)])]
  transfers between devices with their start and end apart: 23 -> 23, of which waited for: 5 -> 7; matrix products, arithmetic and copies ran while one was open for 0% -> 0% of each run, Pallas kernels for 41% -> 40%
where the time goes in v10:
time: 89.4 us; the launch traced here: 89.1 us
  Pallas kernels  40.7 us (46%)
  starting transfers between devices  35.1 us (39%)
  waiting for transfers between devices  8.47 us (9%)
  local copies, waits for them, and re-layouts  1.94 us (2%)
  between operations  1.51 us (2%)
  other arithmetic  1.46 us (2%)
    pallas_call x5, Pallas kernels, chunk(): pl.pallas_call(lambda *r: chunk_kernel(blocks, len(arrs), len(accs), *r),...  22.6 us
    ppermute x8, starting transfers between devices, body(): two = lambda v, d: lax.ppermute(v, AXES, hops(1, d))  13.6 us
    ppermute x4, starting transfers between devices, body(): lax.ppermute(v, 'row', [(i, i ^ bit) for i in range(NZ)])  10.7 us
    pallas_call x2, Pallas kernels, final(): pl.pallas_call(lambda *r: final_kernel(start, *r), grid=(count,), out_sha...  6.41 us
    pallas_call x1, Pallas kernels, cholesky(): pl.pallas_call(chol_kernel, out_shape=(jax.ShapeDtypeStruct((K, K), F32),...  6.21 us
    ppermute x4, starting transfers between devices, body(): one = lambda v, d: lax.ppermute(v, AXES, hops(0, d))  5.63 us
    ppermute x3, starting transfers between devices, body(): lax.ppermute(parts[0], 'row', [(i, i ^ bits) for i in range(NZ)])  4.42 us
    ppermute x4, waiting for transfers between devices, body(): lax.ppermute(v, 'row', [(i, i ^ bit) for i in range(NZ)])  3.42 us
  transfers between devices with their start and end apart: 23, of which 7 were waited for; matrix products, arithmetic and copies ran while one was open for 0% of the time, Pallas kernels for 40%

profile of v10, /device:TPU:2, one launch (start us, length us, event | category | flops | bytes accessed | tf_op | source)
XLA Modules:
  0.0 89.1 jit_solution(10374814343161100286)
XLA Ops:
  1.3 0.7 fusion
  2.0 1.9 %collective-permute-start.4 = (f32[8,128]{1,0:T(8,128)S(1)}, f32[8,128]{1,0:T(8,128)S(1)}, u32[]{:S(2)}, u32[]{:S(2)}) collective-permute-start(f32[8,128]{1,0:T(8,128)S(1)} %broadcast_in_dim.31), channel_id=1, source_target_pairs={{0,1},{1,0},{2,3},{3,2},{4,5},{5,4},{6,7},{7,6},{8,9},{9,8},{10,11... | collective-permute-start | bytes 12296 | tf_op jit(solution)/shard_map/ppermute | solution.py:481
  3.9 3.3 %pack.1 = (bf16[1536,128]{1,0:T(8,128)(2,1)}, bf16[1536,128]{1,0:T(8,128)(2,1)}, bf16[768,128]{1,0:T(8,128)(2,1)}, bf16[768,128]{1,0:T(8,128)(2,1)}, bf16[256,128]{1,0:T(8,128)(2,1)}) custom-call(s32[1]{0:T(128)} %copy.16.k_ref.r_0_, s32[1,128]{1,0:T(1,128)} %bitcast.25, bf16[1152,256]{1,0:T(8,128)(2,1)} %bitcast.23, bf16[864,256]{1,0:T(8,128)(2,1)} %bitcast.24, ...), custom_call_target="tpu_custom_call" | custom-call | tf_op jit(solution)/shard_map/pack/pallas_call | solution.py:111
  7.2 1.6 %collective-permute-start = (bf16[1536,128]{1,0:T(8,128)(2,1)}, bf16[1536,128]{1,0:T(8,128)(2,1)S(1)}, u32[]{:S(2)}, u32[]{:S(2)}) collective-permute-start(bf16[1536,128]{1,0:T(8,128)(2,1)} %get-tuple-element.87.r_0_), channel_id=1, source_target_pairs={{0,64},{1,65},{2,66},{3,67},{4,68},{5,69},{6,70},{7,71},{8,24},{9,... | collective-permute-start | bytes 1179656 | tf_op jit(solution)/shard_map/ppermute | solution.py:478
  9.3 2.1 %collective-permute-start.2 = (bf16[768,128]{1,0:T(8,128)(2,1)}, bf16[768,128]{1,0:T(8,128)(2,1)S(1)}, u32[]{:S(2)}, u32[]{:S(2)}) collective-permute-start(bf16[768,128]{1,0:T(8,128)(2,1)} %get-tuple-element.89), channel_id=1, source_target_pairs={{0,128},{1,129},{2,130},{3,131},{4,132},{5,133},{6,134},{7,135},{8... | collective-permute-start | bytes 589832 | tf_op jit(solution)/shard_map/ppermute | solution.py:478
  11.4 1.4 %collective-permute-start.3 = (bf16[768,128]{1,0:T(8,128)(2,1)}, bf16[768,128]{1,0:T(8,128)(2,1)S(1)}, u32[]{:S(2)}, u32[]{:S(2)}) collective-permute-start(bf16[768,128]{1,0:T(8,128)(2,1)} %get-tuple-element.90), channel_id=1, source_target_pairs={{0,128},{1,129},{2,130},{3,131},{4,132},{5,133},{6,134},{7,135},{8... | collective-permute-start | bytes 589832 | tf_op jit(solution)/shard_map/ppermute | solution.py:478
  12.9 3.3 %collective-permute-start.5 = (f32[8,128]{1,0:T(8,128)S(1)}, f32[8,128]{1,0:T(8,128)S(1)}, u32[]{:S(2)}, u32[]{:S(2)}) collective-permute-start(f32[8,128]{1,0:T(8,128)S(1)} %broadcast_add_fusion), channel_id=1, source_target_pairs={{0,2},{1,3},{2,0},{3,1},{4,6},{5,7},{6,4},{7,5},{8,10},{9,11},{10,... | collective-permute-start | bytes 12296 | tf_op jit(solution)/shard_map/ppermute | solution.py:481
  16.1 1.0 %copy-done = bf16[1536,128]{1,0:T(8,128)(2,1)S(1)} copy-done((bf16[1536,128]{1,0:T(8,128)(2,1)S(1)}, bf16[1536,128]{1,0:T(8,128)(2,1)}, u32[]{:S(2)}) %copy-start) | copy-done | bytes 393240
  17.1 0.8 copy-done.1
  18.0 1.9 %chunk_own.1 = (f32[1536,384]{1,0:T(8,128)S(1)}, f32[1536,384]{1,0:T(8,128)S(1)}, f32[1536,256]{1,0:T(8,128)S(1)}, f32[384,128]{1,0:T(8,128)S(1)}, f32[384,128]{1,0:T(8,128)S(1)}, /*index=5*/f32[144,128]{1,0:T(8,128)S(1)}) custom-call(bf16[1536,128]{1,0:T(8,128)(2,1)S(1)} %copy-done, bf16[256,128]{1,0:T(8,128)(2,1)S(1)} %copy-done.1), custom_call_target="tpu_custom_call" | custom-call | flops 1012531200 | bytes 4000000 | tf_op jit(solution)/shard_map/chunk_own/pallas_call | solution.py:270
  19.9 1.7 %collective-permute-done.3.r_2_.r_3_ = bf16[768,128]{1,0:T(8,128)(2,1)S(1)} collective-permute-done((bf16[768,128]{1,0:T(8,128)(2,1)}, bf16[768,128]{1,0:T(8,128)(2,1)S(1)}, u32[]{:S(2)}, u32[]{:S(2)}) %collective-permute-start.3) | collective-permute-done | bytes 196640 | tf_op jit(solution)/shard_map/ppermute | solution.py:478
  21.8 1.7 %collective-permute-start.8 = (bf16[2752,128]{1,0:T(8,128)(2,1)S(1)}, bf16[2752,128]{1,0:T(8,128)(2,1)S(1)}, u32[]{:S(2)}, u32[]{:S(2)}) collective-permute-start(bf16[2752,128]{1,0:T(8,128)(2,1)S(1)} %get-tuple-element.104), channel_id=1, source_target_pairs={{0,16},{1,17},{2,18},{3,19},{4,20},{5,21},{6,22},{7,23},{8,72},{9,... | collective-permute-start | bytes 2113544 | tf_op jit(solution)/shard_map/ppermute | solution.py:479
  23.4 1.7 %collective-permute-start.9 = (bf16[2752,128]{1,0:T(8,128)(2,1)S(1)}, bf16[2752,128]{1,0:T(8,128)(2,1)S(1)}, u32[]{:S(2)}, u32[]{:S(2)}) collective-permute-start(bf16[2752,128]{1,0:T(8,128)(2,1)S(1)} %get-tuple-element.105), channel_id=1, source_target_pairs={{0,48},{1,49},{2,50},{3,51},{4,52},{5,53},{6,54},{7,55},{8,200},{9... | collective-permute-start | bytes 2113544 | tf_op jit(solution)/shard_map/ppermute | solution.py:479
  25.7 2.9 %collective-permute-start.7 = (bf16[2752,128]{1,0:T(8,128)(2,1)S(1)}, bf16[2752,128]{1,0:T(8,128)(2,1)S(1)}, u32[]{:S(2)}, u32[]{:S(2)}) collective-permute-start(bf16[2752,128]{1,0:T(8,128)(2,1)S(1)} %get-tuple-element.102), channel_id=1, source_target_pairs={{0,48},{1,49},{2,50},{3,51},{4,52},{5,53},{6,54},{7,55},{8,200},{9... | collective-permute-start | bytes 2113544 | tf_op jit(solution)/shard_map/ppermute | solution.py:479
  28.5 4.5 %chunk_line.1 = (f32[1536,384]{1,0:T(8,128)S(1)}, f32[1536,384]{1,0:T(8,128)S(1)}, f32[1536,256]{1,0:T(8,128)S(1)}, f32[384,128]{1,0:T(8,128)S(1)}, f32[384,128]{1,0:T(8,128)S(1)}, /*index=5*/f32[144,128]{1,0:T(8,128)S(1)}) custom-call(bf16[1536,128]{1,0:T(8,128)(2,1)S(1)} %collective-permute-done.r_2_.r_0_, ...), custom_call_target="tpu_custom_call" | custom-call | flops 3037593600 | bytes 12000000 | tf_op jit(solution)/shard_map/chunk_line/pallas_call | solution.py:270
  33.1 1.1 %collective-permute-done.8.r_0_ = bf16[2752,128]{1,0:T(8,128)(2,1)S(1)} collective-permute-done((bf16[2752,128]{1,0:T(8,128)(2,1)S(1)}, bf16[2752,128]{1,0:T(8,128)(2,1)S(1)}, u32[]{:S(2)}, u32[]{:S(2)}) %collective-permute-start.8) | collective-permute-done | bytes 704544 | tf_op jit(solution)/shard_map/ppermute | solution.py:479
  34.5 5.4 %collective-permute-start.10 = (f32[8,128]{1,0:T(8,128)S(1)}, f32[8,128]{1,0:T(8,128)S(1)}, u32[]{:S(2)}, u32[]{:S(2)}) collective-permute-start(f32[8,128]{1,0:T(8,128)S(1)} %fusion.1), channel_id=1, source_target_pairs={{0,6},{1,7},{2,4},{3,5},{4,2},{5,3},{6,0},{7,1},{8,14},{9,15},{10,... | collective-permute-start | bytes 12296 | tf_op jit(solution)/shard_map/ppermute | solution.py:481
  40.0 1.8 %collective-permute-start.13 = (bf16[1344,128]{1,0:T(8,128)(2,1)S(1)}, bf16[1344,128]{1,0:T(8,128)(2,1)S(1)}, u32[]{:S(2)}, u32[]{:S(2)}) collective-permute-start(bf16[1344,128]{1,0:T(8,128)(2,1)S(1)} %slice.14), channel_id=1, source_target_pairs={{0,16},{1,17},{2,18},{3,19},{4,20},{5,21},{6,22},{7,23},{8,72},{9,... | collective-permute-start | bytes 1032200 | tf_op jit(solution)/shard_map/ppermute | solution.py:479
  41.8 1.7 %collective-permute-start.14 = (bf16[1344,128]{1,0:T(8,128)(2,1)S(1)}, bf16[1344,128]{1,0:T(8,128)(2,1)S(1)}, u32[]{:S(2)}, u32[]{:S(2)}) collective-permute-start(bf16[1344,128]{1,0:T(8,128)(2,1)S(1)} %slice.15), channel_id=1, source_target_pairs={{0,48},{1,49},{2,50},{3,51},{4,52},{5,53},{6,54},{7,55},{8,200},{9... | collective-permute-start | bytes 1032200 | tf_op jit(solution)/shard_map/ppermute | solution.py:479
  43.6 5.3 %chunk_near1.1 = (f32[1536,384]{1,0:T(8,128)S(1)}, f32[1536,384]{1,0:T(8,128)S(1)}, f32[1536,256]{1,0:T(8,128)S(1)}, f32[384,128]{1,0:T(8,128)S(1)}, f32[384,128]{1,0:T(8,128)S(1)}, /*index=5*/f32[144,128]{1,0:T(8,128)S(1)}) custom-call(bf16[2752,128]{1,0:T(8,128)(2,1)S(1)} %collective-permute-done.8.r_0_, ...), custom_call_target="tpu_custom_call" | custom-call | flops 4050124800 | bytes 16000000 | tf_op jit(solution)/shard_map/chunk_near1/pallas_call | solution.py:270
  49.5 2.9 %collective-permute-start.12 = (bf16[1344,128]{1,0:T(8,128)(2,1)S(1)}, bf16[1344,128]{1,0:T(8,128)(2,1)S(1)}, u32[]{:S(2)}, u32[]{:S(2)}) collective-permute-start(bf16[1344,128]{1,0:T(8,128)(2,1)S(1)} %slice.13), channel_id=1, source_target_pairs={{0,48},{1,49},{2,50},{3,51},{4,52},{5,53},{6,54},{7,55},{8,200},{9... | collective-permute-start | bytes 1032200 | tf_op jit(solution)/shard_map/ppermute | solution.py:479
  52.4 7.9 %chunk_far1.1 = (f32[1536,384]{1,0:T(8,128)S(1)}, f32[1536,384]{1,0:T(8,128)S(1)}, f32[1536,256]{1,0:T(8,128)S(1)}, f32[384,128]{1,0:T(8,128)S(1)}, f32[384,128]{1,0:T(8,128)S(1)}, /*index=5*/f32[144,128]{1,0:T(8,128)S(1)}) custom-call(bf16[1344,128]{1,0:T(8,128)(2,1)S(1)} %collective-permute-done.13.r_0_, ...), custom_call_target="tpu_custom_call" | custom-call | flops 6075187200 | bytes 24000000 | tf_op jit(solution)/shard_map/chunk_far1/pallas_call | solution.py:270
  60.4 2.9 %chunk_far2.1 = (f32[1536,384]{1,0:T(8,128)S(1)}, f32[1536,384]{1,0:T(8,128)S(1)}, f32[1536,256]{1,0:T(8,128)S(1)}, f32[384,128]{1,0:T(8,128)S(1)}, f32[384,128]{1,0:T(8,128)S(1)}, /*index=5*/f32[144,128]{1,0:T(8,128)S(1)}) custom-call(bf16[1344,128]{1,0:T(8,128)(2,1)S(1)} %collective-permute-done.11.r_0_, ...), custom_call_target="tpu_custom_call" | custom-call | flops 2025062400 | bytes 8000000 | tf_op jit(solution)/shard_map/chunk_far2/pallas_call | solution.py:270
  63.3 1.3 %collective-permute-done.15.b_ref = f32[144,128]{1,0:T(8,128)S(1)} collective-permute-done((f32[144,128]{1,0:T(8,128)S(1)}, f32[144,128]{1,0:T(8,128)S(1)}, u32[]{:S(2)}, u32[]{:S(2)}) %collective-permute-start.15) | collective-permute-done | bytes 73760 | tf_op jit(solution)/shard_map/ppermute | solution.py:480
  65.3 6.2 %panel_factor.1 = (f32[128,128]{1,0:T(8,128)S(1)}, f32[128,128]{1,0:T(8,128)S(1)}, f32[16,128]{1,0:T(8,128)S(1)}) custom-call(f32[144,128]{1,0:T(8,128)S(1)} %get-tuple-element.149.a_ref, f32[144,128]{1,0:T(8,128)S(1)} %collective-permute-done.15.b_ref, f32[8,128]{1,0:T(8,128)S(1)} %add.34.d_ref), custom_call_target="tpu_custom_call" | custom-call | tf_op jit(solution)/shard_map/panel_factor/pallas_call | solution.py:344
  71.7 1.9 %panel_solve.1 = (f32[12,128]{1,0:T(8,128)S(1)}, f32[1536,128]{1,0:T(8,128)S(1)}, bf16[1536,384]{1,0:T(8,128)(2,1)S(1)}, bf16[384,384]{1,0:T(8,128)(2,1)S(1)}) custom-call(s32[1]{0:T(128)} %copy.16.k_ref.r_0_, f32[1536,256]{1,0:T(8,128)S(1)} %get-tuple-element.153.p_ref, f32[1536,256]{1,0:T(8,128)S(1)} %collective-permute-done.16.pr_ref, ...), custom_call_target="tpu_custom_call" | custom-call | tf_op jit(solution)/shard_map/panel_solve/pallas_call | solution.py:398
  73.7 1.0 %collective-permute-start.19 = (f32[12,8,128]{2,1,0:T(8,128)S(1)}, f32[12,8,128]{2,1,0:T(8,128)S(1)}, u32[]{:S(2)}, u32[]{:S(2)}) collective-permute-start(f32[12,8,128]{2,1,0:T(8,128)S(1)} %broadcast_select_fusion), channel_id=1, source_target_pairs={{0,1},{1,0},{2,3},{3,2},{4,5},{5,4},{6,7},{7,6},{8,9},{9,8},{10,11... | collective-permute-start | bytes 147464 | tf_op jit(solution)/shard_map/ppermute | solution.py:523
  74.7 1.4 %collective-permute-start.20 = (f32[12,8,128]{2,1,0:T(8,128)S(1)}, f32[12,8,128]{2,1,0:T(8,128)S(1)}, u32[]{:S(2)}, u32[]{:S(2)}) collective-permute-start(f32[12,8,128]{2,1,0:T(8,128)S(1)} %broadcast_select_fusion), channel_id=1, source_target_pairs={{0,2},{1,3},{2,0},{3,1},{4,6},{5,7},{6,4},{7,5},{8,10},{9,11},{10,... | collective-permute-start | bytes 147464 | tf_op jit(solution)/shard_map/ppermute | solution.py:523
  76.1 1.9 %collective-permute-start.21 = (f32[12,8,128]{2,1,0:T(8,128)S(1)}, f32[12,8,128]{2,1,0:T(8,128)S(1)}, u32[]{:S(2)}, u32[]{:S(2)}) collective-permute-start(f32[12,8,128]{2,1,0:T(8,128)S(1)} %broadcast_select_fusion), channel_id=1, source_target_pairs={{0,3},{1,2},{2,1},{3,0},{4,7},{5,6},{6,5},{7,4},{8,11},{9,10},{10,... | collective-permute-start | bytes 147464 | tf_op jit(solution)/shard_map/ppermute | solution.py:523
  78.1 3.6 %trailing_update.2.r_8_ = f32[4608,128]{1,0:T(8,128)} custom-call(s32[1]{0:T(128)} %copy.16.k_ref.r_0_, f32[1536,384]{1,0:T(8,128)S(1)} %get-tuple-element.148.r_1_, f32[1536,384]{1,0:T(8,128)S(1)} %collective-permute-done.18.r_2_, bf16[1536,384]{1,0:T(8,128)(2,1)S(1)} %get-tuple-element.165.r_3_, bf16[384,384]{1,0:T(8,128)(2,1)S(1)} %get-tuple-element.166.r_4_, ...), custom_call_target="tpu_custom_call" | custom-call | flops 1 | bytes 6000000 | tf_op jit(solution)/shard_map/trailing_update/pallas_call | solution.py:442
  82.3 2.8 %trailing_update.3 = f32[4608,128]{1,0:T(8,128)} custom-call(s32[1]{0:T(128)} %copy.16.k_ref.r_0_, f32[1536,384]{1,0:T(8,128)S(1)} %get-tuple-element.148.r_1_, f32[1536,384]{1,0:T(8,128)S(1)} %collective-permute-done.18.r_2_, bf16[1536,384]{1,0:T(8,128)(2,1)S(1)} %get-tuple-element.165.r_3_, ...), custom_call_target="tpu_custom_call", output_to_operand_aliasing={{}: (8, {})} | custom-call | flops 1 | bytes 6000000 | tf_op jit(solution)/shard_map/trailing_update/pallas_call | solution.py:442
  85.1 3.4 %collective-permute-done.22 = f32[12,8,128]{2,1,0:T(8,128)S(1)} collective-permute-done((f32[12,8,128]{2,1,0:T(8,128)S(1)}, f32[12,8,128]{2,1,0:T(8,128)S(1)}, u32[]{:S(2)}, u32[]{:S(2)}) %collective-permute-start.22) | collective-permute-done | bytes 49184 | tf_op jit(solution)/shard_map/ppermute | solution.py:481
  (46 shorter events, 4.4 us)
Async XLA Ops:
  2.0 10.9 %collective-permute-start.4 = (f32[8,128]{1,0:T(8,128)S(1)}, f32[8,128]{1,0:T(8,128)S(1)}, u32[]{:S(2)}, u32[]{:S(2)}) collective-permute-start(f32[8,128]{1,0:T(8,128)S(1)} %broadcast_in_dim.31), channel_id=1, source_target_pairs={{0,1},{1,0},{2,3},{3,2},{4,5},{5,4},{6,7},{7,6},{8,9},{9,8},{10,11... | collective-permute-start | bytes 12296 | tf_op jit(solution)/shard_map/ppermute | solution.py:481
  7.2 14.4 %collective-permute-start = (bf16[1536,128]{1,0:T(8,128)(2,1)}, bf16[1536,128]{1,0:T(8,128)(2,1)S(1)}, u32[]{:S(2)}, u32[]{:S(2)}) collective-permute-start(bf16[1536,128]{1,0:T(8,128)(2,1)} %get-tuple-element.87.r_0_), channel_id=1, source_target_pairs={{0,64},{1,65},{2,66},{3,67},{4,68},{5,69},{6,70},{7,71},{8,24},{9,... | collective-permute-start | bytes 1179656 | tf_op jit(solution)/shard_map/ppermute | solution.py:478
  8.8 12.8 %collective-permute-start.1 = (bf16[1536,128]{1,0:T(8,128)(2,1)}, bf16[1536,128]{1,0:T(8,128)(2,1)S(1)}, u32[]{:S(2)}, u32[]{:S(2)}) collective-permute-start(bf16[1536,128]{1,0:T(8,128)(2,1)} %get-tuple-element.88), channel_id=1, source_target_pairs={{0,192},{1,193},{2,194},{3,195},{4,196},{5,197},{6,198},{7,199},{8... | collective-permute-start | bytes 1179656 | tf_op jit(solution)/shard_map/ppermute | solution.py:478
  9.3 10.6 %collective-permute-start.2 = (bf16[768,128]{1,0:T(8,128)(2,1)}, bf16[768,128]{1,0:T(8,128)(2,1)S(1)}, u32[]{:S(2)}, u32[]{:S(2)}) collective-permute-start(bf16[768,128]{1,0:T(8,128)(2,1)} %get-tuple-element.89), channel_id=1, source_target_pairs={{0,128},{1,129},{2,130},{3,131},{4,132},{5,133},{6,134},{7,135},{8... | collective-permute-start | bytes 589832 | tf_op jit(solution)/shard_map/ppermute | solution.py:478
  11.4 10.2 %collective-permute-start.3 = (bf16[768,128]{1,0:T(8,128)(2,1)}, bf16[768,128]{1,0:T(8,128)(2,1)S(1)}, u32[]{:S(2)}, u32[]{:S(2)}) collective-permute-start(bf16[768,128]{1,0:T(8,128)(2,1)} %get-tuple-element.90), channel_id=1, source_target_pairs={{0,128},{1,129},{2,130},{3,131},{4,132},{5,133},{6,134},{7,135},{8... | collective-permute-start | bytes 589832 | tf_op jit(solution)/shard_map/ppermute | solution.py:478
  12.9 7.0 %collective-permute-start.5 = (f32[8,128]{1,0:T(8,128)S(1)}, f32[8,128]{1,0:T(8,128)S(1)}, u32[]{:S(2)}, u32[]{:S(2)}) collective-permute-start(f32[8,128]{1,0:T(8,128)S(1)} %broadcast_add_fusion), channel_id=1, source_target_pairs={{0,2},{1,3},{2,0},{3,1},{4,6},{5,7},{6,4},{7,5},{8,10},{9,11},{10,... | collective-permute-start | bytes 12296 | tf_op jit(solution)/shard_map/ppermute | solution.py:481
  16.1 1.0 %copy-start = (bf16[1536,128]{1,0:T(8,128)(2,1)S(1)}, bf16[1536,128]{1,0:T(8,128)(2,1)}, u32[]{:S(2)}) copy-start(bf16[1536,128]{1,0:T(8,128)(2,1)} %get-tuple-element.87.r_0_) | copy-start | bytes 1179652
  17.1 0.8 copy-start.1
  21.8 12.4 %collective-permute-start.8 = (bf16[2752,128]{1,0:T(8,128)(2,1)S(1)}, bf16[2752,128]{1,0:T(8,128)(2,1)S(1)}, u32[]{:S(2)}, u32[]{:S(2)}) collective-permute-start(bf16[2752,128]{1,0:T(8,128)(2,1)S(1)} %get-tuple-element.104), channel_id=1, source_target_pairs={{0,16},{1,17},{2,18},{3,19},{4,20},{5,21},{6,22},{7,23},{8,72},{9,... | collective-permute-start | bytes 2113544 | tf_op jit(solution)/shard_map/ppermute | solution.py:479
  23.4 11.1 %collective-permute-start.9 = (bf16[2752,128]{1,0:T(8,128)(2,1)S(1)}, bf16[2752,128]{1,0:T(8,128)(2,1)S(1)}, u32[]{:S(2)}, u32[]{:S(2)}) collective-permute-start(bf16[2752,128]{1,0:T(8,128)(2,1)S(1)} %get-tuple-element.105), channel_id=1, source_target_pairs={{0,48},{1,49},{2,50},{3,51},{4,52},{5,53},{6,54},{7,55},{8,200},{9... | collective-permute-start | bytes 2113544 | tf_op jit(solution)/shard_map/ppermute | solution.py:479
  25.2 23.7 %collective-permute-start.6 = (bf16[2752,128]{1,0:T(8,128)(2,1)S(1)}, bf16[2752,128]{1,0:T(8,128)(2,1)S(1)}, u32[]{:S(2)}, u32[]{:S(2)}) collective-permute-start(bf16[2752,128]{1,0:T(8,128)(2,1)S(1)} %get-tuple-element.101), channel_id=1, source_target_pairs={{0,16},{1,17},{2,18},{3,19},{4,20},{5,21},{6,22},{7,23},{8,72},{9,... | collective-permute-start | bytes 2113544 | tf_op jit(solution)/shard_map/ppermute | solution.py:479
  25.7 23.3 %collective-permute-start.7 = (bf16[2752,128]{1,0:T(8,128)(2,1)S(1)}, bf16[2752,128]{1,0:T(8,128)(2,1)S(1)}, u32[]{:S(2)}, u32[]{:S(2)}) collective-permute-start(bf16[2752,128]{1,0:T(8,128)(2,1)S(1)} %get-tuple-element.102), channel_id=1, source_target_pairs={{0,48},{1,49},{2,50},{3,51},{4,52},{5,53},{6,54},{7,55},{8,200},{9... | collective-permute-start | bytes 2113544 | tf_op jit(solution)/shard_map/ppermute | solution.py:479
  34.5 14.4 %collective-permute-start.10 = (f32[8,128]{1,0:T(8,128)S(1)}, f32[8,128]{1,0:T(8,128)S(1)}, u32[]{:S(2)}, u32[]{:S(2)}) collective-permute-start(f32[8,128]{1,0:T(8,128)S(1)} %fusion.1), channel_id=1, source_target_pairs={{0,6},{1,7},{2,4},{3,5},{4,2},{5,3},{6,0},{7,1},{8,14},{9,15},{10,... | collective-permute-start | bytes 12296 | tf_op jit(solution)/shard_map/ppermute | solution.py:481
  40.0 12.4 %collective-permute-start.13 = (bf16[1344,128]{1,0:T(8,128)(2,1)S(1)}, bf16[1344,128]{1,0:T(8,128)(2,1)S(1)}, u32[]{:S(2)}, u32[]{:S(2)}) collective-permute-start(bf16[1344,128]{1,0:T(8,128)(2,1)S(1)} %slice.14), channel_id=1, source_target_pairs={{0,16},{1,17},{2,18},{3,19},{4,20},{5,21},{6,22},{7,23},{8,72},{9,... | collective-permute-start | bytes 1032200 | tf_op jit(solution)/shard_map/ppermute | solution.py:479
  41.8 10.6 %collective-permute-start.14 = (bf16[1344,128]{1,0:T(8,128)(2,1)S(1)}, bf16[1344,128]{1,0:T(8,128)(2,1)S(1)}, u32[]{:S(2)}, u32[]{:S(2)}) collective-permute-start(bf16[1344,128]{1,0:T(8,128)(2,1)S(1)} %slice.15), channel_id=1, source_target_pairs={{0,48},{1,49},{2,50},{3,51},{4,52},{5,53},{6,54},{7,55},{8,200},{9... | collective-permute-start | bytes 1032200 | tf_op jit(solution)/shard_map/ppermute | solution.py:479
  49.0 11.4 %collective-permute-start.11 = (bf16[1344,128]{1,0:T(8,128)(2,1)S(1)}, bf16[1344,128]{1,0:T(8,128)(2,1)S(1)}, u32[]{:S(2)}, u32[]{:S(2)}) collective-permute-start(bf16[1344,128]{1,0:T(8,128)(2,1)S(1)} %slice.12), channel_id=1, source_target_pairs={{0,16},{1,17},{2,18},{3,19},{4,20},{5,21},{6,22},{7,23},{8,72},{9,... | collective-permute-start | bytes 1032200 | tf_op jit(solution)/shard_map/ppermute | solution.py:479
  49.5 10.9 %collective-permute-start.12 = (bf16[1344,128]{1,0:T(8,128)(2,1)S(1)}, bf16[1344,128]{1,0:T(8,128)(2,1)S(1)}, u32[]{:S(2)}, u32[]{:S(2)}) collective-permute-start(bf16[1344,128]{1,0:T(8,128)(2,1)S(1)} %slice.13), channel_id=1, source_target_pairs={{0,48},{1,49},{2,50},{3,51},{4,52},{5,53},{6,54},{7,55},{8,200},{9... | collective-permute-start | bytes 1032200 | tf_op jit(solution)/shard_map/ppermute | solution.py:479
  63.2 14.9 %copy-start.2 = (f32[12,1,128]{2,1,0:T(1,128)S(1)}, f32[12,1,128]{2,1,0:T(1,128)}, u32[]{:S(2)}) copy-start(f32[12,1,128]{2,1,0:T(1,128)} %param.12) | copy-start | bytes 18436
  63.2 1.4 %collective-permute-start.15 = (f32[144,128]{1,0:T(8,128)S(1)}, f32[144,128]{1,0:T(8,128)S(1)}, u32[]{:S(2)}, u32[]{:S(2)}) collective-permute-start(f32[144,128]{1,0:T(8,128)S(1)} %get-tuple-element.149.a_ref), channel_id=1, source_target_pairs={{0,8},{8,0},{1,9},{9,1},{2,10},{10,2},{3,11},{11,3},{4,12},{12,4},... | collective-permute-start | bytes 221192 | tf_op jit(solution)/shard_map/ppermute | solution.py:480
  64.6 7.1 %collective-permute-start.18 = (f32[1536,384]{1,0:T(8,128)S(1)}, f32[1536,384]{1,0:T(8,128)S(1)}, u32[]{:S(2)}, u32[]{:S(2)}) collective-permute-start(f32[1536,384]{1,0:T(8,128)S(1)} %get-tuple-element.155), channel_id=1, source_target_pairs={{0,8},{8,0},{1,9},{9,1},{2,10},{10,2},{3,11},{11,3},{4,12},{12,4},... | collective-permute-start | bytes 7077896 | tf_op jit(solution)/shard_map/ppermute | solution.py:480
  64.7 6.9 %collective-permute-start.16 = (f32[1536,256]{1,0:T(8,128)S(1)}, f32[1536,256]{1,0:T(8,128)S(1)}, u32[]{:S(2)}, u32[]{:S(2)}) collective-permute-start(f32[1536,256]{1,0:T(8,128)S(1)} %get-tuple-element.153.p_ref), channel_id=1, source_target_pairs={{0,8},{8,0},{1,9},{9,1},{2,10},{10,2},{3,11},{11,3},{4,12},{12,4},... | collective-permute-start | bytes 4718600 | tf_op jit(solution)/shard_map/ppermute | solution.py:480
  65.1 6.6 %collective-permute-start.17 = (f32[384,128]{1,0:T(8,128)S(1)}, f32[384,128]{1,0:T(8,128)S(1)}, u32[]{:S(2)}, u32[]{:S(2)}) collective-permute-start(f32[384,128]{1,0:T(8,128)S(1)} %get-tuple-element.154), channel_id=1, source_target_pairs={{0,8},{8,0},{1,9},{9,1},{2,10},{10,2},{3,11},{11,3},{4,12},{12,4},... | collective-permute-start | bytes 589832 | tf_op jit(solution)/shard_map/ppermute | solution.py:480
  73.7 8.1 %collective-permute-start.19 = (f32[12,8,128]{2,1,0:T(8,128)S(1)}, f32[12,8,128]{2,1,0:T(8,128)S(1)}, u32[]{:S(2)}, u32[]{:S(2)}) collective-permute-start(f32[12,8,128]{2,1,0:T(8,128)S(1)} %broadcast_select_fusion), channel_id=1, source_target_pairs={{0,1},{1,0},{2,3},{3,2},{4,5},{5,4},{6,7},{7,6},{8,9},{9,8},{10,11... | collective-permute-start | bytes 147464 | tf_op jit(solution)/shard_map/ppermute | solution.py:523
  74.7 7.0 %collective-permute-start.20 = (f32[12,8,128]{2,1,0:T(8,128)S(1)}, f32[12,8,128]{2,1,0:T(8,128)S(1)}, u32[]{:S(2)}, u32[]{:S(2)}) collective-permute-start(f32[12,8,128]{2,1,0:T(8,128)S(1)} %broadcast_select_fusion), channel_id=1, source_target_pairs={{0,2},{1,3},{2,0},{3,1},{4,6},{5,7},{6,4},{7,5},{8,10},{9,11},{10,... | collective-permute-start | bytes 147464 | tf_op jit(solution)/shard_map/ppermute | solution.py:523
  76.1 6.0 %collective-permute-start.21 = (f32[12,8,128]{2,1,0:T(8,128)S(1)}, f32[12,8,128]{2,1,0:T(8,128)S(1)}, u32[]{:S(2)}, u32[]{:S(2)}) collective-permute-start(f32[12,8,128]{2,1,0:T(8,128)S(1)} %broadcast_select_fusion), channel_id=1, source_target_pairs={{0,3},{1,2},{2,1},{3,0},{4,7},{5,6},{6,5},{7,4},{8,11},{9,10},{10,... | collective-permute-start | bytes 147464 | tf_op jit(solution)/shard_map/ppermute | solution.py:523
  82.2 6.3 %collective-permute-start.22 = (f32[12,8,128]{2,1,0:T(8,128)S(1)}, f32[12,8,128]{2,1,0:T(8,128)S(1)}, u32[]{:S(2)}, u32[]{:S(2)}) collective-permute-start(f32[12,8,128]{2,1,0:T(8,128)S(1)} %add_add_fusion), channel_id=1, source_target_pairs={{0,6},{1,7},{2,4},{3,5},{4,2},{5,3},{6,0},{7,1},{8,14},{9,15},{10,... | collective-permute-start | bytes 147464 | tf_op jit(solution)/shard_map/ppermute | solution.py:481
